TPU v7x, 32 devices: a whole 2x2x4 slice. The times are simulated.
32 devices in a mesh: docs: 8 (over z, x), heads: 4 (over y, core).
Axes of the slice: x: 2, y: 2, z: 4, core: 2. Of those that a mesh axis runs over, the one named last changes fastest.
Arguments:
- enc_out: bfloat16 [768, 512, 768], P('docs', 'heads'), may hold values from -6 to 6
- enc_len: int32 [384], replicated, may hold values from 64 to 512
- group_docs: int32 [8], replicated, may hold values from 1 to 96, 384 in all
- list_len: int32 [24], replicated, may hold values from 1 to 50, 384 in all
- relevance: float32 [384], replicated, may hold values from 0.1 to 10
- start_token: bfloat16 [768], replicated, may hold values from -6 to 6
- score_row: bfloat16 [768], replicated, may hold values from -6 to 6
- g_self: float32 [768], replicated, may hold values from 0.1 to 1.9
- w_value_self: bfloat16 [768, 768], P(None, 'heads'), may hold values from -0.21875 to 0.21875
- w_out_self: bfloat16 [768, 768], P('heads'), may hold values from -0.21875 to 0.21875
- g_cross: float32 [768], replicated, may hold values from 0.1 to 1.9
- w_query: bfloat16 [768, 768], P(None, 'heads'), may hold values from -0.0546875 to 0.0546875
- w_key: bfloat16 [768, 768], P(None, 'heads'), may hold values from -0.21875 to 0.21875
- w_value: bfloat16 [768, 768], P(None, 'heads'), may hold values from -0.21875 to 0.21875
- w_out: bfloat16 [768, 768], P('heads'), may hold values from -1.25 to 1.25
- g_ff: float32 [768], replicated, may hold values from 0.1 to 1.9
- w_in: bfloat16 [768, 3072], P(None, 'heads'), may hold values from -0.21875 to 0.21875
- w_down: bfloat16 [3072, 768], P('heads'), may hold values from -0.109375 to 0.109375
- g_final: float32 [768], replicated, may hold values from 0.1 to 1.9
Outputs:
- scores: float32 [384], replicated
- loss: float32 [], replicated
- enc_grad: bfloat16 [768, 512, 768], P('docs', 'heads')
- start_grad: float32 [768], replicated
- score_row_grad: float32 [768], replicated
- g_self_grad: float32 [768], replicated
- w_value_self_grad: float32 [768, 768], P(None, 'heads')
- w_out_self_grad: float32 [768, 768], P('heads')
- g_cross_grad: float32 [768], replicated
- w_query_grad: float32 [768, 768], P(None, 'heads')
- key_weight_gradient: float32 [768, 768], P(None, 'heads')
- value_weight_gradient: float32 [768, 768], P(None, 'heads')
- w_out_grad: float32 [768, 768], P('heads')
- g_ff_grad: float32 [768], replicated
- w_in_grad: float32 [768, 3072], P(None, 'heads')
- w_down_grad: float32 [3072, 768], P('heads')
- g_final_grad: float32 [768], replicated
Inputs may be any that keep to these rules, and one draw needn't show every extreme that they name: Group g holds documents S_g to S_g + group_docs[g] - 1 in its first slots, S_g the sum of group_docs over earlier groups; the counts total 384. Query j's list is the next list_len[j] documents after the earlier lists; the lengths total 384.
All inputs are finite; a program needn't handle non-finite values.
Results may differ from a plain program's by a relative error of at most 0.03.
Values may be sent and summed in bfloat16 or wider, within the bound.
No kernel may reach another device: no remote copies, remote signals or barrier semaphores. Data moves between devices by JAX's collectives and lax.ppermute only.
A program may use at most 256 MiB of HBM per device.

v0:
```python
import jax
import jax.numpy as jnp
from jax import lax
from jax.sharding import PartitionSpec as P

D = 768
HEADS = 12
HEAD_DIM = 64


EPSILON = 1e-06
MASKED = -1e30


def rms_parts(value_rows):
    scale = lax.rsqrt(jnp.mean(value_rows * value_rows, axis=-1, keepdims=True) + EPSILON)
    return (value_rows * scale, scale)


def rms_back(grad_normed, normed, scale):
    inner = jnp.mean(grad_normed * normed, axis=-1, keepdims=True)
    return scale * (grad_normed - normed * inner)


def row_dot(left, right):
    return jnp.dot(left, right, preferred_element_type=jnp.float32)


def left_dot(left, right):
    return lax.dot_general(
        left, right, (((0,), (0,)), ((), ())), preferred_element_type=jnp.float32
    )


def right_dot(left, right):
    return lax.dot_general(
        left, right, (((1,), (1,)), ((), ())), preferred_element_type=jnp.float32
    )


def gelu_exact(value_rows):
    return jax.nn.gelu(value_rows, approximate=False)


def attend_logits(enc_rows, kv_weight, query_vec, count, tokens, visible):
    inner_width = HEADS * HEAD_DIM
    keys_values = row_dot(enc_rows, kv_weight).astype(jnp.bfloat16)
    key_rows = keys_values[:, :inner_width].reshape(count, tokens, HEADS, HEAD_DIM)
    value_rows = keys_values[:, inner_width:].reshape(count, tokens, HEADS, HEAD_DIM)
    logits = jnp.einsum("mthd,hd->mht", key_rows, query_vec, preferred_element_type=jnp.float32)
    logits = jnp.where(visible[:, None, :], logits, MASKED)
    return (key_rows, value_rows, logits)


def list_terms(all_scores, list_len, relevance):
    list_ends = jnp.cumsum(list_len)
    begins = list_ends - list_len
    places = jnp.arange(all_scores.shape[0], dtype=jnp.int32)
    member = (places[None, :] >= begins[:, None]) & (places[None, :] < list_ends[:, None])
    owner = jnp.sum((places[None, :] >= list_ends[:, None]).astype(jnp.int32), axis=0)
    peak_val = jnp.max(jnp.where(member, all_scores[None, :], MASKED), axis=1)
    shifted = jnp.exp(all_scores - peak_val[owner])
    totals = jnp.sum(jnp.where(member, shifted[None, :], 0.0), axis=1)
    log_total = peak_val + jnp.log(totals)
    weight_sum = jnp.sum(jnp.where(member, relevance[None, :], 0.0), axis=1)
    target = relevance / weight_sum[owner]
    picked = jnp.sum(jnp.where(member, (target * all_scores)[None, :], 0.0), axis=1)
    loss_value = jnp.mean(log_total - picked)
    grad_all = (jnp.exp(all_scores - log_total[owner]) - target) / list_len.shape[0]
    return (loss_value, grad_all)


def per_device(
    enc_out,
    enc_len,
    group_docs,
    list_len,
    relevance,
    start_token,
    score_row,
    g_self,
    w_value_self,
    w_out_self,
    g_cross,
    w_query,
    w_key,
    w_value,
    w_out,
    g_ff,
    w_in,
    w_down,
    g_final,
):
    groups = lax.axis_size("docs")
    head_parts = lax.axis_size("heads")
    my_group = lax.axis_index("docs")
    my_part = lax.axis_index("heads")
    slot_count = enc_out.shape[0]
    docs_total = enc_len.shape[0]
    starts = jnp.cumsum(group_docs) - group_docs
    my_start = starts[my_group]
    my_count = group_docs[my_group]
    slot_index = jnp.arange(slot_count, dtype=jnp.int32)
    pair_slots = (slot_count + groups - 1) // groups
    balanced = docs_total // groups
    peer_index = jnp.arange(groups, dtype=jnp.int32)[:, None]
    ranking_index = jnp.arange(pair_slots, dtype=jnp.int32)[None, :]
    outgoing = jnp.minimum(
        (peer_index - my_start) % groups + ranking_index * groups, slot_count - 1
    ).reshape(-1)
    arrived = lax.all_to_all(enc_out[outgoing], "docs", split_axis=0, concat_axis=0, tiled=True)
    all_ids = (
        jnp.arange(balanced, dtype=jnp.int32)[None, :] * groups
        + jnp.arange(groups, dtype=jnp.int32)[:, None]
    )
    wanted = jnp.arange(balanced, dtype=jnp.int32) * groups + my_group
    source = jnp.sum((starts[None, :] <= wanted[:, None]).astype(jnp.int32), axis=1) - 1
    position = (wanted - starts[source]) // groups
    local_rows = arrived[source * pair_slots + position]
    per_part = local_rows.shape[0] // head_parts
    value_self, query_w, key_w, value_w, inner_w, out_self, out_w, down_w = (
        lax.all_gather(w_value_self, "heads", axis=1, tiled=True),
        lax.all_gather(w_query, "heads", axis=1, tiled=True),
        lax.all_gather(w_key, "heads", axis=1, tiled=True),
        lax.all_gather(w_value, "heads", axis=1, tiled=True),
        lax.all_gather(w_in, "heads", axis=1, tiled=True),
        lax.all_gather(w_out_self, "heads", axis=0, tiled=True),
        lax.all_gather(w_out, "heads", axis=0, tiled=True),
        lax.all_gather(w_down, "heads", axis=0, tiled=True),
    )
    start_vec = start_token.astype(jnp.float32)
    normed0, scale0 = rms_parts(start_vec)
    first_in = (normed0 * g_self).astype(jnp.bfloat16)
    self_value = row_dot(first_in, value_self).astype(jnp.bfloat16)
    hidden1 = start_vec + row_dot(self_value, out_self)
    normed1, scale1 = rms_parts(hidden1)
    second_in = (normed1 * g_cross).astype(jnp.bfloat16)
    query_vec = row_dot(second_in, query_w).astype(jnp.bfloat16).reshape(HEADS, HEAD_DIM)
    inner_width = HEADS * HEAD_DIM
    kv_weight = jnp.concatenate([key_w, value_w], axis=1)
    length_table = jnp.concatenate([enc_len, jnp.ones((1,), jnp.int32)])
    documents = lax.all_to_all(local_rows, "heads", split_axis=0, concat_axis=1, tiled=True)
    doc_ids = lax.dynamic_slice_in_dim(all_ids[my_group], my_part * per_part, per_part)
    tokens = documents.shape[1]
    enc_rows = documents.reshape(per_part * tokens, D)
    visible = jnp.arange(tokens, dtype=jnp.int32)[None, :] < length_table[doc_ids][:, None]
    key_rows, value_rows, logits = attend_logits(
        enc_rows, kv_weight, query_vec, per_part, tokens, visible
    )
    peak_val = jnp.max(logits, axis=-1, keepdims=True)
    raised = jnp.exp(logits - peak_val)
    attn_prob = raised / jnp.sum(raised, axis=-1, keepdims=True)
    weights_reduced = attn_prob.astype(jnp.bfloat16)
    context = (
        jnp.einsum("pzj,pjzk->pzk", weights_reduced, value_rows, preferred_element_type=jnp.float32)
        .astype(jnp.bfloat16)
        .reshape(per_part, inner_width)
    )
    hidden2 = hidden1[None, :] + row_dot(context, out_w)
    normed2, scale2 = rms_parts(hidden2)
    third_in = (normed2 * g_ff).astype(jnp.bfloat16)
    pre_act = row_dot(third_in, inner_w)
    activated, gelu_back = jax.vjp(gelu_exact, pre_act)
    act_low = activated.astype(jnp.bfloat16)
    hidden3 = hidden2 + row_dot(act_low, down_w)
    normed3, scale3 = rms_parts(hidden3)
    final_vec = normed3 * g_final
    row_vec = score_row.astype(jnp.float32)
    factor = D ** (-0.5)
    local_scores = jnp.sum(final_vec * row_vec[None, :], axis=1) * factor
    gathered = lax.all_gather(local_scores, ("docs", "heads"), axis=0, tiled=True)
    all_scores = (
        jnp.zeros((docs_total + 1,), jnp.float32).at[all_ids.reshape(-1)].set(gathered)[:docs_total]
    )
    loss_value, grad_all = list_terms(all_scores, list_len, relevance)
    grad_local = jnp.concatenate([grad_all, jnp.zeros((1,), jnp.float32)])[doc_ids]
    grad_final = grad_local[:, None] * factor * row_vec[None, :]
    row_grad = jnp.sum(grad_local[:, None] * factor * final_vec, axis=0)
    final_gain_grad = jnp.sum(grad_final * normed3, axis=0)
    grad_h3 = rms_back(grad_final * g_final, normed3, scale3).astype(jnp.bfloat16)
    down_grad = left_dot(act_low, grad_h3)
    (grad_act,) = gelu_back(right_dot(grad_h3, down_w))
    grad_act = grad_act.astype(jnp.bfloat16)
    inner_grad = left_dot(third_in, grad_act)
    grad_third = right_dot(grad_act, inner_w)
    ff_gain_grad = jnp.sum(grad_third * normed2, axis=0)
    grad_h2 = (grad_h3.astype(jnp.float32) + rms_back(grad_third * g_ff, normed2, scale2)).astype(
        jnp.bfloat16
    )
    out_grad = left_dot(context, grad_h2)
    context_gradient = (
        right_dot(grad_h2, out_w).astype(jnp.bfloat16).reshape(per_part, HEADS, HEAD_DIM)
    )
    value_grads = jnp.einsum(
        "wps,wpg->wspg", weights_reduced, context_gradient, preferred_element_type=jnp.float32
    ).astype(jnp.bfloat16)
    grad_probs = jnp.einsum(
        "vok,viok->voi", context_gradient, value_rows, preferred_element_type=jnp.float32
    )
    local_inner = jnp.sum(attn_prob * grad_probs, axis=-1)
    grad_logits = (attn_prob * (grad_probs - local_inner[..., None])).astype(jnp.bfloat16)
    query_grad_part = jnp.einsum(
        "mht,mthd->hd", grad_logits, key_rows, preferred_element_type=jnp.float32
    ).reshape(inner_width)
    key_grads = jnp.einsum(
        "mht,hd->mthd", grad_logits, query_vec, preferred_element_type=jnp.float32
    ).astype(jnp.bfloat16)
    grad_pairs = jnp.concatenate(
        [
            key_grads.reshape(per_part * tokens, inner_width),
            value_grads.reshape(per_part * tokens, inner_width),
        ],
        axis=1,
    )
    pair_grad = left_dot(enc_rows, grad_pairs)
    enc_grad_local = (
        right_dot(grad_pairs, kv_weight).astype(jnp.bfloat16).reshape(per_part, tokens, D)
    )
    summed_h2 = jnp.sum(grad_h2.astype(jnp.float32), axis=0)
    head_cols = inner_width // head_parts
    returned = lax.all_to_all(enc_grad_local, "heads", split_axis=1, concat_axis=0, tiled=True)
    key_portion, value_share, inner_share, out_share, down_share = (
        lax.psum_scatter(
            pair_grad[:, :inner_width].astype(jnp.bfloat16),
            "heads",
            scatter_dimension=1,
            tiled=True,
        ).astype(jnp.float32),
        lax.psum_scatter(
            pair_grad[:, inner_width:].astype(jnp.bfloat16),
            "heads",
            scatter_dimension=1,
            tiled=True,
        ).astype(jnp.float32),
        lax.psum_scatter(
            inner_grad.astype(jnp.bfloat16), "heads", scatter_dimension=1, tiled=True
        ).astype(jnp.float32),
        lax.psum_scatter(
            out_grad.astype(jnp.bfloat16), "heads", scatter_dimension=0, tiled=True
        ).astype(jnp.float32),
        lax.psum_scatter(
            down_grad.astype(jnp.bfloat16), "heads", scatter_dimension=0, tiled=True
        ).astype(jnp.float32),
    )
    counted = jnp.ones((), jnp.float32)
    key_total, value_total, inner_total, out_total, down_total = lax.psum(
        (key_portion, value_share, inner_share, out_share, down_share), "docs"
    )
    query_total_vec, h2_total, row_total, ff_gain_total, final_gain_total = lax.psum(
        (
            query_grad_part,
            summed_h2 * counted,
            row_grad * counted,
            ff_gain_grad * counted,
            final_gain_grad * counted,
        ),
        ("docs", "heads"),
    )
    own_query = lax.dynamic_slice_in_dim(query_total_vec, my_part * head_cols, head_cols)
    query_total = second_in.astype(jnp.float32)[:, None] * own_query[None, :]
    grad_second = jnp.sum(query_w.astype(jnp.float32) * query_total_vec[None, :], axis=1)
    cross_gain_total = grad_second * normed1
    grad_h1 = h2_total + rms_back(grad_second * g_cross, normed1, scale1)
    own_self_value = lax.dynamic_slice_in_dim(
        self_value.astype(jnp.float32), my_part * head_cols, head_cols
    )
    os_total = own_self_value[:, None] * grad_h1[None, :]
    grad_value_self = jnp.sum(out_self.astype(jnp.float32) * grad_h1[None, :], axis=1)
    own_value_self = lax.dynamic_slice_in_dim(grad_value_self, my_part * head_cols, head_cols)
    vs_total = first_in.astype(jnp.float32)[:, None] * own_value_self[None, :]
    grad_first = jnp.sum(value_self.astype(jnp.float32) * grad_value_self[None, :], axis=1)
    self_gain_total = grad_first * normed0
    start_total = grad_h1 + rms_back(grad_first * g_self, normed0, scale0)
    sender_index = jnp.arange(groups, dtype=jnp.int32)[:, None]
    doc_number = (
        starts[sender_index] + (my_group - starts[sender_index]) % groups + ranking_index * groups
    )
    take_index = jnp.minimum(doc_number // groups, balanced - 1).reshape(-1)
    homecoming = lax.all_to_all(
        returned[take_index], "docs", split_axis=0, concat_axis=0, tiled=True
    )
    fetch = (my_start + slot_index) % groups * pair_slots + slot_index // groups
    enc_grad = jnp.where(
        (slot_index < my_count)[:, None, None], homecoming[fetch], jnp.zeros((), jnp.bfloat16)
    )
    return (
        all_scores,
        loss_value,
        enc_grad,
        start_total,
        row_total,
        self_gain_total,
        vs_total,
        os_total,
        cross_gain_total,
        query_total,
        key_total,
        value_total,
        out_total,
        ff_gain_total,
        inner_total,
        down_total,
        final_gain_total,
    )


def solution(mesh):
    placed = (
        P("docs", "heads", None),
        P(),
        P(),
        P(),
        P(),
        P(),
        P(),
        P(),
        P(None, "heads"),
        P("heads", None),
        P(),
        P(None, "heads"),
        P(None, "heads"),
        P(None, "heads"),
        P("heads", None),
        P(),
        P(None, "heads"),
        P("heads", None),
        P(),
    )
    return jax.shard_map(
        per_device,
        mesh=mesh,
        in_specs=placed,
        out_specs=(
            P(),
            P(),
            P("docs", "heads", None),
            P(),
            P(),
            P(),
            P(None, "heads"),
            P("heads", None),
            P(),
            P(None, "heads"),
            P(None, "heads"),
            P(None, "heads"),
            P("heads", None),
            P(),
            P(None, "heads"),
            P("heads", None),
            P(),
        ),
        check_vma=False,
    )
```

profile of v0, /device:TPU:0, one launch (start us, length us, event | category | flops | bytes accessed | tf_op | source)
XLA Modules:
  0.0 1925.6 jit_solution(7985458981345871358)
XLA Ops:
  11.4 15.8 gather_fusion.1
  27.2 7.3 all-to-all-start
  39.3 5.2 fusion.61
  44.5 398.2 %all-to-all-done = bf16[96,128,768]{2,1,0:T(8,128)(2,1)} async-done(((bf16[96,128,768]{2,1,0:T(8,128)(2,1)}), bf16[96,128,768]{2,1,0:T(8,128)(2,1)}, u32[]{:S(2)}, u32[]{:S(2)}) %all-to-all-start) | async-done | bytes 18874400 | tf_op jit(solution)/shard_map/all_to_all | solution.py:111
  442.7 12.9 gather_fusion.2
  455.7 6.0 all-to-all-start.1
  465.7 1.7 convolution_reduce_fusion.2
  468.0 1.6 convolution_reduce_fusion.1
  471.5 1.8 convolution_reduce_fusion
  473.5 1.4 constant_dynamic-update-slice_fusion.1
  474.9 1.3 constant_dynamic-update-slice_fusion
  476.2 115.1 %all-to-all-done.1 = bf16[48,128,768]{2,1,0:T(8,128)(2,1)} async-done(((bf16[48,128,768]{2,1,0:T(8,128)(2,1)}), bf16[48,128,768]{2,1,0:T(8,128)(2,1)}, u32[]{:S(2)}, u32[]{:S(2)}) %all-to-all-start.1) | async-done | bytes 9437216 | tf_op jit(solution)/shard_map/all_to_all | solution.py:142
  591.3 8.3 copy.64
  599.6 22.2 %convolution_convert_fusion = bf16[6144,1536]{1,0:T(8,128)(2,1)} fusion(bf16[6144,768]{1,0:T(8,128)(2,1)} %bitcast.232, bf16[768,1536]{0,1:T(8,128)(2,1)S(1)} %constant_dynamic-update-slice_fusion), kind=kOutput, calls=%fused_computation.13 | convolution fusion | flops 14504951808 | bytes 30670848 | tf_op jit(solution)/shard_map/dot_general | solution.py:26
  621.8 14.5 fusion.79
  636.3 28.7 %reshape.956 = bf16[12,512,12,64]{3,2,1,0:T(8,128)(2,1)} reshape(bf16[6144,768]{1,0:T(8,128)(2,1)} %get-tuple-element.156) | data formatting | bytes 18874368 | tf_op jit(solution)/shard_map/reshape | solution.py:48
  665.1 26.2 %copy.75 = bf16[12,512,12,64]{1,3,0,2:T(8,128)(2,1)} copy(bf16[12,512,12,64]{3,2,1,0:T(8,128)(2,1)} %reshape.956) | data formatting | bytes 18874368 | tf_op jit(solution)/shard_map/reshape | solution.py:48
  691.3 28.7 %reshape.957 = bf16[12,512,12,64]{3,2,1,0:T(8,128)(2,1)} reshape(bf16[6144,768]{1,0:T(8,128)(2,1)} %get-tuple-element.157) | data formatting | bytes 18874368 | tf_op jit(solution)/shard_map/reshape | solution.py:49
  720.0 25.9 %copy.78 = bf16[12,512,12,64]{1,3,2,0:T(8,128)(2,1)} copy(bf16[12,512,12,64]{3,2,1,0:T(8,128)(2,1)} %reshape.957) | data formatting | bytes 18874368 | tf_op jit(solution)/shard_map/reshape | solution.py:49
  745.9 5.0 fusion.88
  751.2 6.2 fusion.14
  757.6 1.7 multiply_reduce_fusion.8
  759.4 3.4 multiply_convert_fusion.2
  762.8 3.3 multiply_reduce_fusion.7
  766.5 37.5 %all-reduce = f32[384]{0:T(512)S(1)} all-reduce(f32[384]{0:T(512)S(1)} %multiply_dynamic-update-slice_fusion), channel_id=1, replica_groups=mesh['docs'=8,'heads'=4] {'docs','heads'}, use_global_device_ids=true, to_apply=%add | all-reduce | flops 384 | bytes 3072
  804.0 2.9 scatter_custom_fusion
  808.5 4.5 select_reduce_fusion.6
  813.1 10.8 fusion.46
  826.9 8.8 select_reduce_fusion.4
  835.7 22.0 %fusion.45 = (f32[384]{0:T(512)S(1)}, f32[384]{0:T(512)}) fusion(pred[384]{0:T(512)(128)(4,1)S(1)} %get-tuple-element.125, pred[384]{0:T(512)(128)(4,1)S(1)} %get-tuple-element.124, pred[384]{0:T(512)(128)(4,1)S(1)} %get-tuple-element.121, pred[384]{0:T(512)(128)(4,1)S(1)} %get-tuple-element.122, pred[384]{0:T(512)(128)(4,1)S(1)} %get-tuple-element.123, ...), kind=kLoop, calls=%fused_computation.166 | loop fusion | flops 14592 | bytes 15880 | tf_op jit(solution)/shard_map/div | solution.py:69
  859.1 3.7 add_convert_fusion
  862.8 4.3 multiply_reduce_fusion.3
  868.5 5.0 fusion.89
  873.9 5.9 multiply_convert_fusion
  879.8 19.2 copy.94
  899.1 7.0 multiply_convert_fusion.1
  906.1 19.4 %copy.93 = bf16[96,8,12,512]{3,1,2,0:T(8,128)(2,1)} copy(bf16[96,8,12,512]{3,2,1,0:T(8,128)(2,1)} %bitcast.229) | data formatting | bytes 18874368
  925.5 8.6 constant_dynamic-update-slice_fusion.3
  934.1 8.8 constant_dynamic-update-slice_fusion.2
  942.9 18.4 convolution_convert_fusion.1
  961.3 30.9 %copy.69 = bf16[12,512,768]{2,0,1:T(8,128)(2,1)S(1)} copy(bf16[12,512,768]{2,1,0:T(8,128)(2,1)S(1)} %bitcast.234) | data formatting | bytes 18874368 | tf_op jit(solution)/shard_map/reshape | solution.py:217
  992.2 142.4 %all_to_all.43 = bf16[12,512,768]{2,0,1:T(8,128)(2,1)} all-to-all(bf16[12,512,768]{2,0,1:T(8,128)(2,1)S(1)} %copy.69), channel_id=1, replica_groups=mesh['docs'=8,'heads'=4] {'heads'}, dimensions={1} | all-to-all | bytes 18874368 | tf_op jit(solution)/shard_map/all_to_all | solution.py:221
  1134.6 11.9 copy.71
  1146.5 13.1 gather_fusion.5
  1159.6 6.0 all-to-all-start.3
  1165.6 20.8 %convolution_convert_fusion.4 = bf16[768,1536]{1,0:T(8,128)(2,1)S(1)} fusion(bf16[6144,768]{1,0:T(8,128)(2,1)} %bitcast.233, bf16[6144,1536]{0,1:T(8,128)(2,1)} %constant_dynamic-update-slice_fusion.2), kind=kOutput, calls=%fused_computation.18 | convolution fusion | flops 14496694272 | bytes 30670848 | tf_op jit(solution)/shard_map/dot_general | solution.py:30
  1186.6 1.5 copy.91
  1188.1 1.5 copy.89
  1189.9 1.5 convolution_convert_fusion.5
  1191.5 3.5 convolution_convert_fusion.2
  1195.1 4.8 convolution_convert_fusion.3
  1199.9 1.3 dynamic_slice.24
  1204.9 6.3 fusion.12
  1211.9 1.4 reshape.648
  1213.2 380.6 %all-reduce.1 = (f32[768]{0:T(1024)}, f32[768]{0:T(1024)}, f32[768]{0:T(1024)}, f32[768]{0:T(1024)}, f32[768]{0:T(1024)}) all-reduce(f32[768]{0:T(1024)} %get-tuple-element.146, f32[768]{0:T(1024)} %reshape.648, f32[768]{0:T(1024)} %get-tuple-element.106, ...), channel_id=1, replica_groups=mesh['docs'=8,'heads'=4] {'docs','heads'}, use_global_device_ids=true, to_apply=%region_21.22 | all-reduce | flops 3840 | bytes 30720 | tf_op jit(solution)/shard_map/psum | solution.py:249
  1593.8 1.3 dynamic_slice.27
  1596.2 1.9 multiply_reduce_fusion.9
  1600.1 1.9 fusion.38
  1606.1 1.6 broadcast_multiply_fusion.1
  1607.7 1.6 broadcast_multiply_fusion.2
  1609.3 1.6 broadcast_multiply_fusion
  1613.3 269.3 %all-reduce.4 = (f32[768,192]{1,0:T(8,128)S(1)}, f32[768,192]{1,0:T(8,128)S(1)}, f32[192,768]{1,0:T(8,128)}, f32[768,768]{1,0:T(8,128)}, f32[768,768]{1,0:T(8,128)}) all-reduce(bf16[768,192]{1,0:T(8,128)(2,1)S(1)} %copy.90, bf16[768,192]{1,0:T(8,128)(2,1)S(1)} %copy.92, ...), channel_id=1, replica_groups=mesh['docs'=8,'heads'=4] {'docs'}, use_global_device_ids=true, to_apply=%region_31.32 | all-reduce | flops 1622016 | bytes 9732096 | tf_op jit(solution)/shard_map/psum | solution.py:246
  1884.7 15.9 gather_fusion.6
  1900.6 16.9 broadcast_select_fusion
  (188 shorter events, 37.4 us)
Async XLA Ops:
  27.2 415.5 %all-to-all-start = ((bf16[96,128,768]{2,1,0:T(8,128)(2,1)}), bf16[96,128,768]{2,1,0:T(8,128)(2,1)}, u32[]{:S(2)}, u32[]{:S(2)}) async-start(bf16[96,128,768]{2,1,0:T(8,128)(2,1)} %gather_fusion.1), calls=%async_computation | async-start | bytes 37748736 | tf_op jit(solution)/shard_map/all_to_all | solution.py:111
  34.5 431.2 %all-gather.9.cloned.1.call-start = ((), (), s32[]{:S(2)}) async-start(), calls=%async_computation.9 | async-start | bytes 1474560 | tf_op jit(solution)/shard_map/all_gather | solution.py:122
  35.2 432.8 %all-gather.11.cloned.1.call-start = ((), (), s32[]{:S(2)}) async-start(), calls=%async_computation.10 | async-start | bytes 1474560 | tf_op jit(solution)/shard_map/all_gather | solution.py:127
  36.0 435.5 %all-gather.13.cloned.1.call-start = ((), (), s32[]{:S(2)}) async-start(), calls=%async_computation.11 | async-start | bytes 1474560 | tf_op jit(solution)/shard_map/all_gather | solution.py:123
  36.7 436.8 %all-gather.15.cloned.1.call-start = ((), (), s32[]{:S(2)}) async-start(), calls=%async_computation.12 | async-start | bytes 1474560 | tf_op jit(solution)/shard_map/all_gather | solution.py:124
  37.3 437.6 %all-gather.17.cloned.1.call-start = ((), (), s32[]{:S(2)}) async-start(), calls=%async_computation.13 | async-start | bytes 1474560 | tf_op jit(solution)/shard_map/all_gather | solution.py:125
  37.9 719.7 %all-gather.19.cloned.1.call-start = ((), (), s32[]{:S(2)}) async-start(), calls=%async_computation.14 | async-start | bytes 1474560 | tf_op jit(solution)/shard_map/all_gather | solution.py:128
  38.4 720.9 %all-gather.21.cloned.1.call-start = ((), (), s32[]{:S(2)}) async-start(), calls=%async_computation.15 | async-start | bytes 5898240 | tf_op jit(solution)/shard_map/all_gather | solution.py:126
  455.6 6.8 copy-start.13
  455.6 8.2 copy-start.23
  455.6 8.2 copy-start.16
  455.6 8.8 copy-start.26
  455.6 9.2 copy-start.24
  455.6 15.3 copy-start.17
  455.7 135.6 %all-to-all-start.1 = ((bf16[48,128,768]{2,1,0:T(8,128)(2,1)}), bf16[48,128,768]{2,1,0:T(8,128)(2,1)}, u32[]{:S(2)}, u32[]{:S(2)}) async-start(bf16[48,128,768]{2,1,0:T(8,128)(2,1)} %gather_fusion.2), calls=%async_computation.1 | async-start | bytes 18874368 | tf_op jit(solution)/shard_map/all_to_all | solution.py:142
  461.6 301.1 %all-gather.23.cloned.1.call-start = ((), (), s32[]{:S(2)}) async-start(), calls=%async_computation.16 | async-start | bytes 5898240 | tf_op jit(solution)/shard_map/all_gather | solution.py:129
  464.7 359.2 %copy-start.19 = (s32[24]{0:T(128)}, s32[24]{0:T(128)S(1)}, u32[]{:S(2)}) copy-start(s32[24]{0:T(128)S(1)} %reduce.4) | copy-start | bytes 292
  464.7 359.2 %copy-start.21 = (s32[24]{0:T(128)}, s32[24]{0:T(128)S(1)}, u32[]{:S(2)}) copy-start(s32[24]{0:T(128)S(1)} %sub.111) | copy-start | bytes 292
  467.4 0.6 copy-start.18
  470.2 287.4 %copy-start.9 = (f32[768]{0:T(1024)}, f32[768]{0:T(1024)S(1)}, u32[]{:S(2)}) copy-start(f32[768]{0:T(1024)S(1)} %get-tuple-element.155) | copy-start | bytes 9220
  476.2 123.3 %copy-start.7 = (bf16[768,1536]{0,1:T(8,128)(2,1)}, bf16[768,1536]{0,1:T(8,128)(2,1)S(1)}, u32[]{:S(2)}) copy-start(bf16[768,1536]{0,1:T(8,128)(2,1)S(1)} %constant_dynamic-update-slice_fusion) | copy-start | bytes 7077892
  750.9 8.4 copy-start.15
  751.2 14.8 copy-start.11
  751.2 72.7 %copy-start.20 = (f32[384]{0:T(512)S(1)}, f32[384]{0:T(512)}, u32[]{:S(2)}) copy-start(f32[384]{0:T(512)} %param.23) | copy-start | bytes 4612
  759.3 107.8 %copy-start.4 = (f32[12,768]{1,0:T(8,128)}, f32[12,768]{1,0:T(8,128)S(1)}, u32[]{:S(2)}) copy-start(f32[12,768]{1,0:T(8,128)S(1)} %get-tuple-element.248) | copy-start | bytes 110596
  759.3 107.8 %copy-start.22 = (f32[12]{0:T(128)}, f32[12]{0:T(128)S(1)}, u32[]{:S(2)}) copy-start(f32[12]{0:T(128)S(1)} %add_rsqrt_fusion.1) | copy-start | bytes 148
  762.7 105.1 %copy-start.3 = (bf16[768,768]{1,0:T(8,128)(2,1)S(1)}, bf16[768,768]{1,0:T(8,128)(2,1)}, u32[]{:S(2)}) copy-start(bf16[768,768]{1,0:T(8,128)(2,1)} %all-gather.19.cloned.1.call-done) | copy-start | bytes 3538948
  806.9 795.7 %copy-start.12 = (f32[385]{0:T(512)}, f32[385]{0:T(512)S(1)}, u32[]{:S(2)}) copy-start(f32[385]{0:T(512)S(1)} %scatter_custom_fusion) | copy-start | bytes 4624
  862.8 10.7 copy-start.5
  873.7 25.4 %copy-start.6 = (bf16[12,12,512]{2,0,1:T(8,128)(2,1)}, bf16[12,12,512]{2,0,1:T(8,128)(2,1)S(1)}, u32[]{:S(2)}) copy-start(bf16[12,12,512]{2,0,1:T(8,128)(2,1)S(1)} %fusion.8) | copy-start | bytes 442372
  934.1 8.8 copy-start.8
  1159.6 725.1 %all-to-all-start.3 = ((bf16[96,128,768]{2,1,0:T(8,128)(2,1)}), bf16[96,128,768]{2,1,0:T(8,128)(2,1)}, u32[]{:S(2)}, u32[]{:S(2)}) async-start(bf16[96,128,768]{2,1,0:T(8,128)(2,1)} %gather_fusion.5), calls=%async_computation.3 | async-start | bytes 37748736 | tf_op jit(solution)/shard_map/all_to_all | solution.py:279
  1165.6 445.3 %reduce-scatter.18.cloned.1.call-start = ((), (), s32[]{:S(2)}) async-start(), calls=%async_computation.21 | async-start | bytes 1474560
  1188.0 424.0 %reduce-scatter.16.cloned.1.call-start = ((), (), s32[]{:S(2)}) async-start(), calls=%async_computation.20 | async-start | bytes 1474560
  1189.6 423.6 %reduce-scatter.10.cloned.1.call-start = ((), (), s32[]{:S(2)}) async-start(), calls=%async_computation.17 | async-start | bytes 1474560 | tf_op jit(solution)/shard_map/reduce_scatter | solution.py:238
  1191.4 421.8 %reduce-scatter.14.cloned.1.call-start = ((), (), s32[]{:S(2)}) async-start(), calls=%async_computation.19 | async-start | bytes 5898240 | tf_op jit(solution)/shard_map/reduce_scatter | solution.py:241
  1195.0 400.1 %copy-start.2 = (bf16[768,768]{0,1:T(8,128)(2,1)S(1)}, bf16[768,768]{0,1:T(8,128)(2,1)}, u32[]{:S(2)}) copy-start(bf16[768,768]{0,1:T(8,128)(2,1)} %all-gather.13.cloned.1.call-done) | copy-start | bytes 3538948
  1195.0 401.1 %copy-start.10 = (f32[768]{0:T(1024)S(1)}, f32[768]{0:T(1024)}, u32[]{:S(2)}) copy-start(f32[768]{0:T(1024)} %copy-done.9) | copy-start | bytes 9220
  1195.1 404.3 %copy-start.1 = (bf16[768,768]{1,0:T(8,128)(2,1)S(1)}, bf16[768,768]{1,0:T(8,128)(2,1)}, u32[]{:S(2)}) copy-start(bf16[768,768]{1,0:T(8,128)(2,1)} %all-gather.11.cloned.1.call-done) | copy-start | bytes 3538948
  1195.1 418.2 %reduce-scatter.12.cloned.1.call-start = ((), (), s32[]{:S(2)}) async-start(), calls=%async_computation.18 | async-start | bytes 5898240 | tf_op jit(solution)/shard_map/reduce_scatter | solution.py:235
  1199.9 399.9 %copy-start = (bf16[768,768]{0,1:T(8,128)(2,1)S(1)}, bf16[768,768]{0,1:T(8,128)(2,1)}, u32[]{:S(2)}) copy-start(bf16[768,768]{0,1:T(8,128)(2,1)} %all-gather.9.cloned.1.call-done) | copy-start | bytes 3538948
  1199.9 400.2 %copy-start.14 = (bf16[768]{0:T(1024)(128)(2,1)S(1)}, bf16[768]{0:T(1024)(128)(2,1)}, u32[]{:S(2)}) copy-start(bf16[768]{0:T(1024)(128)(2,1)} %param.24) | copy-start | bytes 4612
  1884.7 15.9 copy-start.25
Sparse Core Ops, SparseCore 0:
  36.9 18.9 all-gather.8
  57.4 17.4 all-gather.10
  76.4 17.4 all-gather.12
  95.4 17.4 all-gather.14
  114.3 17.4 all-gather.16
  133.2 17.4 all-gather.18
  152.2 37.4 all-gather.20
  464.0 62.2 all-gather.22
  1188.2 26.1 reduce-scatter.17
  1217.5 25.7 reduce-scatter.15
  1245.8 25.7 reduce-scatter.9
  1274.1 48.0 reduce-scatter.13
  1325.3 47.8 reduce-scatter.11
where the time goes:
time: 1940 us; the launch traced here: 1930 us
  blocking collectives  830 us (43%)
  waiting for transfers between devices  519 us (27%)
  local copies, waits for them, and re-layouts  317 us (16%)
  matrix products  116 us (6%)
  other arithmetic  106 us (5%)
  starting transfers between devices  19.9 us (1%)
  between operations  19.5 us (1%)
    all_to_all x1, waiting for transfers between devices, per_device(): lax.all_to_all(enc_out[outgoing], 'docs', split_axis=0, concat_axis=0, ti...  398 us
    psum x1, blocking collectives, per_device(): lax.psum((query_grad_part, summed_h2 * counted, row_grad * counted, ff_ga...  381 us
    psum x1, blocking collectives, per_device(): lax.psum((key_portion, value_share, inner_share, out_share, down_share),...  269 us
    all_to_all x1, blocking collectives, per_device(): lax.all_to_all(enc_grad_local, 'heads', split_axis=1, concat_axis=0, tile...  142 us
    all_to_all x1, waiting for transfers between devices, per_device(): lax.all_to_all(local_rows, 'heads', split_axis=0, concat_axis=1, tiled=True)  115 us
    unnamed x65, local copies, waits for them, and re-layouts  56.6 us
    reshape x2, local copies, waits for them, and re-layouts, attend_logits(): keys_values[:, :inner_width].reshape(count, tokens, HEADS, HEAD_DIM)  55 us
    reshape x2, local copies, waits for them, and re-layouts, attend_logits(): keys_values[:, inner_width:].reshape(count, tokens, HEADS, HEAD_DIM)  54.6 us
  transfers between devices with their start and end apart: 16, of which 2 were waited for; matrix products, arithmetic and copies ran while one was open for 14% of the time, Pallas kernels for 0%

commit v1 on v0

v1 whole, which is shorter than its diff:
```python
import functools

import jax
import jax.numpy as jnp
from jax import lax
from jax.experimental import pallas as pl
from jax.experimental.pallas import tpu as pltpu
from jax.sharding import PartitionSpec as P

D = 768
HEADS = 12
HEAD_DIM = 64
ROWS = 16
BLOCK = 16
LANES = 128

EPSILON = 1e-06
MASKED = -1e30
FACTOR = D ** (-0.5)
ROOT_HALF = 0.5**0.5
DENSITY = 0.3989422804014327
f32, bf16, i32 = jnp.float32, jnp.bfloat16, jnp.int32
EXACT = lax.Precision.HIGHEST
MIB = 1 << 20


def nn(a, b, precision=None):
    return lax.dot_general(
        a, b, (((1,), (0,)), ((), ())), precision=precision, preferred_element_type=f32
    )


def nt(a, b, precision=None):
    return lax.dot_general(
        a, b, (((1,), (1,)), ((), ())), precision=precision, preferred_element_type=f32
    )


def tn(a, b, precision=None):
    return lax.dot_general(
        a, b, (((0,), (0,)), ((), ())), precision=precision, preferred_element_type=f32
    )


def iota(shape, dim):
    return lax.broadcasted_iota(i32, shape, dim)


def split2(x):
    high = x.astype(bf16)
    return high, (x - high.astype(f32)).astype(bf16)


def split3(x):
    high = x.astype(bf16)
    rest = x - high.astype(f32)
    mid = rest.astype(bf16)
    return high, mid, (rest - mid.astype(f32)).astype(bf16)


def stack3(row, height=ROWS):
    at = iota((height, row.shape[1]), 0)
    parts = split3(row)
    zero = jnp.zeros((), f32)
    out = jnp.where(at == 0, parts[0].astype(f32), zero)
    out = jnp.where(at == 1, parts[1].astype(f32), out)
    return jnp.where(at == 2, parts[2].astype(f32), out).astype(bf16)


def repeat3(row, height=ROWS):
    at = iota((height, row.shape[1]), 0)
    return jnp.where(at < 3, row.astype(f32), 0.0).astype(bf16)


def rms_parts(rows):
    scale = lax.rsqrt(jnp.mean(rows * rows, axis=-1, keepdims=True) + EPSILON)
    return rows * scale, scale


def rms_back(grad_normed, normed, scale):
    inner = jnp.mean(grad_normed * normed, axis=-1, keepdims=True)
    return scale * (grad_normed - normed * inner)


def phi(z):
    return 0.5 * (1.0 + lax.erf(z * ROOT_HALF))


def gelu_slope(z):
    return phi(z) + z * (DENSITY * jnp.exp(-0.5 * z * z))


def head_of(shape, dim):
    return iota(shape, dim) // HEAD_DIM


def spread(small):
    hot = (iota((LANES, D), 0) == head_of((LANES, D), 1)).astype(f32)
    return nn(small, hot, EXACT)


def self_kernel(start, g_self, wvs, wos, part_out, s1_out, y1_out):
    x0 = start[...].astype(f32)
    n0, _ = rms_parts(x0)
    y1 = jnp.broadcast_to(n0 * g_self[...], (ROWS, D)).astype(bf16)
    s1 = nn(y1, wvs[...]).astype(bf16)
    part_out[...] = nn(s1, wos[...])[:8]
    s1_out[...] = s1
    y1_out[...] = y1


def query_kernel(scal, part_a, part_b, start, g_cross, wq, wk, qk_out, h1_out, q_out, y2_out):
    h1 = start[...].astype(f32) + (part_a[0:1] + part_b[0:1])
    n1, _ = rms_parts(h1)
    y2 = jnp.broadcast_to(n1 * g_cross[...], (ROWS, D)).astype(bf16)
    q = nn(y2, wq[...]).astype(bf16)
    width = q.shape[1]
    first = scal[0] * (width // HEAD_DIM)
    own = iota((ROWS, width), 0) == first + head_of((ROWS, width), 1)
    qm = jnp.where(own, q.astype(f32), 0.0).astype(bf16)
    qk_out[...] = nt(qm, wk[...])
    h1_out[...] = h1
    q_out[...] = qm
    y2_out[...] = y2


def select_docs(height, width):
    r, c = iota((height, width), 0), iota((height, width), 1)
    return (((r // BLOCK) == (c % ROWS)) & ((r % BLOCK) == (c // ROWS))).astype(bf16)


def attend_kernel(scal, qa, qb, enc, wv, p_out, e_out, pay_out, qk_s):
    step = pl.program_id(0)
    tokens = enc.shape[1]
    count = scal[0]
    tall = BLOCK * ROWS

    @pl.when(step == 0)
    def _():
        high, low = split2(qa[...] + qb[...])
        qk_s[0:ROWS] = high
        qk_s[ROWS : 2 * ROWS] = low

    @pl.when(step * BLOCK < count)
    def _():
        rows = enc[...].reshape(BLOCK * tokens, D)
        both = nt(qk_s[...], rows)
        logits = both[:ROWS] + both[ROWS:]
        logits = jnp.concatenate(
            [logits[:, b * tokens : (b + 1) * tokens] for b in range(BLOCK)], axis=0
        )
        lane = iota((ROWS, tokens), 1)
        seen = jnp.concatenate(
            [
                jnp.broadcast_to(scal[8 + step * BLOCK + b], (ROWS, tokens))
                for b in range(BLOCK)
            ],
            axis=0,
        )
        seen = iota((tall, tokens), 1) < seen
        logits = jnp.where(seen, logits, MASKED)
        peak = jnp.max(logits, axis=1, keepdims=True)
        raised = jnp.where(seen, jnp.exp(logits - peak), 0.0)
        total = jnp.sum(raised, axis=1, keepdims=True)
        p_out[...] = raised.reshape(BLOCK, ROWS, tokens)
        low = raised.astype(bf16)
        sums = []
        upper = iota((2 * ROWS, tokens), 0) < ROWS
        zero = jnp.zeros((2 * ROWS, tokens), bf16)
        for k in range(BLOCK // 2):
            pair = low[2 * ROWS * k : 2 * ROWS * (k + 1)]
            left = jnp.concatenate(
                [jnp.where(upper, pair, zero), jnp.where(upper, zero, pair)], axis=1
            )
            sums.append(nn(left, rows[2 * tokens * k : 2 * tokens * (k + 1)]))
        summed = jnp.concatenate(sums, axis=0).astype(bf16)
        e_out[...] = (
            nn(select_docs(HEADS * BLOCK, tall), summed)
            .astype(bf16)
            .reshape(HEADS, BLOCK, D)
        )
        context = nn(summed, wv[...])
        own = (iota((tall, D), 0) % ROWS) == head_of((tall, D), 1)
        context = jnp.where(own, context, 0.0).astype(bf16)
        gather = (iota((BLOCK, tall), 0) == iota((BLOCK, tall), 1) // ROWS).astype(bf16)
        pay_out[:, :D] = nn(gather, context).astype(bf16)
        parts = split3(peak) + split3(total)
        at = iota((tall, LANES), 1)
        extra = jnp.zeros((tall, LANES), f32)
        for k, part in enumerate(parts):
            extra = jnp.where(at // ROWS == k, part.astype(f32), extra)
        extra = jnp.where(at % ROWS == iota((tall, LANES), 0) % ROWS, extra, 0.0)
        pay_out[:, D:] = nn(gather, extra.astype(bf16)).astype(bf16)

    @pl.when(step * BLOCK >= count)
    def _():
        p_out[...] = jnp.zeros_like(p_out)
        e_out[...] = jnp.zeros_like(e_out)
        pay_out[:, :D] = jnp.zeros((BLOCK, D), bf16)
        pay_out[:, D:] = jnp.where(iota((BLOCK, LANES), 1) < ROWS, MASKED, 0.0).astype(bf16)


def decode(pay):
    extra = pay[:, D:].astype(f32)

    def lane(k):
        return pltpu.roll(extra, LANES - k * ROWS, 1) if k else extra

    first = iota(extra.shape, 1) < ROWS
    peak = jnp.where(first, (lane(0) + lane(1)) + lane(2), 0.0)
    total = jnp.where(first, (lane(3) + lane(4)) + lane(5), 0.0)
    return peak, total


def merge(one, two):
    peak1, total1 = decode(one)
    peak2, total2 = decode(two)
    peak = jnp.maximum(peak1, peak2)
    up1, up2 = jnp.exp(peak1 - peak), jnp.exp(peak2 - peak)
    total = up1 * total1 + up2 * total2
    first = iota(peak.shape, 1) < ROWS
    up1, up2 = jnp.where(first, up1, 0.0), jnp.where(first, up2, 0.0)
    context = spread(up1) * one[:, :D].astype(f32) + spread(up2) * two[:, :D].astype(f32)
    return peak, total, context


def ordered(bit, own, other):
    swap = jnp.broadcast_to(bit, own.shape) == 1
    return jnp.where(swap, other, own), jnp.where(swap, own, other)


def merge_kernel(scal, own, other, pay_out):
    one, two = ordered(scal[0], own[...].astype(f32), other[...].astype(f32))
    peak, total, context = merge(one, two)
    pay_out[:, :D] = context.astype(bf16)
    extra = jnp.zeros(peak.shape, f32)
    at = iota(peak.shape, 1) // ROWS
    for k, part in enumerate(split3(peak) + split3(total)):
        part = part.astype(f32)
        extra = jnp.where(at == k, pltpu.roll(part, k * ROWS, 1) if k else part, extra)
    pay_out[:, D:] = extra.astype(bf16)


def forward_kernel(
    scal, own, other, first, h1, wout, g_ff, win, wdown,
    c_out, c32_out, scale_out, h2_out, z_out, part_out,
):
    one, two = ordered(scal[0], own[...].astype(f32), other[...].astype(f32))
    peak, total, context = merge(one, two)
    lanes = iota(peak.shape, 1) < ROWS
    inverse = jnp.where(lanes & (total > 0.0), 1.0 / jnp.where(total > 0.0, total, 1.0), 0.0)
    context = context * spread(inverse)
    mine, _ = decode(first[...].astype(f32))
    scale_out[...] = jnp.exp(jnp.minimum(mine - peak, 0.0)) * inverse
    c32_out[...] = context
    low = context.astype(bf16)
    c_out[...] = low
    h2 = h1[...] + nn(low, wout[...])
    h2_out[...] = h2
    n2, _ = rms_parts(h2)
    y3 = (n2 * g_ff[...]).astype(bf16)
    z = nn(y3, win[...])
    z_out[...] = z
    u = (z * phi(z)).astype(bf16)
    part_out[...] = nn(u, wdown[...]).astype(bf16)


def score_kernel(
    scal, part_a, part_b, h2, z, g_final, row, wdown, win,
    scores_out, n3_out, dh3_out, part_out,
):
    h3 = h2[...] + (part_a[...].astype(f32) + part_b[...].astype(f32))
    n3, r3 = rms_parts(h3)
    n3_out[...] = n3
    row_f = row[...].astype(f32)
    gained = jnp.broadcast_to(g_final[...] * row_f * FACTOR, (8, D))
    scores = nt(gained, n3, EXACT)[0:1]
    slots = n3.shape[0]
    groups = scores_out.shape[0]
    wide = jnp.concatenate([scores, jnp.zeros((1, LANES - slots), f32)], axis=1)
    scores_out[...] = jnp.where(iota((groups, LANES), 0) == scal[1], wide, 0.0)
    dh3 = rms_back(gained[0:1], n3, r3).astype(bf16)
    dh3_out[...] = dh3
    du = nt(dh3, wdown[...])
    dz = (du * gelu_slope(z[...])).astype(bf16)
    part_out[...] = nt(dz, win[...]).astype(bf16)


def list_kernel(scal, sc_a, sc_b, begins, ends, relevance, scores_out, loss_out, ds_out, mine_out):
    groups = sc_a.shape[0]
    docs = scores_out.shape[1]
    wide = docs + LANES
    queries = begins.shape[0]
    scores = sc_a[...] + sc_b[...]
    lane = iota((8, LANES), 1)
    blank = jnp.zeros((8, wide - LANES), f32)
    placed = jnp.zeros((8, wide), f32)
    for g in range(groups):
        start, count = scal[2 + g], scal[2 + groups + g]
        kept = jnp.where(lane < count, scores[g : g + 1], 0.0)
        placed = placed + pltpu.roll(jnp.concatenate([kept, blank], axis=1), start, 1)
    values = placed[0:1, :docs]
    scores_out[...] = values
    place = iota((queries, docs), 1)
    member = (place >= begins[...]) & (place < ends[...])
    peak = jnp.max(jnp.where(member, values, MASKED), axis=1, keepdims=True)
    raised = jnp.where(member, jnp.exp(jnp.where(member, values - peak, 0.0)), 0.0)
    log_total = peak + jnp.log(jnp.sum(raised, axis=1, keepdims=True))
    weight = jnp.sum(jnp.where(member, relevance[...], 0.0), axis=1, keepdims=True)
    target = jnp.where(member, relevance[...] / weight, 0.0)
    picked = jnp.sum(target * values, axis=1, keepdims=True)
    loss_out[...] = jnp.sum(log_total - picked, axis=0, keepdims=True) / queries
    chance = jnp.where(member, jnp.exp(jnp.where(member, values - log_total, 0.0)), 0.0)
    ds = jnp.sum(chance - target, axis=0, keepdims=True) / queries
    ds = jnp.broadcast_to(jnp.concatenate([ds, jnp.zeros((1, LANES), f32)], axis=1), (8, wide))
    at = iota((groups, LANES), 0)
    slotted = jnp.zeros((groups, LANES), f32)
    for g in range(groups):
        start, count = scal[2 + g], scal[2 + groups + g]
        back = pltpu.roll(ds, lax.rem(wide - start, wide), 1)[:, :LANES]
        back = jnp.where(lane < count, back, 0.0)[0:1]
        slotted = jnp.where(at == g, back, slotted)
    ds_out[...] = slotted
    mine = jnp.sum(jnp.where(at == scal[1], slotted, 0.0), axis=0, keepdims=True)
    mine_out[...] = jnp.broadcast_to(mine, (8, LANES))


def context_kernel(
    part_a, part_b, h2, dh3, c32, g_ff, wout, wout_own,
    dh2_out, dc_out, own_out, inner_out, ff_out,
):
    n2, r2 = rms_parts(h2[...])
    dy3 = part_a[...].astype(f32) + part_b[...].astype(f32)
    ff_out[...] = dy3 * n2
    dh2 = (dh3[...].astype(f32) + rms_back(dy3 * g_ff[...], n2, r2)).astype(bf16)
    dh2_out[...] = dh2
    dc = nt(dh2, wout[...]).astype(bf16)
    dc_out[...] = dc
    own_out[...] = nt(dh2, wout_own[...]).astype(bf16)
    hot = (head_of((D, LANES), 0) == iota((D, LANES), 1)).astype(f32)
    inner_out[...] = nn(dc.astype(f32) * c32[...], hot, EXACT)


def column(rows):
    tall = BLOCK * ROWS
    pick = (iota((tall, BLOCK), 0) // ROWS == iota((tall, BLOCK), 1)).astype(f32)
    wide = nn(pick, rows, EXACT)
    own = iota((tall, LANES), 0) % ROWS == iota((tall, LANES), 1)
    return jnp.sum(jnp.where(own, wide, 0.0), axis=1, keepdims=True)


def back_kernel(
    scal, ds, enc, p, scale, inner, dc, wv, dh2, n3, ff,
    dap_out, vd_out, sums_out,
):
    step = pl.program_id(0)
    tokens = enc.shape[1]
    tall = BLOCK * ROWS

    @pl.when(step == 0)
    def _():
        slots = dh2.shape[0]
        row = ds[...][:, :slots] * scal[1].astype(f32) * (1.0 / 1024.0)
        at = iota((ROWS, D), 0)
        out = jnp.where(at == HEADS, nn(row, dh2[...].astype(f32), EXACT)[0:1], 0.0)
        out = jnp.where(at == HEADS + 1, nn(row, n3[...], EXACT)[0:1], out)
        sums_out[...] = jnp.where(at == HEADS + 2, nn(row, ff[...], EXACT)[0:1], out)

    @pl.when(step * BLOCK < scal[0])
    def _():
        rows = enc[...].reshape(BLOCK * tokens, D)
        lane = iota((BLOCK, LANES), 1)
        own_slot = lane == step * BLOCK + iota((BLOCK, LANES), 0)
        ds_col = jnp.sum(jnp.where(own_slot, ds[0:1], 0.0), axis=1, keepdims=True)
        grad = (dc[...].astype(f32) * ds_col).astype(bf16)
        pick = (iota((tall, BLOCK), 0) // ROWS == iota((tall, BLOCK), 1)).astype(bf16)
        own = (iota((tall, D), 0) % ROWS) == head_of((tall, D), 1)
        grad = jnp.where(own, nn(pick, grad), 0.0).astype(bf16)
        vd = nt(grad, wv[...]).astype(bf16)
        vd_out[...] = vd.reshape(BLOCK, ROWS, D)
        grad_probs = []
        for k in range(BLOCK // 2):
            pair = nt(
                vd[2 * ROWS * k : 2 * ROWS * (k + 1)],
                rows[2 * tokens * k : 2 * tokens * (k + 1)],
            )
            grad_probs += [pair[:ROWS, :tokens], pair[ROWS:, tokens:]]
        grad_probs = jnp.concatenate(grad_probs, axis=0)
        prob = p[...].reshape(tall, tokens) * column(scale[...])
        da = (prob * (grad_probs - column(inner[...] * ds_col))).astype(bf16)
        dap_out[:, :ROWS] = da.reshape(BLOCK, ROWS, tokens)
        dap_out[:, ROWS:] = prob.astype(bf16).reshape(BLOCK, ROWS, tokens)
        flat = jnp.concatenate([da[ROWS * b : ROWS * (b + 1)] for b in range(BLOCK)], axis=1)
        sums_out[...] += nn(flat, rows)

    @pl.when(step * BLOCK >= scal[0])
    def _():
        dap_out[...] = jnp.zeros_like(dap_out)
        vd_out[...] = jnp.zeros_like(vd_out)


def enc_grad_kernel(scal, qa, qb, dap, vd, grad_out):
    step = pl.program_id(0)

    @pl.when(step * BLOCK < scal[0])
    def _():
        qk = (qa[...] + qb[...]).astype(bf16)
        for b in range(BLOCK):
            right = jnp.concatenate([qk, vd[b]], axis=0)
            grad_out[b] = tn(dap[b], right).astype(bf16)

    @pl.when(step * BLOCK >= scal[0])
    def _():
        grad_out[...] = jnp.zeros_like(grad_out)


def value_kernel(scal, keep, other, dc, ds, grad_out):
    slots = keep.shape[1]
    own_slot = iota((slots, LANES), 0) == iota((slots, LANES), 1)
    ds_col = jnp.sum(jnp.where(own_slot, ds[0:1], 0.0), axis=1, keepdims=True)
    grad = (dc[...].astype(f32) * ds_col).astype(bf16)
    for h in range(keep.shape[0]):
        summed = (keep[h].astype(f32) + other[h].astype(f32)).astype(bf16)
        part = tn(grad[:, h * HEAD_DIM : (h + 1) * HEAD_DIM], summed)
        grad_out[h * HEAD_DIM : (h + 1) * HEAD_DIM] = part.astype(bf16)


def weights_kernel(
    cd, dh2, c_own, ds, h1, g_ff, wout, win, wdown,
    win_out, wdown_out, wout_out,
):
    @pl.when(pl.program_id(0) == 0)
    def _():
        win_out[...] = jnp.zeros_like(win_out)
        wdown_out[...] = jnp.zeros_like(wdown_out)
        wout_out[...] = jnp.zeros_like(wout_out)

    h2 = h1[...] + nn(cd[:, :D], wout[...])
    n2, _ = rms_parts(h2)
    y3 = (n2 * g_ff[...]).astype(bf16)
    z = nn(y3, win[...])
    u = (z * phi(z)).astype(bf16)
    ds_col = ds[...]
    dh3 = (cd[:, D:].astype(f32) * ds_col).astype(bf16)
    dz = (nt(dh3, wdown[...]) * gelu_slope(z)).astype(bf16)
    win_out[...] += tn(y3, dz)
    wdown_out[...] += tn(u, dh3)
    wout_out[...] += tn(c_own[...], (dh2[...].astype(f32) * ds_col).astype(bf16))


def key_kernel(scal, sum_a, sum_b, wk, wq, qm, y2, key_out, query_out, part_out):
    g = sum_a[...] + sum_b[...]
    g = jnp.where(iota((ROWS, D), 0) < HEADS, g, 0.0)
    high, low = split2(g)
    both = jnp.concatenate([high, low], axis=0)
    dq = nn(both, wk[...])
    dq = dq[:ROWS] + dq[ROWS:]
    width = dq.shape[1]
    first = scal[0] * (width // HEAD_DIM)
    own = iota((ROWS, width), 0) == first + head_of((ROWS, width), 1)
    dq = jnp.sum(jnp.where(own, dq, 0.0), axis=0, keepdims=True)
    key_out[...] = tn(both, jnp.concatenate([qm[...], qm[...]], axis=0))
    dq_parts = stack3(dq)
    query_out[...] = tn(repeat3(y2[0:1]), dq_parts)
    part = jnp.sum(nt(dq_parts, wq[...]), axis=0, keepdims=True)
    part_out[...] = jnp.broadcast_to(part, (8, D))


def hidden_kernel(
    part_a, part_b, sum_a, sum_b, h1, g_cross, s1, y1, wos, wvs, g_final, row,
    cross_out, dh1_out, wos_out, wvs_out, part_out, final_out, row_out, ff_out,
):
    dy2 = part_a[0:1] + part_b[0:1]
    sums = sum_a[...] + sum_b[...]
    n1, r1 = rms_parts(h1[...])
    cross_out[...] = dy2 * n1
    dh1 = sums[HEADS : HEADS + 1] + rms_back(dy2 * g_cross[...], n1, r1)
    dh1_out[...] = dh1
    dh1_parts = stack3(dh1)
    wos_out[...] = tn(repeat3(s1[0:1]), dh1_parts)
    ds1 = jnp.sum(nt(dh1_parts, wos[...]), axis=0, keepdims=True)
    ds1_parts = stack3(ds1)
    wvs_out[...] = tn(repeat3(y1[0:1]), ds1_parts)
    part = jnp.sum(nt(ds1_parts, wvs[...]), axis=0, keepdims=True)
    part_out[...] = jnp.broadcast_to(part, (8, D))
    total = sums[HEADS + 1 : HEADS + 2] * FACTOR
    final_out[...] = total * row[...].astype(f32)
    row_out[...] = total * g_final[...]
    ff_out[...] = sums[HEADS + 2 : HEADS + 3]


def start_kernel(part_a, part_b, dh1, start, g_self, gain_out, start_out):
    dy1 = part_a[0:1] + part_b[0:1]
    n0, r0 = rms_parts(start[...].astype(f32))
    gain_out[...] = dy1 * n0
    start_out[...] = dh1[...] + rms_back(dy1 * g_self[...], n0, r0)


def shape(dims, dtype=f32):
    return jax.ShapeDtypeStruct(dims, dtype)


def whole_spec(memory=pltpu.VMEM):
    return pl.BlockSpec(memory_space=memory)


def plain(kernel, outs, *args, smem=0, flops=0, limit=32):
    size = sum(a.size * a.dtype.itemsize for a in args)
    return pl.pallas_call(
        kernel,
        out_shape=outs,
        in_specs=[whole_spec(pltpu.SMEM if k < smem else pltpu.VMEM) for k in range(len(args))],
        out_specs=jax.tree.map(lambda _: whole_spec(), outs),
        compiler_params=pltpu.CompilerParams(vmem_limit_bytes=limit * MIB),
        cost_estimate=pl.CostEstimate(flops=flops, bytes_accessed=size, transcendentals=0),
        name=kernel.__name__,
    )(*args)


def gridded(kernel, steps, scal, ins, outs, scratch=(), flops=0, limit=40):
    size = sum(a.size * a.dtype.itemsize for a, _, _ in ins)
    size += sum(s.size * s.dtype.itemsize for s, _, _ in outs)
    return pl.pallas_call(
        kernel,
        out_shape=[s for s, _, _ in outs],
        grid_spec=pltpu.PrefetchScalarGridSpec(
            num_scalar_prefetch=1,
            grid=(steps,),
            in_specs=[pl.BlockSpec(block, index) for _, block, index in ins],
            out_specs=[pl.BlockSpec(block, index) for _, block, index in outs],
            scratch_shapes=list(scratch),
        ),
        compiler_params=pltpu.CompilerParams(
            vmem_limit_bytes=limit * MIB, dimension_semantics=("arbitrary",)
        ),
        cost_estimate=pl.CostEstimate(flops=flops, bytes_accessed=size, transcendentals=0),
        name=kernel.__name__,
    )(scal, *[a for a, _, _ in ins])


def bits_of(size):
    return [1 << b for b in range(size.bit_length() - 1)]


def swap(x, axis, bit):
    size = lax.axis_size(axis)
    return lax.ppermute(x, axis, [(i, i ^ bit) for i in range(size)])


def sum_last(x, axes):
    steps = [(axis, bit) for axis in axes for bit in bits_of(lax.axis_size(axis))]
    for axis, bit in steps[:-1]:
        x = (x.astype(f32) + swap(x, axis, bit).astype(f32)).astype(x.dtype)
    axis, bit = steps[-1]
    return x, swap(x, axis, bit)


def gather_rows(x, axis, bits):
    me = lax.axis_index(axis)
    x = x[None]
    for bit in bits:
        other = swap(x, axis, bit)
        mine = (me & bit) > 0
        x = jnp.concatenate([jnp.where(mine, other, x), jnp.where(mine, x, other)], axis=0)
    return x


def gather_all(x, groups):
    me = lax.axis_index("heads")
    half = x.shape[0] // 2
    piece = lax.dynamic_slice_in_dim(x, (me & 1) * half, half)
    pieces = gather_rows(piece, "docs", bits_of(groups))
    halves = gather_rows(pieces, "heads", [1])
    return halves.reshape(2 * groups * half, x.shape[1])


def per_device(
    enc_out,
    enc_len,
    group_docs,
    list_len,
    relevance,
    start_token,
    score_row,
    g_self,
    w_value_self,
    w_out_self,
    g_cross,
    w_query,
    w_key,
    w_value,
    w_out,
    g_ff,
    w_in,
    w_down,
    g_final,
):
    groups = lax.axis_size("docs")
    parts = lax.axis_size("heads")
    me_g = lax.axis_index("docs")
    me_j = lax.axis_index("heads")
    slots, tokens = enc_out.shape[:2]
    docs = enc_len.shape[0]
    queries = list_len.shape[0]
    width = w_value.shape[1]
    own_heads = HEADS // parts
    hidden = w_in.shape[1]
    blocks = slots // BLOCK

    ends = jnp.cumsum(group_docs)
    starts = ends - group_docs
    my_start, my_count = starts[me_g], group_docs[me_g]
    lengths = lax.dynamic_slice_in_dim(
        jnp.concatenate([enc_len, jnp.zeros((slots,), i32)]), my_start, slots
    )
    slot = jnp.arange(slots, dtype=i32)
    seen = jnp.where(slot < my_count, jnp.clip(lengths - me_j * tokens, 0, tokens), 0)
    list_ends = jnp.cumsum(list_len)
    begins = list_ends - list_len
    scal_doc = jnp.concatenate(
        [jnp.stack([my_count] + [jnp.full((), 1024 // parts, i32)] + [me_j] * 6), seen]
    )
    scal_j = jnp.stack([me_j, me_g])
    scal_list = jnp.concatenate([scal_j, starts, group_docs])
    bit_scal = [jnp.stack([(me_j // bit) & 1, me_g]) for bit in bits_of(parts)]

    def as_row(x):
        return x.reshape(1, -1)

    start_row, row = as_row(start_token), as_row(score_row)
    gain0, gain1, gain2, gain3 = (as_row(g) for g in (g_self, g_cross, g_ff, g_final))

    value_full = lax.all_gather(w_value, "heads", axis=1, tiled=True)
    out_full = lax.all_gather(w_out, "heads", axis=0, tiled=True)

    part, s1, y1 = plain(
        self_kernel,
        [shape((8, D)), shape((ROWS, width), bf16), shape((ROWS, D), bf16)],
        start_row,
        gain0,
        w_value_self,
        w_out_self,
    )
    part_a, part_b = sum_last(part, ["heads"])
    qk, h1, qm, y2 = plain(
        query_kernel,
        [shape((ROWS, D)), shape((1, D)), shape((ROWS, width), bf16), shape((ROWS, D), bf16)],
        scal_j,
        part_a,
        part_b,
        start_row,
        gain1,
        w_query,
        w_key,
        smem=1,
    )
    qk_a, qk_b = sum_last(qk, ["heads"])

    def last(scal):
        return jnp.maximum((scal[0] - 1) // BLOCK, 0)

    const2 = lambda i, scal: (0, 0)
    step2 = lambda i, scal: (i, 0)
    step3 = lambda i, scal: (i, 0, 0)
    enc_map = lambda i, scal: (jnp.minimum(i, last(scal)), 0, 0)
    pass_flops = 2 * slots * tokens * D * 256
    prob, summed, pay = gridded(
        attend_kernel,
        blocks,
        scal_doc,
        [
            (qk_a, (ROWS, D), const2),
            (qk_b, (ROWS, D), const2),
            (enc_out, (BLOCK, tokens, D), enc_map),
            (value_full, (D, D), const2),
        ],
        [
            (shape((slots, ROWS, tokens)), (BLOCK, ROWS, tokens), step3),
            (shape((HEADS, slots, D), bf16), (HEADS, BLOCK, D), lambda i, scal: (0, i, 0)),
            (shape((slots, D + LANES), bf16), (BLOCK, D + LANES), step2),
        ],
        scratch=[pltpu.VMEM((2 * ROWS, D), bf16)],
        flops=2 * pass_flops,
    )
    merged = pay
    for bit, scal in zip(bits_of(parts)[:-1], bit_scal[:-1]):
        merged = plain(
            merge_kernel,
            shape(pay.shape, bf16),
            scal,
            merged,
            swap(merged, "heads", bit),
            smem=1,
        )
    other = swap(merged, "heads", bits_of(parts)[-1])

    c, c32, scale, h2, z, part = plain(
        forward_kernel,
        [
            shape((slots, D), bf16),
            shape((slots, D)),
            shape((slots, LANES)),
            shape((slots, D)),
            shape((slots, hidden)),
            shape((slots, D), bf16),
        ],
        bit_scal[-1],
        merged,
        other,
        pay,
        h1,
        out_full,
        gain2,
        w_in,
        w_down,
        smem=1,
    )
    part_a, part_b = sum_last(part, ["heads"])
    scores, n3, dh3, part = plain(
        score_kernel,
        [
            shape((groups, LANES)),
            shape((slots, D)),
            shape((slots, D), bf16),
            shape((slots, D), bf16),
        ],
        scal_j,
        part_a,
        part_b,
        h2,
        z,
        gain3,
        row,
        w_down,
        w_in,
        smem=1,
    )
    score_a, score_b = sum_last(scores, ["docs"])
    all_scores, loss, ds_slots, ds_mine = plain(
        list_kernel,
        [shape((1, docs)), shape((1, 1)), shape((groups, LANES)), shape((8, LANES))],
        scal_list,
        score_a,
        score_b,
        begins.reshape(-1, 1),
        list_ends.reshape(-1, 1),
        as_row(relevance),
        smem=1,
    )
    part_a, part_b = sum_last(part, ["heads"])
    dh2, dc, dc_own, inner, ff = plain(
        context_kernel,
        [
            shape((slots, D), bf16),
            shape((slots, D), bf16),
            shape((slots, width), bf16),
            shape((slots, LANES)),
            shape((slots, D)),
        ],
        part_a,
        part_b,
        h2,
        dh3,
        c32,
        gain2,
        out_full,
        w_out,
    )

    scaled = summed.astype(f32) * scale[:, :HEADS].T[:, :, None]
    piece = scaled.astype(bf16).reshape(parts, own_heads, slots, D)
    keep = piece
    count = parts
    bits = bits_of(parts)
    for k, bit in enumerate(bits):
        mine = (me_j // bit) & 1
        keep = keep.reshape(count // 2, 2, own_heads, slots, D)
        sent = lax.dynamic_index_in_dim(keep, 1 - mine, 1, keepdims=False)
        keep = lax.dynamic_index_in_dim(keep, mine, 1, keepdims=False)
        other = swap(sent, "heads", bit)
        if k < len(bits) - 1:
            keep = (keep.astype(f32) + other.astype(f32)).astype(bf16)
        count //= 2
    keep, other = keep.reshape(own_heads, slots, D), other.reshape(own_heads, slots, D)
    value_part = plain(
        value_kernel,
        shape((width, D), bf16),
        scal_j,
        keep,
        other,
        dc_own,
        ds_mine,
        smem=1,
    )

    dap, vd, sums = gridded(
        back_kernel,
        blocks,
        scal_doc,
        [
            (ds_mine, (8, LANES), const2),
            (enc_out, (BLOCK, tokens, D), enc_map),
            (prob, (BLOCK, ROWS, tokens), step3),
            (scale, (BLOCK, LANES), step2),
            (inner, (BLOCK, LANES), step2),
            (dc, (BLOCK, D), step2),
            (value_full, (D, D), const2),
            (dh2, (slots, D), const2),
            (n3, (slots, D), const2),
            (ff, (slots, D), const2),
        ],
        [
            (shape((slots, 2 * ROWS, tokens), bf16), (BLOCK, 2 * ROWS, tokens), step3),
            (shape((slots, ROWS, D), bf16), (BLOCK, ROWS, D), step3),
            (shape((ROWS, D)), (ROWS, D), const2),
        ],
        flops=2 * pass_flops,
    )
    (enc_grad,) = gridded(
        enc_grad_kernel,
        blocks,
        scal_doc,
        [
            (qk_a, (ROWS, D), const2),
            (qk_b, (ROWS, D), const2),
            (dap, (BLOCK, 2 * ROWS, tokens), step3),
            (vd, (BLOCK, ROWS, D), step3),
        ],
        [(shape(enc_out.shape, bf16), (BLOCK, tokens, D), step3)],
        flops=pass_flops,
    )

    cd_all = gather_all(jnp.concatenate([c, dh3], axis=1), groups)
    dh2_all = gather_all(dh2, groups)
    half = slots // 2
    ds_all = (
        ds_slots[:, :slots].reshape(groups, 2, half).transpose(1, 0, 2).reshape(-1, 1)
    )
    c_own = lax.dynamic_slice_in_dim(cd_all[:, :D], me_j * width, width, axis=1)
    total_rows = groups * slots
    tile = 192
    once = lambda i, scal: (0, 0)
    w_in_grad, w_down_grad, w_out_grad = gridded(
        lambda scal, *refs: weights_kernel(*refs),
        total_rows // tile,
        scal_j,
        [
            (cd_all, (tile, 2 * D), step2),
            (dh2_all, (tile, D), step2),
            (c_own, (tile, width), step2),
            (ds_all, (tile, 1), step2),
            (h1, (1, D), once),
            (gain2, (1, D), once),
            (out_full, (D, D), once),
            (w_in, (D, hidden), once),
            (w_down, (hidden, D), once),
        ],
        [
            (shape((D, hidden)), (D, hidden), once),
            (shape((hidden, D)), (hidden, D), once),
            (shape((width, D)), (width, D), once),
        ],
        flops=10 * total_rows * D * hidden,
        limit=48,
    )

    value_a, value_b = sum_last(value_part, ["docs"])
    value_grad = (value_a.astype(f32) + value_b.astype(f32)).T

    sum_a, sum_b = sum_last(sums, ["heads", "docs"])
    key_grad, query_grad, part = plain(
        key_kernel,
        [shape((D, width)), shape((D, width)), shape((8, D))],
        scal_j,
        sum_a,
        sum_b,
        w_key,
        w_query,
        qm,
        y2,
        smem=1,
    )
    part_a, part_b = sum_last(part, ["heads"])
    cross, dh1, wos_grad, wvs_grad, part, final_gain, row_grad, ff_gain = plain(
        hidden_kernel,
        [shape((1, D))] * 2
        + [shape((width, D)), shape((D, width)), shape((8, D))]
        + [shape((1, D))] * 3,
        part_a,
        part_b,
        sum_a,
        sum_b,
        h1,
        gain1,
        s1,
        y1,
        w_out_self,
        w_value_self,
        gain3,
        row,
    )
    part_a, part_b = sum_last(part, ["heads"])
    self_gain, start_grad = plain(
        start_kernel, [shape((1, D))] * 2, part_a, part_b, dh1, start_row, gain0
    )

    def flat(x):
        return x.reshape(-1)

    return (
        flat(all_scores),
        loss.reshape(()),
        enc_grad,
        flat(start_grad),
        flat(row_grad),
        flat(self_gain),
        wvs_grad,
        wos_grad,
        flat(cross),
        query_grad,
        key_grad,
        value_grad,
        w_out_grad,
        flat(ff_gain),
        w_in_grad,
        w_down_grad,
        flat(final_gain),
    )


def solution(mesh):
    placed = (
        P("docs", "heads", None),
        P(),
        P(),
        P(),
        P(),
        P(),
        P(),
        P(),
        P(None, "heads"),
        P("heads", None),
        P(),
        P(None, "heads"),
        P(None, "heads"),
        P(None, "heads"),
        P("heads", None),
        P(),
        P(None, "heads"),
        P("heads", None),
        P(),
    )
    return jax.shard_map(
        per_device,
        mesh=mesh,
        in_specs=placed,
        out_specs=(
            P(),
            P(),
            P("docs", "heads", None),
            P(),
            P(),
            P(),
            P(None, "heads"),
            P("heads", None),
            P(),
            P(None, "heads"),
            P(None, "heads"),
            P(None, "heads"),
            P("heads", None),
            P(),
            P(None, "heads"),
            P("heads", None),
            P(),
        ),
        check_vma=False,
    )
```

time: 1940 us -> 277 us (0.14)
  blocking collectives: 830 us -> 0 us
  waiting for transfers between devices: 519 us -> 95.3 us
  local copies, waits for them, and re-layouts: 317 us -> 36.6 us
  matrix products: 116 us -> 0 us
  other arithmetic: 106 us -> 25.1 us
  Pallas kernels: 0 us -> 62.5 us
    psum x2 -> x0, blocking collectives: 650 us -> none  [the longest x1 381 us: per_device(): lax.psum((query_grad_part, summed_h2 * counted, row_grad * counted, ff_ga...]
    all_to_all x3 -> x0, waiting for transfers between devices: 513 us -> none  [the longest x1 398 us: per_device(): lax.all_to_all(enc_out[outgoing], 'docs', split_axis=0, concat_axis=0, ti...]
    all_to_all x1 -> x0, blocking collectives: 142 us -> none  [per_device(): lax.all_to_all(enc_grad_local, 'heads', split_axis=1, concat_axis=0, tile...]
    reshape x11, local copies, waits for them, and re-layouts: 142 us -> 5.53 us  [the longest x3 3.58 us: per_device(): ds_slots[:, :slots].reshape(groups, 2, half).transpose(1, 0, 2)]
    dot_general x19 -> x0, matrix products: 116 us -> none  [the longest x7 35.6 us: row_dot(): return jnp.dot(left, right, preferred_element_type=jnp.float32)]
    ppermute x0 -> x35, waiting for transfers between devices: none -> 89.7 us  [swap(): return lax.ppermute(x, axis, [(i, i ^ bit) for i in range(size)])]
    gather x14 -> x0, local copies, waits for them, and re-layouts: 64.5 us -> none  [the longest x1 15.9 us: per_device(): homecoming[fetch]]
    pallas_call x0 -> x15, Pallas kernels: none -> 62.5 us  [the longest x4 47.4 us: gridded(): pl.pallas_call(kernel, out_shape=[s for s, _, _ in outs], grid_spec=pltpu...]
  transfers between devices with their start and end apart: 16 -> 37, of which waited for: 2 -> 19; matrix products, arithmetic and copies ran while one was open for 14% -> 15% of each run, Pallas kernels for 0% -> 17%
where the time goes in v1:
time: 277 us; the launch traced here: 276 us
  waiting for transfers between devices  95.3 us (34%)
  Pallas kernels  62.5 us (23%)
  starting transfers between devices  38.8 us (14%)
  local copies, waits for them, and re-layouts  36.6 us (13%)
  other arithmetic  25.1 us (9%)
  between operations  17.4 us (6%)
    ppermute x35, waiting for transfers between devices, swap(): return lax.ppermute(x, axis, [(i, i ^ bit) for i in range(size)])  89.7 us
    pallas_call x4, Pallas kernels, gridded(): pl.pallas_call(kernel, out_shape=[s for s, _, _ in outs], grid_spec=pltpu...  47.4 us
    ppermute x35, starting transfers between devices, swap(): return lax.ppermute(x, axis, [(i, i ^ bit) for i in range(size)])  38.7 us
    unnamed x238, local copies, waits for them, and re-layouts  26.2 us
    pallas_call x11, Pallas kernels, plain(): pl.pallas_call(kernel, out_shape=outs, in_specs=[whole_spec(pltpu.SMEM if...  15.1 us
    pallas_call x7, other arithmetic, plain(): pl.pallas_call(kernel, out_shape=outs, in_specs=[whole_spec(pltpu.SMEM if...  8.97 us
  transfers between devices with their start and end apart: 37, of which 19 were waited for; matrix products, arithmetic and copies ran while one was open for 15% of the time, Pallas kernels for 17%

profile of v1, /device:TPU:0, one launch (start us, length us, event | category | flops | bytes accessed | tf_op | source)
XLA Modules:
  0.0 275.7 jit_solution(5424288266183022890)
XLA Ops:
  9.4 1.1 copy.66.wvs
  12.4 2.9 %collective-permute-start.1 = (f32[8,768]{1,0:T(8,128)S(1)}, f32[8,768]{1,0:T(8,128)S(1)}, u32[]{:S(2)}, u32[]{:S(2)}) collective-permute-start(f32[8,768]{1,0:T(8,128)S(1)} %add.84.part_a), channel_id=1, source_target_pairs={{0,2},{1,3},{2,0},{3,1},{4,6},{5,7},{6,4},{7,5},{8,10},{9,11},{10,... | collective-permute-start | bytes 73736 | tf_op jit(solution)/shard_map/ppermute | solution.py:547
  16.0 1.1 collective-permute-done.1.part_b
  17.1 1.0 query_kernel.1
  23.1 2.1 collective-permute-start.3
  26.6 4.2 %all-gather.3.cloned.1.call-done = bf16[768,768]{0,1:T(8,128)(2,1)} async-done(((bf16[768,192]{0,1:T(8,128)(2,1)}), bf16[768,768]{0,1:T(8,128)(2,1)}) %all-gather.3.cloned.1.call-update) | async-done | bytes 1179664 | tf_op jit(solution)/shard_map/all_gather | solution.py:633
  30.9 1.6 copy.69.wv
  34.8 13.3 %attend_kernel.1 = (f32[96,16,128]{2,1,0:T(8,128)S(1)}, bf16[12,96,768]{2,1,0:T(8,128)(2,1)S(1)}, bf16[96,896]{1,0:T(8,128)(2,1)}) custom-call(s32[104]{0:T(128)S(1)} %concatenate.39.scal, f32[16,768]{1,0:T(8,128)S(1)} %copy-done.31, f32[16,768]{1,0:T(8,128)S(1)} %copy-done.36, bf16[96,128,768]{2,1,0:T(8,128)(2,1)} %enc.3, bf16[768,768]{1,0:T(8,128)(2,1)S(1)} %copy.69.wv), custom_call_target="tpu_custom_call" | custom-call | flops 9663676416 | bytes 22880256 | tf_op jit(solution)/shard_map/attend_kernel/pallas_call | solution.py:523
  48.1 1.2 copy-done.12
  50.5 1.3 collective-permute-done.4.other
  51.8 1.7 merge_kernel.1.own
  53.9 6.1 %collective-permute-done.5.other = bf16[96,896]{1,0:T(8,128)(2,1)S(1)} collective-permute-done((bf16[96,896]{1,0:T(8,128)(2,1)S(1)}, bf16[96,896]{1,0:T(8,128)(2,1)S(1)}, u32[]{:S(2)}, u32[]{:S(2)}) %collective-permute-start.5) | collective-permute-done | bytes 172064 | tf_op jit(solution)/shard_map/ppermute | solution.py:547
  60.1 1.3 copy-done.2
  62.1 2.8 %forward_kernel.1 = (bf16[96,768]{1,0:T(8,128)(2,1)S(1)}, f32[96,768]{1,0:T(8,128)S(1)}, f32[96,128]{1,0:T(8,128)S(1)}, f32[96,768]{1,0:T(8,128)S(1)}, f32[96,76...) custom-call(s32[2]{0:T(128)S(1)} %pad_add_fusion.2.scal, bf16[96,896]{1,0:T(8,128)(2,1)S(1)} %merge_kernel.1.own, ...), custom_call_target="tpu_custom_call" | custom-call | bytes 4061192 | tf_op jit(solution)/shard_map/forward_kernel/pallas_call | solution.py:509
  68.7 5.9 %collective-permute-done.7.part_b = bf16[96,768]{1,0:T(8,128)(2,1)S(1)} collective-permute-done((bf16[96,768]{1,0:T(8,128)(2,1)S(1)}, bf16[96,768]{1,0:T(8,128)(2,1)S(1)}, u32[]{:S(2)}, u32[]{:S(2)}) %collective-permute-start.7) | collective-permute-done | bytes 147488 | tf_op jit(solution)/shard_map/ppermute | solution.py:547
  74.6 1.8 score_kernel.1
  76.5 3.4 %collective-permute-start.8 = (f32[8,128]{1,0:T(8,128)S(1)}, f32[8,128]{1,0:T(8,128)S(1)}, u32[]{:S(2)}, u32[]{:S(2)}) collective-permute-start(f32[8,128]{1,0:T(8,128)S(1)} %get-tuple-element.72), channel_id=1, source_target_pairs={{0,4},{4,0},{8,12},{12,8},{16,20},{20,16},{24,28},{28,24},{1,5},{5... | collective-permute-start | bytes 12296 | tf_op jit(solution)/shard_map/ppermute | solution.py:547
  80.2 1.2 collective-permute-done.8
  82.1 2.9 %collective-permute-done.9 = f32[8,128]{1,0:T(8,128)S(1)} collective-permute-done((f32[8,128]{1,0:T(8,128)S(1)}, f32[8,128]{1,0:T(8,128)S(1)}, u32[]{:S(2)}, u32[]{:S(2)}) %collective-permute-start.9) | collective-permute-done | bytes 4128 | tf_op jit(solution)/shard_map/ppermute | solution.py:547
  85.0 5.2 %collective-permute-start.10 = (f32[8,128]{1,0:T(8,128)S(1)}, f32[8,128]{1,0:T(8,128)S(1)}, u32[]{:S(2)}, u32[]{:S(2)}) collective-permute-start(f32[8,128]{1,0:T(8,128)S(1)} %add.88.sc_a), channel_id=1, source_target_pairs={{0,16},{4,20},{8,24},{12,28},{16,0},{20,4},{24,8},{28,12},{1,17},{... | collective-permute-start | bytes 12296 | tf_op jit(solution)/shard_map/ppermute | solution.py:547
  90.3 1.5 collective-permute-done.10.sc_b
  91.8 1.4 list_kernel.1
  95.5 4.2 %collective-permute-done.12.part_b = bf16[96,768]{1,0:T(8,128)(2,1)S(1)} collective-permute-done((bf16[96,768]{1,0:T(8,128)(2,1)S(1)}, bf16[96,768]{1,0:T(8,128)(2,1)S(1)}, u32[]{:S(2)}, u32[]{:S(2)}) %collective-permute-start.12) | collective-permute-done | bytes 147488 | tf_op jit(solution)/shard_map/ppermute | solution.py:547
  99.8 1.0 context_kernel.1
  101.4 12.9 %back_kernel.1 = (bf16[96,32,128]{2,1,0:T(8,128)(2,1)S(1)}, bf16[96,16,768]{2,1,0:T(8,128)(2,1)S(1)}, f32[16,768]{1,0:T(8,128)S(1)}) custom-call(s32[104]{0:T(128)S(1)} %copy-done.82, f32[8,128]{1,0:T(8,128)S(1)} %get-tuple-element.75.ds, bf16[96,128,768]{2,1,0:T(8,128)(2,1)} %enc.3, f32[96,16,128]{2,1,0:T(8,128)S(1)} %copy-done.87, ...), custom_call_target="tpu_custom_call" | custom-call | flops 9663676416 | bytes 25022464 | tf_op jit(solution)/shard_map/back_kernel/pallas_call | solution.py:523
  115.4 1.1 collective-permute-done.13
  116.9 1.0 collective-permute-start.32
  117.9 2.8 %collective-permute-done.14 = f32[16,768]{1,0:T(8,128)S(1)} collective-permute-done((f32[16,768]{1,0:T(8,128)S(1)}, f32[16,768]{1,0:T(8,128)S(1)}, u32[]{:S(2)}, u32[]{:S(2)}) %collective-permute-start.14) | collective-permute-done | bytes 49184 | tf_op jit(solution)/shard_map/ppermute | solution.py:547
  120.7 3.9 %collective-permute-start.15 = (f32[16,768]{1,0:T(8,128)S(1)}, f32[16,768]{1,0:T(8,128)S(1)}, u32[]{:S(2)}, u32[]{:S(2)}) collective-permute-start(f32[16,768]{1,0:T(8,128)S(1)} %add.91), channel_id=1, source_target_pairs={{0,4},{4,0},{8,12},{12,8},{16,20},{20,16},{24,28},{28,24},{1,5},{5... | collective-permute-start | bytes 147464 | tf_op jit(solution)/shard_map/ppermute | solution.py:547
  125.3 1.4 collective-permute-done.15
  128.5 5.7 %collective-permute-start.29 = (bf16[4,48,1536]{2,1,0:T(8,128)(2,1)}, bf16[4,48,1536]{2,1,0:T(8,128)(2,1)}, u32[]{:S(2)}, u32[]{:S(2)}) collective-permute-start(bf16[4,48,1536]{2,1,0:T(8,128)(2,1)} %pad_maximum_fusion.2), channel_id=1, source_target_pairs={{0,16},{4,20},{8,24},{12,28},{16,0},{20,4},{24,8},{28,12},{1,17},{... | collective-permute-start | bytes 1769480 | tf_op jit(solution)/shard_map/ppermute | solution.py:547
  134.2 3.4 %collective-permute-start.17 = (f32[16,768]{1,0:T(8,128)S(1)}, f32[16,768]{1,0:T(8,128)S(1)}, u32[]{:S(2)}, u32[]{:S(2)}) collective-permute-start(f32[16,768]{1,0:T(8,128)S(1)} %add.93.sum_a), channel_id=1, source_target_pairs={{0,16},{4,20},{8,24},{12,28},{16,0},{20,4},{24,8},{28,12},{1,17},{... | collective-permute-start | bytes 147464 | tf_op jit(solution)/shard_map/ppermute | solution.py:547
  138.5 30.8 %collective-permute-done.17.sum_b = f32[16,768]{1,0:T(8,128)S(1)} collective-permute-done((f32[16,768]{1,0:T(8,128)S(1)}, f32[16,768]{1,0:T(8,128)S(1)}, u32[]{:S(2)}, u32[]{:S(2)}) %collective-permute-start.17) | collective-permute-done | bytes 49184 | tf_op jit(solution)/shard_map/ppermute | solution.py:547
  169.3 1.1 key_kernel.1
  171.7 1.0 constant_dynamic-slice_fusion.1
  172.9 1.8 collective-permute-start.19
  174.7 10.4 %collective-permute-done.19.part_b = f32[8,768]{1,0:T(8,128)S(1)} collective-permute-done((f32[8,768]{1,0:T(8,128)S(1)}, f32[8,768]{1,0:T(8,128)S(1)}, u32[]{:S(2)}, u32[]{:S(2)}) %collective-permute-start.19) | collective-permute-done | bytes 24608 | tf_op jit(solution)/shard_map/ppermute | solution.py:547
  185.2 1.5 hidden_kernel.1
  190.0 1.3 copy.85
  191.3 1.6 reshape.175.refs_3_
  192.9 1.3 reduce.1
  194.2 1.4 add.95.part_a
  196.0 1.1 broadcast_select_fusion.7
  198.3 1.4 value_kernel.1
  199.9 1.1 broadcast_select_fusion.5
  201.1 1.1 maximum_bitcast_fusion
  202.6 6.3 %collective-permute-done.24 = bf16[192,768]{1,0:T(8,128)(2,1)S(1)} collective-permute-done((bf16[192,768]{1,0:T(8,128)(2,1)S(1)}, bf16[192,768]{1,0:T(8,128)(2,1)S(1)}, u32[]{:S(2)}, u32[]{:S(2)}) %collective-permute-start.24) | collective-permute-done | bytes 294944 | tf_op jit(solution)/shard_map/ppermute | solution.py:547
  209.8 8.8 %enc_grad_kernel.1 = bf16[96,128,768]{2,1,0:T(8,128)(2,1)} custom-call(s32[104]{0:T(128)S(1)} %copy-done.83, f32[16,768]{1,0:T(8,128)S(1)} %copy-done.32, f32[16,768]{1,0:T(8,128)S(1)} %copy-done.37, bf16[96,32,128]{2,1,0:T(8,128)(2,1)S(1)} %copy-done.23, bf16[96,16,768]{2,1,0:T(8,128)(2,1)S(1)} %copy-done.11), custom_call_target="tpu_custom_call" | custom-call | flops 4831838208 | bytes 22118400 | tf_op jit(solution)/shard_map/enc_grad_kernel/pallas_call | solution.py:523
  218.6 2.2 copy.81
  220.8 2.2 copy.82
  223.0 2.2 copy.80
  225.2 1.3 reduce.3
  226.5 1.3 reduce.5
  227.8 1.3 reduce.6
  229.1 1.3 reduce.7
  232.5 1.3 reduce.2
  233.8 1.3 reduce.4
  235.1 1.1 add_convert_fusion
  236.2 4.0 %collective-permute-start.26 = (bf16[192,768]{1,0:T(8,128)(2,1)S(1)}, bf16[192,768]{1,0:T(8,128)(2,1)S(1)}, u32[]{:S(2)}, u32[]{:S(2)}) collective-permute-start(bf16[192,768]{1,0:T(8,128)(2,1)S(1)} %add_convert_fusion), channel_id=1, source_target_pairs={{0,16},{4,20},{8,24},{12,28},{16,0},{20,4},{24,8},{28,12},{1,17},{... | collective-permute-start | bytes 884744 | tf_op jit(solution)/shard_map/ppermute | solution.py:547
  240.2 1.3 broadcast_select_fusion.3
  241.7 10.6 %collective-permute-done.26 = bf16[192,768]{1,0:T(8,128)(2,1)S(1)} collective-permute-done((bf16[192,768]{1,0:T(8,128)(2,1)S(1)}, bf16[192,768]{1,0:T(8,128)(2,1)S(1)}, u32[]{:S(2)}, u32[]{:S(2)}) %collective-permute-start.26) | collective-permute-done | bytes 294944 | tf_op jit(solution)/shard_map/ppermute | solution.py:547
  253.1 1.6 broadcast_select_fusion.1
  255.1 1.3 copy-done.92
  256.6 12.3 %_lambda_.1 = (f32[768,768]{1,0:T(8,128)}, f32[768,768]{1,0:T(8,128)}, f32[192,768]{1,0:T(8,128)}) custom-call(s32[2]{0:T(128)S(1)} %copy-done.69, bf16[768,1536]{1,0:T(8,128)(2,1)} %bitcast.57, bf16[768,768]{1,0:T(8,128)(2,1)S(1)} %bitcast.52, bf16[768,192]{1,0:T(8,128)(2,1)S(1)} %constant_dynamic-slice_fusion.refs_2_, f32[768,1]{1,0:T(8,128)S(1)} %copy-done.27, ...), custom_call_target="tpu_custom_call" | custom-call | flops 4529848320 | bytes 12690432 | tf_op jit(solution)/shard_map/<lambda>/pallas_call | solution.py:523
  (339 shorter events, 37.5 us)
Async XLA Ops:
  7.2 23.6 %all-gather.3.cloned.1.call-start = ((), (), s32[]{:S(2)}) async-start(), calls=%async_computation | async-start | bytes 1474560 | tf_op jit(solution)/shard_map/all_gather | solution.py:633
  8.0 46.0 %all-gather.5.cloned.1.call-start = ((), (), s32[]{:S(2)}) async-start(), calls=%async_computation.1 | async-start | bytes 1474560 | tf_op jit(solution)/shard_map/all_gather | solution.py:634
  11.1 1.3 collective-permute-start
  12.4 4.7 %collective-permute-start.1 = (f32[8,768]{1,0:T(8,128)S(1)}, f32[8,768]{1,0:T(8,128)S(1)}, u32[]{:S(2)}, u32[]{:S(2)}) collective-permute-start(f32[8,768]{1,0:T(8,128)S(1)} %add.84.part_a), channel_id=1, source_target_pairs={{0,2},{1,3},{2,0},{3,1},{4,6},{5,7},{6,4},{7,5},{8,10},{9,11},{10,... | collective-permute-start | bytes 73736 | tf_op jit(solution)/shard_map/ppermute | solution.py:547
  15.5 16.9 %copy-start.6 = (bf16[768,192]{1,0:T(8,128)(2,1)}, bf16[768,192]{1,0:T(8,128)(2,1)S(1)}, u32[]{:S(2)}) copy-start(bf16[768,192]{1,0:T(8,128)(2,1)S(1)} %copy.67.wq) | copy-start | bytes 884740
  15.7 16.7 %copy-start.8 = (bf16[768,192]{1,0:T(8,128)(2,1)}, bf16[768,192]{1,0:T(8,128)(2,1)S(1)}, u32[]{:S(2)}) copy-start(bf16[768,192]{1,0:T(8,128)(2,1)S(1)} %copy.68.wk) | copy-start | bytes 884740
  15.8 16.7 %copy-start.43 = (f32[1,768]{1,0:T(1,128)}, f32[1,768]{1,0:T(1,128)S(1)}, u32[]{:S(2)}) copy-start(f32[1,768]{1,0:T(1,128)S(1)} %reshape.151.g_cross) | copy-start | bytes 9220
  19.9 3.1 %collective-permute-start.2 = (f32[16,768]{1,0:T(8,128)S(1)}, f32[16,768]{1,0:T(8,128)S(1)}, u32[]{:S(2)}, u32[]{:S(2)}) collective-permute-start(f32[16,768]{1,0:T(8,128)S(1)} %get-tuple-element.66), channel_id=1, source_target_pairs={{0,1},{1,0},{2,3},{3,2},{4,5},{5,4},{6,7},{7,6},{8,9},{9,8},{10,11... | collective-permute-start | bytes 147464 | tf_op jit(solution)/shard_map/ppermute | solution.py:547
  23.1 9.4 %collective-permute-start.3 = (f32[16,768]{1,0:T(8,128)S(1)}, f32[16,768]{1,0:T(8,128)S(1)}, u32[]{:S(2)}, u32[]{:S(2)}) collective-permute-start(f32[16,768]{1,0:T(8,128)S(1)} %add.85.qa), channel_id=1, source_target_pairs={{0,2},{1,3},{2,0},{3,1},{4,6},{5,7},{6,4},{7,5},{8,10},{9,11},{10,... | collective-permute-start | bytes 147464 | tf_op jit(solution)/shard_map/ppermute | solution.py:547
  26.6 21.5 %copy-start.81 = (s32[104]{0:T(128)}, s32[104]{0:T(128)S(1)}, u32[]{:S(2)}) copy-start(s32[104]{0:T(128)S(1)} %concatenate.39.scal) | copy-start | bytes 1252
  32.5 15.6 %copy-start.17 = (bf16[768,768]{1,0:T(8,128)(2,1)}, bf16[768,768]{1,0:T(8,128)(2,1)S(1)}, u32[]{:S(2)}) copy-start(bf16[768,768]{1,0:T(8,128)(2,1)S(1)} %copy.69.wv) | copy-start | bytes 3538948
  34.8 18.8 %copy-start.105 = (f32[768]{0:T(1024)S(1)}, f32[768]{0:T(1024)}, u32[]{:S(2)}) copy-start(f32[768]{0:T(1024)} %param.34) | copy-start | bytes 9220
  34.8 18.8 %copy-start.110 = (s32[24]{0:T(128)S(1)}, s32[24]{0:T(128)}, u32[]{:S(2)}) copy-start(s32[24]{0:T(128)} %param.22) | copy-start | bytes 292
  34.8 25.3 %copy-start = (bf16[768,768]{1,0:T(8,128)(2,1)S(1)}, bf16[768,768]{1,0:T(8,128)(2,1)}, u32[]{:S(2)}) copy-start(bf16[768,768]{1,0:T(8,128)(2,1)} %refs_7_.1) | copy-start | bytes 3538948
  34.8 25.3 %copy-start.1 = (bf16[768,768]{1,0:T(8,128)(2,1)S(1)}, bf16[768,768]{1,0:T(8,128)(2,1)}, u32[]{:S(2)}) copy-start(bf16[768,768]{1,0:T(8,128)(2,1)} %refs_8_.1) | copy-start | bytes 3538948
  50.2 1.6 collective-permute-start.4
  53.5 6.6 %collective-permute-start.5 = (bf16[96,896]{1,0:T(8,128)(2,1)S(1)}, bf16[96,896]{1,0:T(8,128)(2,1)S(1)}, u32[]{:S(2)}, u32[]{:S(2)}) collective-permute-start(bf16[96,896]{1,0:T(8,128)(2,1)S(1)} %merge_kernel.1.own), channel_id=1, source_target_pairs={{0,2},{1,3},{2,0},{3,1},{4,6},{5,7},{6,4},{7,5},{8,10},{9,11},{10,... | collective-permute-start | bytes 516104 | tf_op jit(solution)/shard_map/ppermute | solution.py:547
  66.3 1.9 collective-permute-start.6
  68.3 6.3 %collective-permute-start.7 = (bf16[96,768]{1,0:T(8,128)(2,1)S(1)}, bf16[96,768]{1,0:T(8,128)(2,1)S(1)}, u32[]{:S(2)}, u32[]{:S(2)}) collective-permute-start(bf16[96,768]{1,0:T(8,128)(2,1)S(1)} %add_convert_fusion.3.part_a), channel_id=1, source_target_pairs={{0,2},{1,3},{2,0},{3,1},{4,6},{5,7},{6,4},{7,5},{8,10},{9,11},{10,... | collective-permute-start | bytes 442376 | tf_op jit(solution)/shard_map/ppermute | solution.py:547
  76.5 4.9 %collective-permute-start.8 = (f32[8,128]{1,0:T(8,128)S(1)}, f32[8,128]{1,0:T(8,128)S(1)}, u32[]{:S(2)}, u32[]{:S(2)}) collective-permute-start(f32[8,128]{1,0:T(8,128)S(1)} %get-tuple-element.72), channel_id=1, source_target_pairs={{0,4},{4,0},{8,12},{12,8},{16,20},{20,16},{24,28},{28,24},{1,5},{5... | collective-permute-start | bytes 12296 | tf_op jit(solution)/shard_map/ppermute | solution.py:547
  81.4 3.6 %collective-permute-start.9 = (f32[8,128]{1,0:T(8,128)S(1)}, f32[8,128]{1,0:T(8,128)S(1)}, u32[]{:S(2)}, u32[]{:S(2)}) collective-permute-start(f32[8,128]{1,0:T(8,128)S(1)} %add.87), channel_id=1, source_target_pairs={{0,8},{4,12},{8,0},{12,4},{16,24},{20,28},{24,16},{28,20},{1,9},{5... | collective-permute-start | bytes 12296 | tf_op jit(solution)/shard_map/ppermute | solution.py:547
  81.4 18.3 %copy-start.21 = (bf16[192,768]{1,0:T(8,128)(2,1)S(1)}, bf16[192,768]{1,0:T(8,128)(2,1)}, u32[]{:S(2)}) copy-start(bf16[192,768]{1,0:T(8,128)(2,1)} %wout_own.1) | copy-start | bytes 884740
  81.4 18.3 %copy-start.29 = (f32[96,768]{1,0:T(8,128)S(1)}, f32[96,768]{1,0:T(8,128)}, u32[]{:S(2)}) copy-start(f32[96,768]{1,0:T(8,128)} %copy-done.28) | copy-start | bytes 884740
  81.5 18.2 %copy-start.3 = (bf16[768,768]{1,0:T(8,128)(2,1)S(1)}, bf16[768,768]{1,0:T(8,128)(2,1)}, u32[]{:S(2)}) copy-start(bf16[768,768]{1,0:T(8,128)(2,1)} %all-gather.5.cloned.1.call-done.wout.refs_6_) | copy-start | bytes 3538948
  81.5 18.2 %copy-start.16 = (f32[96,768]{1,0:T(8,128)S(1)}, f32[96,768]{1,0:T(8,128)}, u32[]{:S(2)}) copy-start(f32[96,768]{1,0:T(8,128)} %copy-done.15) | copy-start | bytes 884740
  81.5 18.2 %copy-start.52 = (f32[1,768]{1,0:T(1,128)S(1)}, f32[1,768]{1,0:T(1,128)}, u32[]{:S(2)}) copy-start(f32[1,768]{1,0:T(1,128)} %copy-done.51) | copy-start | bytes 9220
  81.5 89.0 %collective-permute-start.22 = (bf16[2,3,96,768]{3,2,1,0:T(8,128)(2,1)S(1)}, bf16[2,3,96,768]{3,2,1,0:T(8,128)(2,1)S(1)}, u32[]{:S(2)}, u32[]{:S(2)}) collective-permute-start(bf16[2,3,96,768]{3,2,1,0:T(8,128)(2,1)S(1)} %dynamic-slice_bitcast_fusion), channel_id=1, source_target_pairs={{0,1},{1,0},{2,3},{3,2},{4,5},{5,4},{6,7},{7,6},{8,9},{9,8},{10,11... | collective-permute-start | bytes 2654216 | tf_op jit(solution)/shard_map/ppermute | solution.py:547
  81.6 12.8 %collective-permute-start.11 = (bf16[96,768]{1,0:T(8,128)(2,1)S(1)}, bf16[96,768]{1,0:T(8,128)(2,1)S(1)}, u32[]{:S(2)}, u32[]{:S(2)}) collective-permute-start(bf16[96,768]{1,0:T(8,128)(2,1)S(1)} %get-tuple-element.78), channel_id=1, source_target_pairs={{0,1},{1,0},{2,3},{3,2},{4,5},{5,4},{6,7},{7,6},{8,9},{9,8},{10,11... | collective-permute-start | bytes 442376 | tf_op jit(solution)/shard_map/ppermute | solution.py:547
  85.0 6.8 %collective-permute-start.10 = (f32[8,128]{1,0:T(8,128)S(1)}, f32[8,128]{1,0:T(8,128)S(1)}, u32[]{:S(2)}, u32[]{:S(2)}) collective-permute-start(f32[8,128]{1,0:T(8,128)S(1)} %add.88.sc_a), channel_id=1, source_target_pairs={{0,16},{4,20},{8,24},{12,28},{16,0},{20,4},{24,8},{28,12},{1,17},{... | collective-permute-start | bytes 12296 | tf_op jit(solution)/shard_map/ppermute | solution.py:547
  90.2 5.2 %collective-permute-start.27 = (bf16[1,48,1536]{2,1,0:T(8,128)(2,1)S(1)}, bf16[1,48,1536]{2,1,0:T(8,128)(2,1)S(1)}, u32[]{:S(2)}, u32[]{:S(2)}) collective-permute-start(bf16[1,48,1536]{2,1,0:T(8,128)(2,1)S(1)} %fusion.2), channel_id=1, source_target_pairs={{0,4},{4,0},{8,12},{12,8},{16,20},{20,16},{24,28},{28,24},{1,5},{5... | collective-permute-start | bytes 442376 | tf_op jit(solution)/shard_map/ppermute | solution.py:547
  94.5 5.2 %collective-permute-start.12 = (bf16[96,768]{1,0:T(8,128)(2,1)S(1)}, bf16[96,768]{1,0:T(8,128)(2,1)S(1)}, u32[]{:S(2)}, u32[]{:S(2)}) collective-permute-start(bf16[96,768]{1,0:T(8,128)(2,1)S(1)} %add_convert_fusion.2.part_a), channel_id=1, source_target_pairs={{0,2},{1,3},{2,0},{3,1},{4,6},{5,7},{6,4},{7,5},{8,10},{9,11},{10,... | collective-permute-start | bytes 442376 | tf_op jit(solution)/shard_map/ppermute | solution.py:547
  100.8 16.0 %collective-permute-start.31 = (bf16[1,48,768]{2,1,0:T(8,128)(2,1)S(1)}, bf16[1,48,768]{2,1,0:T(8,128)(2,1)S(1)}, u32[]{:S(2)}, u32[]{:S(2)}) collective-permute-start(bf16[1,48,768]{2,1,0:T(8,128)(2,1)S(1)} %dynamic-slice_bitcast_fusion.2), channel_id=1, source_target_pairs={{0,4},{4,0},{8,12},{12,8},{16,20},{20,16},{24,28},{28,24},{1,5},{5... | collective-permute-start | bytes 221192 | tf_op jit(solution)/shard_map/ppermute | solution.py:547
  115.3 1.2 collective-permute-start.13
  115.3 9.9 %collective-permute-start.28 = (bf16[2,48,1536]{2,1,0:T(8,128)(2,1)S(1)}, bf16[2,48,1536]{2,1,0:T(8,128)(2,1)S(1)}, u32[]{:S(2)}, u32[]{:S(2)}) collective-permute-start(bf16[2,48,1536]{2,1,0:T(8,128)(2,1)S(1)} %pad_maximum_fusion.3), channel_id=1, source_target_pairs={{0,8},{4,12},{8,0},{12,4},{16,24},{20,28},{24,16},{28,20},{1,9},{5... | collective-permute-start | bytes 884744 | tf_op jit(solution)/shard_map/ppermute | solution.py:547
  116.5 4.1 %collective-permute-start.14 = (f32[16,768]{1,0:T(8,128)S(1)}, f32[16,768]{1,0:T(8,128)S(1)}, u32[]{:S(2)}, u32[]{:S(2)}) collective-permute-start(f32[16,768]{1,0:T(8,128)S(1)} %add.90), channel_id=1, source_target_pairs={{0,2},{1,3},{2,0},{3,1},{4,6},{5,7},{6,4},{7,5},{8,10},{9,11},{10,... | collective-permute-start | bytes 147464 | tf_op jit(solution)/shard_map/ppermute | solution.py:547
  116.9 20.7 %collective-permute-start.32 = (bf16[2,48,768]{2,1,0:T(8,128)(2,1)S(1)}, bf16[2,48,768]{2,1,0:T(8,128)(2,1)S(1)}, u32[]{:S(2)}, u32[]{:S(2)}) collective-permute-start(bf16[2,48,768]{2,1,0:T(8,128)(2,1)S(1)} %pad_maximum_fusion.5), channel_id=1, source_target_pairs={{0,8},{4,12},{8,0},{12,4},{16,24},{20,28},{24,16},{28,20},{1,9},{5... | collective-permute-start | bytes 442376 | tf_op jit(solution)/shard_map/ppermute | solution.py:547
  120.7 5.9 %collective-permute-start.15 = (f32[16,768]{1,0:T(8,128)S(1)}, f32[16,768]{1,0:T(8,128)S(1)}, u32[]{:S(2)}, u32[]{:S(2)}) collective-permute-start(f32[16,768]{1,0:T(8,128)S(1)} %add.91), channel_id=1, source_target_pairs={{0,4},{4,0},{8,12},{12,8},{16,20},{20,16},{24,28},{28,24},{1,5},{5... | collective-permute-start | bytes 147464 | tf_op jit(solution)/shard_map/ppermute | solution.py:547
  126.6 7.5 %collective-permute-start.16 = (f32[16,768]{1,0:T(8,128)S(1)}, f32[16,768]{1,0:T(8,128)S(1)}, u32[]{:S(2)}, u32[]{:S(2)}) collective-permute-start(f32[16,768]{1,0:T(8,128)S(1)} %add.92), channel_id=1, source_target_pairs={{0,8},{4,12},{8,0},{12,4},{16,24},{20,28},{24,16},{28,20},{1,9},{5... | collective-permute-start | bytes 147464 | tf_op jit(solution)/shard_map/ppermute | solution.py:547
  127.6 41.7 %copy-start.7 = (bf16[768,192]{1,0:T(8,128)(2,1)S(1)}, bf16[768,192]{1,0:T(8,128)(2,1)}, u32[]{:S(2)}) copy-start(bf16[768,192]{1,0:T(8,128)(2,1)} %copy-done.6) | copy-start | bytes 884740
  127.6 41.7 %copy-start.9 = (bf16[768,192]{1,0:T(8,128)(2,1)S(1)}, bf16[768,192]{1,0:T(8,128)(2,1)}, u32[]{:S(2)}) copy-start(bf16[768,192]{1,0:T(8,128)(2,1)} %copy-done.8) | copy-start | bytes 884740
  127.6 41.7 %copy-start.57 = (bf16[16,768]{1,0:T(8,128)(2,1)S(1)}, bf16[16,768]{1,0:T(8,128)(2,1)}, u32[]{:S(2)}) copy-start(bf16[16,768]{1,0:T(8,128)(2,1)} %copy-done.56) | copy-start | bytes 73732
  127.6 41.7 %copy-start.65 = (bf16[16,192]{1,0:T(8,128)(2,1)S(1)}, bf16[16,192]{1,0:T(8,128)(2,1)}, u32[]{:S(2)}) copy-start(bf16[16,192]{1,0:T(8,128)(2,1)} %copy-done.64) | copy-start | bytes 18436
  127.6 41.7 %copy-start.68 = (s32[2]{0:T(128)S(1)}, s32[2]{0:T(128)}, u32[]{:S(2)}) copy-start(s32[2]{0:T(128)} %copy-done.66) | copy-start | bytes 28
  128.5 71.4 %collective-permute-start.29 = (bf16[4,48,1536]{2,1,0:T(8,128)(2,1)}, bf16[4,48,1536]{2,1,0:T(8,128)(2,1)}, u32[]{:S(2)}, u32[]{:S(2)}) collective-permute-start(bf16[4,48,1536]{2,1,0:T(8,128)(2,1)} %pad_maximum_fusion.2), channel_id=1, source_target_pairs={{0,16},{4,20},{8,24},{12,28},{16,0},{20,4},{24,8},{28,12},{1,17},{... | collective-permute-start | bytes 1769480 | tf_op jit(solution)/shard_map/ppermute | solution.py:547
  134.2 35.1 %collective-permute-start.17 = (f32[16,768]{1,0:T(8,128)S(1)}, f32[16,768]{1,0:T(8,128)S(1)}, u32[]{:S(2)}, u32[]{:S(2)}) collective-permute-start(f32[16,768]{1,0:T(8,128)S(1)} %add.93.sum_a), channel_id=1, source_target_pairs={{0,16},{4,20},{8,24},{12,28},{16,0},{20,4},{24,8},{28,12},{1,17},{... | collective-permute-start | bytes 147464 | tf_op jit(solution)/shard_map/ppermute | solution.py:547
  137.6 33.1 %copy-start.99 = (bf16[2,48,768]{2,1,0:T(8,128)(2,1)}, bf16[2,48,768]{2,1,0:T(8,128)(2,1)S(1)}, u32[]{:S(2)}) copy-start(bf16[2,48,768]{2,1,0:T(8,128)(2,1)S(1)} %get-tuple-element.176) | copy-start | bytes 442372
  137.6 33.1 %copy-start.100 = (bf16[2,48,768]{2,1,0:T(8,128)(2,1)}, bf16[2,48,768]{2,1,0:T(8,128)(2,1)S(1)}, u32[]{:S(2)}) copy-start(bf16[2,48,768]{2,1,0:T(8,128)(2,1)S(1)} %get-tuple-element.177) | copy-start | bytes 442372
  138.4 57.5 %collective-permute-start.33 = (bf16[4,48,768]{2,1,0:T(8,128)(2,1)}, bf16[4,48,768]{2,1,0:T(8,128)(2,1)}, u32[]{:S(2)}, u32[]{:S(2)}) collective-permute-start(bf16[4,48,768]{2,1,0:T(8,128)(2,1)} %pad_maximum_fusion.4), channel_id=1, source_target_pairs={{0,16},{4,20},{8,24},{12,28},{16,0},{20,4},{24,8},{28,12},{1,17},{... | collective-permute-start | bytes 884744 | tf_op jit(solution)/shard_map/ppermute | solution.py:547
  170.4 2.5 collective-permute-start.18
  171.6 13.6 %copy-start.46 = (f32[1,768]{1,0:T(1,128)S(1)}, f32[1,768]{1,0:T(1,128)}, u32[]{:S(2)}) copy-start(f32[1,768]{1,0:T(1,128)} %copy-done.45) | copy-start | bytes 9220
  171.6 13.6 %copy-start.48 = (bf16[1,768]{1,0:T(2,128)(2,1)S(1)}, bf16[1,768]{1,0:T(2,128)(2,1)}, u32[]{:S(2)}) copy-start(bf16[1,768]{1,0:T(2,128)(2,1)} %copy-done.47) | copy-start | bytes 4612
  171.6 13.6 %copy-start.55 = (bf16[16,768]{1,0:T(8,128)(2,1)S(1)}, bf16[16,768]{1,0:T(8,128)(2,1)}, u32[]{:S(2)}) copy-start(bf16[16,768]{1,0:T(8,128)(2,1)} %copy-done.54) | copy-start | bytes 73732
  171.6 13.6 %copy-start.60 = (f32[1,768]{1,0:T(1,128)S(1)}, f32[1,768]{1,0:T(1,128)}, u32[]{:S(2)}) copy-start(f32[1,768]{1,0:T(1,128)} %copy-done.58) | copy-start | bytes 9220
  171.6 13.6 %copy-start.63 = (bf16[16,192]{1,0:T(8,128)(2,1)S(1)}, bf16[16,192]{1,0:T(8,128)(2,1)}, u32[]{:S(2)}) copy-start(bf16[16,192]{1,0:T(8,128)(2,1)} %copy-done.62) | copy-start | bytes 18436
  171.6 17.7 %copy-start.74 = (f32[8,128]{1,0:T(8,128)S(1)}, f32[8,128]{1,0:T(8,128)}, u32[]{:S(2)}) copy-start(f32[8,128]{1,0:T(8,128)} %copy-done.73) | copy-start | bytes 12292
  172.6 25.7 %collective-permute-start.23 = (bf16[1,3,96,768]{3,2,1,0:T(8,128)(2,1)}, bf16[1,3,96,768]{3,2,1,0:T(8,128)(2,1)}, u32[]{:S(2)}, u32[]{:S(2)}) collective-permute-start(bf16[1,3,96,768]{3,2,1,0:T(8,128)(2,1)} %get-tuple-element.170), channel_id=1, source_target_pairs={{0,2},{1,3},{2,0},{3,1},{4,6},{5,7},{6,4},{7,5},{8,10},{9,11},{10,... | collective-permute-start | bytes 1327112 | tf_op jit(solution)/shard_map/ppermute | solution.py:547
  172.9 12.2 %collective-permute-start.19 = (f32[8,768]{1,0:T(8,128)S(1)}, f32[8,768]{1,0:T(8,128)S(1)}, u32[]{:S(2)}, u32[]{:S(2)}) collective-permute-start(f32[8,768]{1,0:T(8,128)S(1)} %add.94.part_a), channel_id=1, source_target_pairs={{0,2},{1,3},{2,0},{3,1},{4,6},{5,7},{6,4},{7,5},{8,10},{9,11},{10,... | collective-permute-start | bytes 73736 | tf_op jit(solution)/shard_map/ppermute | solution.py:547
  189.3 4.9 %collective-permute-start.20 = (f32[8,768]{1,0:T(8,128)}, f32[8,768]{1,0:T(8,128)}, u32[]{:S(2)}, u32[]{:S(2)}) collective-permute-start(f32[8,768]{1,0:T(8,128)} %get-tuple-element.94), channel_id=1, source_target_pairs={{0,1},{1,0},{2,3},{3,2},{4,5},{5,4},{6,7},{7,6},{8,9},{9,8},{10,11... | collective-permute-start | bytes 73736 | tf_op jit(solution)/shard_map/ppermute | solution.py:547
  195.6 34.8 %collective-permute-start.21 = (f32[8,768]{1,0:T(8,128)}, f32[8,768]{1,0:T(8,128)}, u32[]{:S(2)}, u32[]{:S(2)}) collective-permute-start(f32[8,768]{1,0:T(8,128)} %add.95.part_a), channel_id=1, source_target_pairs={{0,2},{1,3},{2,0},{3,1},{4,6},{5,7},{6,4},{7,5},{8,10},{9,11},{10,... | collective-permute-start | bytes 73736 | tf_op jit(solution)/shard_map/ppermute | solution.py:547
  198.0 42.2 %collective-permute-start.34 = (bf16[1,8,48,768]{3,2,1,0:T(8,128)(2,1)}, bf16[1,8,48,768]{3,2,1,0:T(8,128)(2,1)}, u32[]{:S(2)}, u32[]{:S(2)}) collective-permute-start(bf16[1,8,48,768]{3,2,1,0:T(8,128)(2,1)} %maximum_bitcast_fusion.1), channel_id=1, source_target_pairs={{0,1},{1,0},{2,3},{3,2},{4,5},{5,4},{6,7},{7,6},{8,9},{9,8},{10,11... | collective-permute-start | bytes 1769480 | tf_op jit(solution)/shard_map/ppermute | solution.py:547
  199.8 9.2 %collective-permute-start.24 = (bf16[192,768]{1,0:T(8,128)(2,1)S(1)}, bf16[192,768]{1,0:T(8,128)(2,1)S(1)}, u32[]{:S(2)}, u32[]{:S(2)}) collective-permute-start(bf16[192,768]{1,0:T(8,128)(2,1)S(1)} %value_kernel.1), channel_id=1, source_target_pairs={{0,4},{4,0},{8,12},{12,8},{16,20},{20,16},{24,28},{28,24},{1,5},{5... | collective-permute-start | bytes 884744 | tf_op jit(solution)/shard_map/ppermute | solution.py:547
  202.4 50.7 %collective-permute-start.30 = (bf16[1,8,48,1536]{3,2,1,0:T(8,128)(2,1)}, bf16[1,8,48,1536]{3,2,1,0:T(8,128)(2,1)}, u32[]{:S(2)}, u32[]{:S(2)}) collective-permute-start(bf16[1,8,48,1536]{3,2,1,0:T(8,128)(2,1)} %maximum_bitcast_fusion), channel_id=1, source_target_pairs={{0,1},{1,0},{2,3},{3,2},{4,5},{5,4},{6,7},{7,6},{8,9},{9,8},{10,11... | collective-permute-start | bytes 3538952 | tf_op jit(solution)/shard_map/ppermute | solution.py:547
  209.8 25.3 %collective-permute-start.25 = (bf16[192,768]{1,0:T(8,128)(2,1)}, bf16[192,768]{1,0:T(8,128)(2,1)}, u32[]{:S(2)}, u32[]{:S(2)}) collective-permute-start(bf16[192,768]{1,0:T(8,128)(2,1)} %add_convert_fusion.1), channel_id=1, source_target_pairs={{0,8},{4,12},{8,0},{12,4},{16,24},{20,28},{24,16},{28,20},{1,9},{5... | collective-permute-start | bytes 884744 | tf_op jit(solution)/shard_map/ppermute | solution.py:547
  236.2 16.1 %collective-permute-start.26 = (bf16[192,768]{1,0:T(8,128)(2,1)S(1)}, bf16[192,768]{1,0:T(8,128)(2,1)S(1)}, u32[]{:S(2)}, u32[]{:S(2)}) collective-permute-start(bf16[192,768]{1,0:T(8,128)(2,1)S(1)} %add_convert_fusion), channel_id=1, source_target_pairs={{0,16},{4,20},{8,24},{12,28},{16,0},{20,4},{24,8},{28,12},{1,17},{... | collective-permute-start | bytes 884744 | tf_op jit(solution)/shard_map/ppermute | solution.py:547
  (89 other events, 448.6 us)
Sparse Core Ops, SparseCore 0:
  9.6 21.2 all-gather.2
  32.4 17.4 all-gather.4

commit v2 on v1

v2 whole, which is shorter than its diff:
```python
import functools

import jax
import jax.numpy as jnp
from jax import lax
from jax.experimental import pallas as pl
from jax.experimental.pallas import tpu as pltpu
from jax.sharding import PartitionSpec as P

D = 768
HEADS = 12
HEAD_DIM = 64
ROWS = 16
BLOCK = 16
LANES = 128
PARTS = 4

EPSILON = 1e-06
MASKED = -1e30
FACTOR = D ** (-0.5)
ROOT_HALF = 0.5**0.5
DENSITY = 0.3989422804014327
f32, bf16, i32 = jnp.float32, jnp.bfloat16, jnp.int32
EXACT = lax.Precision.HIGHEST
MIB = 1 << 20


def nn(a, b, precision=None):
    return lax.dot_general(
        a, b, (((1,), (0,)), ((), ())), precision=precision, preferred_element_type=f32
    )


def nt(a, b, precision=None):
    return lax.dot_general(
        a, b, (((1,), (1,)), ((), ())), precision=precision, preferred_element_type=f32
    )


def tn(a, b, precision=None):
    return lax.dot_general(
        a, b, (((0,), (0,)), ((), ())), precision=precision, preferred_element_type=f32
    )


def iota(shape, dim):
    return lax.broadcasted_iota(i32, shape, dim)


def split2(x):
    high = x.astype(bf16)
    return high, (x - high.astype(f32)).astype(bf16)


def split3(x):
    high = x.astype(bf16)
    rest = x - high.astype(f32)
    mid = rest.astype(bf16)
    return high, mid, (rest - mid.astype(f32)).astype(bf16)


def stack3(row, height=ROWS):
    at = iota((height, row.shape[1]), 0)
    parts = split3(row)
    zero = jnp.zeros((), f32)
    out = jnp.where(at == 0, parts[0].astype(f32), zero)
    out = jnp.where(at == 1, parts[1].astype(f32), out)
    return jnp.where(at == 2, parts[2].astype(f32), out).astype(bf16)


def repeat3(row, height=ROWS):
    at = iota((height, row.shape[1]), 0)
    return jnp.where(at < 3, row.astype(f32), 0.0).astype(bf16)


def rms_parts(rows):
    scale = lax.rsqrt(jnp.mean(rows * rows, axis=-1, keepdims=True) + EPSILON)
    return rows * scale, scale


def rms_back(grad_normed, normed, scale):
    inner = jnp.mean(grad_normed * normed, axis=-1, keepdims=True)
    return scale * (grad_normed - normed * inner)


def phi(z):
    return 0.5 * (1.0 + lax.erf(z * ROOT_HALF))


def gelu_slope(z):
    return phi(z) + z * (DENSITY * jnp.exp(-0.5 * z * z))


def head_of(shape, dim):
    return iota(shape, dim) // HEAD_DIM


def spread(small):
    hot = (iota((LANES, D), 0) == head_of((LANES, D), 1)).astype(f32)
    return nn(small, hot, EXACT)


def row_of(ref):
    return ref[...].astype(f32).reshape(1, D)


def gained(n, gain):
    return jnp.broadcast_to(n * row_of(gain), (ROWS, D)).astype(bf16)


def self_parts(start, g_self, wvs):
    x0 = row_of(start)
    n0, _ = rms_parts(x0)
    y1 = gained(n0, g_self)
    return y1, nt(y1, wvs[...]).astype(bf16)


def query_parts(scal, h1, g_cross, wq):
    n1, _ = rms_parts(h1[...])
    y2 = gained(n1, g_cross)
    q = nt(y2, wq[...]).astype(bf16)
    width = q.shape[1]
    first = scal[0] * (width // HEAD_DIM)
    own = iota((ROWS, width), 0) == first + head_of((ROWS, width), 1)
    return y2, jnp.where(own, q.astype(f32), 0.0).astype(bf16)


def self_kernel(start, g_self, wvs, wos, part_out):
    _, s1 = self_parts(start, g_self, wvs)
    part_out[...] = nn(s1, wos[...])[:8]


def query_kernel(scal, part_a, part_b, start, g_cross, wq, wk, qk_out, h1_out):
    h1_out[...] = row_of(start) + (part_a[0:1] + part_b[0:1])
    _, qm = query_parts(scal, h1_out, g_cross, wq)
    qk_out[...] = nn(qm, wk[...])


def select_docs(height, width):
    r, c = iota((height, width), 0), iota((height, width), 1)
    return (((r // BLOCK) == (c % ROWS)) & ((r % BLOCK) == (c // ROWS))).astype(bf16)


def load_kernel(lo, hi, scal, sizes, enc, *refs):
    held, sems = refs[-2:]
    count = sizes[scal[1]]

    def piece(k):
        part = pl.ds(lo + k * BLOCK, BLOCK)
        return pltpu.make_async_copy(enc.at[part], held.at[part], sems.at[k])

    for k in range((hi - lo) // BLOCK):

        @pl.when(lo + k * BLOCK < count)
        def _():
            piece(k).start()

    for k in range((hi - lo) // BLOCK):

        @pl.when(lo + k * BLOCK < count)
        def _():
            piece(k).wait()


def first_doc(scal, sizes):
    groups = sizes.shape[0]

    def body(g, total):
        return total + jnp.where(g < scal[1], sizes[g], 0)

    return lax.fori_loop(0, groups, body, jnp.int32(0), unroll=groups <= 8)


def attend_kernel(base, scal, sizes, lengths, qa, qb, enc, *refs):
    p_out, e_out, ext_out, qk_s = refs[-4:]
    step = pl.program_id(0) + base
    tokens = enc.shape[1]
    count = sizes[scal[1]]
    block = pl.ds(step * BLOCK, BLOCK)
    tall = BLOCK * ROWS

    @pl.when(pl.program_id(0) == 0)
    def _():
        high, low = split2(qa[...] + qb[...])
        qk_s[0:ROWS] = high
        qk_s[ROWS : 2 * ROWS] = low

    @pl.when(step * BLOCK < count)
    def _():
        rows = enc[block].reshape(BLOCK * tokens, D)
        both = nt(qk_s[...], rows)
        logits = both[:ROWS] + both[ROWS:]
        logits = jnp.concatenate(
            [logits[:, b * tokens : (b + 1) * tokens] for b in range(BLOCK)], axis=0
        )
        begin = first_doc(scal, sizes)
        shown = []
        for b in range(BLOCK):
            slot = step * BLOCK + b
            doc = jnp.minimum(begin + slot, lengths.shape[0] - 1)
            length = jnp.where(slot < count, lengths[doc] - scal[0] * tokens, 0)
            shown.append(jnp.broadcast_to(length, (ROWS, tokens)))
        seen = jnp.concatenate(shown, axis=0)
        seen = iota((tall, tokens), 1) < seen
        logits = jnp.where(seen, logits, MASKED)
        peak = jnp.max(logits, axis=1, keepdims=True)
        raised = jnp.where(seen, jnp.exp(logits - peak), 0.0)
        total = jnp.sum(raised, axis=1, keepdims=True)
        p_out[...] = raised.reshape(BLOCK, ROWS, tokens)
        low = raised.astype(bf16)
        sums = []
        upper = iota((2 * ROWS, tokens), 0) < ROWS
        zero = jnp.zeros((2 * ROWS, tokens), bf16)
        for k in range(BLOCK // 2):
            pair = low[2 * ROWS * k : 2 * ROWS * (k + 1)]
            left = jnp.concatenate(
                [jnp.where(upper, pair, zero), jnp.where(upper, zero, pair)], axis=1
            )
            sums.append(nn(left, rows[2 * tokens * k : 2 * tokens * (k + 1)]))
        summed = jnp.concatenate(sums, axis=0).astype(bf16)
        e_out[...] = (
            nn(select_docs(HEADS * BLOCK, tall), summed)
            .astype(bf16)
            .reshape(HEADS, BLOCK, D)
        )
        gather = (iota((BLOCK, tall), 0) == iota((BLOCK, tall), 1) // ROWS).astype(bf16)
        parts = split3(peak) + split3(total)
        at = iota((tall, LANES), 1)
        extra = jnp.zeros((tall, LANES), f32)
        for k, part in enumerate(parts):
            extra = jnp.where(at // ROWS == k, part.astype(f32), extra)
        extra = jnp.where(at % ROWS == iota((tall, LANES), 0) % ROWS, extra, 0.0)
        ext_out[...] = nn(gather, extra.astype(bf16)).astype(bf16)

    @pl.when(step * BLOCK >= count)
    def _():
        p_out[...] = jnp.zeros_like(p_out)
        e_out[...] = jnp.zeros_like(e_out)
        ext_out[...] = jnp.where(iota((BLOCK, LANES), 1) < ROWS, MASKED, 0.0).astype(bf16)


def place_parts(scal, full, own, by2, by1, by3):
    height = own.shape[0]
    for mask, piece in ((0, own), (2, by2), (1, by1), (3, by3)):
        at = pl.multiple_of((scal[0] ^ mask) * height, height)
        full[pl.ds(at, height)] = piece[...]


def project_kernel(scal, summed, extra, own, by2, by1, by3, pay_out, wv):
    place_parts(scal, wv, own, by2, by1, by3)
    even = iota((summed.shape[1], LANES), 1) < HEAD_DIM
    for k in range(HEADS // 2):
        pair = wv[k * LANES : (k + 1) * LANES]
        one, two = nt(summed[2 * k], pair), nt(summed[2 * k + 1], pair)
        pay_out[:, k * LANES : (k + 1) * LANES] = jnp.where(even, one, two).astype(bf16)
    pay_out[:, D:] = extra[...]


def decode(pay):
    extra = pay[:, D:].astype(f32)

    def lane(k):
        return pltpu.roll(extra, LANES - k * ROWS, 1) if k else extra

    first = iota(extra.shape, 1) < ROWS
    peak = jnp.where(first, (lane(0) + lane(1)) + lane(2), 0.0)
    total = jnp.where(first, (lane(3) + lane(4)) + lane(5), 0.0)
    return peak, total


def merge(one, two):
    peak1, total1 = decode(one)
    peak2, total2 = decode(two)
    peak = jnp.maximum(peak1, peak2)
    up1, up2 = jnp.exp(peak1 - peak), jnp.exp(peak2 - peak)
    total = up1 * total1 + up2 * total2
    first = iota(peak.shape, 1) < ROWS
    up1, up2 = jnp.where(first, up1, 0.0), jnp.where(first, up2, 0.0)
    context = spread(up1) * one[:, :D].astype(f32) + spread(up2) * two[:, :D].astype(f32)
    return peak, total, context


def ordered(bit, own, other):
    swap = jnp.broadcast_to(bit, own.shape) == 1
    return jnp.where(swap, other, own), jnp.where(swap, own, other)


def merge_kernel(scal, own, other, pay_out):
    one, two = ordered(scal[0] & 1, own[...].astype(f32), other[...].astype(f32))
    peak, total, context = merge(one, two)
    pay_out[:, :D] = context.astype(bf16)
    extra = jnp.zeros(peak.shape, f32)
    at = iota(peak.shape, 1) // ROWS
    for k, part in enumerate(split3(peak) + split3(total)):
        part = part.astype(f32)
        extra = jnp.where(at == k, pltpu.roll(part, k * ROWS, 1) if k else part, extra)
    pay_out[:, D:] = extra.astype(bf16)


def own_half(scal, rows, held, out):
    half = out.shape[0]
    held[...] = rows
    out[...] = held[pl.ds(pl.multiple_of((scal[0] & 1) * half, half), half)]


def forward_kernel(
    scal, own, other, first, h1, wo_own, wo_by2, wo_by1, wo_by3, g_ff, win, wdown,
    c_out, c32_out, scale_out, h2_out, z_out, part_out, wo, c_s,
):
    place_parts(scal, wo, wo_own, wo_by2, wo_by1, wo_by3)
    bit = lax.shift_right_logical(scal[0], 1) & 1
    one, two = ordered(bit, own[...].astype(f32), other[...].astype(f32))
    peak, total, context = merge(one, two)
    lanes = iota(peak.shape, 1) < ROWS
    inverse = jnp.where(lanes & (total > 0.0), 1.0 / jnp.where(total > 0.0, total, 1.0), 0.0)
    context = context * spread(inverse)
    mine, _ = decode(first[...].astype(f32))
    scale_out[...] = jnp.exp(jnp.minimum(mine - peak, 0.0)) * inverse
    c32_out[...] = context
    low = context.astype(bf16)
    own_half(scal, low, c_s, c_out)
    h2 = h1[...] + nn(low, wo[...])
    h2_out[...] = h2
    n2, _ = rms_parts(h2)
    y3 = (n2 * row_of(g_ff)).astype(bf16)
    z = nn(y3, win[...])
    z_out[...] = z
    u = (z * phi(z)).astype(bf16)
    part_out[...] = nn(u, wdown[...]).astype(bf16)


def score_kernel(
    scal, part_a, part_b, h2, z, g_final, row, wdown, win,
    scores_out, n3_out, dh3_out, part_out,
):
    h3 = h2[...] + (part_a[...].astype(f32) + part_b[...].astype(f32))
    n3, r3 = rms_parts(h3)
    n3_out[...] = n3
    wanted = jnp.broadcast_to(row_of(g_final) * row_of(row) * FACTOR, (8, D))
    scores = nt(wanted, n3, EXACT)[0:1]
    slots = n3.shape[0]
    groups = scores_out.shape[0]
    wide = jnp.concatenate([scores, jnp.zeros((1, LANES - slots), f32)], axis=1)
    scores_out[...] = jnp.where(iota((groups, LANES), 0) == scal[1], wide, 0.0)
    dh3 = rms_back(wanted[0:1], n3, r3).astype(bf16)
    dh3_out[...] = dh3
    du = nt(dh3, wdown[...])
    dz = (du * gelu_slope(z[...])).astype(bf16)
    part_out[...] = nt(dz, win[...]).astype(bf16)


def list_kernel(scal, sizes, lens, sc_a, sc_b, rel, scores_out, loss_out, ds_out, mine_out):
    groups = sc_a.shape[0]
    docs = ds_out.shape[1]
    wide = docs + LANES
    queries = lens.shape[0]
    relevance = rel[...].reshape(1, docs)
    scores = sc_a[...] + sc_b[...]
    lane = iota((8, LANES), 1)
    blank = jnp.zeros((8, wide - LANES), f32)
    placed = jnp.zeros((8, wide), f32)
    start = jnp.int32(0)
    for g in range(groups):
        kept = jnp.where(lane < sizes[g], scores[g : g + 1], 0.0)
        placed = placed + pltpu.roll(jnp.concatenate([kept, blank], axis=1), start, 1)
        start = start + sizes[g]
    at = iota((queries, 1), 0)

    def one_list(j, found):
        begin, begins, ends = found
        end = begin + lens[j]
        return end, jnp.where(at == j, begin, begins), jnp.where(at == j, end, ends)

    none = jnp.zeros((queries, 1), i32)
    _, begins, ends = lax.fori_loop(
        0, queries, one_list, (jnp.int32(0), none, none), unroll=queries <= 32
    )
    values = placed[0:1, :docs]
    scores_out[...] = values.reshape(scores_out.shape)
    place = iota((queries, docs), 1)
    member = (place >= begins) & (place < ends)
    peak = jnp.max(jnp.where(member, values, MASKED), axis=1, keepdims=True)
    raised = jnp.where(member, jnp.exp(jnp.where(member, values - peak, 0.0)), 0.0)
    log_total = peak + jnp.log(jnp.sum(raised, axis=1, keepdims=True))
    weight = jnp.sum(jnp.where(member, relevance, 0.0), axis=1, keepdims=True)
    target = jnp.where(member, relevance / weight, 0.0)
    picked = jnp.sum(target * values, axis=1, keepdims=True)
    loss_out[...] = jnp.sum(log_total - picked, axis=0, keepdims=True) / queries
    chance = jnp.where(member, jnp.exp(jnp.where(member, values - log_total, 0.0)), 0.0)
    ds = jnp.sum(chance - target, axis=0, keepdims=True) / queries
    ds_out[...] = ds
    ds = jnp.broadcast_to(jnp.concatenate([ds, jnp.zeros((1, LANES), f32)], axis=1), (8, wide))
    start = first_doc(scal, sizes)
    back = pltpu.roll(ds, lax.rem(wide - start, wide), 1)[:, :LANES]
    mine_out[...] = jnp.where(lane < sizes[scal[1]], back, 0.0)


def context_kernel(
    scal, part_a, part_b, h2, dh3, c32, g_ff, wo_own, wo_by2, wo_by1, wo_by3,
    dh2_out, half_out, dc_out, own_out, inner_out, ff_out, wout, both_s,
):
    place_parts(scal, wout, wo_own, wo_by2, wo_by1, wo_by3)
    n2, r2 = rms_parts(h2[...])
    dy3 = part_a[...].astype(f32) + part_b[...].astype(f32)
    ff_out[...] = dy3 * n2
    dh2 = (dh3[...].astype(f32) + rms_back(dy3 * row_of(g_ff), n2, r2)).astype(bf16)
    dh2_out[...] = dh2
    own_half(scal, jnp.concatenate([dh3[...], dh2], axis=1), both_s, half_out)
    dc = nt(dh2, wout[...]).astype(bf16)
    dc_out[...] = dc
    own_out[...] = nt(dh2, wo_own[...]).astype(bf16)
    hot = (head_of((D, LANES), 0) == iota((D, LANES), 1)).astype(f32)
    inner_out[...] = nn(dc.astype(f32) * c32[...], hot, EXACT)


def column(rows):
    tall = BLOCK * ROWS
    pick = (iota((tall, BLOCK), 0) // ROWS == iota((tall, BLOCK), 1)).astype(f32)
    wide = nn(pick, rows, EXACT)
    own = iota((tall, LANES), 0) % ROWS == iota((tall, LANES), 1)
    return jnp.sum(jnp.where(own, wide, 0.0), axis=1, keepdims=True)


def back_kernel(
    scal, sizes, enc, p, scale, inner, dc, wv_own, wv_by2, wv_by1, wv_by3,
    dap_out, vd_out, wv,
):
    step = pl.program_id(0)

    @pl.when(step == 0)
    def _():
        place_parts(scal, wv, wv_own, wv_by2, wv_by1, wv_by3)

    tokens = enc.shape[1]
    tall = BLOCK * ROWS

    @pl.when(step * BLOCK < sizes[scal[1]])
    def _():
        rows = enc[pl.ds(step * BLOCK, BLOCK)].reshape(BLOCK * tokens, D)
        pick = (iota((tall, BLOCK), 0) // ROWS == iota((tall, BLOCK), 1)).astype(bf16)
        own = (iota((tall, D), 0) % ROWS) == head_of((tall, D), 1)
        grad = jnp.where(own, nn(pick, dc[...]), 0.0).astype(bf16)
        vd = nn(grad, wv[...]).astype(bf16)
        vd_out[...] = vd.reshape(BLOCK, ROWS, D)
        grad_probs = []
        for k in range(BLOCK // 2):
            pair = nt(
                vd[2 * ROWS * k : 2 * ROWS * (k + 1)],
                rows[2 * tokens * k : 2 * tokens * (k + 1)],
            )
            grad_probs += [pair[:ROWS, :tokens], pair[ROWS:, tokens:]]
        grad_probs = jnp.concatenate(grad_probs, axis=0)
        prob = p[...].reshape(tall, tokens) * column(scale[...])
        da = (prob * (grad_probs - column(inner[...]))).astype(bf16)
        dap_out[:, :ROWS] = da.reshape(BLOCK, ROWS, tokens)
        dap_out[:, ROWS:] = prob.astype(bf16).reshape(BLOCK, ROWS, tokens)

    @pl.when(step * BLOCK >= sizes[scal[1]])
    def _():
        dap_out[...] = jnp.zeros_like(dap_out)
        vd_out[...] = jnp.zeros_like(vd_out)


def key_sum_kernel(scal, sizes, ds, enc, da, dh2, n3, ff, sums_out):
    step = pl.program_id(0)
    tokens = enc.shape[1]
    tall = BLOCK * ROWS

    @pl.when(step == 0)
    def _():
        slots = dh2.shape[0]
        row = ds[...][:, :slots] * (1.0 / PARTS)
        at = iota((ROWS, D), 0)
        out = jnp.where(at == HEADS, nn(row, dh2[...].astype(f32), EXACT)[0:1], 0.0)
        out = jnp.where(at == HEADS + 1, nn(row, n3[...], EXACT)[0:1], out)
        sums_out[...] = jnp.where(at == HEADS + 2, nn(row, ff[...], EXACT)[0:1], out)

    @pl.when(step * BLOCK < sizes[scal[1]])
    def _():
        rows = enc[pl.ds(step * BLOCK, BLOCK)].reshape(BLOCK * tokens, D)
        own_slot = iota((tall, LANES), 1) == step * BLOCK + iota((tall, LANES), 0) // ROWS
        ds_col = jnp.sum(jnp.where(own_slot, ds[0:1], 0.0), axis=1, keepdims=True)
        scaled = (da[...].reshape(tall, tokens).astype(f32) * ds_col).astype(bf16)
        flat = jnp.concatenate(
            [scaled[ROWS * b : ROWS * (b + 1)] for b in range(BLOCK)], axis=1
        )
        sums_out[...] += nn(flat, rows)


def enc_grad_kernel(base, scal, sizes, ds, qa, qb, dap, vd, *refs):
    grad_out = refs[-1]
    step = pl.program_id(0) + base

    @pl.when(step * BLOCK < sizes[scal[1]])
    def _():
        qk = qa[...] + qb[...]
        lane = iota((1, LANES), 1)
        for b in range(BLOCK):
            scale = jnp.sum(
                jnp.where(lane == step * BLOCK + b, ds[0:1], 0.0), axis=1, keepdims=True
            )
            right = jnp.concatenate([qk, vd[b].astype(f32)], axis=0) * scale
            grad_out[b] = tn(dap[b], right.astype(bf16)).astype(bf16)

    @pl.when(step * BLOCK >= sizes[scal[1]])
    def _():
        grad_out[...] = jnp.zeros_like(grad_out)


def share_kernel(scal, summed, scale, keep_out, send_out):
    core = scal[0] & 1
    lane = iota(scale.shape, 1)
    for out, bit in ((send_out, 1 - core), (keep_out, core)):
        for y in range(out.shape[0]):
            for k in range(out.shape[1]):
                head = (2 * y + bit) * out.shape[1] + k
                col = jnp.sum(jnp.where(lane == head, scale[...], 0.0), axis=1, keepdims=True)
                out[y, k] = (summed[head].astype(f32) * col).astype(bf16)


def away_kernel(scal, keep, got, out):
    part = 1 - (lax.shift_right_logical(scal[0], 1) & 1)
    for h in range(out.shape[0]):
        out[h] = (keep[part, h].astype(f32) + got[part, h].astype(f32)).astype(bf16)


def value_kernel(scal, keep, got, other, dc, ds, grad_out):
    slots = keep.shape[2]
    part = lax.shift_right_logical(scal[0], 1) & 1
    own_slot = iota((slots, LANES), 0) == iota((slots, LANES), 1)
    ds_col = jnp.sum(jnp.where(own_slot, ds[0:1], 0.0), axis=1, keepdims=True)
    grad = (dc[...].astype(f32) * ds_col).astype(bf16)
    for h in range(keep.shape[1]):
        pair = (keep[part, h].astype(f32) + got[part, h].astype(f32)).astype(bf16)
        summed = (pair.astype(f32) + other[h].astype(f32)).astype(bf16)
        out = tn(grad[:, h * HEAD_DIM : (h + 1) * HEAD_DIM], summed)
        grad_out[h * HEAD_DIM : (h + 1) * HEAD_DIM] = out.astype(bf16)


def document_picks(order, tile, scal, sizes, held, first):
    groups = 1 << len(order)
    half = held // groups
    core = scal[0] & 1
    doc = first + iota((tile, 1), 0)

    def one_group(g, found):
        start, at, upper = found
        mask = g ^ scal[1]
        pos = 0
        for k, bit in enumerate(order):
            pos = pos + (lax.shift_right_logical(mask, bit.bit_length() - 1) & 1) * (1 << k)
        slot = doc - start
        inside = (slot >= 0) & (slot < sizes[g])
        later = (slot >= half).astype(i32)
        at = jnp.where(inside, pos * half + slot - half * later, at)
        return start + sizes[g], at, jnp.where(inside, later, upper)

    zero = jnp.zeros((tile, 1), i32)
    _, at, upper = lax.fori_loop(
        0, groups, one_group, (jnp.int32(0), zero, zero), unroll=groups <= 8
    )
    hit = iota((tile, held), 1) == at
    mine = (hit & (upper == core)).astype(bf16)
    theirs = (hit & (upper != core)).astype(bf16)
    return lambda own, other: (nn(mine, own[...]) + nn(theirs, other[...])).astype(bf16)


def ds_column(ds, first, tile):
    eye = iota((tile, tile), 0) == iota((tile, tile), 1)
    return jnp.sum(jnp.where(eye, ds[0:1, pl.ds(first, tile)], 0.0), axis=1, keepdims=True)


def over_tiles(docs, tile, one_tile):
    one_tile(0, True)
    if docs > tile:

        @pl.loop(1, docs // tile)
        def _(t):
            one_tile(pl.multiple_of(t * tile, tile), False)


def put(out, value, new):
    if new:
        out[...] = value
    else:
        out[...] += value


def weights_kernel(
    order, tile, scal, sizes, c_own, c_other, both_own, both_other, ds,
    h1, g_ff, wo_own, wo_by2, wo_by1, wo_by3, win, wdown,
    win_out, wdown_out, wout_out, wout,
):
    place_parts(scal, wout, wo_own, wo_by2, wo_by1, wo_by3)

    def one_tile(first, new):
        rows = document_picks(order, tile, scal, sizes, c_own.shape[0], first)
        c = rows(c_own, c_other)
        h2 = h1[...] + nn(c, wout[...])
        n2, _ = rms_parts(h2)
        y3 = (n2 * row_of(g_ff)).astype(bf16)
        z = nn(y3, win[...])
        u = (z * phi(z)).astype(bf16)
        both = rows(both_own, both_other).astype(f32) * ds_column(ds, first, tile)
        dh3, dh2 = both[:, :D].astype(bf16), both[:, D:].astype(bf16)
        dz = (nt(dh3, wdown[...]) * gelu_slope(z)).astype(bf16)
        put(win_out, tn(y3, dz), new)
        put(wdown_out, tn(u, dh3), new)
        width = wout_out.shape[0]
        pick = (iota((D, width), 0) == scal[0] * width + iota((D, width), 1)).astype(bf16)
        put(wout_out, tn(nn(c, pick).astype(bf16), dh2), new)

    over_tiles(ds.shape[1], tile, one_tile)


def key_kernel(scal, sum_a, sum_b, h1, g_cross, wk, wq, key_out, query_out, part_out):
    y2, qm = query_parts(scal, h1, g_cross, wq)
    g = sum_a[...] + sum_b[...]
    g = jnp.where(iota((ROWS, D), 0) < HEADS, g, 0.0)
    high, low = split2(g)
    both = jnp.concatenate([high, low], axis=0)
    dq = nt(both, wk[...])
    dq = dq[:ROWS] + dq[ROWS:]
    width = dq.shape[1]
    first = scal[0] * (width // HEAD_DIM)
    own = iota((ROWS, width), 0) == first + head_of((ROWS, width), 1)
    dq = jnp.sum(jnp.where(own, dq, 0.0), axis=0, keepdims=True)
    key_out[...] = tn(jnp.concatenate([qm, qm], axis=0), both)
    dq_parts = stack3(dq)
    query_out[...] = tn(dq_parts, repeat3(y2[0:1]))
    part = jnp.sum(nn(dq_parts, wq[...]), axis=0, keepdims=True)
    part_out[...] = jnp.broadcast_to(part, (8, D))


def hidden_kernel(
    part_a, part_b, sum_a, sum_b, h1, g_cross, start, g_self, wos, wvs, g_final, row,
    dh1_out, wos_out, wvs_out, part_out, cross_out, final_out, row_out, ff_out,
):
    y1, s1 = self_parts(start, g_self, wvs)
    dy2 = part_a[0:1] + part_b[0:1]
    sums = sum_a[...] + sum_b[...]
    n1, r1 = rms_parts(h1[...])
    cross_out[...] = (dy2 * n1).reshape(cross_out.shape)
    dh1 = sums[HEADS : HEADS + 1] + rms_back(dy2 * row_of(g_cross), n1, r1)
    dh1_out[...] = dh1
    dh1_parts = stack3(dh1)
    wos_out[...] = tn(repeat3(s1[0:1]), dh1_parts)
    ds1 = jnp.sum(nt(dh1_parts, wos[...]), axis=0, keepdims=True)
    ds1_parts = stack3(ds1)
    wvs_out[...] = tn(ds1_parts, repeat3(y1[0:1]))
    part = jnp.sum(nn(ds1_parts, wvs[...]), axis=0, keepdims=True)
    part_out[...] = jnp.broadcast_to(part, (8, D))
    total = sums[HEADS + 1 : HEADS + 2] * FACTOR
    final_out[...] = (total * row_of(row)).reshape(final_out.shape)
    row_out[...] = (total * row_of(g_final)).reshape(row_out.shape)
    ff_out[...] = sums[HEADS + 2 : HEADS + 3].reshape(ff_out.shape)


def start_kernel(part_a, part_b, dh1, start, g_self, gain_out, start_out):
    dy1 = part_a[0:1] + part_b[0:1]
    n0, r0 = rms_parts(row_of(start))
    gain_out[...] = (dy1 * n0).reshape(gain_out.shape)
    back = dh1[...] + rms_back(dy1 * row_of(g_self), n0, r0)
    start_out[...] = back.reshape(start_out.shape)


def shape(dims, dtype=f32):
    return jax.ShapeDtypeStruct(dims, dtype)


def whole_spec(memory=pltpu.VMEM):
    return pl.BlockSpec(memory_space=memory)


def name_of(kernel):
    return getattr(kernel, "func", kernel).__name__


def in_hbm(x):
    return pltpu.with_memory_space_constraint(x, pltpu.HBM)


def plain(kernel, outs, *args, smem=0, flops=0, limit=12, scratch=()):
    size = sum(a.size * a.dtype.itemsize for a in args)
    return pl.pallas_call(
        kernel,
        out_shape=outs,
        in_specs=[whole_spec(pltpu.SMEM if k < smem else pltpu.VMEM) for k in range(len(args))],
        out_specs=jax.tree.map(lambda _: whole_spec(), outs),
        scratch_shapes=list(scratch),
        compiler_params=pltpu.CompilerParams(vmem_limit_bytes=limit * MIB),
        cost_estimate=pl.CostEstimate(flops=flops, bytes_accessed=size, transcendentals=0),
        name=name_of(kernel),
    )(*args)


def gridded(kernel, steps, scalars, ins, outs, scratch=(), flops=0, limit=14, onto=()):
    size = sum(a.size * a.dtype.itemsize for a, _, _ in ins)
    size += sum(s.size * s.dtype.itemsize for s, _, _ in outs)
    count = len(scalars) + len(ins)
    return pl.pallas_call(
        kernel,
        out_shape=[s for s, _, _ in outs],
        grid_spec=pltpu.PrefetchScalarGridSpec(
            num_scalar_prefetch=len(scalars),
            grid=(steps,),
            in_specs=[
                pl.BlockSpec(block, index) if block else whole_spec() for _, block, index in ins
            ]
            + [pl.BlockSpec(memory_space=pl.ANY)] * len(onto),
            out_specs=[pl.BlockSpec(block, index) for _, block, index in outs],
            scratch_shapes=list(scratch),
        ),
        input_output_aliases={count + k: k for k in range(len(onto))},
        compiler_params=pltpu.CompilerParams(
            vmem_limit_bytes=limit * MIB, dimension_semantics=("arbitrary",)
        ),
        cost_estimate=pl.CostEstimate(flops=flops, bytes_accessed=size, transcendentals=0),
        name=name_of(kernel),
    )(*scalars, *[a for a, _, _ in ins], *onto)


def bits_of(size):
    return [1 << b for b in range(size.bit_length() - 1)]


def long_first(size):
    bits = bits_of(size)
    return bits[1:] + bits[:1]


def swap(x, axis, bit):
    size = lax.axis_size(axis)
    return lax.ppermute(x, axis, [(i, i ^ bit) for i in range(size)])


def after(x, *deps):
    return lax.optimization_barrier((x, *deps))[0]


def add(x, y):
    return (x.astype(f32) + y.astype(f32)).astype(x.dtype)


def sum_last(x, steps):
    for axis, bit in steps[:-1]:
        x = add(x, swap(x, axis, bit))
    axis, bit = steps[-1]
    return x, swap(x, axis, bit)


def per_device(
    enc_out,
    enc_len,
    group_docs,
    list_len,
    relevance,
    start_token,
    score_row,
    g_self,
    w_value_self,
    w_out_self,
    g_cross,
    w_query,
    w_key,
    w_value,
    w_out,
    g_ff,
    w_in,
    w_down,
    g_final,
):
    groups = lax.axis_size("docs")
    parts = lax.axis_size("heads")
    assert parts == PARTS
    me_g = lax.axis_index("docs")
    me_j = lax.axis_index("heads")
    slots, tokens = enc_out.shape[:2]
    docs = enc_len.shape[0]
    width = w_value.shape[1]
    own_heads = HEADS // parts
    hidden = w_in.shape[1]
    blocks = slots // BLOCK
    over_heads = [("heads", 1), ("heads", 2)]
    order = long_first(groups)
    over_docs = [("docs", bit) for bit in order]

    scal = jnp.stack([me_j, me_g])
    wvs_t, wq_t, wk_t, wv_t = (w.T for w in (w_value_self, w_query, w_key, w_value))

    wv_by1, wo_by1 = swap(wv_t, "heads", 1), swap(w_out, "heads", 1)

    part = plain(
        self_kernel,
        shape((8, D)),
        *map(in_hbm, (start_token, g_self, wvs_t, w_out_self)),
    )

    def load(lo, hi, onto=()):
        return pl.pallas_call(
            functools.partial(load_kernel, lo, hi),
            out_shape=pltpu.VMEM(enc_out.shape, bf16),
            in_specs=[whole_spec(pltpu.SMEM)] * 2
            + [whole_spec(pltpu.HBM)]
            + [whole_spec()] * len(onto),
            out_specs=whole_spec(),
            scratch_shapes=[pltpu.SemaphoreType.DMA(((hi - lo) // BLOCK,))],
            input_output_aliases={3: 0} if onto else {},
            compiler_params=pltpu.CompilerParams(vmem_limit_bytes=MIB),
            cost_estimate=pl.CostEstimate(
                flops=0, bytes_accessed=(hi - lo) * tokens * D * 4, transcendentals=0
            ),
            name="load_kernel",
        )(scal, group_docs, in_hbm(enc_out), *onto)

    middle = slots // 2
    part = add(part, swap(part, "heads", 1))
    part_a, part_b = part, swap(part, "heads", 2)
    held = load(0, middle)
    part_b, held = lax.optimization_barrier((part_b, held))
    qk, h1 = plain(
        query_kernel,
        [shape((ROWS, D)), shape((1, D))],
        scal,
        part_a,
        part_b,
        *map(in_hbm, (start_token, g_cross, wq_t, wk_t)),
        smem=1,
    )
    qk, held = lax.optimization_barrier((qk, held))
    qk_a, qk_b = sum_last(qk, over_heads)
    held = load(middle, slots, (held,))

    const2 = lambda i, *_: (0, 0)
    step2 = lambda i, *_: (i, 0)
    step3 = lambda i, *_: (i, 0, 0)
    pass_flops = 2 * slots * tokens * D * 256

    def attend(base, steps, onto=()):
        return gridded(
            functools.partial(attend_kernel, base),
            steps,
            [scal, group_docs, enc_len],
            [
                (qk_a, (ROWS, D), const2),
                (qk_b, (ROWS, D), const2),
                (held, None, None),
            ],
            [
                (
                    shape((slots, ROWS, tokens)),
                    (BLOCK, ROWS, tokens),
                    lambda i, *_: (i + base, 0, 0),
                ),
                (
                    shape((HEADS, slots, D), bf16),
                    (HEADS, BLOCK, D),
                    lambda i, *_: (0, i + base, 0),
                ),
                (
                    shape((slots, LANES), bf16),
                    (BLOCK, LANES),
                    lambda i, *_: (i + base, 0),
                ),
            ],
            scratch=[pltpu.VMEM((2 * ROWS, D), bf16)],
            flops=2 * pass_flops * steps // blocks,
            onto=onto,
        )

    split = 4
    wv_by2 = swap(after(wv_t, qk_b), "heads", 2)
    prob, summed, extra = attend(0, split)
    prob, wv_by2 = lax.optimization_barrier((prob, wv_by2))
    wv_by3 = swap(wv_by2, "heads", 1)
    wo_by2 = swap(after(w_out, wv_by2), "heads", 2)
    prob, summed, extra = attend(split, blocks - split, (prob, summed, extra))
    wv_parts = (wv_t, wv_by2, wv_by1, wv_by3)
    full = [pltpu.VMEM((D, D), bf16)]
    pay = plain(
        project_kernel,
        shape((slots, D + LANES), bf16),
        scal,
        summed,
        extra,
        *wv_parts,
        smem=1,
        scratch=full,
    )
    wo_by3 = swap(wo_by2, "heads", 1)
    wo_parts = (w_out, wo_by2, wo_by1, wo_by3)
    merged = plain(
        merge_kernel, shape(pay.shape, bf16), scal, pay, swap(pay, "heads", 1), smem=1
    )
    other = swap(merged, "heads", 2)

    c, c32, scale, h2, z, part = plain(
        forward_kernel,
        [
            shape((slots // 2, D), bf16),
            shape((slots, D)),
            shape((slots, LANES)),
            shape((slots, D)),
            shape((slots, hidden)),
            shape((slots, D), bf16),
        ],
        scal,
        merged,
        other,
        pay,
        h1,
        *wo_parts,
        g_ff,
        w_in,
        w_down,
        smem=1,
        scratch=full + [pltpu.VMEM((slots, D), bf16)],
    )

    half = slots // 2

    def grow(x, k):
        return jnp.concatenate([x, swap(x, *over_docs[k])], axis=0)

    def tie(*xs):
        return lax.optimization_barrier(xs)

    last = len(over_docs) - 1
    part = add(part, swap(part, "heads", 1))
    part, c, summed = tie(part, c, summed)
    part_a, part_b = part, swap(part, "heads", 2)
    c_all = grow(c, 0)
    keep, sent = plain(
        share_kernel, [shape((2, own_heads, slots, D), bf16)] * 2, scal, summed, scale, smem=1
    )
    part_b, c_all, sent = tie(part_b, c_all, sent)
    scores, n3, dh3, part = plain(
        score_kernel,
        [
            shape((groups, LANES)),
            shape((slots, D)),
            shape((slots, D), bf16),
            shape((slots, D), bf16),
        ],
        scal,
        part_a,
        part_b,
        h2,
        z,
        g_final,
        score_row,
        w_down,
        w_in,
        smem=1,
    )
    part = add(part, swap(part, "heads", 1))
    got = swap(sent, "heads", 1)
    part_a, part_b = part, swap(part, "heads", 2)
    near_first = [("docs", bit) for bit in bits_of(groups)]
    score_a, score_b = scores, swap(scores, *near_first[0])
    part_b, got, score_b = tie(part_b, got, score_b)
    for k in range(1, last):
        score_a = score_a + score_b
        score_b = swap(score_a, *near_first[k])
    for k in range(1, last):
        c_all = grow(c_all, k)
    dh2, grads, dc, dc_own, inner, ff = plain(
        context_kernel,
        [
            shape((slots, D), bf16),
            shape((half, 2 * D), bf16),
            shape((slots, D), bf16),
            shape((slots, width), bf16),
            shape((slots, LANES)),
            shape((slots, D)),
        ],
        scal,
        part_a,
        part_b,
        h2,
        dh3,
        c32,
        g_ff,
        *wo_parts,
        smem=1,
        scratch=full + [pltpu.VMEM((slots, 2 * D), bf16)],
    )

    away = plain(
        away_kernel, shape((own_heads, slots, D), bf16), scal, keep, got, smem=1
    )
    score_a = score_a + score_b
    score_a, c_all, away, dc, grads = tie(score_a, c_all, away, dc, grads)
    score_b = swap(score_a, *near_first[last])
    other = swap(away, "heads", 2)
    grads = grow(grads, 0)
    c_all = grow(c_all, last)

    dap, vd = gridded(
        back_kernel,
        blocks,
        [scal, group_docs],
        [
            (held, None, None),
            (prob, (BLOCK, ROWS, tokens), step3),
            (scale, (BLOCK, LANES), step2),
            (inner, (BLOCK, LANES), step2),
            (dc, (BLOCK, D), step2),
        ]
        + [(w, (width, D), const2) for w in wv_parts],
        [
            (shape((slots, 2 * ROWS, tokens), bf16), (BLOCK, 2 * ROWS, tokens), step3),
            (shape((slots, ROWS, D), bf16), (BLOCK, ROWS, D), step3),
        ],
        scratch=full,
        flops=pass_flops,
    )
    dap, score_b, grads, c_all, other = tie(dap, score_b, grads, c_all, other)
    all_scores, loss, ds_docs, ds_mine = plain(
        list_kernel,
        [shape((docs,)), shape((1, 1)), shape((1, docs)), shape((8, LANES))],
        scal,
        group_docs,
        list_len,
        score_a,
        score_b,
        in_hbm(relevance),
        smem=3,
    )
    value_part = plain(
        value_kernel,
        shape((width, D), bf16),
        scal,
        keep,
        got,
        other,
        dc_own,
        ds_mine,
        smem=1,
    )
    dap, value_part, grads = tie(dap, value_part, grads)
    value_far = swap(value_part, *near_first[0])
    grads_far = swap(grads, *over_docs[1])
    (sums,) = gridded(
        key_sum_kernel,
        blocks,
        [scal, group_docs],
        [
            (ds_mine, (8, LANES), const2),
            (held, None, None),
            (dap, (BLOCK, ROWS, tokens), step3),
            (dh2, (slots, D), const2),
            (n3, (slots, D), const2),
            (ff, (slots, D), const2),
        ],
        [(shape((ROWS, D)), (ROWS, D), const2)],
        flops=pass_flops,
    )
    sums, value_far = tie(sums, value_far)
    value_part = add(value_part, value_far)

    def enc_grads(base, steps, onto=()):
        def moved(i, *_):
            return (i + base, 0, 0)

        return gridded(
            functools.partial(enc_grad_kernel, base),
            steps,
            [scal, group_docs],
            [
                (ds_mine, (8, LANES), const2),
                (qk_a, (ROWS, D), const2),
                (qk_b, (ROWS, D), const2),
                (dap, (BLOCK, 2 * ROWS, tokens), moved),
                (vd, (BLOCK, ROWS, D), moved),
            ],
            [(shape(enc_out.shape, bf16), (BLOCK, tokens, D), moved)],
            flops=pass_flops * steps // blocks,
            onto=onto,
        )

    sums = add(sums, swap(sums, "heads", 1))
    steps = [over_heads[1]] + near_first
    share = [2, 2, 2] + [0] * len(steps)
    enc_grad, done = (), 0
    sum_a = sums
    value_step, grads_step = 1, 1
    for k, step in enumerate(steps):
        sum_b = swap(sum_a, *step)
        if k == 1:
            value_far = swap(value_part, *near_first[1])
        if share[k]:
            enc_grad = tuple(enc_grads(done, share[k], enc_grad))
            done += share[k]
        if k < len(steps) - 1:
            sum_b, *enc_grad = tie(sum_b, *enc_grad)
            if k >= 2:
                sum_b, value_far, grads_far = tie(sum_b, value_far, grads_far)
                value_part = add(value_part, value_far)
                grads = jnp.concatenate([grads, grads_far], axis=0)
                if k < last:
                    value_far = swap(value_part, *near_first[k])
                    grads_far = swap(grads, *over_docs[k])
            sum_a = sum_a + sum_b
    (enc_grad,) = enc_grad
    value_part, sum_b = tie(value_part, sum_b)
    grads = grow(grads, last)
    c_all, grads = ((x, swap(x, "heads", 1)) for x in (c_all, grads))
    value_a, value_b = value_part, swap(value_part, *near_first[last])
    value_grad = (value_a.astype(f32) + value_b.astype(f32)).T

    w_in_grad, w_down_grad, w_out_grad = plain(
        functools.partial(weights_kernel, order, 384),
        [shape((D, hidden)), shape((hidden, D)), shape((width, D))],
        scal,
        group_docs,
        *c_all,
        *grads,
        ds_docs,
        h1,
        g_ff,
        *wo_parts,
        w_in,
        w_down,
        smem=2,
        flops=10 * docs * D * hidden,
        limit=60 if docs > 384 else 36,
        scratch=full,
    )

    key_grad, query_grad, part = plain(
        key_kernel,
        [shape((width, D)), shape((width, D)), shape((8, D))],
        scal,
        sum_a,
        sum_b,
        h1,
        g_cross,
        wk_t,
        wq_t,
        smem=1,
    )
    part_a, part_b = sum_last(part, over_heads)
    part_b, w_in_grad = tie(part_b, w_in_grad)
    dh1, wos_grad, wvs_grad, part, cross, final_gain, row_grad, ff_gain = plain(
        hidden_kernel,
        [shape((1, D)), shape((width, D)), shape((width, D)), shape((8, D))] + [shape((D,))] * 4,
        part_a,
        part_b,
        sum_a,
        sum_b,
        h1,
        g_cross,
        start_token,
        g_self,
        w_out_self,
        wvs_t,
        g_final,
        score_row,
    )
    part_a, part_b = sum_last(part, over_heads)
    self_gain, start_grad = plain(
        start_kernel, [shape((D,))] * 2, part_a, part_b, dh1, start_token, g_self
    )

    return (
        all_scores,
        loss.reshape(()),
        enc_grad,
        start_grad,
        row_grad,
        self_gain,
        wvs_grad.T,
        wos_grad,
        cross,
        query_grad.T,
        key_grad.T,
        value_grad,
        w_out_grad,
        ff_gain,
        w_in_grad,
        w_down_grad,
        final_gain,
    )


def solution(mesh):
    placed = (
        P("docs", "heads", None),
        P(),
        P(),
        P(),
        P(),
        P(),
        P(),
        P(),
        P(None, "heads"),
        P("heads", None),
        P(),
        P(None, "heads"),
        P(None, "heads"),
        P(None, "heads"),
        P("heads", None),
        P(),
        P(None, "heads"),
        P("heads", None),
        P(),
    )
    return jax.shard_map(
        per_device,
        mesh=mesh,
        in_specs=placed,
        out_specs=(
            P(),
            P(),
            P("docs", "heads", None),
            P(),
            P(),
            P(),
            P(None, "heads"),
            P("heads", None),
            P(),
            P(None, "heads"),
            P(None, "heads"),
            P(None, "heads"),
            P("heads", None),
            P(),
            P(None, "heads"),
            P("heads", None),
            P(),
        ),
        check_vma=False,
    )
```

time: 277 us -> 159 us (0.57)
  local copies, waits for them, and re-layouts: 36.6 us -> 0.83 us
  waiting for transfers between devices: 95.3 us -> 65.9 us
  other arithmetic: 25.1 us -> 1.36 us
  between operations: 17.4 us -> 1.07 us
  Pallas kernels: 62.5 us -> 51 us
    pallas_call x4 -> x7, Pallas kernels: 47.4 us -> 19.4 us  [gridded(): pl.pallas_call(kernel, out_shape=[s for s, _, _ in outs], grid_spec=pltpu...]
    unnamed x238 -> x38, local copies, waits for them, and re-layouts: 26.2 us -> 0.79 us
    ppermute x35 -> x41, waiting for transfers between devices: 89.7 us -> 65.9 us  [swap(): return lax.ppermute(x, axis, [(i, i ^ bit) for i in range(size)])]
    pallas_call x11 -> x15, Pallas kernels: 15.1 us -> 28.5 us  [plain(): pl.pallas_call(kernel, out_shape=outs, in_specs=[whole_spec(pltpu.SMEM if...]
    pallas_call x7 -> x0, other arithmetic: 8.97 us -> none  [plain(): pl.pallas_call(kernel, out_shape=outs, in_specs=[whole_spec(pltpu.SMEM if...]
    select_n x9 -> x0, other arithmetic: 6.01 us -> none  [the longest x8 5.28 us: gather_rows(): jnp.where(mine, other, x)]
    reshape x11 -> x0, local copies, waits for them, and re-layouts: 5.53 us -> none  [the longest x3 3.58 us: per_device(): ds_slots[:, :slots].reshape(groups, 2, half).transpose(1, 0, 2)]
    all_gather x2 -> x0, waiting for transfers between devices: 4.25 us -> none  [the longest x1 4.25 us: per_device(): value_full = lax.all_gather(w_value, 'heads', axis=1, tiled=True)]
  transfers between devices with their start and end apart: 37 -> 41, of which waited for: 19 -> 21; matrix products, arithmetic and copies ran while one was open for 15% -> 1% of each run, Pallas kernels for 17% -> 26%
where the time goes in v2:
time: 159 us
  waiting for transfers between devices  65.9 us (41%)
  Pallas kernels  51 us (32%)
  starting transfers between devices  39.3 us (25%)
    ppermute x41, waiting for transfers between devices, swap(): return lax.ppermute(x, axis, [(i, i ^ bit) for i in range(size)])  65.9 us
    ppermute x41, starting transfers between devices, swap(): return lax.ppermute(x, axis, [(i, i ^ bit) for i in range(size)])  39.3 us
    pallas_call x15, Pallas kernels, plain(): pl.pallas_call(kernel, out_shape=outs, in_specs=[whole_spec(pltpu.SMEM if...  28.5 us
    pallas_call x7, Pallas kernels, gridded(): pl.pallas_call(kernel, out_shape=[s for s, _, _ in outs], grid_spec=pltpu...  19.4 us
  transfers between devices with their start and end apart: 41, of which 21 were waited for; matrix products, arithmetic and copies ran while one was open for 1% of the time, Pallas kernels for 26%

profile of v2, /device:TPU:0, one launch (start us, length us, event | category | flops | bytes accessed | tf_op | source)
XLA Modules:
  0.0 159.4 jit_solution(349834956969929564)
XLA Ops:
  0.7 1.5 self_kernel.1
  2.6 0.8 collective-permute-done
  3.5 2.9 %collective-permute-start.1 = (f32[8,768]{1,0:T(8,128)S(1)}, f32[8,768]{1,0:T(8,128)S(1)}, u32[]{:S(2)}, u32[]{:S(2)}) collective-permute-start(f32[8,768]{1,0:T(8,128)S(1)} %add.45.part_a), channel_id=1, source_target_pairs={{0,2},{1,3},{2,0},{3,1},{4,6},{5,7},{6,4},{7,5},{8,10},{9,11},{10,... | collective-permute-start | bytes 73736 | tf_op jit(solution)/shard_map/ppermute | solution.py:734
  6.4 0.7 copy-done.8
  7.1 2.5 %load_kernel.2.refs_0_ = bf16[96,128,768]{2,1,0:T(8,128)(2,1)S(1)} custom-call(s32[2]{0:T(128)S(1)} %pad_add_fusion.scal, s32[8]{0:T(128)S(1)} %copy-done.8, bf16[96,128,768]{2,1,0:T(8,128)(2,1)} %enc.3), custom_call_target="tpu_custom_call" | custom-call | bytes 18874368 | tf_op jit(solution)/shard_map/load_kernel/pallas_call | solution.py:800
  9.6 1.5 query_kernel.1
  11.1 1.2 collective-permute-done.2
  12.4 0.7 collective-permute-start.3
  13.0 0.6 load_kernel.3.enc
  13.6 2.9 %collective-permute-done.3.qb = f32[16,768]{1,0:T(8,128)S(1)} collective-permute-done((f32[16,768]{1,0:T(8,128)S(1)}, f32[16,768]{1,0:T(8,128)S(1)}, u32[]{:S(2)}, u32[]{:S(2)}) %collective-permute-start.3) | collective-permute-done | bytes 49184 | tf_op jit(solution)/shard_map/ppermute | solution.py:734
  16.5 0.6 collective-permute-start.4
  17.1 2.6 %attend_kernel.2 = (f32[96,16,128]{2,1,0:T(8,128)S(1)}, bf16[12,96,768]{2,1,0:T(8,128)(2,1)S(1)}, bf16[96,128]{1,0:T(8,128)(2,1)S(1)}) custom-call(s32[2]{0:T(128)S(1)} %pad_add_fusion.scal, s32[8]{0:T(128)S(1)} %copy-done.8, s32[384]{0:T(512)S(1)} %copy-done.16, f32[16,768]{1,0:T(8,128)S(1)} %add.46.qa, f32[16,768]{1,0:T(8,128)S(1)} %collective-permute-done.3.qb, ...), custom_call_target="tpu_custom_call" | custom-call | flops 6442450944 | bytes 21553152 | tf_op jit(solution)/shard_map/attend_kernel/pallas_call | solution.py:701
  19.8 4.6 %collective-permute-done.4.by2.wv_by2 = bf16[192,768]{1,0:T(8,128)(2,1)S(1)} collective-permute-done((bf16[192,768]{1,0:T(8,128)(2,1)S(1)}, bf16[192,768]{1,0:T(8,128)(2,1)S(1)}, u32[]{:S(2)}, u32[]{:S(2)}) %collective-permute-start.4) | collective-permute-done | bytes 294944 | tf_op jit(solution)/shard_map/ppermute | solution.py:734
  24.4 0.6 collective-permute-start.9
  25.0 0.7 attend_kernel.3
  26.0 1.5 project_kernel.1.own.first
  28.0 5.8 %collective-permute-done.9.wo_by2 = bf16[192,768]{1,0:T(8,128)(2,1)S(1)} collective-permute-done((bf16[192,768]{1,0:T(8,128)(2,1)S(1)}, bf16[192,768]{1,0:T(8,128)(2,1)S(1)}, u32[]{:S(2)}, u32[]{:S(2)}) %collective-permute-start.9) | collective-permute-done | bytes 294944 | tf_op jit(solution)/shard_map/ppermute | solution.py:734
  33.8 1.3 merge_kernel.1.own
  35.1 0.7 collective-permute-start.8
  35.8 6.2 %collective-permute-done.8.other = bf16[96,896]{1,0:T(8,128)(2,1)S(1)} collective-permute-done((bf16[96,896]{1,0:T(8,128)(2,1)S(1)}, bf16[96,896]{1,0:T(8,128)(2,1)S(1)}, u32[]{:S(2)}, u32[]{:S(2)}) %collective-permute-start.8) | collective-permute-done | bytes 172064 | tf_op jit(solution)/shard_map/ppermute | solution.py:734
  41.9 2.5 %forward_kernel.1 = (bf16[48,768]{1,0:T(8,128)(2,1)S(1)}, f32[96,768]{1,0:T(8,128)S(1)}, f32[96,128]{1,0:T(8,128)S(1)}, f32[96,768]{1,0:T(8,128)S(1)}, f32[96,76...) custom-call(s32[2]{0:T(128)S(1)} %pad_add_fusion.scal, bf16[96,896]{1,0:T(8,128)(2,1)S(1)} %merge_kernel.1.own, ...), custom_call_target="tpu_custom_call" | custom-call | bytes 4061192 | tf_op jit(solution)/shard_map/forward_kernel/pallas_call | solution.py:685
  44.5 1.4 collective-permute-done.12
  45.9 5.9 %collective-permute-start.14 = (bf16[48,768]{1,0:T(8,128)(2,1)S(1)}, bf16[48,768]{1,0:T(8,128)(2,1)S(1)}, u32[]{:S(2)}, u32[]{:S(2)}) collective-permute-start(bf16[48,768]{1,0:T(8,128)(2,1)S(1)} %get-tuple-element.128), channel_id=1, source_target_pairs={{0,8},{4,12},{8,0},{12,4},{16,24},{20,28},{24,16},{28,20},{1,9},{5... | collective-permute-start | bytes 221192 | tf_op jit(solution)/shard_map/ppermute | solution.py:734
  51.8 1.5 collective-permute-start.13
  53.3 0.9 share_kernel.1
  54.4 3.0 %collective-permute-done.13.part_b = bf16[96,768]{1,0:T(8,128)(2,1)S(1)} collective-permute-done((bf16[96,768]{1,0:T(8,128)(2,1)S(1)}, bf16[96,768]{1,0:T(8,128)(2,1)S(1)}, u32[]{:S(2)}, u32[]{:S(2)}) %collective-permute-start.13) | collective-permute-done | bytes 147488 | tf_op jit(solution)/shard_map/ppermute | solution.py:734
  57.5 1.8 %score_kernel.1 = (f32[8,128]{1,0:T(8,128)S(1)}, f32[96,768]{1,0:T(8,128)S(1)}, bf16[96,768]{1,0:T(8,128)(2,1)S(1)}, bf16[96,768]{1,0:T(8,128)(2,1)S(1)}) custom-call(s32[2]{0:T(128)S(1)} %pad_add_fusion.scal, bf16[96,768]{1,0:T(8,128)(2,1)S(1)} %add_convert_fusion.3.part_a, bf16[96,768]{1,0:T(8,128)(2,1)S(1)} %collective-permute-done.13.part_b, ...), custom_call_target="tpu_custom_call" | custom-call | bytes 3248648 | tf_op jit(solution)/shard_map/score_kernel/pallas_call | solution.py:685
  59.3 0.6 collective-permute-start.15
  59.9 1.0 collective-permute-done.15
  60.9 1.6 %collective-permute-start.16 = (bf16[96,768]{1,0:T(8,128)(2,1)S(1)}, bf16[96,768]{1,0:T(8,128)(2,1)S(1)}, u32[]{:S(2)}, u32[]{:S(2)}) collective-permute-start(bf16[96,768]{1,0:T(8,128)(2,1)S(1)} %add_convert_fusion.2.part_a), channel_id=1, source_target_pairs={{0,2},{1,3},{2,0},{3,1},{4,6},{5,7},{6,4},{7,5},{8,10},{9,11},{10,... | collective-permute-start | bytes 442376 | tf_op jit(solution)/shard_map/ppermute | solution.py:734
  62.5 1.7 %collective-permute-start.20 = (bf16[96,768]{1,0:T(8,128)(2,1)S(1)}, bf16[96,768]{1,0:T(8,128)(2,1)S(1)}, u32[]{:S(2)}, u32[]{:S(2)}) collective-permute-start(bf16[96,768]{1,0:T(8,128)(2,1)S(1)} %pad_maximum_fusion.4), channel_id=1, source_target_pairs={{0,16},{4,20},{8,24},{12,28},{16,0},{20,4},{24,8},{28,12},{1,17},{... | collective-permute-start | bytes 442376 | tf_op jit(solution)/shard_map/ppermute | solution.py:734
  64.5 3.3 %collective-permute-done.18 = f32[8,128]{1,0:T(8,128)S(1)} collective-permute-done((f32[8,128]{1,0:T(8,128)S(1)}, f32[8,128]{1,0:T(8,128)S(1)}, u32[]{:S(2)}, u32[]{:S(2)}) %collective-permute-start.18) | collective-permute-done | bytes 4128 | tf_op jit(solution)/shard_map/ppermute | solution.py:734
  68.2 4.0 %collective-permute-done.20 = bf16[96,768]{1,0:T(8,128)(2,1)S(1)} collective-permute-done((bf16[96,768]{1,0:T(8,128)(2,1)S(1)}, bf16[96,768]{1,0:T(8,128)(2,1)S(1)}, u32[]{:S(2)}, u32[]{:S(2)}) %collective-permute-start.20) | collective-permute-done | bytes 147488 | tf_op jit(solution)/shard_map/ppermute | solution.py:734
  72.3 0.7 away_kernel.1
  73.0 1.6 context_kernel.1
  75.3 3.5 %collective-permute-start.21 = (f32[8,128]{1,0:T(8,128)S(1)}, f32[8,128]{1,0:T(8,128)S(1)}, u32[]{:S(2)}, u32[]{:S(2)}) collective-permute-start(f32[8,128]{1,0:T(8,128)S(1)} %add.50.sc_a), channel_id=1, source_target_pairs={{0,16},{4,20},{8,24},{12,28},{16,0},{20,4},{24,8},{28,12},{1,17},{... | collective-permute-start | bytes 12296 | tf_op jit(solution)/shard_map/ppermute | solution.py:734
  78.7 2.7 %back_kernel.1 = (bf16[96,32,128]{2,1,0:T(8,128)(2,1)S(1)}, bf16[96,16,768]{2,1,0:T(8,128)(2,1)S(1)}) custom-call(s32[2]{0:T(128)S(1)} %pad_add_fusion.scal, s32[8]{0:T(128)S(1)} %copy-done.9, bf16[96,128,768]{2,1,0:T(8,128)(2,1)S(1)} %load_kernel.3.enc, f32[96,16,128]{2,1,0:T(8,128)S(1)} %get-tuple-element.148.p, f32[96,128]{1,0:T(8,128)S(1)} %get-tuple-element.130.scale, ...), custom_call_target="tpu_custom_call" | custom-call | flops 4831838208 | bytes 24231936 | tf_op jit(solution)/shard_map/back_kernel/pallas_call | solution.py:701
  81.5 1.9 %collective-permute-done.23 = bf16[192,768]{1,0:T(8,128)(2,1)S(1)} collective-permute-done((bf16[192,768]{1,0:T(8,128)(2,1)S(1)}, bf16[192,768]{1,0:T(8,128)(2,1)S(1)}, u32[]{:S(2)}, u32[]{:S(2)}) %collective-permute-start.23) | collective-permute-done | bytes 294944 | tf_op jit(solution)/shard_map/ppermute | solution.py:734
  83.5 3.3 %collective-permute-done.24.other = bf16[3,96,768]{2,1,0:T(8,128)(2,1)S(1)} collective-permute-done((bf16[3,96,768]{2,1,0:T(8,128)(2,1)S(1)}, bf16[3,96,768]{2,1,0:T(8,128)(2,1)S(1)}, u32[]{:S(2)}, u32[]{:S(2)}) %collective-permute-start.24) | collective-permute-done | bytes 442400 | tf_op jit(solution)/shard_map/ppermute | solution.py:734
  86.8 1.6 list_kernel.1
  88.4 1.0 value_kernel.1
  89.4 2.4 %collective-permute-start.25 = (bf16[192,768]{1,0:T(8,128)(2,1)S(1)}, bf16[192,768]{1,0:T(8,128)(2,1)S(1)}, u32[]{:S(2)}, u32[]{:S(2)}) collective-permute-start(bf16[192,768]{1,0:T(8,128)(2,1)S(1)} %value_kernel.1), channel_id=1, source_target_pairs={{0,4},{4,0},{8,12},{12,8},{16,20},{20,16},{24,28},{28,24},{1,5},{5... | collective-permute-start | bytes 884744 | tf_op jit(solution)/shard_map/ppermute | solution.py:734
  91.8 0.9 collective-permute-start.31
  92.7 1.8 %key_sum_kernel.1 = f32[16,768]{1,0:T(8,128)S(1)} custom-call(s32[2]{0:T(128)S(1)} %pad_add_fusion.scal, s32[8]{0:T(128)S(1)} %copy-done.9, f32[8,128]{1,0:T(8,128)S(1)} %get-tuple-element.158.ds, bf16[96,128,768]{2,1,0:T(8,128)(2,1)S(1)} %load_kernel.3.enc, bf16[96,32,128]{2,1,0:T(8,128)(2,1)S(1)} %get-tuple-element.163.da.dap, ...), custom_call_target="tpu_custom_call" | custom-call | flops 4831838208 | bytes 20451328 | tf_op jit(solution)/shard_map/key_sum_kernel/pallas_call | solution.py:701
  94.6 3.0 %collective-permute-done.25 = bf16[192,768]{1,0:T(8,128)(2,1)S(1)} collective-permute-done((bf16[192,768]{1,0:T(8,128)(2,1)S(1)}, bf16[192,768]{1,0:T(8,128)(2,1)S(1)}, u32[]{:S(2)}, u32[]{:S(2)}) %collective-permute-start.25) | collective-permute-done | bytes 294944 | tf_op jit(solution)/shard_map/ppermute | solution.py:734
  97.5 4.5 %enc_grad_kernel.3.refs_0_ = bf16[96,128,768]{2,1,0:T(8,128)(2,1)} custom-call(s32[2]{0:T(128)S(1)} %pad_add_fusion.scal, s32[8]{0:T(128)S(1)} %copy-done.9, f32[8,128]{1,0:T(8,128)S(1)} %get-tuple-element.158.ds, f32[16,768]{1,0:T(8,128)S(1)} %add.46.qa, f32[16,768]{1,0:T(8,128)S(1)} %collective-permute-done.3.qb, ...), custom_call_target="tpu_custom_call" | custom-call | flops 1610612736 | bytes 22122496 | tf_op jit(solution)/shard_map/enc_grad_kernel/pallas_call | solution.py:701
  102.0 1.6 %collective-permute-start.27 = (f32[16,768]{1,0:T(8,128)S(1)}, f32[16,768]{1,0:T(8,128)S(1)}, u32[]{:S(2)}, u32[]{:S(2)}) collective-permute-start(f32[16,768]{1,0:T(8,128)S(1)} %add.51), channel_id=1, source_target_pairs={{0,2},{1,3},{2,0},{3,1},{4,6},{5,7},{6,4},{7,5},{8,10},{9,11},{10,... | collective-permute-start | bytes 147464 | tf_op jit(solution)/shard_map/ppermute | solution.py:734
  103.7 3.4 %collective-permute-start.30 = (bf16[192,768]{1,0:T(8,128)(2,1)S(1)}, bf16[192,768]{1,0:T(8,128)(2,1)S(1)}, u32[]{:S(2)}, u32[]{:S(2)}) collective-permute-start(bf16[192,768]{1,0:T(8,128)(2,1)S(1)} %add_convert_fusion.1), channel_id=1, source_target_pairs={{0,8},{4,12},{8,0},{12,4},{16,24},{20,28},{24,16},{28,20},{1,9},{5... | collective-permute-start | bytes 884744 | tf_op jit(solution)/shard_map/ppermute | solution.py:734
  107.1 1.0 collective-permute-start.28
  108.1 3.5 %enc_grad_kernel.4.refs_0_ = bf16[96,128,768]{2,1,0:T(8,128)(2,1)} custom-call(s32[2]{0:T(128)S(1)} %pad_add_fusion.scal, s32[8]{0:T(128)S(1)} %copy-done.9, f32[8,128]{1,0:T(8,128)S(1)} %get-tuple-element.158.ds, f32[16,768]{1,0:T(8,128)S(1)} %add.46.qa, f32[16,768]{1,0:T(8,128)S(1)} %collective-permute-done.3.qb, ...), custom_call_target="tpu_custom_call", output_to_operand_aliasing={{}: (7, {})} | custom-call | flops 1610612736 | bytes 22122496 | tf_op jit(solution)/shard_map/enc_grad_kernel/pallas_call | solution.py:701
  111.6 2.7 %collective-permute-start.29 = (f32[16,768]{1,0:T(8,128)S(1)}, f32[16,768]{1,0:T(8,128)S(1)}, u32[]{:S(2)}, u32[]{:S(2)}) collective-permute-start(f32[16,768]{1,0:T(8,128)S(1)} %add.53), channel_id=1, source_target_pairs={{0,8},{4,12},{8,0},{12,4},{16,24},{20,28},{24,16},{28,20},{1,9},{5... | collective-permute-start | bytes 147464 | tf_op jit(solution)/shard_map/ppermute | solution.py:734
  114.3 3.5 %enc_grad_kernel.5 = bf16[96,128,768]{2,1,0:T(8,128)(2,1)} custom-call(s32[2]{0:T(128)S(1)} %pad_add_fusion.scal, s32[8]{0:T(128)S(1)} %copy-done.9, f32[8,128]{1,0:T(8,128)S(1)} %get-tuple-element.158.ds, f32[16,768]{1,0:T(8,128)S(1)} %add.46.qa, f32[16,768]{1,0:T(8,128)S(1)} %collective-permute-done.3.qb, ...), custom_call_target="tpu_custom_call", output_to_operand_aliasing={{}: (7, {})} | custom-call | flops 1610612736 | bytes 22122496 | tf_op jit(solution)/shard_map/enc_grad_kernel/pallas_call | solution.py:701
  117.9 1.8 %collective-permute-start.36 = (bf16[192,1536]{1,0:T(8,128)(2,1)S(1)}, bf16[192,1536]{1,0:T(8,128)(2,1)S(1)}, u32[]{:S(2)}, u32[]{:S(2)}) collective-permute-start(bf16[192,1536]{1,0:T(8,128)(2,1)S(1)} %pad_maximum_fusion.1), channel_id=1, source_target_pairs={{0,4},{4,0},{8,12},{12,8},{16,20},{20,16},{24,28},{28,24},{1,5},{5... | collective-permute-start | bytes 1769480 | tf_op jit(solution)/shard_map/ppermute | solution.py:734
  119.7 12.6 %collective-permute-done.36 = bf16[192,1536]{1,0:T(8,128)(2,1)S(1)} collective-permute-done((bf16[192,1536]{1,0:T(8,128)(2,1)S(1)}, bf16[192,1536]{1,0:T(8,128)(2,1)S(1)}, u32[]{:S(2)}, u32[]{:S(2)}) %collective-permute-start.36) | collective-permute-done | bytes 589856 | tf_op jit(solution)/shard_map/ppermute | solution.py:734
  133.1 5.6 %collective-permute-done.32.sum_b = f32[16,768]{1,0:T(8,128)S(1)} collective-permute-done((f32[16,768]{1,0:T(8,128)S(1)}, f32[16,768]{1,0:T(8,128)S(1)}, u32[]{:S(2)}, u32[]{:S(2)}) %collective-permute-start.32) | collective-permute-done | bytes 49184 | tf_op jit(solution)/shard_map/ppermute | solution.py:734
  138.8 2.1 %key_kernel.1 = (f32[192,768]{1,0:T(8,128)}, f32[192,768]{1,0:T(8,128)}, f32[8,768]{1,0:T(8,128)S(1)}) custom-call(s32[2]{0:T(128)S(1)} %pad_add_fusion.scal, f32[16,768]{1,0:T(8,128)S(1)} %add.55.sum_a, f32[16,768]{1,0:T(8,128)S(1)} %collective-permute-done.32.sum_b, f32[1,768]{1,0:T(1,128)S(1)} %get-tuple-element.123.h1, f32[768]{0:T(1024)S(1)} %copy-done.10, ...), custom_call_target="tpu_custom_call" | custom-call | bytes 694280 | tf_op jit(solution)/shard_map/key_kernel/pallas_call | solution.py:685
  141.0 1.2 collective-permute-done.33
  142.2 1.5 collective-permute-start.34
  143.7 7.9 %weights_kernel.1 = (f32[768,768]{1,0:T(8,128)}, f32[768,768]{1,0:T(8,128)}, f32[192,768]{1,0:T(8,128)}) custom-call(s32[2]{0:T(128)S(1)} %pad_add_fusion.scal, s32[8]{0:T(128)S(1)} %copy-done.9, bf16[384,768]{1,0:T(8,128)(2,1)S(1)} %pad_maximum_fusion.c_own, bf16[384,768]{1,0:T(8,128)(2,1)S(1)} %collective-permute-done.35.c_other, ...), custom_call_target="tpu_custom_call" | custom-call | flops 2264924160 | bytes 7085608 | tf_op jit(solution)/shard_map/weights_kernel/pallas_call | solution.py:685
  151.7 1.9 %hidden_kernel.1 = (f32[1,768]{1,0:T(1,128)S(1)}, f32[192,768]{1,0:T(8,128)}, f32[192,768]{1,0:T(8,128)}, f32[8,768]{1,0:T(8,128)S(1)}, f32[768]{0:T(1024)}, /*i...) custom-call(f32[8,768]{1,0:T(8,128)S(1)} %add.57.part_a, f32[8,768]{1,0:T(8,128)S(1)} %collective-permute-done.34.part_b, ...), custom_call_target="tpu_custom_call" | custom-call | bytes 752640 | tf_op jit(solution)/shard_map/hidden_kernel/pallas_call | solution.py:685
  153.6 1.2 collective-permute-done.38
  155.3 0.9 add_bitcast_fusion
  156.2 2.4 %collective-permute-done.39.part_b = f32[8,768]{1,0:T(8,128)S(1)} collective-permute-done((f32[8,768]{1,0:T(8,128)S(1)}, f32[8,768]{1,0:T(8,128)S(1)}, u32[]{:S(2)}, u32[]{:S(2)}) %collective-permute-start.39) | collective-permute-done | bytes 24608 | tf_op jit(solution)/shard_map/ppermute | solution.py:734
  158.6 0.8 start_kernel.1
  (102 shorter events, 4.8 us)
Async XLA Ops:
  2.2 1.3 collective-permute-start
  3.5 6.1 %collective-permute-start.1 = (f32[8,768]{1,0:T(8,128)S(1)}, f32[8,768]{1,0:T(8,128)S(1)}, u32[]{:S(2)}, u32[]{:S(2)}) collective-permute-start(f32[8,768]{1,0:T(8,128)S(1)} %add.45.part_a), channel_id=1, source_target_pairs={{0,2},{1,3},{2,0},{3,1},{4,6},{5,7},{6,4},{7,5},{8,10},{9,11},{10,... | collective-permute-start | bytes 73736 | tf_op jit(solution)/shard_map/ppermute | solution.py:734
  6.4 0.7 copy-start.8
  7.1 6.0 %copy-start.7 = (bf16[768,192]{0,1:T(8,128)(2,1)S(1)}, bf16[768,192]{0,1:T(8,128)(2,1)}, u32[]{:S(2)}) copy-start(bf16[768,192]{0,1:T(8,128)(2,1)} %param.32) | copy-start | bytes 884740
  11.1 1.3 collective-permute-start.2
  12.4 4.2 %collective-permute-start.3 = (f32[16,768]{1,0:T(8,128)S(1)}, f32[16,768]{1,0:T(8,128)S(1)}, u32[]{:S(2)}, u32[]{:S(2)}) collective-permute-start(f32[16,768]{1,0:T(8,128)S(1)} %add.46.qa), channel_id=1, source_target_pairs={{0,2},{1,3},{2,0},{3,1},{4,6},{5,7},{6,4},{7,5},{8,10},{9,11},{10,... | collective-permute-start | bytes 147464 | tf_op jit(solution)/shard_map/ppermute | solution.py:734
  13.0 4.1 %copy-start.16 = (s32[384]{0:T(512)S(1)}, s32[384]{0:T(512)}, u32[]{:S(2)}) copy-start(s32[384]{0:T(512)} %lengths.3) | copy-start | bytes 4612
  13.0 12.7 %collective-permute-start.5 = (bf16[192,768]{1,0:T(8,128)(2,1)S(1)}, bf16[192,768]{1,0:T(8,128)(2,1)S(1)}, u32[]{:S(2)}, u32[]{:S(2)}) collective-permute-start(bf16[192,768]{1,0:T(8,128)(2,1)S(1)} %bitcast.18), channel_id=1, source_target_pairs={{0,1},{1,0},{2,3},{3,2},{4,5},{5,4},{6,7},{7,6},{8,9},{9,8},{10,11... | collective-permute-start | bytes 884744 | tf_op jit(solution)/shard_map/ppermute | solution.py:734
  13.6 10.8 %copy-start.2 = (bf16[192,768]{1,0:T(8,128)(2,1)S(1)}, bf16[192,768]{1,0:T(8,128)(2,1)}, u32[]{:S(2)}) copy-start(bf16[192,768]{1,0:T(8,128)(2,1)} %wo_own.5) | copy-start | bytes 884740
  16.5 7.9 %collective-permute-start.4 = (bf16[192,768]{1,0:T(8,128)(2,1)S(1)}, bf16[192,768]{1,0:T(8,128)(2,1)S(1)}, u32[]{:S(2)}, u32[]{:S(2)}) collective-permute-start(bf16[192,768]{1,0:T(8,128)(2,1)S(1)} %bitcast.19), channel_id=1, source_target_pairs={{0,2},{1,3},{2,0},{3,1},{4,6},{5,7},{6,4},{7,5},{8,10},{9,11},{10,... | collective-permute-start | bytes 884744 | tf_op jit(solution)/shard_map/ppermute | solution.py:734
  24.4 1.6 collective-permute-start.6
  24.4 9.4 %collective-permute-start.9 = (bf16[192,768]{1,0:T(8,128)(2,1)S(1)}, bf16[192,768]{1,0:T(8,128)(2,1)S(1)}, u32[]{:S(2)}, u32[]{:S(2)}) collective-permute-start(bf16[192,768]{1,0:T(8,128)(2,1)S(1)} %copy-done.2), channel_id=1, source_target_pairs={{0,2},{1,3},{2,0},{3,1},{4,6},{5,7},{6,4},{7,5},{8,10},{9,11},{10,... | collective-permute-start | bytes 884744 | tf_op jit(solution)/shard_map/ppermute | solution.py:734
  26.0 16.0 %copy-start = (bf16[768,768]{1,0:T(8,128)(2,1)S(1)}, bf16[768,768]{1,0:T(8,128)(2,1)}, u32[]{:S(2)}) copy-start(bf16[768,768]{1,0:T(8,128)(2,1)} %win.5) | copy-start | bytes 3538948
  26.0 16.0 %copy-start.1 = (bf16[768,768]{1,0:T(8,128)(2,1)S(1)}, bf16[768,768]{1,0:T(8,128)(2,1)}, u32[]{:S(2)}) copy-start(bf16[768,768]{1,0:T(8,128)(2,1)} %wdown.5) | copy-start | bytes 3538948
  26.0 16.0 %copy-start.13 = (f32[768]{0:T(1024)S(1)}, f32[768]{0:T(1024)}, u32[]{:S(2)}) copy-start(f32[768]{0:T(1024)} %g_ff.5) | copy-start | bytes 9220
  27.5 6.3 %collective-permute-start.7 = (bf16[96,896]{1,0:T(8,128)(2,1)S(1)}, bf16[96,896]{1,0:T(8,128)(2,1)S(1)}, u32[]{:S(2)}, u32[]{:S(2)}) collective-permute-start(bf16[96,896]{1,0:T(8,128)(2,1)S(1)} %project_kernel.1.own.first), channel_id=1, source_target_pairs={{0,1},{1,0},{2,3},{3,2},{4,5},{5,4},{6,7},{7,6},{8,9},{9,8},{10,11... | collective-permute-start | bytes 516104 | tf_op jit(solution)/shard_map/ppermute | solution.py:734
  27.7 8.1 %collective-permute-start.10 = (bf16[192,768]{1,0:T(8,128)(2,1)S(1)}, bf16[192,768]{1,0:T(8,128)(2,1)S(1)}, u32[]{:S(2)}, u32[]{:S(2)}) collective-permute-start(bf16[192,768]{1,0:T(8,128)(2,1)S(1)} %copy-done.2), channel_id=1, source_target_pairs={{0,1},{1,0},{2,3},{3,2},{4,5},{5,4},{6,7},{7,6},{8,9},{9,8},{10,11... | collective-permute-start | bytes 884744 | tf_op jit(solution)/shard_map/ppermute | solution.py:734
  33.8 2.0 %collective-permute-start.11 = (bf16[192,768]{1,0:T(8,128)(2,1)S(1)}, bf16[192,768]{1,0:T(8,128)(2,1)S(1)}, u32[]{:S(2)}, u32[]{:S(2)}) collective-permute-start(bf16[192,768]{1,0:T(8,128)(2,1)S(1)} %collective-permute-done.9.wo_by2), channel_id=1, source_target_pairs={{0,1},{1,0},{2,3},{3,2},{4,5},{5,4},{6,7},{7,6},{8,9},{9,8},{10,11... | collective-permute-start | bytes 884744 | tf_op jit(solution)/shard_map/ppermute | solution.py:734
  35.1 6.8 %collective-permute-start.8 = (bf16[96,896]{1,0:T(8,128)(2,1)S(1)}, bf16[96,896]{1,0:T(8,128)(2,1)S(1)}, u32[]{:S(2)}, u32[]{:S(2)}) collective-permute-start(bf16[96,896]{1,0:T(8,128)(2,1)S(1)} %merge_kernel.1.own), channel_id=1, source_target_pairs={{0,2},{1,3},{2,0},{3,1},{4,6},{5,7},{6,4},{7,5},{8,10},{9,11},{10,... | collective-permute-start | bytes 516104 | tf_op jit(solution)/shard_map/ppermute | solution.py:734
  44.4 13.0 %copy-start.14 = (f32[768]{0:T(1024)S(1)}, f32[768]{0:T(1024)}, u32[]{:S(2)}) copy-start(f32[768]{0:T(1024)} %g_final.3) | copy-start | bytes 9220
  44.4 13.0 %copy-start.15 = (bf16[768]{0:T(1024)(128)(2,1)S(1)}, bf16[768]{0:T(1024)(128)(2,1)}, u32[]{:S(2)}) copy-start(bf16[768]{0:T(1024)(128)(2,1)} %row.3) | copy-start | bytes 4612
  44.4 1.4 collective-permute-start.12
  45.9 8.5 %collective-permute-start.14 = (bf16[48,768]{1,0:T(8,128)(2,1)S(1)}, bf16[48,768]{1,0:T(8,128)(2,1)S(1)}, u32[]{:S(2)}, u32[]{:S(2)}) collective-permute-start(bf16[48,768]{1,0:T(8,128)(2,1)S(1)} %get-tuple-element.128), channel_id=1, source_target_pairs={{0,8},{4,12},{8,0},{12,4},{16,24},{20,28},{24,16},{28,20},{1,9},{5... | collective-permute-start | bytes 221192 | tf_op jit(solution)/shard_map/ppermute | solution.py:734
  51.8 5.6 %collective-permute-start.13 = (bf16[96,768]{1,0:T(8,128)(2,1)S(1)}, bf16[96,768]{1,0:T(8,128)(2,1)S(1)}, u32[]{:S(2)}, u32[]{:S(2)}) collective-permute-start(bf16[96,768]{1,0:T(8,128)(2,1)S(1)} %add_convert_fusion.3.part_a), channel_id=1, source_target_pairs={{0,2},{1,3},{2,0},{3,1},{4,6},{5,7},{6,4},{7,5},{8,10},{9,11},{10,... | collective-permute-start | bytes 442376 | tf_op jit(solution)/shard_map/ppermute | solution.py:734
  57.4 10.4 %collective-permute-start.17 = (bf16[2,3,96,768]{3,2,1,0:T(8,128)(2,1)S(1)}, bf16[2,3,96,768]{3,2,1,0:T(8,128)(2,1)S(1)}, u32[]{:S(2)}, u32[]{:S(2)}) collective-permute-start(bf16[2,3,96,768]{3,2,1,0:T(8,128)(2,1)S(1)} %get-tuple-element.137), channel_id=1, source_target_pairs={{0,1},{1,0},{2,3},{3,2},{4,5},{5,4},{6,7},{7,6},{8,9},{9,8},{10,11... | collective-permute-start | bytes 2654216 | tf_op jit(solution)/shard_map/ppermute | solution.py:734
  59.3 1.6 collective-permute-start.15
  60.9 6.9 %collective-permute-start.16 = (bf16[96,768]{1,0:T(8,128)(2,1)S(1)}, bf16[96,768]{1,0:T(8,128)(2,1)S(1)}, u32[]{:S(2)}, u32[]{:S(2)}) collective-permute-start(bf16[96,768]{1,0:T(8,128)(2,1)S(1)} %add_convert_fusion.2.part_a), channel_id=1, source_target_pairs={{0,2},{1,3},{2,0},{3,1},{4,6},{5,7},{6,4},{7,5},{8,10},{9,11},{10,... | collective-permute-start | bytes 442376 | tf_op jit(solution)/shard_map/ppermute | solution.py:734
  62.5 9.8 %collective-permute-start.20 = (bf16[96,768]{1,0:T(8,128)(2,1)S(1)}, bf16[96,768]{1,0:T(8,128)(2,1)S(1)}, u32[]{:S(2)}, u32[]{:S(2)}) collective-permute-start(bf16[96,768]{1,0:T(8,128)(2,1)S(1)} %pad_maximum_fusion.4), channel_id=1, source_target_pairs={{0,16},{4,20},{8,24},{12,28},{16,0},{20,4},{24,8},{28,12},{1,17},{... | collective-permute-start | bytes 442376 | tf_op jit(solution)/shard_map/ppermute | solution.py:734
  64.2 3.6 %collective-permute-start.18 = (f32[8,128]{1,0:T(8,128)S(1)}, f32[8,128]{1,0:T(8,128)S(1)}, u32[]{:S(2)}, u32[]{:S(2)}) collective-permute-start(f32[8,128]{1,0:T(8,128)S(1)} %get-tuple-element.135), channel_id=1, source_target_pairs={{0,4},{4,0},{8,12},{12,8},{16,20},{20,16},{24,28},{28,24},{1,5},{5... | collective-permute-start | bytes 12296 | tf_op jit(solution)/shard_map/ppermute | solution.py:734
  67.8 6.7 %collective-permute-start.19 = (f32[8,128]{1,0:T(8,128)S(1)}, f32[8,128]{1,0:T(8,128)S(1)}, u32[]{:S(2)}, u32[]{:S(2)}) collective-permute-start(f32[8,128]{1,0:T(8,128)S(1)} %add.49), channel_id=1, source_target_pairs={{0,8},{4,12},{8,0},{12,4},{16,24},{20,28},{24,16},{28,20},{1,9},{5... | collective-permute-start | bytes 12296 | tf_op jit(solution)/shard_map/ppermute | solution.py:734
  72.9 5.8 %copy-start.9 = (s32[8]{0:T(128)S(1)}, s32[8]{0:T(128)}, u32[]{:S(2)}) copy-start(s32[8]{0:T(128)} %sizes.21) | copy-start | bytes 100
  74.6 8.9 %collective-permute-start.23 = (bf16[192,768]{1,0:T(8,128)(2,1)S(1)}, bf16[192,768]{1,0:T(8,128)(2,1)S(1)}, u32[]{:S(2)}, u32[]{:S(2)}) collective-permute-start(bf16[192,768]{1,0:T(8,128)(2,1)S(1)} %pad_maximum_fusion.2), channel_id=1, source_target_pairs={{0,4},{4,0},{8,12},{12,8},{16,20},{20,16},{24,28},{28,24},{1,5},{5... | collective-permute-start | bytes 884744 | tf_op jit(solution)/shard_map/ppermute | solution.py:734
  74.6 6.9 %collective-permute-start.22 = (bf16[48,1536]{1,0:T(8,128)(2,1)S(1)}, bf16[48,1536]{1,0:T(8,128)(2,1)S(1)}, u32[]{:S(2)}, u32[]{:S(2)}) collective-permute-start(bf16[48,1536]{1,0:T(8,128)(2,1)S(1)} %get-tuple-element.152), channel_id=1, source_target_pairs={{0,8},{4,12},{8,0},{12,4},{16,24},{20,28},{24,16},{28,20},{1,9},{5... | collective-permute-start | bytes 442376 | tf_op jit(solution)/shard_map/ppermute | solution.py:734
  74.8 12.0 %collective-permute-start.24 = (bf16[3,96,768]{2,1,0:T(8,128)(2,1)S(1)}, bf16[3,96,768]{2,1,0:T(8,128)(2,1)S(1)}, u32[]{:S(2)}, u32[]{:S(2)}) collective-permute-start(bf16[3,96,768]{2,1,0:T(8,128)(2,1)S(1)} %away_kernel.1), channel_id=1, source_target_pairs={{0,2},{1,3},{2,0},{3,1},{4,6},{5,7},{6,4},{7,5},{8,10},{9,11},{10,... | collective-permute-start | bytes 1327112 | tf_op jit(solution)/shard_map/ppermute | solution.py:734
  75.3 8.2 %collective-permute-start.21 = (f32[8,128]{1,0:T(8,128)S(1)}, f32[8,128]{1,0:T(8,128)S(1)}, u32[]{:S(2)}, u32[]{:S(2)}) collective-permute-start(f32[8,128]{1,0:T(8,128)S(1)} %add.50.sc_a), channel_id=1, source_target_pairs={{0,16},{4,20},{8,24},{12,28},{16,0},{20,4},{24,8},{28,12},{1,17},{... | collective-permute-start | bytes 12296 | tf_op jit(solution)/shard_map/ppermute | solution.py:734
  81.5 5.3 %copy-start.17 = (s32[24]{0:T(128)S(1)}, s32[24]{0:T(128)}, u32[]{:S(2)}) copy-start(s32[24]{0:T(128)} %lens.1) | copy-start | bytes 292
  89.4 8.2 %collective-permute-start.25 = (bf16[192,768]{1,0:T(8,128)(2,1)S(1)}, bf16[192,768]{1,0:T(8,128)(2,1)S(1)}, u32[]{:S(2)}, u32[]{:S(2)}) collective-permute-start(bf16[192,768]{1,0:T(8,128)(2,1)S(1)} %value_kernel.1), channel_id=1, source_target_pairs={{0,4},{4,0},{8,12},{12,8},{16,20},{20,16},{24,28},{28,24},{1,5},{5... | collective-permute-start | bytes 884744 | tf_op jit(solution)/shard_map/ppermute | solution.py:734
  91.8 26.0 %collective-permute-start.31 = (bf16[96,1536]{1,0:T(8,128)(2,1)S(1)}, bf16[96,1536]{1,0:T(8,128)(2,1)S(1)}, u32[]{:S(2)}, u32[]{:S(2)}) collective-permute-start(bf16[96,1536]{1,0:T(8,128)(2,1)S(1)} %pad_maximum_fusion.3), channel_id=1, source_target_pairs={{0,16},{4,20},{8,24},{12,28},{16,0},{20,4},{24,8},{28,12},{1,17},{... | collective-permute-start | bytes 884744 | tf_op jit(solution)/shard_map/ppermute | solution.py:734
  97.5 4.5 %collective-permute-start.26 = (f32[16,768]{1,0:T(8,128)S(1)}, f32[16,768]{1,0:T(8,128)S(1)}, u32[]{:S(2)}, u32[]{:S(2)}) collective-permute-start(f32[16,768]{1,0:T(8,128)S(1)} %key_sum_kernel.1), channel_id=1, source_target_pairs={{0,1},{1,0},{2,3},{3,2},{4,5},{5,4},{6,7},{7,6},{8,9},{9,8},{10,11... | collective-permute-start | bytes 147464 | tf_op jit(solution)/shard_map/ppermute | solution.py:734
  102.0 5.1 %collective-permute-start.27 = (f32[16,768]{1,0:T(8,128)S(1)}, f32[16,768]{1,0:T(8,128)S(1)}, u32[]{:S(2)}, u32[]{:S(2)}) collective-permute-start(f32[16,768]{1,0:T(8,128)S(1)} %add.51), channel_id=1, source_target_pairs={{0,2},{1,3},{2,0},{3,1},{4,6},{5,7},{6,4},{7,5},{8,10},{9,11},{10,... | collective-permute-start | bytes 147464 | tf_op jit(solution)/shard_map/ppermute | solution.py:734
  103.7 14.1 %collective-permute-start.30 = (bf16[192,768]{1,0:T(8,128)(2,1)S(1)}, bf16[192,768]{1,0:T(8,128)(2,1)S(1)}, u32[]{:S(2)}, u32[]{:S(2)}) collective-permute-start(bf16[192,768]{1,0:T(8,128)(2,1)S(1)} %add_convert_fusion.1), channel_id=1, source_target_pairs={{0,8},{4,12},{8,0},{12,4},{16,24},{20,28},{24,16},{28,20},{1,9},{5... | collective-permute-start | bytes 884744 | tf_op jit(solution)/shard_map/ppermute | solution.py:734
  107.1 4.5 %collective-permute-start.28 = (f32[16,768]{1,0:T(8,128)S(1)}, f32[16,768]{1,0:T(8,128)S(1)}, u32[]{:S(2)}, u32[]{:S(2)}) collective-permute-start(f32[16,768]{1,0:T(8,128)S(1)} %add.52), channel_id=1, source_target_pairs={{0,4},{4,0},{8,12},{12,8},{16,20},{20,16},{24,28},{28,24},{1,5},{5... | collective-permute-start | bytes 147464 | tf_op jit(solution)/shard_map/ppermute | solution.py:734
  111.6 6.2 %collective-permute-start.29 = (f32[16,768]{1,0:T(8,128)S(1)}, f32[16,768]{1,0:T(8,128)S(1)}, u32[]{:S(2)}, u32[]{:S(2)}) collective-permute-start(f32[16,768]{1,0:T(8,128)S(1)} %add.53), channel_id=1, source_target_pairs={{0,8},{4,12},{8,0},{12,4},{16,24},{20,28},{24,16},{28,20},{1,9},{5... | collective-permute-start | bytes 147464 | tf_op jit(solution)/shard_map/ppermute | solution.py:734
  117.9 14.5 %collective-permute-start.36 = (bf16[192,1536]{1,0:T(8,128)(2,1)S(1)}, bf16[192,1536]{1,0:T(8,128)(2,1)S(1)}, u32[]{:S(2)}, u32[]{:S(2)}) collective-permute-start(bf16[192,1536]{1,0:T(8,128)(2,1)S(1)} %pad_maximum_fusion.1), channel_id=1, source_target_pairs={{0,4},{4,0},{8,12},{12,8},{16,20},{20,16},{24,28},{28,24},{1,5},{5... | collective-permute-start | bytes 1769480 | tf_op jit(solution)/shard_map/ppermute | solution.py:734
  119.7 19.1 %copy-start.3 = (bf16[768,192]{0,1:T(8,128)(2,1)S(1)}, bf16[768,192]{0,1:T(8,128)(2,1)}, u32[]{:S(2)}) copy-start(bf16[768,192]{0,1:T(8,128)(2,1)} %param.30) | copy-start | bytes 884740
  119.7 19.1 %copy-start.4 = (bf16[768,192]{0,1:T(8,128)(2,1)S(1)}, bf16[768,192]{0,1:T(8,128)(2,1)}, u32[]{:S(2)}) copy-start(bf16[768,192]{0,1:T(8,128)(2,1)} %param.31) | copy-start | bytes 884740
  119.7 19.1 %copy-start.10 = (f32[768]{0:T(1024)S(1)}, f32[768]{0:T(1024)}, u32[]{:S(2)}) copy-start(f32[768]{0:T(1024)} %g_cross.5) | copy-start | bytes 9220
  132.4 11.3 %collective-permute-start.37 = (bf16[384,1536]{1,0:T(8,128)(2,1)S(1)}, bf16[384,1536]{1,0:T(8,128)(2,1)S(1)}, u32[]{:S(2)}, u32[]{:S(2)}) collective-permute-start(bf16[384,1536]{1,0:T(8,128)(2,1)S(1)} %constant_dynamic-update-slice_fusion.both_own), channel_id=1, source_target_pairs={{0,1},{1,0},{2,3},{3,2},{4,5},{5,4},{6,7},{7,6},{8,9},{9,8},{10,11... | collective-permute-start | bytes 3538952 | tf_op jit(solution)/shard_map/ppermute | solution.py:734
  132.5 11.2 %collective-permute-start.35 = (bf16[384,768]{1,0:T(8,128)(2,1)S(1)}, bf16[384,768]{1,0:T(8,128)(2,1)S(1)}, u32[]{:S(2)}, u32[]{:S(2)}) collective-permute-start(bf16[384,768]{1,0:T(8,128)(2,1)S(1)} %pad_maximum_fusion.c_own), channel_id=1, source_target_pairs={{0,1},{1,0},{2,3},{3,2},{4,5},{5,4},{6,7},{7,6},{8,9},{9,8},{10,11... | collective-permute-start | bytes 1769480 | tf_op jit(solution)/shard_map/ppermute | solution.py:734
  133.0 5.8 %collective-permute-start.32 = (f32[16,768]{1,0:T(8,128)S(1)}, f32[16,768]{1,0:T(8,128)S(1)}, u32[]{:S(2)}, u32[]{:S(2)}) collective-permute-start(f32[16,768]{1,0:T(8,128)S(1)} %add.55.sum_a), channel_id=1, source_target_pairs={{0,16},{4,20},{8,24},{12,28},{16,0},{20,4},{24,8},{28,12},{1,17},{... | collective-permute-start | bytes 147464 | tf_op jit(solution)/shard_map/ppermute | solution.py:734
  138.8 16.5 %collective-permute-start.40 = (bf16[192,768]{1,0:T(8,128)(2,1)S(1)}, bf16[192,768]{1,0:T(8,128)(2,1)S(1)}, u32[]{:S(2)}, u32[]{:S(2)}) collective-permute-start(bf16[192,768]{1,0:T(8,128)(2,1)S(1)} %add_convert_fusion), channel_id=1, source_target_pairs={{0,16},{4,20},{8,24},{12,28},{16,0},{20,4},{24,8},{28,12},{1,17},{... | collective-permute-start | bytes 884744 | tf_op jit(solution)/shard_map/ppermute | solution.py:734
  141.0 1.2 collective-permute-start.33
  142.2 9.5 %collective-permute-start.34 = (f32[8,768]{1,0:T(8,128)S(1)}, f32[8,768]{1,0:T(8,128)S(1)}, u32[]{:S(2)}, u32[]{:S(2)}) collective-permute-start(f32[8,768]{1,0:T(8,128)S(1)} %add.57.part_a), channel_id=1, source_target_pairs={{0,2},{1,3},{2,0},{3,1},{4,6},{5,7},{6,4},{7,5},{8,10},{9,11},{10,... | collective-permute-start | bytes 73736 | tf_op jit(solution)/shard_map/ppermute | solution.py:734
  143.7 8.0 %copy-start.5 = (bf16[768,192]{0,1:T(8,128)(2,1)S(1)}, bf16[768,192]{0,1:T(8,128)(2,1)}, u32[]{:S(2)}) copy-start(bf16[768,192]{0,1:T(8,128)(2,1)} %param.27) | copy-start | bytes 884740
  143.7 8.0 %copy-start.6 = (bf16[192,768]{1,0:T(8,128)(2,1)S(1)}, bf16[192,768]{1,0:T(8,128)(2,1)}, u32[]{:S(2)}) copy-start(bf16[192,768]{1,0:T(8,128)(2,1)} %wos.3) | copy-start | bytes 884740
  143.7 8.0 %copy-start.11 = (f32[768]{0:T(1024)S(1)}, f32[768]{0:T(1024)}, u32[]{:S(2)}) copy-start(f32[768]{0:T(1024)} %g_self.5) | copy-start | bytes 9220
  143.7 8.0 %copy-start.12 = (bf16[768]{0:T(1024)(128)(2,1)S(1)}, bf16[768]{0:T(1024)(128)(2,1)}, u32[]{:S(2)}) copy-start(bf16[768]{0:T(1024)(128)(2,1)} %start.7) | copy-start | bytes 4612
  153.6 1.2 collective-permute-start.38
  154.8 3.8 %collective-permute-start.39 = (f32[8,768]{1,0:T(8,128)S(1)}, f32[8,768]{1,0:T(8,128)S(1)}, u32[]{:S(2)}, u32[]{:S(2)}) collective-permute-start(f32[8,768]{1,0:T(8,128)S(1)} %add.58.part_a), channel_id=1, source_target_pairs={{0,2},{1,3},{2,0},{3,1},{4,6},{5,7},{6,4},{7,5},{8,10},{9,11},{10,... | collective-permute-start | bytes 73736 | tf_op jit(solution)/shard_map/ppermute | solution.py:734

commit v3 on v2

--- a/solution.py
+++ b/solution.py
@@ -12,7 +12,9 @@
 HEAD_DIM = 64
 ROWS = 16
 BLOCK = 16
+SPAN = 2 * BLOCK
 LANES = 128
+PANELS = D // LANES
 PARTS = 4
 
 EPSILON = 1e-06
@@ -130,38 +132,45 @@
     part_out[...] = nn(s1, wos[...])[:8]
 
 
+def load_kernel(first, last, enc, since, scal, *refs):
+    held, sems = refs[-2:]
+    loads = []
+    for k in range(first, last):
+        part = pl.ds(k * BLOCK, BLOCK)
+        loads.append(pltpu.make_async_copy(enc.at[part], held.at[part], sems.at[k - first]))
+        loads[-1].start()
+    for load in loads:
+        load.wait()
+
+
 def query_kernel(scal, part_a, part_b, start, g_cross, wq, wk, qk_out, h1_out):
     h1_out[...] = row_of(start) + (part_a[0:1] + part_b[0:1])
     _, qm = query_parts(scal, h1_out, g_cross, wq)
     qk_out[...] = nn(qm, wk[...])
 
 
+def load_kernel(first, last, enc, since, scal, *refs):
+    held, sems = refs[-2:]
+    loads = []
+    for k in range(first, last):
+        part = pl.ds(k * BLOCK, BLOCK)
+        loads.append(pltpu.make_async_copy(enc.at[part], held.at[part], sems.at[k - first]))
+        loads[-1].start()
+    for load in loads:
+        load.wait()
+
+
+def query_kernel(scal, part_a, part_b, start, g_cross, wq, wk, qk_out, h1_out):
+    h1_out[...] = row_of(start) + (part_a[0:1] + part_b[0:1])
+    _, qm = query_parts(scal, h1_out, g_cross, wq)
+    qk_out[...] = nn(qm, wk[...])
+
+
 def select_docs(height, width):
     r, c = iota((height, width), 0), iota((height, width), 1)
     return (((r // BLOCK) == (c % ROWS)) & ((r % BLOCK) == (c // ROWS))).astype(bf16)
 
 
-def load_kernel(lo, hi, scal, sizes, enc, *refs):
-    held, sems = refs[-2:]
-    count = sizes[scal[1]]
-
-    def piece(k):
-        part = pl.ds(lo + k * BLOCK, BLOCK)
-        return pltpu.make_async_copy(enc.at[part], held.at[part], sems.at[k])
-
-    for k in range((hi - lo) // BLOCK):
-
-        @pl.when(lo + k * BLOCK < count)
-        def _():
-            piece(k).start()
-
-    for k in range((hi - lo) // BLOCK):
-
-        @pl.when(lo + k * BLOCK < count)
-        def _():
-            piece(k).wait()
-
-
 def first_doc(scal, sizes):
     groups = sizes.shape[0]
 
@@ -171,58 +180,62 @@
     return lax.fori_loop(0, groups, body, jnp.int32(0), unroll=groups <= 8)
 
 
-def attend_kernel(base, scal, sizes, lengths, qa, qb, enc, *refs):
-    p_out, e_out, ext_out, qk_s = refs[-4:]
-    step = pl.program_id(0) + base
+def rounds_of(scal, sizes):
+    return (sizes[scal[1]] + SPAN - 1) // SPAN
+
+
+def attend_kernel(
+    loaded, scal, sizes, lengths, qa, qb, enc, _, held, p_out, e_out, ext_out, qk_s, sems
+):
     tokens = enc.shape[1]
+    blocks = enc.shape[0] // BLOCK
+    rounds = rounds_of(scal, sizes)
+    per_round = SPAN // BLOCK
     count = sizes[scal[1]]
-    block = pl.ds(step * BLOCK, BLOCK)
+    begin = first_doc(scal, sizes)
     tall = BLOCK * ROWS
 
-    @pl.when(pl.program_id(0) == 0)
-    def _():
-        high, low = split2(qa[...] + qb[...])
-        qk_s[0:ROWS] = high
-        qk_s[ROWS : 2 * ROWS] = low
-
-    @pl.when(step * BLOCK < count)
-    def _():
-        rows = enc[block].reshape(BLOCK * tokens, D)
+    def piece(k):
+        part = pl.ds(k * BLOCK, BLOCK)
+        return pltpu.make_async_copy(enc.at[part], held.at[part], sems.at[k])
+
+    for k in range(loaded, blocks):
+        pl.when(k // per_round < rounds)(lambda k=k: piece(k).start())
+    high, low = split2(qa[...] + qb[...])
+    qk_s[0:ROWS] = high
+    qk_s[ROWS : 2 * ROWS] = low
+
+    def one_block(step):
+        block = pl.ds(pl.multiple_of(step * BLOCK, BLOCK), BLOCK)
+        flat = pl.ds(pl.multiple_of(step * tall, tall), tall)
+        rows = held[block].reshape(BLOCK * tokens, D)
         both = nt(qk_s[...], rows)
         logits = both[:ROWS] + both[ROWS:]
         logits = jnp.concatenate(
             [logits[:, b * tokens : (b + 1) * tokens] for b in range(BLOCK)], axis=0
         )
-        begin = first_doc(scal, sizes)
         shown = []
         for b in range(BLOCK):
             slot = step * BLOCK + b
             doc = jnp.minimum(begin + slot, lengths.shape[0] - 1)
             length = jnp.where(slot < count, lengths[doc] - scal[0] * tokens, 0)
             shown.append(jnp.broadcast_to(length, (ROWS, tokens)))
-        seen = jnp.concatenate(shown, axis=0)
-        seen = iota((tall, tokens), 1) < seen
+        seen = iota((tall, tokens), 1) < jnp.concatenate(shown, axis=0)
         logits = jnp.where(seen, logits, MASKED)
         peak = jnp.max(logits, axis=1, keepdims=True)
         raised = jnp.where(seen, jnp.exp(logits - peak), 0.0)
         total = jnp.sum(raised, axis=1, keepdims=True)
-        p_out[...] = raised.reshape(BLOCK, ROWS, tokens)
+        p_out[block] = raised.reshape(BLOCK, ROWS, tokens)
         low = raised.astype(bf16)
-        sums = []
-        upper = iota((2 * ROWS, tokens), 0) < ROWS
-        zero = jnp.zeros((2 * ROWS, tokens), bf16)
-        for k in range(BLOCK // 2):
-            pair = low[2 * ROWS * k : 2 * ROWS * (k + 1)]
-            left = jnp.concatenate(
-                [jnp.where(upper, pair, zero), jnp.where(upper, zero, pair)], axis=1
-            )
-            sums.append(nn(left, rows[2 * tokens * k : 2 * tokens * (k + 1)]))
-        summed = jnp.concatenate(sums, axis=0).astype(bf16)
-        e_out[...] = (
-            nn(select_docs(HEADS * BLOCK, tall), summed)
-            .astype(bf16)
-            .reshape(HEADS, BLOCK, D)
+        summed = jnp.concatenate(
+            [
+                nn(low[ROWS * b : ROWS * (b + 1)], rows[tokens * b : tokens * (b + 1)])
+                for b in range(BLOCK)
+            ],
+            axis=0,
         )
+        for k in range(PANELS):
+            e_out[k, flat] = summed[:, k * LANES : (k + 1) * LANES]
         gather = (iota((BLOCK, tall), 0) == iota((BLOCK, tall), 1) // ROWS).astype(bf16)
         parts = split3(peak) + split3(total)
         at = iota((tall, LANES), 1)
@@ -230,13 +243,29 @@
         for k, part in enumerate(parts):
             extra = jnp.where(at // ROWS == k, part.astype(f32), extra)
         extra = jnp.where(at % ROWS == iota((tall, LANES), 0) % ROWS, extra, 0.0)
-        ext_out[...] = nn(gather, extra.astype(bf16)).astype(bf16)
-
-    @pl.when(step * BLOCK >= count)
-    def _():
-        p_out[...] = jnp.zeros_like(p_out)
-        e_out[...] = jnp.zeros_like(e_out)
-        ext_out[...] = jnp.where(iota((BLOCK, LANES), 1) < ROWS, MASKED, 0.0).astype(bf16)
+        ext_out[block] = nn(gather, extra.astype(bf16)).astype(bf16)
+
+    @pl.loop(0, rounds)
+    def _(i):
+        for j in range(per_round):
+            k = i * per_round + j
+            pl.when(k >= loaded)(lambda k=k: piece(k).wait())
+        for j in range(per_round):
+            one_block(i * per_round + j)
+
+    @pl.loop(rounds, enc.shape[0] // SPAN)
+    def _(i):
+        span = pl.ds(pl.multiple_of(i * SPAN, SPAN), SPAN)
+        flat = pl.ds(pl.multiple_of(i * SPAN * ROWS, SPAN * ROWS), SPAN * ROWS)
+        p_out[span] = jnp.zeros((SPAN, ROWS, tokens), f32)
+        for k in range(PANELS):
+            e_out[k, flat] = jnp.zeros((SPAN * ROWS, LANES), f32)
+        ext_out[span] = jnp.where(iota((SPAN, LANES), 1) < ROWS, MASKED, 0.0).astype(bf16)
+
+
+def sums_of_head(summed, head, slots):
+    rows = pl.ds(head, slots, stride=ROWS)
+    return jnp.concatenate([summed[k, rows, :] for k in range(PANELS)], axis=1)
 
 
 def place_parts(scal, full, own, by2, by1, by3):
@@ -246,12 +275,15 @@
         full[pl.ds(at, height)] = piece[...]
 
 
-def project_kernel(scal, summed, extra, own, by2, by1, by3, pay_out, wv):
+def project_kernel(scal, summed, extra, own, by2, by1, by3, pay_out, heads_out, wv):
     place_parts(scal, wv, own, by2, by1, by3)
-    even = iota((summed.shape[1], LANES), 1) < HEAD_DIM
+    slots = pay_out.shape[0]
+    even = iota((slots, LANES), 1) < HEAD_DIM
     for k in range(HEADS // 2):
         pair = wv[k * LANES : (k + 1) * LANES]
-        one, two = nt(summed[2 * k], pair), nt(summed[2 * k + 1], pair)
+        for head in (2 * k, 2 * k + 1):
+            heads_out[head] = sums_of_head(summed, head, slots).astype(bf16)
+        one, two = (nt(heads_out[2 * k + odd], pair) for odd in range(2))
         pay_out[:, k * LANES : (k + 1) * LANES] = jnp.where(even, one, two).astype(bf16)
     pay_out[:, D:] = extra[...]
 
@@ -329,10 +361,7 @@
     part_out[...] = nn(u, wdown[...]).astype(bf16)
 
 
-def score_kernel(
-    scal, part_a, part_b, h2, z, g_final, row, wdown, win,
-    scores_out, n3_out, dh3_out, part_out,
-):
+def score_kernel(scal, part_a, part_b, h2, g_final, row, scores_out, n3_out, dh3_out):
     h3 = h2[...] + (part_a[...].astype(f32) + part_b[...].astype(f32))
     n3, r3 = rms_parts(h3)
     n3_out[...] = n3
@@ -342,9 +371,11 @@
     groups = scores_out.shape[0]
     wide = jnp.concatenate([scores, jnp.zeros((1, LANES - slots), f32)], axis=1)
     scores_out[...] = jnp.where(iota((groups, LANES), 0) == scal[1], wide, 0.0)
-    dh3 = rms_back(wanted[0:1], n3, r3).astype(bf16)
-    dh3_out[...] = dh3
-    du = nt(dh3, wdown[...])
+    dh3_out[...] = rms_back(wanted[0:1], n3, r3).astype(bf16)
+
+
+def down_kernel(dh3, z, wdown, win, part_out):
+    du = nt(dh3[...], wdown[...])
     dz = (du * gelu_slope(z[...])).astype(bf16)
     part_out[...] = nt(dz, win[...]).astype(bf16)
 
@@ -413,35 +444,38 @@
     inner_out[...] = nn(dc.astype(f32) * c32[...], hot, EXACT)
 
 
-def column(rows):
+def columns(one, two):
     tall = BLOCK * ROWS
-    pick = (iota((tall, BLOCK), 0) // ROWS == iota((tall, BLOCK), 1)).astype(f32)
-    wide = nn(pick, rows, EXACT)
-    own = iota((tall, LANES), 0) % ROWS == iota((tall, LANES), 1)
-    return jnp.sum(jnp.where(own, wide, 0.0), axis=1, keepdims=True)
-
-
-def back_kernel(
-    scal, sizes, enc, p, scale, inner, dc, wv_own, wv_by2, wv_by1, wv_by3,
-    dap_out, vd_out, wv,
-):
-    step = pl.program_id(0)
-
-    @pl.when(step == 0)
-    def _():
-        place_parts(scal, wv, wv_own, wv_by2, wv_by1, wv_by3)
-
+    half = LANES // 2
+    both = jnp.where(iota((BLOCK, LANES), 1) < half, one, pltpu.roll(two, half, 1))
+    parts = jnp.concatenate(split3(both), axis=0)
+    r, c = iota((tall, 3 * BLOCK), 0), iota((tall, 3 * BLOCK), 1)
+    wide = nn((r // ROWS == c % BLOCK).astype(bf16), parts)
+    lane, head = iota((tall, LANES), 1), iota((tall, LANES), 0) % ROWS
+    return tuple(
+        jnp.sum(jnp.where(lane == head + k * half, wide, 0.0), axis=1, keepdims=True)
+        for k in range(2)
+    )
+
+
+def back_kernel(first, last, scal, sizes, enc, p, scale, inner, dc, *refs):
+    if first:
+        wv, dap_out, vd_out = refs[0], *refs[-2:]
+    else:
+        dap_out, vd_out, wv = refs[-3:]
+        place_parts(scal, wv, *refs[:4])
     tokens = enc.shape[1]
     tall = BLOCK * ROWS
-
-    @pl.when(step * BLOCK < sizes[scal[1]])
-    def _():
-        rows = enc[pl.ds(step * BLOCK, BLOCK)].reshape(BLOCK * tokens, D)
+    rounds = jnp.clip(rounds_of(scal, sizes), first, last)
+
+    def one_block(step):
+        block = pl.ds(pl.multiple_of(step * BLOCK, BLOCK), BLOCK)
+        rows = enc[block].reshape(BLOCK * tokens, D)
         pick = (iota((tall, BLOCK), 0) // ROWS == iota((tall, BLOCK), 1)).astype(bf16)
         own = (iota((tall, D), 0) % ROWS) == head_of((tall, D), 1)
-        grad = jnp.where(own, nn(pick, dc[...]), 0.0).astype(bf16)
+        grad = jnp.where(own, nn(pick, dc[block]), 0.0).astype(bf16)
         vd = nn(grad, wv[...]).astype(bf16)
-        vd_out[...] = vd.reshape(BLOCK, ROWS, D)
+        vd_out[block] = vd.reshape(BLOCK, ROWS, D)
         grad_probs = []
         for k in range(BLOCK // 2):
             pair = nt(
@@ -450,61 +484,75 @@
             )
             grad_probs += [pair[:ROWS, :tokens], pair[ROWS:, tokens:]]
         grad_probs = jnp.concatenate(grad_probs, axis=0)
-        prob = p[...].reshape(tall, tokens) * column(scale[...])
-        da = (prob * (grad_probs - column(inner[...]))).astype(bf16)
-        dap_out[:, :ROWS] = da.reshape(BLOCK, ROWS, tokens)
-        dap_out[:, ROWS:] = prob.astype(bf16).reshape(BLOCK, ROWS, tokens)
-
-    @pl.when(step * BLOCK >= sizes[scal[1]])
-    def _():
-        dap_out[...] = jnp.zeros_like(dap_out)
-        vd_out[...] = jnp.zeros_like(vd_out)
-
-
-def key_sum_kernel(scal, sizes, ds, enc, da, dh2, n3, ff, sums_out):
-    step = pl.program_id(0)
+        scale_col, inner_col = columns(scale[block], inner[block])
+        prob = p[block].reshape(tall, tokens) * scale_col
+        da = (prob * (grad_probs - inner_col)).astype(bf16)
+        dap_out[block, :ROWS] = da.reshape(BLOCK, ROWS, tokens)
+        dap_out[block, ROWS:] = prob.astype(bf16).reshape(BLOCK, ROWS, tokens)
+
+    @pl.loop(first, rounds)
+    def _(i):
+        for j in range(SPAN // BLOCK):
+            one_block(i * (SPAN // BLOCK) + j)
+
+    @pl.loop(rounds, last)
+    def _(i):
+        span = pl.ds(pl.multiple_of(i * SPAN, SPAN), SPAN)
+        dap_out[span] = jnp.zeros((SPAN, 2 * ROWS, tokens), bf16)
+        vd_out[span] = jnp.zeros((SPAN, ROWS, D), bf16)
+
+
+def key_sum_kernel(scal, sizes, ds, enc, dap, dh2, n3, ff, sums_out):
     tokens = enc.shape[1]
     tall = BLOCK * ROWS
-
-    @pl.when(step == 0)
-    def _():
-        slots = dh2.shape[0]
-        row = ds[...][:, :slots] * (1.0 / PARTS)
-        at = iota((ROWS, D), 0)
-        out = jnp.where(at == HEADS, nn(row, dh2[...].astype(f32), EXACT)[0:1], 0.0)
-        out = jnp.where(at == HEADS + 1, nn(row, n3[...], EXACT)[0:1], out)
-        sums_out[...] = jnp.where(at == HEADS + 2, nn(row, ff[...], EXACT)[0:1], out)
-
-    @pl.when(step * BLOCK < sizes[scal[1]])
-    def _():
-        rows = enc[pl.ds(step * BLOCK, BLOCK)].reshape(BLOCK * tokens, D)
+    slots = dh2.shape[0]
+    row = ds[...][:, :slots] * (1.0 / PARTS)
+    at = iota((ROWS, D), 0)
+    out = jnp.where(at == HEADS, nn(row, dh2[...].astype(f32), EXACT)[0:1], 0.0)
+    out = jnp.where(at == HEADS + 1, nn(row, n3[...], EXACT)[0:1], out)
+    sums_out[...] = jnp.where(at == HEADS + 2, nn(row, ff[...], EXACT)[0:1], out)
+
+    def one_block(step):
+        block = pl.ds(pl.multiple_of(step * BLOCK, BLOCK), BLOCK)
         own_slot = iota((tall, LANES), 1) == step * BLOCK + iota((tall, LANES), 0) // ROWS
         ds_col = jnp.sum(jnp.where(own_slot, ds[0:1], 0.0), axis=1, keepdims=True)
-        scaled = (da[...].reshape(tall, tokens).astype(f32) * ds_col).astype(bf16)
+        scaled = (dap[block, :ROWS].reshape(tall, tokens).astype(f32) * ds_col).astype(bf16)
         flat = jnp.concatenate(
             [scaled[ROWS * b : ROWS * (b + 1)] for b in range(BLOCK)], axis=1
         )
-        sums_out[...] += nn(flat, rows)
-
-
-def enc_grad_kernel(base, scal, sizes, ds, qa, qb, dap, vd, *refs):
-    grad_out = refs[-1]
-    step = pl.program_id(0) + base
-
-    @pl.when(step * BLOCK < sizes[scal[1]])
-    def _():
-        qk = qa[...] + qb[...]
-        lane = iota((1, LANES), 1)
-        for b in range(BLOCK):
-            scale = jnp.sum(
-                jnp.where(lane == step * BLOCK + b, ds[0:1], 0.0), axis=1, keepdims=True
+        return nn(flat, enc[block].reshape(BLOCK * tokens, D))
+
+    @pl.loop(0, rounds_of(scal, sizes))
+    def _(i):
+        per_round = SPAN // BLOCK
+        total = one_block(i * per_round)
+        for j in range(1, per_round):
+            total = total + one_block(i * per_round + j)
+        sums_out[...] += total
+
+
+def enc_grad_kernel(first, last, ds, qa, qb, dap, vd, *refs):
+    grad_out, slots, sems = refs[-3:]
+    pieces, size = slots.shape[:2]
+    qk = qa[...] + qb[...]
+    lane = iota((1, LANES), 1)
+    copies = []
+    for k in range((last - first) // size):
+        if k >= pieces:
+            copies[k - pieces].wait()
+        start = first + k * size
+        for b in range(size):
+            scale = jnp.sum(jnp.where(lane == start + b, ds[0:1], 0.0), axis=1, keepdims=True)
+            right = jnp.concatenate([qk, vd[start + b].astype(f32)], axis=0) * scale
+            slots[k % pieces, b] = tn(dap[start + b], right.astype(bf16)).astype(bf16)
+        copies.append(
+            pltpu.make_async_copy(
+                slots.at[k % pieces], grad_out.at[pl.ds(start, size)], sems.at[k % pieces]
             )
-            right = jnp.concatenate([qk, vd[b].astype(f32)], axis=0) * scale
-            grad_out[b] = tn(dap[b], right.astype(bf16)).astype(bf16)
-
-    @pl.when(step * BLOCK >= sizes[scal[1]])
-    def _():
-        grad_out[...] = jnp.zeros_like(grad_out)
+        )
+        copies[-1].start()
+    for copy in copies[-pieces:]:
+        copy.wait()
 
 
 def share_kernel(scal, summed, scale, keep_out, send_out):
@@ -586,31 +634,53 @@
         out[...] += value
 
 
-def weights_kernel(
-    order, tile, scal, sizes, c_own, c_other, both_own, both_other, ds,
-    h1, g_ff, wo_own, wo_by2, wo_by1, wo_by3, win, wdown,
-    win_out, wdown_out, wout_out, wout,
+def weights_before_kernel(
+    order, tile, scal, sizes, c_own, c_other, h1, g_ff, wo_own, wo_by2, wo_by1, wo_by3, win,
+    y3_out, u_out, slope_out, c_out, wout,
 ):
     place_parts(scal, wout, wo_own, wo_by2, wo_by1, wo_by3)
 
     def one_tile(first, new):
+        here = pl.ds(first, tile)
         rows = document_picks(order, tile, scal, sizes, c_own.shape[0], first)
         c = rows(c_own, c_other)
         h2 = h1[...] + nn(c, wout[...])
         n2, _ = rms_parts(h2)
         y3 = (n2 * row_of(g_ff)).astype(bf16)
+        y3_out[here] = y3
         z = nn(y3, win[...])
-        u = (z * phi(z)).astype(bf16)
+        u_out[here] = (z * phi(z)).astype(bf16)
+        slope_out[here] = gelu_slope(z)
+        width = c_out.shape[1]
+        pick = (iota((D, width), 0) == scal[0] * width + iota((D, width), 1)).astype(bf16)
+        c_out[here] = nn(c, pick).astype(bf16)
+
+    over_tiles(y3_out.shape[0], tile, one_tile)
+
+
+def weights_kernel(
+    order, tile, scal, sizes, y3, slope, both_own, both_other, ds, wdown,
+    win_out, grads_out,
+):
+    def one_tile(first, new):
+        here = pl.ds(first, tile)
+        rows = document_picks(order, tile, scal, sizes, both_own.shape[0], first)
         both = rows(both_own, both_other).astype(f32) * ds_column(ds, first, tile)
-        dh3, dh2 = both[:, :D].astype(bf16), both[:, D:].astype(bf16)
-        dz = (nt(dh3, wdown[...]) * gelu_slope(z)).astype(bf16)
-        put(win_out, tn(y3, dz), new)
-        put(wdown_out, tn(u, dh3), new)
-        width = wout_out.shape[0]
-        pick = (iota((D, width), 0) == scal[0] * width + iota((D, width), 1)).astype(bf16)
-        put(wout_out, tn(nn(c, pick).astype(bf16), dh2), new)
+        both = both.astype(bf16)
+        grads_out[here] = both
+        dz = (nt(both[:, :D], wdown[...]) * slope[here]).astype(bf16)
+        put(win_out, tn(y3[here], dz), new)
 
     over_tiles(ds.shape[1], tile, one_tile)
+
+
+def weights_after_kernel(tile, u, c, grads, wdown_out, wout_out):
+    def one_tile(first, new):
+        here = pl.ds(first, tile)
+        put(wdown_out, tn(u[here], grads[here, :D]), new)
+        put(wout_out, tn(c[here], grads[here, D:]), new)
+
+    over_tiles(u.shape[0], tile, one_tile)
 
 
 def key_kernel(scal, sum_a, sum_b, h1, g_cross, wk, wq, key_out, query_out, part_out):
@@ -680,53 +750,35 @@
     return pltpu.with_memory_space_constraint(x, pltpu.HBM)
 
 
-def plain(kernel, outs, *args, smem=0, flops=0, limit=12, scratch=()):
-    size = sum(a.size * a.dtype.itemsize for a in args)
+def plain(
+    kernel, outs, *args, smem=0, hbm=(), hbm_out=False, onto=None, flops=0, limit=12, scratch=()
+):
+    size = sum(a.size * a.dtype.itemsize for k, a in enumerate(args) if k not in hbm)
+    spaces = [pltpu.SMEM] * smem + [pltpu.VMEM] * (len(args) - smem)
+    for k in hbm:
+        spaces[k] = pltpu.HBM
+    out_space = pltpu.HBM if hbm_out else pltpu.VMEM
     return pl.pallas_call(
         kernel,
         out_shape=outs,
-        in_specs=[whole_spec(pltpu.SMEM if k < smem else pltpu.VMEM) for k in range(len(args))],
-        out_specs=jax.tree.map(lambda _: whole_spec(), outs),
+        in_specs=[whole_spec(space) for space in spaces],
+        out_specs=[whole_spec(out_space) for _ in outs]
+        if isinstance(outs, list)
+        else whole_spec(out_space),
         scratch_shapes=list(scratch),
+        input_output_aliases=onto or {},
         compiler_params=pltpu.CompilerParams(vmem_limit_bytes=limit * MIB),
         cost_estimate=pl.CostEstimate(flops=flops, bytes_accessed=size, transcendentals=0),
         name=name_of(kernel),
     )(*args)
 
 
-def gridded(kernel, steps, scalars, ins, outs, scratch=(), flops=0, limit=14, onto=()):
-    size = sum(a.size * a.dtype.itemsize for a, _, _ in ins)
-    size += sum(s.size * s.dtype.itemsize for s, _, _ in outs)
-    count = len(scalars) + len(ins)
-    return pl.pallas_call(
-        kernel,
-        out_shape=[s for s, _, _ in outs],
-        grid_spec=pltpu.PrefetchScalarGridSpec(
-            num_scalar_prefetch=len(scalars),
-            grid=(steps,),
-            in_specs=[
-                pl.BlockSpec(block, index) if block else whole_spec() for _, block, index in ins
-            ]
-            + [pl.BlockSpec(memory_space=pl.ANY)] * len(onto),
-            out_specs=[pl.BlockSpec(block, index) for _, block, index in outs],
-            scratch_shapes=list(scratch),
-        ),
-        input_output_aliases={count + k: k for k in range(len(onto))},
-        compiler_params=pltpu.CompilerParams(
-            vmem_limit_bytes=limit * MIB, dimension_semantics=("arbitrary",)
-        ),
-        cost_estimate=pl.CostEstimate(flops=flops, bytes_accessed=size, transcendentals=0),
-        name=name_of(kernel),
-    )(*scalars, *[a for a, _, _ in ins], *onto)
-
-
 def bits_of(size):
     return [1 << b for b in range(size.bit_length() - 1)]
 
 
-def long_first(size):
-    bits = bits_of(size)
-    return bits[1:] + bits[:1]
+def far_first(size):
+    return bits_of(size)[::-1]
 
 
 def swap(x, axis, bit):
@@ -780,9 +832,8 @@
     width = w_value.shape[1]
     own_heads = HEADS // parts
     hidden = w_in.shape[1]
-    blocks = slots // BLOCK
     over_heads = [("heads", 1), ("heads", 2)]
-    order = long_first(groups)
+    order = far_first(groups)
     over_docs = [("docs", bit) for bit in order]
 
     scal = jnp.stack([me_j, me_g])
@@ -796,28 +847,28 @@
         *map(in_hbm, (start_token, g_self, wvs_t, w_out_self)),
     )
 
-    def load(lo, hi, onto=()):
+
+    def load(first, last, since, *onto):
         return pl.pallas_call(
-            functools.partial(load_kernel, lo, hi),
+            functools.partial(load_kernel, first, last),
             out_shape=pltpu.VMEM(enc_out.shape, bf16),
-            in_specs=[whole_spec(pltpu.SMEM)] * 2
-            + [whole_spec(pltpu.HBM)]
+            in_specs=[whole_spec(pltpu.HBM), whole_spec(pl.ANY), whole_spec(pltpu.SMEM)]
             + [whole_spec()] * len(onto),
             out_specs=whole_spec(),
-            scratch_shapes=[pltpu.SemaphoreType.DMA(((hi - lo) // BLOCK,))],
+            scratch_shapes=[pltpu.SemaphoreType.DMA((last - first,))],
             input_output_aliases={3: 0} if onto else {},
             compiler_params=pltpu.CompilerParams(vmem_limit_bytes=MIB),
             cost_estimate=pl.CostEstimate(
-                flops=0, bytes_accessed=(hi - lo) * tokens * D * 4, transcendentals=0
+                flops=0, bytes_accessed=(last - first) * BLOCK * tokens * D * 4, transcendentals=0
             ),
             name="load_kernel",
-        )(scal, group_docs, in_hbm(enc_out), *onto)
-
-    middle = slots // 2
+        )(in_hbm(enc_out), since, scal, *onto)
+
     part = add(part, swap(part, "heads", 1))
     part_a, part_b = part, swap(part, "heads", 2)
-    held = load(0, middle)
+    held = load(0, 1, part)
     part_b, held = lax.optimization_barrier((part_b, held))
+    wv_by2 = swap(after(wv_t, part_b), "heads", 2)
     qk, h1 = plain(
         query_kernel,
         [shape((ROWS, D)), shape((1, D))],
@@ -827,59 +878,45 @@
         *map(in_hbm, (start_token, g_cross, wq_t, wk_t)),
         smem=1,
     )
+    qk = add(qk, swap(qk, "heads", 1))
     qk, held = lax.optimization_barrier((qk, held))
-    qk_a, qk_b = sum_last(qk, over_heads)
-    held = load(middle, slots, (held,))
-
-    const2 = lambda i, *_: (0, 0)
-    step2 = lambda i, *_: (i, 0)
-    step3 = lambda i, *_: (i, 0, 0)
+    qk_a, qk_b = qk, swap(qk, "heads", 2)
+    held = load(1, 3, qk, held)
+    qk_b, held, wv_by2 = lax.optimization_barrier((qk_b, held, wv_by2))
+    wv_by3 = swap(wv_by2, "heads", 1)
+
     pass_flops = 2 * slots * tokens * D * 256
 
-    def attend(base, steps, onto=()):
-        return gridded(
-            functools.partial(attend_kernel, base),
-            steps,
-            [scal, group_docs, enc_len],
-            [
-                (qk_a, (ROWS, D), const2),
-                (qk_b, (ROWS, D), const2),
-                (held, None, None),
-            ],
-            [
-                (
-                    shape((slots, ROWS, tokens)),
-                    (BLOCK, ROWS, tokens),
-                    lambda i, *_: (i + base, 0, 0),
-                ),
-                (
-                    shape((HEADS, slots, D), bf16),
-                    (HEADS, BLOCK, D),
-                    lambda i, *_: (0, i + base, 0),
-                ),
-                (
-                    shape((slots, LANES), bf16),
-                    (BLOCK, LANES),
-                    lambda i, *_: (i + base, 0),
-                ),
-            ],
-            scratch=[pltpu.VMEM((2 * ROWS, D), bf16)],
-            flops=2 * pass_flops * steps // blocks,
-            onto=onto,
-        )
-
-    split = 4
-    wv_by2 = swap(after(wv_t, qk_b), "heads", 2)
-    prob, summed, extra = attend(0, split)
-    prob, wv_by2 = lax.optimization_barrier((prob, wv_by2))
-    wv_by3 = swap(wv_by2, "heads", 1)
-    wo_by2 = swap(after(w_out, wv_by2), "heads", 2)
-    prob, summed, extra = attend(split, blocks - split, (prob, summed, extra))
+    wo_by2 = swap(after(w_out, qk_b), "heads", 2)
+    held, prob, summed, extra = plain(
+        functools.partial(attend_kernel, 3),
+        [
+            pltpu.VMEM(enc_out.shape, bf16),
+            pltpu.VMEM((slots, ROWS, tokens), f32),
+            pltpu.VMEM((PANELS, slots * ROWS, LANES), f32),
+            shape((slots, LANES), bf16),
+        ],
+        scal,
+        group_docs,
+        enc_len,
+        qk_a,
+        qk_b,
+        in_hbm(enc_out),
+        held,
+        smem=3,
+        hbm=(5,),
+        onto={6: 0},
+        flops=2 * pass_flops,
+        scratch=[pltpu.VMEM((2 * ROWS, D), bf16), pltpu.SemaphoreType.DMA((slots // BLOCK,))],
+        limit=16,
+    )
+    summed, wv_by3, wo_by2 = lax.optimization_barrier((summed, wv_by3, wo_by2))
     wv_parts = (wv_t, wv_by2, wv_by1, wv_by3)
+    wo_parts = (w_out, wo_by2, wo_by1, swap(wo_by2, "heads", 1))
     full = [pltpu.VMEM((D, D), bf16)]
-    pay = plain(
+    pay, summed = plain(
         project_kernel,
-        shape((slots, D + LANES), bf16),
+        [shape((slots, D + LANES), bf16), shape((HEADS, slots, D), bf16)],
         scal,
         summed,
         extra,
@@ -887,8 +924,6 @@
         smem=1,
         scratch=full,
     )
-    wo_by3 = swap(wo_by2, "heads", 1)
-    wo_parts = (w_out, wo_by2, wo_by1, wo_by3)
     merged = plain(
         merge_kernel, shape(pay.shape, bf16), scal, pay, swap(pay, "heads", 1), smem=1
     )
@@ -926,44 +961,44 @@
         return lax.optimization_barrier(xs)
 
     last = len(over_docs) - 1
+    near_first = over_docs[::-1]
+    score_steps = near_first[:1] + over_docs[:-1]
     part = add(part, swap(part, "heads", 1))
     part, c, summed = tie(part, c, summed)
     part_a, part_b = part, swap(part, "heads", 2)
-    c_all = grow(c, 0)
+    c_far = swap(c, *over_docs[0])
     keep, sent = plain(
         share_kernel, [shape((2, own_heads, slots, D), bf16)] * 2, scal, summed, scale, smem=1
     )
-    part_b, c_all, sent = tie(part_b, c_all, sent)
-    scores, n3, dh3, part = plain(
+    got = swap(sent, "heads", 1)
+    part_b, keep = tie(part_b, keep)
+    scores, n3, dh3 = plain(
         score_kernel,
-        [
-            shape((groups, LANES)),
-            shape((slots, D)),
-            shape((slots, D), bf16),
-            shape((slots, D), bf16),
-        ],
+        [shape((groups, LANES)), shape((slots, D)), shape((slots, D), bf16)],
         scal,
         part_a,
         part_b,
         h2,
-        z,
         g_final,
         score_row,
-        w_down,
-        w_in,
         smem=1,
     )
-    part = add(part, swap(part, "heads", 1))
-    got = swap(sent, "heads", 1)
+    score_far = swap(scores, *score_steps[0])
+    part = plain(down_kernel, shape((slots, D), bf16), dh3, z, w_down, w_in)
+    part_far = swap(part, "heads", 1)
+    part_far, score_far = tie(part_far, score_far)
+    part = add(part, part_far)
     part_a, part_b = part, swap(part, "heads", 2)
-    near_first = [("docs", bit) for bit in bits_of(groups)]
-    score_a, score_b = scores, swap(scores, *near_first[0])
-    part_b, got, score_b = tie(part_b, got, score_b)
+    score_a = scores + score_far
     for k in range(1, last):
-        score_a = score_a + score_b
-        score_b = swap(score_a, *near_first[k])
-    for k in range(1, last):
-        c_all = grow(c_all, k)
+        score_b = swap(score_a, *score_steps[k])
+        if k < last - 1:
+            score_a = score_a + score_b
+    away = plain(
+        away_kernel, shape((own_heads, slots, D), bf16), scal, keep, got, smem=1
+    )
+    other = swap(away, "heads", 2)
+    part_b, score_b, away, c_far = tie(part_b, score_b, away, c_far)
     dh2, grads, dc, dc_own, inner, ff = plain(
         context_kernel,
         [
@@ -986,36 +1021,32 @@
         scratch=full + [pltpu.VMEM((slots, 2 * D), bf16)],
     )
 
-    away = plain(
-        away_kernel, shape((own_heads, slots, D), bf16), scal, keep, got, smem=1
-    )
     score_a = score_a + score_b
-    score_a, c_all, away, dc, grads = tie(score_a, c_all, away, dc, grads)
-    score_b = swap(score_a, *near_first[last])
-    other = swap(away, "heads", 2)
-    grads = grow(grads, 0)
-    c_all = grow(c_all, last)
-
-    dap, vd = gridded(
-        back_kernel,
-        blocks,
-        [scal, group_docs],
-        [
-            (held, None, None),
-            (prob, (BLOCK, ROWS, tokens), step3),
-            (scale, (BLOCK, LANES), step2),
-            (inner, (BLOCK, LANES), step2),
-            (dc, (BLOCK, D), step2),
-        ]
-        + [(w, (width, D), const2) for w in wv_parts],
-        [
-            (shape((slots, 2 * ROWS, tokens), bf16), (BLOCK, 2 * ROWS, tokens), step3),
-            (shape((slots, ROWS, D), bf16), (BLOCK, ROWS, D), step3),
-        ],
-        scratch=full,
-        flops=pass_flops,
-    )
-    dap, score_b, grads, c_all, other = tie(dap, score_b, grads, c_all, other)
+    c_all = jnp.concatenate([c, c_far], axis=0)
+    for k in range(1, last):
+        c_all = grow(c_all, k)
+    score_a, dc, grads, c_all = tie(score_a, dc, grads, c_all)
+    score_b = swap(score_a, *score_steps[last])
+    grads_far = swap(grads, *over_docs[0])
+    c_far = swap(c_all, *over_docs[last])
+
+    outs = [
+        pltpu.VMEM((slots, 2 * ROWS, tokens), bf16),
+        pltpu.VMEM((slots, ROWS, D), bf16),
+    ]
+    rounds = slots // SPAN
+    middle = 1
+    inputs = (scal, group_docs, held, prob, scale, inner, dc)
+    dap, vd, wv_full = plain(
+        functools.partial(back_kernel, 0, middle),
+        outs + [shape((D, D), bf16)],
+        *inputs,
+        *wv_parts,
+        smem=2,
+        flops=pass_flops * middle // rounds,
+        limit=16,
+    )
+    dap, score_b, grads_far, c_far, other = tie(dap, score_b, grads_far, c_far, other)
     all_scores, loss, ds_docs, ds_mine = plain(
         list_kernel,
         [shape((docs,)), shape((1, 1)), shape((1, docs)), shape((8, LANES))],
@@ -1038,96 +1069,109 @@
         ds_mine,
         smem=1,
     )
-    dap, value_part, grads = tie(dap, value_part, grads)
+    dap, value_part = tie(dap, value_part)
     value_far = swap(value_part, *near_first[0])
-    grads_far = swap(grads, *over_docs[1])
-    (sums,) = gridded(
+    c_all = jnp.concatenate([c_all, c_far], axis=0)
+    c_far = swap(c_all, "heads", 1)
+    grads = jnp.concatenate([grads, grads_far], axis=0)
+    for m in range(1, last):
+        grads_far = swap(grads, *over_docs[m])
+        if m < last - 1:
+            grads = jnp.concatenate([grads, grads_far], axis=0)
+    dap, vd = plain(
+        functools.partial(back_kernel, middle, rounds),
+        outs,
+        *inputs,
+        wv_full,
+        dap,
+        vd,
+        smem=2,
+        onto={8: 0, 9: 1},
+        flops=pass_flops * (rounds - middle) // rounds,
+        limit=16,
+    )
+    dap, value_far, grads_far, c_far = tie(dap, value_far, grads_far, c_far)
+    grads = jnp.concatenate([grads, grads_far], axis=0)
+    grads_far = swap(grads, *over_docs[last])
+    for m in range(1, last):
+        value_part = add(value_part, value_far)
+        value_far = swap(value_part, *near_first[m])
+    sums = plain(
         key_sum_kernel,
-        blocks,
-        [scal, group_docs],
-        [
-            (ds_mine, (8, LANES), const2),
-            (held, None, None),
-            (dap, (BLOCK, ROWS, tokens), step3),
-            (dh2, (slots, D), const2),
-            (n3, (slots, D), const2),
-            (ff, (slots, D), const2),
-        ],
-        [(shape((ROWS, D)), (ROWS, D), const2)],
+        shape((ROWS, D)),
+        scal,
+        group_docs,
+        ds_mine,
+        held,
+        dap,
+        dh2,
+        n3,
+        ff,
+        smem=2,
         flops=pass_flops,
     )
-    sums, value_far = tie(sums, value_far)
-    value_part = add(value_part, value_far)
-
-    def enc_grads(base, steps, onto=()):
-        def moved(i, *_):
-            return (i + base, 0, 0)
-
-        return gridded(
-            functools.partial(enc_grad_kernel, base),
-            steps,
-            [scal, group_docs],
-            [
-                (ds_mine, (8, LANES), const2),
-                (qk_a, (ROWS, D), const2),
-                (qk_b, (ROWS, D), const2),
-                (dap, (BLOCK, 2 * ROWS, tokens), moved),
-                (vd, (BLOCK, ROWS, D), moved),
-            ],
-            [(shape(enc_out.shape, bf16), (BLOCK, tokens, D), moved)],
-            flops=pass_flops * steps // blocks,
-            onto=onto,
+
+    def enc_grads(first, last, grads=None):
+        outs = pltpu.HBM(enc_out.shape, bf16)
+        size = 8
+        args = (ds_mine, qk_a, qk_b, dap, vd)
+        return plain(
+            functools.partial(enc_grad_kernel, first, last),
+            outs,
+            *args,
+            *([] if grads is None else [grads]),
+            hbm=() if grads is None else (len(args),),
+            hbm_out=True,
+            onto={} if grads is None else {len(args): 0},
+            flops=pass_flops * (last - first) // slots,
+            scratch=[pltpu.VMEM((4, size, tokens, D), bf16), pltpu.SemaphoreType.DMA((4,))],
+            limit=16,
         )
 
     sums = add(sums, swap(sums, "heads", 1))
-    steps = [over_heads[1]] + near_first
-    share = [2, 2, 2] + [0] * len(steps)
-    enc_grad, done = (), 0
+    steps = over_heads[1:] + near_first[:0:-1] + near_first[:1]
+    enc_grad = None
+    third = slots // 3
     sum_a = sums
-    value_step, grads_step = 1, 1
     for k, step in enumerate(steps):
         sum_b = swap(sum_a, *step)
+        if k < 2 or k == len(steps) - 1:
+            part = min(k, 2)
+            enc_grad = enc_grads(part * third, (part + 1) * third, enc_grad)
+            sum_b, enc_grad = tie(sum_b, enc_grad)
         if k == 1:
-            value_far = swap(value_part, *near_first[1])
-        if share[k]:
-            enc_grad = tuple(enc_grads(done, share[k], enc_grad))
-            done += share[k]
+            sum_b, value_far = tie(sum_b, value_far)
+            value_part = add(value_part, value_far)
+        if k == len(steps) - 2:
+            ready = plain(
+                functools.partial(weights_before_kernel, order, 384),
+                [
+                    shape((docs, D), bf16),
+                    shape((docs, hidden), bf16),
+                    shape((docs, hidden)),
+                    shape((docs, width), bf16),
+                ],
+                scal,
+                group_docs,
+                c_all,
+                c_far,
+                h1,
+                g_ff,
+                *wo_parts,
+                w_in,
+                smem=2,
+                flops=4 * docs * D * hidden,
+                limit=60 if docs > 384 else 16,
+                scratch=full,
+            )
+            sum_b, value_part, *ready = tie(sum_b, value_part, *ready)
+            value_b = swap(value_part, *near_first[last])
+        if k == len(steps) - 1:
+            sum_b, grads_far = tie(sum_b, grads_far)
+            grads = jnp.concatenate([grads, grads_far], axis=0)
+            grads_far = swap(grads, "heads", 1)
         if k < len(steps) - 1:
-            sum_b, *enc_grad = tie(sum_b, *enc_grad)
-            if k >= 2:
-                sum_b, value_far, grads_far = tie(sum_b, value_far, grads_far)
-                value_part = add(value_part, value_far)
-                grads = jnp.concatenate([grads, grads_far], axis=0)
-                if k < last:
-                    value_far = swap(value_part, *near_first[k])
-                    grads_far = swap(grads, *over_docs[k])
             sum_a = sum_a + sum_b
-    (enc_grad,) = enc_grad
-    value_part, sum_b = tie(value_part, sum_b)
-    grads = grow(grads, last)
-    c_all, grads = ((x, swap(x, "heads", 1)) for x in (c_all, grads))
-    value_a, value_b = value_part, swap(value_part, *near_first[last])
-    value_grad = (value_a.astype(f32) + value_b.astype(f32)).T
-
-    w_in_grad, w_down_grad, w_out_grad = plain(
-        functools.partial(weights_kernel, order, 384),
-        [shape((D, hidden)), shape((hidden, D)), shape((width, D))],
-        scal,
-        group_docs,
-        *c_all,
-        *grads,
-        ds_docs,
-        h1,
-        g_ff,
-        *wo_parts,
-        w_in,
-        w_down,
-        smem=2,
-        flops=10 * docs * D * hidden,
-        limit=60 if docs > 384 else 36,
-        scratch=full,
-    )
-
     key_grad, query_grad, part = plain(
         key_kernel,
         [shape((width, D)), shape((width, D)), shape((8, D))],
@@ -1141,7 +1185,23 @@
         smem=1,
     )
     part_a, part_b = sum_last(part, over_heads)
-    part_b, w_in_grad = tie(part_b, w_in_grad)
+    y3, u, slope, c_own = ready
+    w_in_grad, grads_docs = plain(
+        functools.partial(weights_kernel, order, 384),
+        [shape((D, hidden)), shape((docs, 2 * D), bf16)],
+        scal,
+        group_docs,
+        y3,
+        slope,
+        grads,
+        grads_far,
+        ds_docs,
+        w_down,
+        smem=2,
+        flops=4 * docs * D * hidden,
+        limit=60 if docs > 384 else 16,
+    )
+    part_b, w_in_grad, grads_docs = tie(part_b, w_in_grad, grads_docs)
     dh1, wos_grad, wvs_grad, part, cross, final_gain, row_grad, ff_gain = plain(
         hidden_kernel,
         [shape((1, D)), shape((width, D)), shape((width, D)), shape((8, D))] + [shape((D,))] * 4,
@@ -1159,6 +1219,17 @@
         score_row,
     )
     part_a, part_b = sum_last(part, over_heads)
+    w_down_grad, w_out_grad = plain(
+        functools.partial(weights_after_kernel, 384),
+        [shape((hidden, D)), shape((width, D))],
+        u,
+        c_own,
+        grads_docs,
+        flops=4 * docs * D * hidden,
+        limit=60 if docs > 384 else 16,
+    )
+    part_b, w_down_grad, value_b = tie(part_b, w_down_grad, value_b)
+    value_grad = (value_part.astype(f32) + value_b.astype(f32)).T
     self_gain, start_grad = plain(
         start_kernel, [shape((D,))] * 2, part_a, part_b, dh1, start_token, g_self
     )

time: 159 us -> 140 us (0.88)
  waiting for transfers between devices: 65.9 us -> 30 us
  Pallas kernels: 51 us -> 70.6 us
  starting transfers between devices: 39.3 us -> 35.7 us
    ppermute x41, waiting for transfers between devices: 65.9 us -> 30 us  [swap(): return lax.ppermute(x, axis, [(i, i ^ bit) for i in range(size)])]
    pallas_call x24 -> x27, Pallas kernels: 51 us -> 70.6 us  [the longest x25 64.7 us: plain(): pl.pallas_call(kernel, out_shape=outs, in_specs=[whole_spec(space) for sp...]
    ppermute x41, starting transfers between devices: 39.3 us -> 35.7 us  [swap(): return lax.ppermute(x, axis, [(i, i ^ bit) for i in range(size)])]
  transfers between devices with their start and end apart: 41 -> 41, of which waited for: 21 -> 17; matrix products, arithmetic and copies ran while one was open for 1% -> 0% of each run, Pallas kernels for 26% -> 41%
where the time goes in v3:
time: 140 us; the launch traced here: 139 us
  Pallas kernels  70.6 us (50%)
  starting transfers between devices  35.7 us (26%)
  waiting for transfers between devices  30 us (21%)
    pallas_call x25, Pallas kernels, plain(): pl.pallas_call(kernel, out_shape=outs, in_specs=[whole_spec(space) for sp...  64.7 us
    ppermute x41, starting transfers between devices, swap(): return lax.ppermute(x, axis, [(i, i ^ bit) for i in range(size)])  35.7 us
    ppermute x41, waiting for transfers between devices, swap(): return lax.ppermute(x, axis, [(i, i ^ bit) for i in range(size)])  30 us
    pallas_call x2, Pallas kernels, load(): pl.pallas_call(functools.partial(load_kernel, first, last), out_shape=plt...  5.84 us
  transfers between devices with their start and end apart: 41, of which 17 were waited for; matrix products, arithmetic and copies ran while one was open for 0% of the time, Pallas kernels for 41%

profile of v3, /device:TPU:0, one launch (start us, length us, event | category | flops | bytes accessed | tf_op | source)
XLA Modules:
  0.0 139.0 jit_solution(2176241542564822384)
XLA Ops:
  0.7 1.5 %self_kernel.1 = f32[8,768]{1,0:T(8,128)S(1)} custom-call(bf16[768]{0:T(1024)(128)(2,1)} %start.7, f32[768]{0:T(1024)} %g_self.5, bf16[192,768]{1,0:T(8,128)(2,1)} %bitcast.16, bf16[192,768]{1,0:T(8,128)(2,1)} %wos.3), custom_call_target="tpu_custom_call" | custom-call | bytes 594432 | tf_op jit(solution)/shard_map/self_kernel/pallas_call | solution.py:761
  2.6 0.8 collective-permute-done
  3.5 2.9 %collective-permute-start.1 = (f32[8,768]{1,0:T(8,128)S(1)}, f32[8,768]{1,0:T(8,128)S(1)}, u32[]{:S(2)}, u32[]{:S(2)}) collective-permute-start(f32[8,768]{1,0:T(8,128)S(1)} %add.45.since.part_a), channel_id=1, source_target_pairs={{0,2},{1,3},{2,0},{3,1},{4,6},{5,7},{6,4},{7,5},{8,10},{9,11},{10,... | collective-permute-start | bytes 73736 | tf_op jit(solution)/shard_map/ppermute | solution.py:786
  6.4 2.4 %load_kernel.2.refs_0_ = bf16[96,128,768]{2,1,0:T(8,128)(2,1)S(1)} custom-call(bf16[96,128,768]{2,1,0:T(8,128)(2,1)} %enc.5, f32[8,768]{1,0:T(8,128)S(1)} %add.45.since.part_a, s32[2]{0:T(128)S(1)} %pad_add_fusion.scal), custom_call_target="tpu_custom_call" | custom-call | bytes 6291456 | tf_op jit(solution)/shard_map/load_kernel/pallas_call | solution.py:852
  8.9 1.3 collective-permute-start.4
  10.2 1.5 %query_kernel.1 = (f32[16,768]{1,0:T(8,128)S(1)}, f32[1,768]{1,0:T(1,128)S(1)}) custom-call(s32[2]{0:T(128)S(1)} %pad_add_fusion.scal, f32[8,768]{1,0:T(8,128)S(1)} %add.45.since.part_a, f32[8,768]{1,0:T(8,128)S(1)} %collective-permute-done.1.part_b, bf16[768]{0:T(1024)(128)(2,1)} %start.7, f32[768]{0:T(1024)} %g_cross.5, bf16[192,768]{1,0:T(8,128)(2,1)} %bitcast.12, ...), custom_call_target="tpu_custom_call" | custom-call | bytes 643592 | tf_op jit(solution)/shard_map/query_kernel/pallas_call | solution.py:761
  11.7 1.2 collective-permute-done.2
  13.0 0.9 collective-permute-start.3
  13.9 3.4 %load_kernel.3._ = bf16[96,128,768]{2,1,0:T(8,128)(2,1)S(1)} custom-call(bf16[96,128,768]{2,1,0:T(8,128)(2,1)} %enc.5, f32[16,768]{1,0:T(8,128)S(1)} %add.46.since.qa, s32[2]{0:T(128)S(1)} %pad_add_fusion.scal, bf16[96,128,768]{2,1,0:T(8,128)(2,1)S(1)} %load_kernel.2.refs_0_), custom_call_target="tpu_custom_call", output_to_operand_aliasing={{}: (3, {})} | custom-call | bytes 12582912 | tf_op jit(solution)/shard_map/load_kernel/pallas_call | solution.py:852
  17.3 1.5 %collective-permute-done.3.qb = f32[16,768]{1,0:T(8,128)S(1)} collective-permute-done((f32[16,768]{1,0:T(8,128)S(1)}, f32[16,768]{1,0:T(8,128)S(1)}, u32[]{:S(2)}, u32[]{:S(2)}) %collective-permute-start.3) | collective-permute-done | bytes 49184 | tf_op jit(solution)/shard_map/ppermute | solution.py:786
  19.2 8.7 %attend_kernel.1 = (bf16[96,128,768]{2,1,0:T(8,128)(2,1)S(1)}, f32[96,16,128]{2,1,0:T(8,128)S(1)}, f32[6,1536,128]{2,1,0:T(8,128)S(1)}, bf16[96,128]{1,0:T(8,128)(2,1)S(1)}) custom-call(s32[2]{0:T(128)S(1)} %pad_add_fusion.scal, s32[8]{0:T(128)S(1)} %copy-done.12, s32[384]{0:T(512)S(1)} %copy-done.15, ...), custom_call_target="tpu_custom_call", output_to_operand_aliasing={{0}: (6, {})} | custom-call | flops 9663676416 | bytes 18974248 | tf_op jit(solution)/shard_map/attend_kernel/pallas_call | solution.py:761
  28.2 1.8 %project_kernel.1 = (bf16[96,896]{1,0:T(8,128)(2,1)S(1)}, bf16[12,96,768]{2,1,0:T(8,128)(2,1)S(1)}) custom-call(s32[2]{0:T(128)S(1)} %pad_add_fusion.scal, f32[6,1536,128]{2,1,0:T(8,128)S(1)} %get-tuple-element.142.summed, bf16[96,128]{1,0:T(8,128)(2,1)S(1)} %get-tuple-element.143.extra, bf16[192,768]{1,0:T(8,128)(2,1)S(1)} %bitcast.20, ...), custom_call_target="tpu_custom_call" | custom-call | bytes 5922824 | tf_op jit(solution)/shard_map/project_kernel/pallas_call | solution.py:761
  30.7 0.8 collective-permute-done.8.other
  31.6 1.3 merge_kernel.1.own
  32.8 1.5 %collective-permute-start.9 = (bf16[96,896]{1,0:T(8,128)(2,1)S(1)}, bf16[96,896]{1,0:T(8,128)(2,1)S(1)}, u32[]{:S(2)}, u32[]{:S(2)}) collective-permute-start(bf16[96,896]{1,0:T(8,128)(2,1)S(1)} %merge_kernel.1.own), channel_id=1, source_target_pairs={{0,2},{1,3},{2,0},{3,1},{4,6},{5,7},{6,4},{7,5},{8,10},{9,11},{10,... | collective-permute-start | bytes 516104 | tf_op jit(solution)/shard_map/ppermute | solution.py:786
  34.4 5.0 %collective-permute-done.9.other = bf16[96,896]{1,0:T(8,128)(2,1)S(1)} collective-permute-done((bf16[96,896]{1,0:T(8,128)(2,1)S(1)}, bf16[96,896]{1,0:T(8,128)(2,1)S(1)}, u32[]{:S(2)}, u32[]{:S(2)}) %collective-permute-start.9) | collective-permute-done | bytes 172064 | tf_op jit(solution)/shard_map/ppermute | solution.py:786
  39.3 2.4 %forward_kernel.1 = (bf16[48,768]{1,0:T(8,128)(2,1)S(1)}, f32[96,768]{1,0:T(8,128)S(1)}, f32[96,128]{1,0:T(8,128)S(1)}, f32[96,768]{1,0:T(8,128)S(1)}, f32[96,76...) custom-call(s32[2]{0:T(128)S(1)} %pad_add_fusion.scal, bf16[96,896]{1,0:T(8,128)(2,1)S(1)} %merge_kernel.1.own, ...), custom_call_target="tpu_custom_call" | custom-call | bytes 4061192 | tf_op jit(solution)/shard_map/forward_kernel/pallas_call | solution.py:761
  41.9 1.4 collective-permute-done.12
  43.3 0.9 share_kernel.1
  44.4 1.5 %collective-permute-start.13 = (bf16[96,768]{1,0:T(8,128)(2,1)S(1)}, bf16[96,768]{1,0:T(8,128)(2,1)S(1)}, u32[]{:S(2)}, u32[]{:S(2)}) collective-permute-start(bf16[96,768]{1,0:T(8,128)(2,1)S(1)} %add_convert_fusion.3.part_a), channel_id=1, source_target_pairs={{0,2},{1,3},{2,0},{3,1},{4,6},{5,7},{6,4},{7,5},{8,10},{9,11},{10,... | collective-permute-start | bytes 442376 | tf_op jit(solution)/shard_map/ppermute | solution.py:786
  45.9 4.6 %collective-permute-done.13.part_b = bf16[96,768]{1,0:T(8,128)(2,1)S(1)} collective-permute-done((bf16[96,768]{1,0:T(8,128)(2,1)S(1)}, bf16[96,768]{1,0:T(8,128)(2,1)S(1)}, u32[]{:S(2)}, u32[]{:S(2)}) %collective-permute-start.13) | collective-permute-done | bytes 147488 | tf_op jit(solution)/shard_map/ppermute | solution.py:786
  50.5 1.0 score_kernel.1
  51.5 0.9 down_kernel.1
  52.6 1.5 %collective-permute-start.15 = (f32[8,128]{1,0:T(8,128)S(1)}, f32[8,128]{1,0:T(8,128)S(1)}, u32[]{:S(2)}, u32[]{:S(2)}) collective-permute-start(f32[8,128]{1,0:T(8,128)S(1)} %get-tuple-element.157), channel_id=1, source_target_pairs={{0,4},{4,0},{8,12},{12,8},{16,20},{20,16},{24,28},{28,24},{1,5},{5... | collective-permute-start | bytes 12296 | tf_op jit(solution)/shard_map/ppermute | solution.py:786
  54.1 2.1 %collective-permute-done.15 = f32[8,128]{1,0:T(8,128)S(1)} collective-permute-done((f32[8,128]{1,0:T(8,128)S(1)}, f32[8,128]{1,0:T(8,128)S(1)}, u32[]{:S(2)}, u32[]{:S(2)}) %collective-permute-start.15) | collective-permute-done | bytes 4128 | tf_op jit(solution)/shard_map/ppermute | solution.py:786
  56.3 1.6 %collective-permute-start.16 = (bf16[96,768]{1,0:T(8,128)(2,1)S(1)}, bf16[96,768]{1,0:T(8,128)(2,1)S(1)}, u32[]{:S(2)}, u32[]{:S(2)}) collective-permute-start(bf16[96,768]{1,0:T(8,128)(2,1)S(1)} %add_convert_fusion.2.part_a), channel_id=1, source_target_pairs={{0,2},{1,3},{2,0},{3,1},{4,6},{5,7},{6,4},{7,5},{8,10},{9,11},{10,... | collective-permute-start | bytes 442376 | tf_op jit(solution)/shard_map/ppermute | solution.py:786
  57.8 2.6 %collective-permute-start.19 = (bf16[48,768]{1,0:T(8,128)(2,1)S(1)}, bf16[48,768]{1,0:T(8,128)(2,1)S(1)}, u32[]{:S(2)}, u32[]{:S(2)}) collective-permute-start(bf16[48,768]{1,0:T(8,128)(2,1)S(1)} %get-tuple-element.164), channel_id=1, source_target_pairs={{0,16},{4,20},{8,24},{12,28},{16,0},{20,4},{24,8},{28,12},{1,17},{... | collective-permute-start | bytes 221192 | tf_op jit(solution)/shard_map/ppermute | solution.py:786
  61.4 2.5 %collective-permute-done.19 = bf16[48,768]{1,0:T(8,128)(2,1)S(1)} collective-permute-done((bf16[48,768]{1,0:T(8,128)(2,1)S(1)}, bf16[48,768]{1,0:T(8,128)(2,1)S(1)}, u32[]{:S(2)}, u32[]{:S(2)}) %collective-permute-start.19) | collective-permute-done | bytes 73760 | tf_op jit(solution)/shard_map/ppermute | solution.py:786
  64.0 1.0 collective-permute-done.17
  65.0 0.7 collective-permute-start.20
  65.6 1.5 %collective-permute-start.24 = (bf16[3,96,768]{2,1,0:T(8,128)(2,1)S(1)}, bf16[3,96,768]{2,1,0:T(8,128)(2,1)S(1)}, u32[]{:S(2)}, u32[]{:S(2)}) collective-permute-start(bf16[3,96,768]{2,1,0:T(8,128)(2,1)S(1)} %away_kernel.1), channel_id=1, source_target_pairs={{0,2},{1,3},{2,0},{3,1},{4,6},{5,7},{6,4},{7,5},{8,10},{9,11},{10,... | collective-permute-start | bytes 1327112 | tf_op jit(solution)/shard_map/ppermute | solution.py:786
  67.1 1.6 %context_kernel.1 = (bf16[96,768]{1,0:T(8,128)(2,1)S(1)}, bf16[48,1536]{1,0:T(8,128)(2,1)S(1)}, bf16[96,768]{1,0:T(8,128)(2,1)S(1)}, bf16[96,192]{1,0:T(8,128)(2...) custom-call(s32[2]{0:T(128)S(1)} %pad_add_fusion.scal, bf16[96,768]{1,0:T(8,128)(2,1)S(1)} %add_convert_fusion.2.part_a, ...), custom_call_target="tpu_custom_call" | custom-call | bytes 2214920 | tf_op jit(solution)/shard_map/context_kernel/pallas_call | solution.py:761
  68.7 1.5 %collective-permute-done.20 = bf16[96,768]{1,0:T(8,128)(2,1)S(1)} collective-permute-done((bf16[96,768]{1,0:T(8,128)(2,1)S(1)}, bf16[96,768]{1,0:T(8,128)(2,1)S(1)}, u32[]{:S(2)}, u32[]{:S(2)}) %collective-permute-start.20) | collective-permute-done | bytes 147488 | tf_op jit(solution)/shard_map/ppermute | solution.py:786
  70.2 0.8 collective-permute-start.22
  71.0 0.8 collective-permute-start.23
  71.8 2.1 %collective-permute-start.21 = (f32[8,128]{1,0:T(8,128)S(1)}, f32[8,128]{1,0:T(8,128)S(1)}, u32[]{:S(2)}, u32[]{:S(2)}) collective-permute-start(f32[8,128]{1,0:T(8,128)S(1)} %add.50.sc_a), channel_id=1, source_target_pairs={{0,8},{4,12},{8,0},{12,4},{16,24},{20,28},{24,16},{28,20},{1,9},{5... | collective-permute-start | bytes 12296 | tf_op jit(solution)/shard_map/ppermute | solution.py:786
  73.9 3.6 %back_kernel.2 = (bf16[96,32,128]{2,1,0:T(8,128)(2,1)S(1)}, bf16[96,16,768]{2,1,0:T(8,128)(2,1)S(1)}, bf16[768,768]{1,0:T(8,128)(2,1)S(1)}) custom-call(s32[2]{0:T(128)S(1)} %pad_add_fusion.scal, s32[8]{0:T(128)S(1)} %copy-done.12, bf16[96,128,768]{2,1,0:T(8,128)(2,1)S(1)} %get-tuple-element.172.enc, f32[96,16,128]{2,1,0:T(8,128)S(1)} %get-tuple-element.173.p, ...), custom_call_target="tpu_custom_call" | custom-call | flops 1610612736 | bytes 21086248 | tf_op jit(solution)/shard_map/back_kernel/pallas_call | solution.py:761
  77.9 1.6 %list_kernel.1 = (f32[384]{0:T(512)}, f32[1,1]{1,0:T(1,128)}, f32[1,384]{1,0:T(1,128)S(1)}, f32[8,128]{1,0:T(8,128)S(1)}) custom-call(s32[2]{0:T(128)S(1)} %pad_add_fusion.scal, s32[8]{0:T(128)S(1)} %copy-done.12, s32[24]{0:T(128)S(1)} %copy-done.16, f32[8,128]{1,0:T(8,128)S(1)} %add.50.sc_a, f32[8,128]{1,0:T(8,128)S(1)} %collective-permute-done.21.sc_b, f32[384]{0:T(512)} %rel.1), custom_call_target="tpu_custom_call" | custom-call | bytes 9864 | tf_op jit(solution)/shard_map/list_kernel/pallas_call | solution.py:761
  79.5 1.0 value_kernel.1
  80.5 0.7 collective-permute-start.25
  81.3 2.1 %collective-permute-start.26 = (bf16[96,1536]{1,0:T(8,128)(2,1)S(1)}, bf16[96,1536]{1,0:T(8,128)(2,1)S(1)}, u32[]{:S(2)}, u32[]{:S(2)}) collective-permute-start(bf16[96,1536]{1,0:T(8,128)(2,1)S(1)} %pad_maximum_fusion.2), channel_id=1, source_target_pairs={{0,8},{4,12},{8,0},{12,4},{16,24},{20,28},{24,16},{28,20},{1,9},{5... | collective-permute-start | bytes 884744 | tf_op jit(solution)/shard_map/ppermute | solution.py:786
  83.4 6.2 %back_kernel.3 = (bf16[96,32,128]{2,1,0:T(8,128)(2,1)S(1)}, bf16[96,16,768]{2,1,0:T(8,128)(2,1)S(1)}) custom-call(s32[2]{0:T(128)S(1)} %pad_add_fusion.scal, s32[8]{0:T(128)S(1)} %copy-done.12, bf16[96,128,768]{2,1,0:T(8,128)(2,1)S(1)} %get-tuple-element.172.enc, ...), custom_call_target="tpu_custom_call", output_to_operand_aliasing={{0}: (8, {}), {1}: (9, {})} | custom-call | flops 3221225472 | bytes 24231976 | tf_op jit(solution)/shard_map/back_kernel/pallas_call | solution.py:761
  89.6 1.5 %collective-permute-done.26 = bf16[96,1536]{1,0:T(8,128)(2,1)S(1)} collective-permute-done((bf16[96,1536]{1,0:T(8,128)(2,1)S(1)}, bf16[96,1536]{1,0:T(8,128)(2,1)S(1)}, u32[]{:S(2)}, u32[]{:S(2)}) %collective-permute-start.26) | collective-permute-done | bytes 294944 | tf_op jit(solution)/shard_map/ppermute | solution.py:786
  91.1 4.0 %key_sum_kernel.1 = f32[16,768]{1,0:T(8,128)S(1)} custom-call(s32[2]{0:T(128)S(1)} %pad_add_fusion.scal, s32[8]{0:T(128)S(1)} %copy-done.12, f32[8,128]{1,0:T(8,128)S(1)} %get-tuple-element.182.ds, bf16[96,128,768]{2,1,0:T(8,128)(2,1)S(1)} %get-tuple-element.172.enc, bf16[96,32,128]{2,1,0:T(8,128)(2,1)S(1)} %get-tuple-element.193.dap, ...), custom_call_target="tpu_custom_call" | custom-call | flops 4831838208 | bytes 20402216 | tf_op jit(solution)/shard_map/key_sum_kernel/pallas_call | solution.py:761
  95.1 0.8 collective-permute-start.31
  96.1 3.4 %enc_grad_kernel.3.refs_0_ = bf16[96,128,768]{2,1,0:T(8,128)(2,1)} custom-call(f32[8,128]{1,0:T(8,128)S(1)} %get-tuple-element.182.ds, f32[16,768]{1,0:T(8,128)S(1)} %add.46.since.qa, f32[16,768]{1,0:T(8,128)S(1)} %collective-permute-done.3.qb, bf16[96,32,128]{2,1,0:T(8,128)(2,1)S(1)} %get-tuple-element.193.dap, bf16[96,16,768]{2,1,0:T(8,128)(2,1)S(1)} %get-tuple-element.197.vd), custom_call_target="tpu_custom_call" | custom-call | flops 1610612736 | bytes 3248128 | tf_op jit(solution)/shard_map/enc_grad_kernel/pallas_call | solution.py:761
  99.5 1.6 %collective-permute-start.29 = (f32[16,768]{1,0:T(8,128)S(1)}, f32[16,768]{1,0:T(8,128)S(1)}, u32[]{:S(2)}, u32[]{:S(2)}) collective-permute-start(f32[16,768]{1,0:T(8,128)S(1)} %add.51), channel_id=1, source_target_pairs={{0,2},{1,3},{2,0},{3,1},{4,6},{5,7},{6,4},{7,5},{8,10},{9,11},{10,... | collective-permute-start | bytes 147464 | tf_op jit(solution)/shard_map/ppermute | solution.py:786
  101.1 3.4 %weights_before_kernel.1 = (bf16[384,768]{1,0:T(8,128)(2,1)S(1)}, bf16[384,768]{1,0:T(8,128)(2,1)S(1)}, f32[384,768]{1,0:T(8,128)S(1)}, bf16[384,192]{1,0:T(8,128)(2,1)S(1)}) custom-call(s32[2]{0:T(128)S(1)} %pad_add_fusion.scal, s32[8]{0:T(128)S(1)} %copy-done.12, bf16[384,768]{1,0:T(8,128)(2,1)S(1)} %constant_dynamic-update-slice_fusion.c_own, ...), custom_call_target="tpu_custom_call" | custom-call | flops 905969664 | bytes 3545128 | tf_op jit(solution)/shard_map/weights_before_kernel/pallas_call | solution.py:761
  104.6 2.9 %collective-permute-start.30 = (f32[16,768]{1,0:T(8,128)S(1)}, f32[16,768]{1,0:T(8,128)S(1)}, u32[]{:S(2)}, u32[]{:S(2)}) collective-permute-start(f32[16,768]{1,0:T(8,128)S(1)} %add.52), channel_id=1, source_target_pairs={{0,16},{4,20},{8,24},{12,28},{16,0},{20,4},{24,8},{28,12},{1,17},{... | collective-permute-start | bytes 147464 | tf_op jit(solution)/shard_map/ppermute | solution.py:786
  107.4 3.4 %enc_grad_kernel.4.refs_0_ = bf16[96,128,768]{2,1,0:T(8,128)(2,1)} custom-call(f32[8,128]{1,0:T(8,128)S(1)} %get-tuple-element.182.ds, f32[16,768]{1,0:T(8,128)S(1)} %add.46.since.qa, f32[16,768]{1,0:T(8,128)S(1)} %collective-permute-done.3.qb, bf16[96,32,128]{2,1,0:T(8,128)(2,1)S(1)} %get-tuple-element.193.dap, ...), custom_call_target="tpu_custom_call", output_to_operand_aliasing={{}: (5, {})} | custom-call | flops 1610612736 | bytes 3248128 | tf_op jit(solution)/shard_map/enc_grad_kernel/pallas_call | solution.py:761
  110.8 0.8 collective-permute-start.32
  111.7 3.3 %collective-permute-done.32 = f32[16,768]{1,0:T(8,128)S(1)} collective-permute-done((f32[16,768]{1,0:T(8,128)S(1)}, f32[16,768]{1,0:T(8,128)S(1)}, u32[]{:S(2)}, u32[]{:S(2)}) %collective-permute-start.32) | collective-permute-done | bytes 49184 | tf_op jit(solution)/shard_map/ppermute | solution.py:786
  115.0 0.9 collective-permute-start.33
  115.9 3.4 %enc_grad_kernel.5 = bf16[96,128,768]{2,1,0:T(8,128)(2,1)} custom-call(f32[8,128]{1,0:T(8,128)S(1)} %get-tuple-element.182.ds, f32[16,768]{1,0:T(8,128)S(1)} %add.46.since.qa, f32[16,768]{1,0:T(8,128)S(1)} %collective-permute-done.3.qb, bf16[96,32,128]{2,1,0:T(8,128)(2,1)S(1)} %get-tuple-element.193.dap, ...), custom_call_target="tpu_custom_call", output_to_operand_aliasing={{}: (5, {})} | custom-call | flops 1610612736 | bytes 3248128 | tf_op jit(solution)/shard_map/enc_grad_kernel/pallas_call | solution.py:761
  119.4 1.6 %collective-permute-start.40 = (bf16[192,768]{1,0:T(8,128)(2,1)S(1)}, bf16[192,768]{1,0:T(8,128)(2,1)S(1)}, u32[]{:S(2)}, u32[]{:S(2)}) collective-permute-start(bf16[192,768]{1,0:T(8,128)(2,1)S(1)} %add_convert_fusion), channel_id=1, source_target_pairs={{0,16},{4,20},{8,24},{12,28},{16,0},{20,4},{24,8},{28,12},{1,17},{... | collective-permute-start | bytes 884744 | tf_op jit(solution)/shard_map/ppermute | solution.py:786
  121.1 2.1 %key_kernel.1 = (f32[192,768]{1,0:T(8,128)}, f32[192,768]{1,0:T(8,128)}, f32[8,768]{1,0:T(8,128)S(1)}) custom-call(s32[2]{0:T(128)S(1)} %pad_add_fusion.scal, f32[16,768]{1,0:T(8,128)S(1)} %add.56.sum_a, f32[16,768]{1,0:T(8,128)S(1)} %collective-permute-done.33.sum_b, f32[1,768]{1,0:T(1,128)S(1)} %get-tuple-element.146.h1, f32[768]{0:T(1024)S(1)} %copy-done.9, ...), custom_call_target="tpu_custom_call" | custom-call | bytes 694280 | tf_op jit(solution)/shard_map/key_kernel/pallas_call | solution.py:761
  123.4 1.0 collective-permute-done.35
  125.0 5.1 %weights_kernel.1 = (f32[768,768]{1,0:T(8,128)}, bf16[384,1536]{1,0:T(8,128)(2,1)S(1)}) custom-call(s32[2]{0:T(128)S(1)} %pad_add_fusion.scal, s32[8]{0:T(128)S(1)} %copy-done.12, bf16[384,768]{1,0:T(8,128)(2,1)S(1)} %get-tuple-element.216.y3, f32[384,768]{1,0:T(8,128)S(1)} %get-tuple-element.217.slope, ...), custom_call_target="tpu_custom_call" | custom-call | flops 905969664 | bytes 5309992 | tf_op jit(solution)/shard_map/weights_kernel/pallas_call | solution.py:761
  130.2 1.9 %hidden_kernel.1 = (f32[1,768]{1,0:T(1,128)S(1)}, f32[192,768]{1,0:T(8,128)}, f32[192,768]{1,0:T(8,128)}, f32[8,768]{1,0:T(8,128)S(1)}, f32[768]{0:T(1024)}, /*i...) custom-call(f32[8,768]{1,0:T(8,128)S(1)} %add.57.part_a, f32[8,768]{1,0:T(8,128)S(1)} %collective-permute-done.36.part_b, ...), custom_call_target="tpu_custom_call" | custom-call | bytes 752640 | tf_op jit(solution)/shard_map/hidden_kernel/pallas_call | solution.py:761
  132.1 1.2 collective-permute-done.38
  133.3 1.4 %collective-permute-start.39 = (f32[8,768]{1,0:T(8,128)S(1)}, f32[8,768]{1,0:T(8,128)S(1)}, u32[]{:S(2)}, u32[]{:S(2)}) collective-permute-start(f32[8,768]{1,0:T(8,128)S(1)} %add.58.part_a), channel_id=1, source_target_pairs={{0,2},{1,3},{2,0},{3,1},{4,6},{5,7},{6,4},{7,5},{8,10},{9,11},{10,... | collective-permute-start | bytes 73736 | tf_op jit(solution)/shard_map/ppermute | solution.py:786
  134.7 2.6 %weights_after_kernel.1 = (f32[768,768]{1,0:T(8,128)}, f32[192,768]{1,0:T(8,128)}) custom-call(bf16[384,768]{1,0:T(8,128)(2,1)S(1)} %get-tuple-element.224.u, bf16[384,192]{1,0:T(8,128)(2,1)S(1)} %get-tuple-element.225.c, bf16[384,1536]{1,0:T(8,128)(2,1)S(1)} %get-tuple-element.226.grads), custom_call_target="tpu_custom_call" | custom-call | flops 905969664 | bytes 1916928 | tf_op jit(solution)/shard_map/weights_after_kernel/pallas_call | solution.py:761
  137.3 0.9 add_bitcast_fusion
  138.2 0.8 start_kernel.1
  (105 shorter events, 5.2 us)
Async XLA Ops:
  2.2 1.3 collective-permute-start
  3.5 5.4 %collective-permute-start.1 = (f32[8,768]{1,0:T(8,128)S(1)}, f32[8,768]{1,0:T(8,128)S(1)}, u32[]{:S(2)}, u32[]{:S(2)}) collective-permute-start(f32[8,768]{1,0:T(8,128)S(1)} %add.45.since.part_a), channel_id=1, source_target_pairs={{0,2},{1,3},{2,0},{3,1},{4,6},{5,7},{6,4},{7,5},{8,10},{9,11},{10,... | collective-permute-start | bytes 73736 | tf_op jit(solution)/shard_map/ppermute | solution.py:786
  6.4 2.5 %copy-start.7 = (bf16[768,192]{0,1:T(8,128)(2,1)S(1)}, bf16[768,192]{0,1:T(8,128)(2,1)}, u32[]{:S(2)}) copy-start(bf16[768,192]{0,1:T(8,128)(2,1)} %param.32) | copy-start | bytes 884740
  8.9 9.9 %collective-permute-start.4 = (bf16[192,768]{1,0:T(8,128)(2,1)S(1)}, bf16[192,768]{1,0:T(8,128)(2,1)S(1)}, u32[]{:S(2)}, u32[]{:S(2)}) collective-permute-start(bf16[192,768]{1,0:T(8,128)(2,1)S(1)} %bitcast.18), channel_id=1, source_target_pairs={{0,2},{1,3},{2,0},{3,1},{4,6},{5,7},{6,4},{7,5},{8,10},{9,11},{10,... | collective-permute-start | bytes 884744 | tf_op jit(solution)/shard_map/ppermute | solution.py:786
  11.7 1.3 collective-permute-start.2
  13.0 5.8 %copy-start.2 = (bf16[192,768]{1,0:T(8,128)(2,1)S(1)}, bf16[192,768]{1,0:T(8,128)(2,1)}, u32[]{:S(2)}) copy-start(bf16[192,768]{1,0:T(8,128)(2,1)} %wo_own.5) | copy-start | bytes 884740
  13.0 6.3 %copy-start.12 = (s32[8]{0:T(128)S(1)}, s32[8]{0:T(128)}, u32[]{:S(2)}) copy-start(s32[8]{0:T(128)} %sizes.13) | copy-start | bytes 100
  13.0 6.2 %copy-start.15 = (s32[384]{0:T(512)S(1)}, s32[384]{0:T(512)}, u32[]{:S(2)}) copy-start(s32[384]{0:T(512)} %lengths.1) | copy-start | bytes 4612
  13.0 5.8 %collective-permute-start.3 = (f32[16,768]{1,0:T(8,128)S(1)}, f32[16,768]{1,0:T(8,128)S(1)}, u32[]{:S(2)}, u32[]{:S(2)}) collective-permute-start(f32[16,768]{1,0:T(8,128)S(1)} %add.46.since.qa), channel_id=1, source_target_pairs={{0,2},{1,3},{2,0},{3,1},{4,6},{5,7},{6,4},{7,5},{8,10},{9,11},{10,... | collective-permute-start | bytes 147464 | tf_op jit(solution)/shard_map/ppermute | solution.py:786
  13.9 14.4 %collective-permute-start.7 = (bf16[192,768]{1,0:T(8,128)(2,1)S(1)}, bf16[192,768]{1,0:T(8,128)(2,1)S(1)}, u32[]{:S(2)}, u32[]{:S(2)}) collective-permute-start(bf16[192,768]{1,0:T(8,128)(2,1)S(1)} %bitcast.19), channel_id=1, source_target_pairs={{0,1},{1,0},{2,3},{3,2},{4,5},{5,4},{6,7},{7,6},{8,9},{9,8},{10,11... | collective-permute-start | bytes 884744 | tf_op jit(solution)/shard_map/ppermute | solution.py:786
  18.8 9.2 %collective-permute-start.5 = (bf16[192,768]{1,0:T(8,128)(2,1)S(1)}, bf16[192,768]{1,0:T(8,128)(2,1)S(1)}, u32[]{:S(2)}, u32[]{:S(2)}) collective-permute-start(bf16[192,768]{1,0:T(8,128)(2,1)S(1)} %collective-permute-done.4.by2.refs_1_), channel_id=1, source_target_pairs={{0,1},{1,0},{2,3},{3,2},{4,5},{5,4},{6,7},{7,6},{8,9},{9,8},{10,11... | collective-permute-start | bytes 884744 | tf_op jit(solution)/shard_map/ppermute | solution.py:786
  18.8 9.4 %collective-permute-start.6 = (bf16[192,768]{1,0:T(8,128)(2,1)S(1)}, bf16[192,768]{1,0:T(8,128)(2,1)S(1)}, u32[]{:S(2)}, u32[]{:S(2)}) collective-permute-start(bf16[192,768]{1,0:T(8,128)(2,1)S(1)} %copy-done.2), channel_id=1, source_target_pairs={{0,2},{1,3},{2,0},{3,1},{4,6},{5,7},{6,4},{7,5},{8,10},{9,11},{10,... | collective-permute-start | bytes 884744 | tf_op jit(solution)/shard_map/ppermute | solution.py:786
  28.2 11.1 %copy-start = (bf16[768,768]{1,0:T(8,128)(2,1)S(1)}, bf16[768,768]{1,0:T(8,128)(2,1)}, u32[]{:S(2)}) copy-start(bf16[768,768]{1,0:T(8,128)(2,1)} %win.5) | copy-start | bytes 3538948
  28.2 11.1 %copy-start.1 = (bf16[768,768]{1,0:T(8,128)(2,1)S(1)}, bf16[768,768]{1,0:T(8,128)(2,1)}, u32[]{:S(2)}) copy-start(bf16[768,768]{1,0:T(8,128)(2,1)} %wdown.5) | copy-start | bytes 3538948
  28.2 11.1 %copy-start.8 = (f32[768]{0:T(1024)S(1)}, f32[768]{0:T(1024)}, u32[]{:S(2)}) copy-start(f32[768]{0:T(1024)} %g_ff.5) | copy-start | bytes 9220
  30.1 1.5 %collective-permute-start.8 = (bf16[96,896]{1,0:T(8,128)(2,1)S(1)}, bf16[96,896]{1,0:T(8,128)(2,1)S(1)}, u32[]{:S(2)}, u32[]{:S(2)}) collective-permute-start(bf16[96,896]{1,0:T(8,128)(2,1)S(1)} %get-tuple-element.145.own.first), channel_id=1, source_target_pairs={{0,1},{1,0},{2,3},{3,2},{4,5},{5,4},{6,7},{7,6},{8,9},{9,8},{10,11... | collective-permute-start | bytes 516104 | tf_op jit(solution)/shard_map/ppermute | solution.py:786
  30.2 4.2 %collective-permute-start.10 = (bf16[192,768]{1,0:T(8,128)(2,1)S(1)}, bf16[192,768]{1,0:T(8,128)(2,1)S(1)}, u32[]{:S(2)}, u32[]{:S(2)}) collective-permute-start(bf16[192,768]{1,0:T(8,128)(2,1)S(1)} %copy-done.2), channel_id=1, source_target_pairs={{0,1},{1,0},{2,3},{3,2},{4,5},{5,4},{6,7},{7,6},{8,9},{9,8},{10,11... | collective-permute-start | bytes 884744 | tf_op jit(solution)/shard_map/ppermute | solution.py:786
  30.7 3.7 %collective-permute-start.11 = (bf16[192,768]{1,0:T(8,128)(2,1)S(1)}, bf16[192,768]{1,0:T(8,128)(2,1)S(1)}, u32[]{:S(2)}, u32[]{:S(2)}) collective-permute-start(bf16[192,768]{1,0:T(8,128)(2,1)S(1)} %collective-permute-done.6.wo_by2), channel_id=1, source_target_pairs={{0,1},{1,0},{2,3},{3,2},{4,5},{5,4},{6,7},{7,6},{8,9},{9,8},{10,11... | collective-permute-start | bytes 884744 | tf_op jit(solution)/shard_map/ppermute | solution.py:786
  32.8 6.5 %collective-permute-start.9 = (bf16[96,896]{1,0:T(8,128)(2,1)S(1)}, bf16[96,896]{1,0:T(8,128)(2,1)S(1)}, u32[]{:S(2)}, u32[]{:S(2)}) collective-permute-start(bf16[96,896]{1,0:T(8,128)(2,1)S(1)} %merge_kernel.1.own), channel_id=1, source_target_pairs={{0,2},{1,3},{2,0},{3,1},{4,6},{5,7},{6,4},{7,5},{8,10},{9,11},{10,... | collective-permute-start | bytes 516104 | tf_op jit(solution)/shard_map/ppermute | solution.py:786
  41.8 8.8 %copy-start.13 = (f32[768]{0:T(1024)S(1)}, f32[768]{0:T(1024)}, u32[]{:S(2)}) copy-start(f32[768]{0:T(1024)} %g_final.3) | copy-start | bytes 9220
  41.8 8.7 %copy-start.14 = (bf16[768]{0:T(1024)(128)(2,1)S(1)}, bf16[768]{0:T(1024)(128)(2,1)}, u32[]{:S(2)}) copy-start(bf16[768]{0:T(1024)(128)(2,1)} %row.3) | copy-start | bytes 4612
  41.8 1.4 %collective-permute-start.12 = (bf16[96,768]{1,0:T(8,128)(2,1)S(1)}, bf16[96,768]{1,0:T(8,128)(2,1)S(1)}, u32[]{:S(2)}, u32[]{:S(2)}) collective-permute-start(bf16[96,768]{1,0:T(8,128)(2,1)S(1)} %get-tuple-element.148), channel_id=1, source_target_pairs={{0,1},{1,0},{2,3},{3,2},{4,5},{5,4},{6,7},{7,6},{8,9},{9,8},{10,11... | collective-permute-start | bytes 442376 | tf_op jit(solution)/shard_map/ppermute | solution.py:786
  44.2 16.6 %collective-permute-start.18 = (bf16[2,3,96,768]{3,2,1,0:T(8,128)(2,1)S(1)}, bf16[2,3,96,768]{3,2,1,0:T(8,128)(2,1)S(1)}, u32[]{:S(2)}, u32[]{:S(2)}) collective-permute-start(bf16[2,3,96,768]{3,2,1,0:T(8,128)(2,1)S(1)} %get-tuple-element.163), channel_id=1, source_target_pairs={{0,1},{1,0},{2,3},{3,2},{4,5},{5,4},{6,7},{7,6},{8,9},{9,8},{10,11... | collective-permute-start | bytes 2654216 | tf_op jit(solution)/shard_map/ppermute | solution.py:786
  44.4 6.1 %collective-permute-start.13 = (bf16[96,768]{1,0:T(8,128)(2,1)S(1)}, bf16[96,768]{1,0:T(8,128)(2,1)S(1)}, u32[]{:S(2)}, u32[]{:S(2)}) collective-permute-start(bf16[96,768]{1,0:T(8,128)(2,1)S(1)} %add_convert_fusion.3.part_a), channel_id=1, source_target_pairs={{0,2},{1,3},{2,0},{3,1},{4,6},{5,7},{6,4},{7,5},{8,10},{9,11},{10,... | collective-permute-start | bytes 442376 | tf_op jit(solution)/shard_map/ppermute | solution.py:786
  52.5 3.8 %collective-permute-start.14 = (bf16[96,768]{1,0:T(8,128)(2,1)S(1)}, bf16[96,768]{1,0:T(8,128)(2,1)S(1)}, u32[]{:S(2)}, u32[]{:S(2)}) collective-permute-start(bf16[96,768]{1,0:T(8,128)(2,1)S(1)} %down_kernel.1), channel_id=1, source_target_pairs={{0,1},{1,0},{2,3},{3,2},{4,5},{5,4},{6,7},{7,6},{8,9},{9,8},{10,11... | collective-permute-start | bytes 442376 | tf_op jit(solution)/shard_map/ppermute | solution.py:786
  52.6 3.7 %collective-permute-start.15 = (f32[8,128]{1,0:T(8,128)S(1)}, f32[8,128]{1,0:T(8,128)S(1)}, u32[]{:S(2)}, u32[]{:S(2)}) collective-permute-start(f32[8,128]{1,0:T(8,128)S(1)} %get-tuple-element.157), channel_id=1, source_target_pairs={{0,4},{4,0},{8,12},{12,8},{16,20},{20,16},{24,28},{28,24},{1,5},{5... | collective-permute-start | bytes 12296 | tf_op jit(solution)/shard_map/ppermute | solution.py:786
  56.3 8.7 %collective-permute-start.16 = (bf16[96,768]{1,0:T(8,128)(2,1)S(1)}, bf16[96,768]{1,0:T(8,128)(2,1)S(1)}, u32[]{:S(2)}, u32[]{:S(2)}) collective-permute-start(bf16[96,768]{1,0:T(8,128)(2,1)S(1)} %add_convert_fusion.2.part_a), channel_id=1, source_target_pairs={{0,2},{1,3},{2,0},{3,1},{4,6},{5,7},{6,4},{7,5},{8,10},{9,11},{10,... | collective-permute-start | bytes 442376 | tf_op jit(solution)/shard_map/ppermute | solution.py:786
  57.8 6.1 %collective-permute-start.19 = (bf16[48,768]{1,0:T(8,128)(2,1)S(1)}, bf16[48,768]{1,0:T(8,128)(2,1)S(1)}, u32[]{:S(2)}, u32[]{:S(2)}) collective-permute-start(bf16[48,768]{1,0:T(8,128)(2,1)S(1)} %get-tuple-element.164), channel_id=1, source_target_pairs={{0,16},{4,20},{8,24},{12,28},{16,0},{20,4},{24,8},{28,12},{1,17},{... | collective-permute-start | bytes 221192 | tf_op jit(solution)/shard_map/ppermute | solution.py:786
  60.4 4.5 %collective-permute-start.17 = (f32[8,128]{1,0:T(8,128)S(1)}, f32[8,128]{1,0:T(8,128)S(1)}, u32[]{:S(2)}, u32[]{:S(2)}) collective-permute-start(f32[8,128]{1,0:T(8,128)S(1)} %add.48), channel_id=1, source_target_pairs={{0,16},{4,20},{8,24},{12,28},{16,0},{20,4},{24,8},{28,12},{1,17},{... | collective-permute-start | bytes 12296 | tf_op jit(solution)/shard_map/ppermute | solution.py:786
  65.0 5.2 %collective-permute-start.20 = (bf16[96,768]{1,0:T(8,128)(2,1)S(1)}, bf16[96,768]{1,0:T(8,128)(2,1)S(1)}, u32[]{:S(2)}, u32[]{:S(2)}) collective-permute-start(bf16[96,768]{1,0:T(8,128)(2,1)S(1)} %pad_maximum_fusion.3), channel_id=1, source_target_pairs={{0,8},{4,12},{8,0},{12,4},{16,24},{20,28},{24,16},{28,20},{1,9},{5... | collective-permute-start | bytes 442376 | tf_op jit(solution)/shard_map/ppermute | solution.py:786
  65.6 12.3 %collective-permute-start.24 = (bf16[3,96,768]{2,1,0:T(8,128)(2,1)S(1)}, bf16[3,96,768]{2,1,0:T(8,128)(2,1)S(1)}, u32[]{:S(2)}, u32[]{:S(2)}) collective-permute-start(bf16[3,96,768]{2,1,0:T(8,128)(2,1)S(1)} %away_kernel.1), channel_id=1, source_target_pairs={{0,2},{1,3},{2,0},{3,1},{4,6},{5,7},{6,4},{7,5},{8,10},{9,11},{10,... | collective-permute-start | bytes 1327112 | tf_op jit(solution)/shard_map/ppermute | solution.py:786
  70.2 7.7 %collective-permute-start.22 = (bf16[48,1536]{1,0:T(8,128)(2,1)S(1)}, bf16[48,1536]{1,0:T(8,128)(2,1)S(1)}, u32[]{:S(2)}, u32[]{:S(2)}) collective-permute-start(bf16[48,1536]{1,0:T(8,128)(2,1)S(1)} %get-tuple-element.177), channel_id=1, source_target_pairs={{0,16},{4,20},{8,24},{12,28},{16,0},{20,4},{24,8},{28,12},{1,17},{... | collective-permute-start | bytes 442376 | tf_op jit(solution)/shard_map/ppermute | solution.py:786
  71.0 6.8 %collective-permute-start.23 = (bf16[192,768]{1,0:T(8,128)(2,1)S(1)}, bf16[192,768]{1,0:T(8,128)(2,1)S(1)}, u32[]{:S(2)}, u32[]{:S(2)}) collective-permute-start(bf16[192,768]{1,0:T(8,128)(2,1)S(1)} %pad_maximum_fusion.1), channel_id=1, source_target_pairs={{0,4},{4,0},{8,12},{12,8},{16,20},{20,16},{24,28},{28,24},{1,5},{5... | collective-permute-start | bytes 884744 | tf_op jit(solution)/shard_map/ppermute | solution.py:786
  71.8 5.7 %collective-permute-start.21 = (f32[8,128]{1,0:T(8,128)S(1)}, f32[8,128]{1,0:T(8,128)S(1)}, u32[]{:S(2)}, u32[]{:S(2)}) collective-permute-start(f32[8,128]{1,0:T(8,128)S(1)} %add.50.sc_a), channel_id=1, source_target_pairs={{0,8},{4,12},{8,0},{12,4},{16,24},{20,28},{24,16},{28,20},{1,9},{5... | collective-permute-start | bytes 12296 | tf_op jit(solution)/shard_map/ppermute | solution.py:786
  73.9 4.0 %copy-start.16 = (s32[24]{0:T(128)S(1)}, s32[24]{0:T(128)}, u32[]{:S(2)}) copy-start(s32[24]{0:T(128)} %lens.1) | copy-start | bytes 292
  80.5 9.1 %collective-permute-start.25 = (bf16[192,768]{1,0:T(8,128)(2,1)S(1)}, bf16[192,768]{1,0:T(8,128)(2,1)S(1)}, u32[]{:S(2)}, u32[]{:S(2)}) collective-permute-start(bf16[192,768]{1,0:T(8,128)(2,1)S(1)} %value_kernel.1), channel_id=1, source_target_pairs={{0,4},{4,0},{8,12},{12,8},{16,20},{20,16},{24,28},{28,24},{1,5},{5... | collective-permute-start | bytes 884744 | tf_op jit(solution)/shard_map/ppermute | solution.py:786
  81.2 9.9 %collective-permute-start.27 = (bf16[384,768]{1,0:T(8,128)(2,1)S(1)}, bf16[384,768]{1,0:T(8,128)(2,1)S(1)}, u32[]{:S(2)}, u32[]{:S(2)}) collective-permute-start(bf16[384,768]{1,0:T(8,128)(2,1)S(1)} %constant_dynamic-update-slice_fusion.c_own), channel_id=1, source_target_pairs={{0,1},{1,0},{2,3},{3,2},{4,5},{5,4},{6,7},{7,6},{8,9},{9,8},{10,11... | collective-permute-start | bytes 1769480 | tf_op jit(solution)/shard_map/ppermute | solution.py:786
  81.3 9.7 %collective-permute-start.26 = (bf16[96,1536]{1,0:T(8,128)(2,1)S(1)}, bf16[96,1536]{1,0:T(8,128)(2,1)S(1)}, u32[]{:S(2)}, u32[]{:S(2)}) collective-permute-start(bf16[96,1536]{1,0:T(8,128)(2,1)S(1)} %pad_maximum_fusion.2), channel_id=1, source_target_pairs={{0,8},{4,12},{8,0},{12,4},{16,24},{20,28},{24,16},{28,20},{1,9},{5... | collective-permute-start | bytes 884744 | tf_op jit(solution)/shard_map/ppermute | solution.py:786
  95.1 4.4 %collective-permute-start.28 = (f32[16,768]{1,0:T(8,128)S(1)}, f32[16,768]{1,0:T(8,128)S(1)}, u32[]{:S(2)}, u32[]{:S(2)}) collective-permute-start(f32[16,768]{1,0:T(8,128)S(1)} %key_sum_kernel.1), channel_id=1, source_target_pairs={{0,1},{1,0},{2,3},{3,2},{4,5},{5,4},{6,7},{7,6},{8,9},{9,8},{10,11... | collective-permute-start | bytes 147464 | tf_op jit(solution)/shard_map/ppermute | solution.py:786
  95.1 15.7 %collective-permute-start.31 = (bf16[192,768]{1,0:T(8,128)(2,1)S(1)}, bf16[192,768]{1,0:T(8,128)(2,1)S(1)}, u32[]{:S(2)}, u32[]{:S(2)}) collective-permute-start(bf16[192,768]{1,0:T(8,128)(2,1)S(1)} %add_convert_fusion.1), channel_id=1, source_target_pairs={{0,8},{4,12},{8,0},{12,4},{16,24},{20,28},{24,16},{28,20},{1,9},{5... | collective-permute-start | bytes 884744 | tf_op jit(solution)/shard_map/ppermute | solution.py:786
  96.0 23.3 %collective-permute-start.34 = (bf16[192,1536]{1,0:T(8,128)(2,1)S(1)}, bf16[192,1536]{1,0:T(8,128)(2,1)S(1)}, u32[]{:S(2)}, u32[]{:S(2)}) collective-permute-start(bf16[192,1536]{1,0:T(8,128)(2,1)S(1)} %pad_maximum_fusion), channel_id=1, source_target_pairs={{0,4},{4,0},{8,12},{12,8},{16,20},{20,16},{24,28},{28,24},{1,5},{5... | collective-permute-start | bytes 1769480 | tf_op jit(solution)/shard_map/ppermute | solution.py:786
  99.5 5.0 %collective-permute-start.29 = (f32[16,768]{1,0:T(8,128)S(1)}, f32[16,768]{1,0:T(8,128)S(1)}, u32[]{:S(2)}, u32[]{:S(2)}) collective-permute-start(f32[16,768]{1,0:T(8,128)S(1)} %add.51), channel_id=1, source_target_pairs={{0,2},{1,3},{2,0},{3,1},{4,6},{5,7},{6,4},{7,5},{8,10},{9,11},{10,... | collective-permute-start | bytes 147464 | tf_op jit(solution)/shard_map/ppermute | solution.py:786
  104.6 6.2 %collective-permute-start.30 = (f32[16,768]{1,0:T(8,128)S(1)}, f32[16,768]{1,0:T(8,128)S(1)}, u32[]{:S(2)}, u32[]{:S(2)}) collective-permute-start(f32[16,768]{1,0:T(8,128)S(1)} %add.52), channel_id=1, source_target_pairs={{0,16},{4,20},{8,24},{12,28},{16,0},{20,4},{24,8},{28,12},{1,17},{... | collective-permute-start | bytes 147464 | tf_op jit(solution)/shard_map/ppermute | solution.py:786
  110.8 4.2 %collective-permute-start.32 = (f32[16,768]{1,0:T(8,128)S(1)}, f32[16,768]{1,0:T(8,128)S(1)}, u32[]{:S(2)}, u32[]{:S(2)}) collective-permute-start(f32[16,768]{1,0:T(8,128)S(1)} %add.54), channel_id=1, source_target_pairs={{0,8},{4,12},{8,0},{12,4},{16,24},{20,28},{24,16},{28,20},{1,9},{5... | collective-permute-start | bytes 147464 | tf_op jit(solution)/shard_map/ppermute | solution.py:786
  115.0 4.3 %collective-permute-start.33 = (f32[16,768]{1,0:T(8,128)S(1)}, f32[16,768]{1,0:T(8,128)S(1)}, u32[]{:S(2)}, u32[]{:S(2)}) collective-permute-start(f32[16,768]{1,0:T(8,128)S(1)} %add.56.sum_a), channel_id=1, source_target_pairs={{0,4},{4,0},{8,12},{12,8},{16,20},{20,16},{24,28},{28,24},{1,5},{5... | collective-permute-start | bytes 147464 | tf_op jit(solution)/shard_map/ppermute | solution.py:786
  119.2 1.8 %copy-start.3 = (bf16[768,192]{0,1:T(8,128)(2,1)S(1)}, bf16[768,192]{0,1:T(8,128)(2,1)}, u32[]{:S(2)}) copy-start(bf16[768,192]{0,1:T(8,128)(2,1)} %param.30) | copy-start | bytes 884740
  119.2 1.8 %copy-start.4 = (bf16[768,192]{0,1:T(8,128)(2,1)S(1)}, bf16[768,192]{0,1:T(8,128)(2,1)}, u32[]{:S(2)}) copy-start(bf16[768,192]{0,1:T(8,128)(2,1)} %param.31) | copy-start | bytes 884740
  119.3 1.8 %copy-start.9 = (f32[768]{0:T(1024)S(1)}, f32[768]{0:T(1024)}, u32[]{:S(2)}) copy-start(f32[768]{0:T(1024)} %g_cross.5) | copy-start | bytes 9220
  119.3 5.7 %collective-permute-start.37 = (bf16[384,1536]{1,0:T(8,128)(2,1)S(1)}, bf16[384,1536]{1,0:T(8,128)(2,1)S(1)}, u32[]{:S(2)}, u32[]{:S(2)}) collective-permute-start(bf16[384,1536]{1,0:T(8,128)(2,1)S(1)} %constant_dynamic-update-slice_fusion.2.both_own), channel_id=1, source_target_pairs={{0,1},{1,0},{2,3},{3,2},{4,5},{5,4},{6,7},{7,6},{8,9},{9,8},{10,11... | collective-permute-start | bytes 3538952 | tf_op jit(solution)/shard_map/ppermute | solution.py:786
  119.4 17.9 %collective-permute-start.40 = (bf16[192,768]{1,0:T(8,128)(2,1)S(1)}, bf16[192,768]{1,0:T(8,128)(2,1)S(1)}, u32[]{:S(2)}, u32[]{:S(2)}) collective-permute-start(bf16[192,768]{1,0:T(8,128)(2,1)S(1)} %add_convert_fusion), channel_id=1, source_target_pairs={{0,16},{4,20},{8,24},{12,28},{16,0},{20,4},{24,8},{28,12},{1,17},{... | collective-permute-start | bytes 884744 | tf_op jit(solution)/shard_map/ppermute | solution.py:786
  123.2 1.2 collective-permute-start.35
  124.4 5.8 %collective-permute-start.36 = (f32[8,768]{1,0:T(8,128)S(1)}, f32[8,768]{1,0:T(8,128)S(1)}, u32[]{:S(2)}, u32[]{:S(2)}) collective-permute-start(f32[8,768]{1,0:T(8,128)S(1)} %add.57.part_a), channel_id=1, source_target_pairs={{0,2},{1,3},{2,0},{3,1},{4,6},{5,7},{6,4},{7,5},{8,10},{9,11},{10,... | collective-permute-start | bytes 73736 | tf_op jit(solution)/shard_map/ppermute | solution.py:786
  125.0 5.2 %copy-start.5 = (bf16[768,192]{0,1:T(8,128)(2,1)S(1)}, bf16[768,192]{0,1:T(8,128)(2,1)}, u32[]{:S(2)}) copy-start(bf16[768,192]{0,1:T(8,128)(2,1)} %param.27) | copy-start | bytes 884740
  125.0 5.2 %copy-start.6 = (bf16[192,768]{1,0:T(8,128)(2,1)S(1)}, bf16[192,768]{1,0:T(8,128)(2,1)}, u32[]{:S(2)}) copy-start(bf16[192,768]{1,0:T(8,128)(2,1)} %wos.3) | copy-start | bytes 884740
  125.0 5.2 %copy-start.10 = (f32[768]{0:T(1024)S(1)}, f32[768]{0:T(1024)}, u32[]{:S(2)}) copy-start(f32[768]{0:T(1024)} %g_self.5) | copy-start | bytes 9220
  125.0 5.2 %copy-start.11 = (bf16[768]{0:T(1024)(128)(2,1)S(1)}, bf16[768]{0:T(1024)(128)(2,1)}, u32[]{:S(2)}) copy-start(bf16[768]{0:T(1024)(128)(2,1)} %start.7) | copy-start | bytes 4612
  132.1 1.2 collective-permute-start.38
  133.3 4.0 %collective-permute-start.39 = (f32[8,768]{1,0:T(8,128)S(1)}, f32[8,768]{1,0:T(8,128)S(1)}, u32[]{:S(2)}, u32[]{:S(2)}) collective-permute-start(f32[8,768]{1,0:T(8,128)S(1)} %add.58.part_a), channel_id=1, source_target_pairs={{0,2},{1,3},{2,0},{3,1},{4,6},{5,7},{6,4},{7,5},{8,10},{9,11},{10,... | collective-permute-start | bytes 73736 | tf_op jit(solution)/shard_map/ppermute | solution.py:786

commit v4 on v3

--- a/solution.py
+++ b/solution.py
@@ -98,8 +98,17 @@
 
 
 def spread(small):
-    hot = (iota((LANES, D), 0) == head_of((LANES, D), 1)).astype(f32)
-    return nn(small, hot, EXACT)
+    high, mid, low = (part.astype(f32) for part in split3(small))
+    packed = high + pltpu.roll(mid, ROWS, 1) + pltpu.roll(low, 2 * ROWS, 1)
+    lane = iota((LANES, D), 0)
+    hot = (lane < 3 * ROWS) & (lane % ROWS == head_of((LANES, D), 1))
+    return nn(packed.astype(bf16), hot.astype(bf16))
+
+
+def row_dot(row, right):
+    high, low = split2(right)
+    parts = stack3(row)
+    return jnp.sum(nn(parts, high) + nn(parts, low), axis=0, keepdims=True)
 
 
 def row_of(ref):
@@ -275,6 +284,10 @@
         full[pl.ds(at, height)] = piece[...]
 
 
+def arrange_kernel(scal, own, by2, by1, by3, full_out):
+    place_parts(scal, full_out, own, by2, by1, by3)
+
+
 def project_kernel(scal, summed, extra, own, by2, by1, by3, pay_out, heads_out, wv):
     place_parts(scal, wv, own, by2, by1, by3)
     slots = pay_out.shape[0]
@@ -300,13 +313,17 @@
     return peak, total
 
 
-def merge(one, two):
+def merge(one, two, last=False):
     peak1, total1 = decode(one)
     peak2, total2 = decode(two)
     peak = jnp.maximum(peak1, peak2)
     up1, up2 = jnp.exp(peak1 - peak), jnp.exp(peak2 - peak)
     total = up1 * total1 + up2 * total2
     first = iota(peak.shape, 1) < ROWS
+    if last:
+        some = first & (total > 0.0)
+        total = jnp.where(some, 1.0 / jnp.where(some, total, 1.0), 0.0)
+        up1, up2 = up1 * total, up2 * total
     up1, up2 = jnp.where(first, up1, 0.0), jnp.where(first, up2, 0.0)
     context = spread(up1) * one[:, :D].astype(f32) + spread(up2) * two[:, :D].astype(f32)
     return peak, total, context
@@ -336,16 +353,12 @@
 
 
 def forward_kernel(
-    scal, own, other, first, h1, wo_own, wo_by2, wo_by1, wo_by3, g_ff, win, wdown,
-    c_out, c32_out, scale_out, h2_out, z_out, part_out, wo, c_s,
+    scal, own, other, first, h1, wo, g_ff, win, wdown,
+    c_out, c32_out, scale_out, h2_out, z_out, part_out, c_s,
 ):
-    place_parts(scal, wo, wo_own, wo_by2, wo_by1, wo_by3)
     bit = lax.shift_right_logical(scal[0], 1) & 1
     one, two = ordered(bit, own[...].astype(f32), other[...].astype(f32))
-    peak, total, context = merge(one, two)
-    lanes = iota(peak.shape, 1) < ROWS
-    inverse = jnp.where(lanes & (total > 0.0), 1.0 / jnp.where(total > 0.0, total, 1.0), 0.0)
-    context = context * spread(inverse)
+    peak, inverse, context = merge(one, two, True)
     mine, _ = decode(first[...].astype(f32))
     scale_out[...] = jnp.exp(jnp.minimum(mine - peak, 0.0)) * inverse
     c32_out[...] = context
@@ -361,16 +374,15 @@
     part_out[...] = nn(u, wdown[...]).astype(bf16)
 
 
-def score_kernel(scal, part_a, part_b, h2, g_final, row, scores_out, n3_out, dh3_out):
+def score_kernel(part_a, part_b, h2, g_final, row, c, pay_out, n3_out, dh3_out):
     h3 = h2[...] + (part_a[...].astype(f32) + part_b[...].astype(f32))
     n3, r3 = rms_parts(h3)
     n3_out[...] = n3
     wanted = jnp.broadcast_to(row_of(g_final) * row_of(row) * FACTOR, (8, D))
     scores = nt(wanted, n3, EXACT)[0:1]
-    slots = n3.shape[0]
-    groups = scores_out.shape[0]
-    wide = jnp.concatenate([scores, jnp.zeros((1, LANES - slots), f32)], axis=1)
-    scores_out[...] = jnp.where(iota((groups, LANES), 0) == scal[1], wide, 0.0)
+    wide = jnp.concatenate([scores, jnp.zeros((1, LANES - n3.shape[0]), f32)], axis=1)
+    pay_out[:, :D] = c[...]
+    pay_out[:, D:] = stack3(wide, c.shape[0])
     dh3_out[...] = rms_back(wanted[0:1], n3, r3).astype(bf16)
 
 
@@ -380,21 +392,9 @@
     part_out[...] = nt(dz, win[...]).astype(bf16)
 
 
-def list_kernel(scal, sizes, lens, sc_a, sc_b, rel, scores_out, loss_out, ds_out, mine_out):
-    groups = sc_a.shape[0]
-    docs = ds_out.shape[1]
-    wide = docs + LANES
-    queries = lens.shape[0]
+def target_kernel(lens, rel, target_out, member_out):
+    queries, docs = target_out.shape
     relevance = rel[...].reshape(1, docs)
-    scores = sc_a[...] + sc_b[...]
-    lane = iota((8, LANES), 1)
-    blank = jnp.zeros((8, wide - LANES), f32)
-    placed = jnp.zeros((8, wide), f32)
-    start = jnp.int32(0)
-    for g in range(groups):
-        kept = jnp.where(lane < sizes[g], scores[g : g + 1], 0.0)
-        placed = placed + pltpu.roll(jnp.concatenate([kept, blank], axis=1), start, 1)
-        start = start + sizes[g]
     at = iota((queries, 1), 0)
 
     def one_list(j, found):
@@ -406,15 +406,52 @@
     _, begins, ends = lax.fori_loop(
         0, queries, one_list, (jnp.int32(0), none, none), unroll=queries <= 32
     )
+    place = iota((queries, docs), 1)
+    member = (place >= begins) & (place < ends)
+    weight = jnp.sum(jnp.where(member, relevance, 0.0), axis=1, keepdims=True)
+    target_out[...] = jnp.where(member, relevance / weight, 0.0)
+    member_out[...] = member.astype(f32)
+
+
+def place_of(order, mask):
+    pos = 0
+    for k, bit in enumerate(order):
+        pos = pos + (lax.shift_right_logical(mask, bit.bit_length() - 1) & 1) * (1 << k)
+    return pos
+
+
+def list_kernel(order, scal, sizes, rows, targets, members, scores_out, loss_out, ds_out, mine_out):
+    groups = 1 << len(order)
+    docs = ds_out.shape[1]
+    wide = docs + LANES
+    queries = targets.shape[0]
+    half = rows.shape[0] // groups
+    lane = iota((8, LANES), 1)
+    blank = jnp.zeros((8, wide - LANES), f32)
+
+    def one_group(g, found):
+        start, placed = found
+        at = pl.multiple_of(place_of(order, g ^ scal[1]) * half, half)
+        parts = rows[pl.ds(at, ROWS), D:].astype(f32)
+        score = (parts[0:1] + parts[1:2]) + parts[2:3]
+        kept = jnp.where(lane < sizes[g], score, 0.0)
+        kept = pltpu.roll(jnp.concatenate([kept, blank], axis=1), start, 1)
+        return start + sizes[g], placed + kept
+
+    _, placed = lax.fori_loop(
+        0,
+        groups,
+        one_group,
+        (jnp.int32(0), jnp.zeros((8, wide), f32)),
+        unroll=groups <= 8,
+    )
     values = placed[0:1, :docs]
     scores_out[...] = values.reshape(scores_out.shape)
-    place = iota((queries, docs), 1)
-    member = (place >= begins) & (place < ends)
+    member = members[...] > 0.0
+    target = targets[...]
     peak = jnp.max(jnp.where(member, values, MASKED), axis=1, keepdims=True)
     raised = jnp.where(member, jnp.exp(jnp.where(member, values - peak, 0.0)), 0.0)
     log_total = peak + jnp.log(jnp.sum(raised, axis=1, keepdims=True))
-    weight = jnp.sum(jnp.where(member, relevance, 0.0), axis=1, keepdims=True)
-    target = jnp.where(member, relevance / weight, 0.0)
     picked = jnp.sum(target * values, axis=1, keepdims=True)
     loss_out[...] = jnp.sum(log_total - picked, axis=0, keepdims=True) / queries
     chance = jnp.where(member, jnp.exp(jnp.where(member, values - log_total, 0.0)), 0.0)
@@ -427,10 +464,9 @@
 
 
 def context_kernel(
-    scal, part_a, part_b, h2, dh3, c32, g_ff, wo_own, wo_by2, wo_by1, wo_by3,
-    dh2_out, half_out, dc_out, own_out, inner_out, ff_out, wout, both_s,
+    scal, part_a, part_b, h2, dh3, c32, g_ff, wout, wo_own,
+    dh2_out, half_out, dc_out, own_out, inner_out, ff_out, both_s,
 ):
-    place_parts(scal, wout, wo_own, wo_by2, wo_by1, wo_by3)
     n2, r2 = rms_parts(h2[...])
     dy3 = part_a[...].astype(f32) + part_b[...].astype(f32)
     ff_out[...] = dy3 * n2
@@ -440,8 +476,9 @@
     dc = nt(dh2, wout[...]).astype(bf16)
     dc_out[...] = dc
     own_out[...] = nt(dh2, wo_own[...]).astype(bf16)
-    hot = (head_of((D, LANES), 0) == iota((D, LANES), 1)).astype(f32)
-    inner_out[...] = nn(dc.astype(f32) * c32[...], hot, EXACT)
+    hot = (head_of((D, LANES), 0) == iota((D, LANES), 1)).astype(bf16)
+    high, low = split2(dc.astype(f32) * c32[...])
+    inner_out[...] = nn(high, hot) + nn(low, hot)
 
 
 def columns(one, two):
@@ -458,12 +495,8 @@
     )
 
 
-def back_kernel(first, last, scal, sizes, enc, p, scale, inner, dc, *refs):
-    if first:
-        wv, dap_out, vd_out = refs[0], *refs[-2:]
-    else:
-        dap_out, vd_out, wv = refs[-3:]
-        place_parts(scal, wv, *refs[:4])
+def back_kernel(first, last, scal, sizes, enc, p, scale, inner, dc, wv, *refs):
+    dap_out, vd_out = refs[-2:]
     tokens = enc.shape[1]
     tall = BLOCK * ROWS
     rounds = jnp.clip(rounds_of(scal, sizes), first, last)
@@ -508,9 +541,10 @@
     slots = dh2.shape[0]
     row = ds[...][:, :slots] * (1.0 / PARTS)
     at = iota((ROWS, D), 0)
-    out = jnp.where(at == HEADS, nn(row, dh2[...].astype(f32), EXACT)[0:1], 0.0)
-    out = jnp.where(at == HEADS + 1, nn(row, n3[...], EXACT)[0:1], out)
-    sums_out[...] = jnp.where(at == HEADS + 2, nn(row, ff[...], EXACT)[0:1], out)
+    row = row[0:1]
+    out = jnp.where(at == HEADS, jnp.sum(nn(stack3(row), dh2[...]), axis=0, keepdims=True), 0.0)
+    out = jnp.where(at == HEADS + 1, row_dot(row, n3[...]), out)
+    sums_out[...] = jnp.where(at == HEADS + 2, row_dot(row, ff[...]), out)
 
     def one_block(step):
         block = pl.ds(pl.multiple_of(step * BLOCK, BLOCK), BLOCK)
@@ -593,10 +627,7 @@
 
     def one_group(g, found):
         start, at, upper = found
-        mask = g ^ scal[1]
-        pos = 0
-        for k, bit in enumerate(order):
-            pos = pos + (lax.shift_right_logical(mask, bit.bit_length() - 1) & 1) * (1 << k)
+        pos = place_of(order, g ^ scal[1])
         slot = doc - start
         inside = (slot >= 0) & (slot < sizes[g])
         later = (slot >= half).astype(i32)
@@ -610,7 +641,11 @@
     hit = iota((tile, held), 1) == at
     mine = (hit & (upper == core)).astype(bf16)
     theirs = (hit & (upper != core)).astype(bf16)
-    return lambda own, other: (nn(mine, own[...]) + nn(theirs, other[...])).astype(bf16)
+
+    def rows(own, other, width):
+        return (nn(mine, own[:, :width]) + nn(theirs, other[:, :width])).astype(bf16)
+
+    return rows
 
 
 def ds_column(ds, first, tile):
@@ -635,15 +670,13 @@
 
 
 def weights_before_kernel(
-    order, tile, scal, sizes, c_own, c_other, h1, g_ff, wo_own, wo_by2, wo_by1, wo_by3, win,
-    y3_out, u_out, slope_out, c_out, wout,
+    order, tile, scal, sizes, c_own, c_other, h1, g_ff, wout, win,
+    y3_out, u_out, slope_out, c_out,
 ):
-    place_parts(scal, wout, wo_own, wo_by2, wo_by1, wo_by3)
-
     def one_tile(first, new):
         here = pl.ds(first, tile)
         rows = document_picks(order, tile, scal, sizes, c_own.shape[0], first)
-        c = rows(c_own, c_other)
+        c = rows(c_own, c_other, D)
         h2 = h1[...] + nn(c, wout[...])
         n2, _ = rms_parts(h2)
         y3 = (n2 * row_of(g_ff)).astype(bf16)
@@ -665,7 +698,7 @@
     def one_tile(first, new):
         here = pl.ds(first, tile)
         rows = document_picks(order, tile, scal, sizes, both_own.shape[0], first)
-        both = rows(both_own, both_other).astype(f32) * ds_column(ds, first, tile)
+        both = rows(both_own, both_other, 2 * D).astype(f32) * ds_column(ds, first, tile)
         both = both.astype(bf16)
         grads_out[here] = both
         dz = (nt(both[:, :D], wdown[...]) * slope[here]).astype(bf16)
@@ -751,9 +784,8 @@
 
 
 def plain(
-    kernel, outs, *args, smem=0, hbm=(), hbm_out=False, onto=None, flops=0, limit=12, scratch=()
+    kernel, outs, *args, smem=0, hbm=(), hbm_out=False, onto=None, limit=12, scratch=()
 ):
-    size = sum(a.size * a.dtype.itemsize for k, a in enumerate(args) if k not in hbm)
     spaces = [pltpu.SMEM] * smem + [pltpu.VMEM] * (len(args) - smem)
     for k in hbm:
         spaces[k] = pltpu.HBM
@@ -768,7 +800,7 @@
         scratch_shapes=list(scratch),
         input_output_aliases=onto or {},
         compiler_params=pltpu.CompilerParams(vmem_limit_bytes=limit * MIB),
-        cost_estimate=pl.CostEstimate(flops=flops, bytes_accessed=size, transcendentals=0),
+        cost_estimate=pl.CostEstimate(flops=0, bytes_accessed=0, transcendentals=0),
         name=name_of(kernel),
     )(*args)
 
@@ -858,9 +890,7 @@
             scratch_shapes=[pltpu.SemaphoreType.DMA((last - first,))],
             input_output_aliases={3: 0} if onto else {},
             compiler_params=pltpu.CompilerParams(vmem_limit_bytes=MIB),
-            cost_estimate=pl.CostEstimate(
-                flops=0, bytes_accessed=(last - first) * BLOCK * tokens * D * 4, transcendentals=0
-            ),
+            cost_estimate=pl.CostEstimate(flops=0, bytes_accessed=0, transcendentals=0),
             name="load_kernel",
         )(in_hbm(enc_out), since, scal, *onto)
 
@@ -884,8 +914,6 @@
     held = load(1, 3, qk, held)
     qk_b, held, wv_by2 = lax.optimization_barrier((qk_b, held, wv_by2))
     wv_by3 = swap(wv_by2, "heads", 1)
-
-    pass_flops = 2 * slots * tokens * D * 256
 
     wo_by2 = swap(after(w_out, qk_b), "heads", 2)
     held, prob, summed, extra = plain(
@@ -906,28 +934,34 @@
         smem=3,
         hbm=(5,),
         onto={6: 0},
-        flops=2 * pass_flops,
         scratch=[pltpu.VMEM((2 * ROWS, D), bf16), pltpu.SemaphoreType.DMA((slots // BLOCK,))],
         limit=16,
     )
     summed, wv_by3, wo_by2 = lax.optimization_barrier((summed, wv_by3, wo_by2))
     wv_parts = (wv_t, wv_by2, wv_by1, wv_by3)
     wo_parts = (w_out, wo_by2, wo_by1, swap(wo_by2, "heads", 1))
-    full = [pltpu.VMEM((D, D), bf16)]
-    pay, summed = plain(
+    pay, summed, wv_full = plain(
         project_kernel,
-        [shape((slots, D + LANES), bf16), shape((HEADS, slots, D), bf16)],
+        [
+            shape((slots, D + LANES), bf16),
+            shape((HEADS, slots, D), bf16),
+            shape((D, D), bf16),
+        ],
         scal,
         summed,
         extra,
         *wv_parts,
         smem=1,
-        scratch=full,
     )
     merged = plain(
         merge_kernel, shape(pay.shape, bf16), scal, pay, swap(pay, "heads", 1), smem=1
     )
     other = swap(merged, "heads", 2)
+    wo_full = plain(arrange_kernel, shape((D, D), bf16), scal, *wo_parts, smem=1)
+    target, member = plain(
+        target_kernel, [shape((list_len.shape[0], docs))] * 2, list_len, relevance, smem=1
+    )
+    other, wo_full, target, member = lax.optimization_barrier((other, wo_full, target, member))
 
     c, c32, scale, h2, z, part = plain(
         forward_kernel,
@@ -944,12 +978,12 @@
         other,
         pay,
         h1,
-        *wo_parts,
+        wo_full,
         g_ff,
         w_in,
         w_down,
         smem=1,
-        scratch=full + [pltpu.VMEM((slots, D), bf16)],
+        scratch=[pltpu.VMEM((slots, D), bf16)],
     )
 
     half = slots // 2
@@ -962,43 +996,32 @@
 
     last = len(over_docs) - 1
     near_first = over_docs[::-1]
-    score_steps = near_first[:1] + over_docs[:-1]
     part = add(part, swap(part, "heads", 1))
-    part, c, summed = tie(part, c, summed)
     part_a, part_b = part, swap(part, "heads", 2)
-    c_far = swap(c, *over_docs[0])
-    keep, sent = plain(
-        share_kernel, [shape((2, own_heads, slots, D), bf16)] * 2, scal, summed, scale, smem=1
-    )
-    got = swap(sent, "heads", 1)
-    part_b, keep = tie(part_b, keep)
-    scores, n3, dh3 = plain(
+    c_all, n3, dh3 = plain(
         score_kernel,
-        [shape((groups, LANES)), shape((slots, D)), shape((slots, D), bf16)],
-        scal,
+        [shape((half, D + LANES), bf16), shape((slots, D)), shape((slots, D), bf16)],
         part_a,
         part_b,
         h2,
         g_final,
         score_row,
-        smem=1,
-    )
-    score_far = swap(scores, *score_steps[0])
+        c,
+    )
     part = plain(down_kernel, shape((slots, D), bf16), dh3, z, w_down, w_in)
-    part_far = swap(part, "heads", 1)
-    part_far, score_far = tie(part_far, score_far)
-    part = add(part, part_far)
+    part = add(part, swap(part, "heads", 1))
+    part, summed = tie(part, summed)
     part_a, part_b = part, swap(part, "heads", 2)
-    score_a = scores + score_far
-    for k in range(1, last):
-        score_b = swap(score_a, *score_steps[k])
-        if k < last - 1:
-            score_a = score_a + score_b
+    c_far = swap(c_all, *over_docs[0])
+    keep, sent = plain(
+        share_kernel, [shape((2, own_heads, slots, D), bf16)] * 2, scal, summed, scale, smem=1
+    )
+    got = swap(sent, "heads", 1)
     away = plain(
         away_kernel, shape((own_heads, slots, D), bf16), scal, keep, got, smem=1
     )
     other = swap(away, "heads", 2)
-    part_b, score_b, away, c_far = tie(part_b, score_b, away, c_far)
+    part_b, away = tie(part_b, away)
     dh2, grads, dc, dc_own, inner, ff = plain(
         context_kernel,
         [
@@ -1016,47 +1039,59 @@
         dh3,
         c32,
         g_ff,
-        *wo_parts,
+        wo_full,
+        w_out,
         smem=1,
-        scratch=full + [pltpu.VMEM((slots, 2 * D), bf16)],
-    )
-
-    score_a = score_a + score_b
-    c_all = jnp.concatenate([c, c_far], axis=0)
+        scratch=[pltpu.VMEM((slots, 2 * D), bf16)],
+    )
+
+    c_all, c_far, dc, grads = tie(c_all, c_far, dc, grads)
+    c_all = jnp.concatenate([c_all, c_far], axis=0)
     for k in range(1, last):
-        c_all = grow(c_all, k)
-    score_a, dc, grads, c_all = tie(score_a, dc, grads, c_all)
-    score_b = swap(score_a, *score_steps[last])
+        c_far = swap(c_all, *over_docs[k])
+        if k < last - 1:
+            c_all = jnp.concatenate([c_all, c_far], axis=0)
     grads_far = swap(grads, *over_docs[0])
-    c_far = swap(c_all, *over_docs[last])
 
     outs = [
         pltpu.VMEM((slots, 2 * ROWS, tokens), bf16),
         pltpu.VMEM((slots, ROWS, D), bf16),
     ]
     rounds = slots // SPAN
-    middle = 1
-    inputs = (scal, group_docs, held, prob, scale, inner, dc)
-    dap, vd, wv_full = plain(
-        functools.partial(back_kernel, 0, middle),
-        outs + [shape((D, D), bf16)],
-        *inputs,
-        *wv_parts,
-        smem=2,
-        flops=pass_flops * middle // rounds,
-        limit=16,
-    )
-    dap, score_b, grads_far, c_far, other = tie(dap, score_b, grads_far, c_far, other)
+    inputs = (scal, group_docs, held, prob, scale, inner, dc, wv_full)
+
+    def back(first, last, *onto):
+        return plain(
+            functools.partial(back_kernel, first, last),
+            outs,
+            *inputs,
+            *onto,
+            smem=2,
+            onto={8: 0, 9: 1} if onto else None,
+            limit=16,
+        )
+
+    dap, vd = back(0, 1)
+    dap, c_far = tie(dap, c_far)
+    c_all = jnp.concatenate([c_all, c_far], axis=0)
+    c_far = swap(c_all, *over_docs[last])
+    dap, vd = back(1, rounds, dap, vd)
+    dap, c_far, other, grads_far = tie(dap, c_far, other, grads_far)
+    grads = jnp.concatenate([grads, grads_far], axis=0)
+    for m in range(1, last):
+        grads_far = swap(grads, *over_docs[m])
+        if m < last - 1:
+            grads = jnp.concatenate([grads, grads_far], axis=0)
+    c_all = jnp.concatenate([c_all, c_far], axis=0)
     all_scores, loss, ds_docs, ds_mine = plain(
-        list_kernel,
+        functools.partial(list_kernel, order),
         [shape((docs,)), shape((1, 1)), shape((1, docs)), shape((8, LANES))],
         scal,
         group_docs,
-        list_len,
-        score_a,
-        score_b,
-        in_hbm(relevance),
-        smem=3,
+        c_all,
+        target,
+        member,
+        smem=2,
     )
     value_part = plain(
         value_kernel,
@@ -1071,31 +1106,7 @@
     )
     dap, value_part = tie(dap, value_part)
     value_far = swap(value_part, *near_first[0])
-    c_all = jnp.concatenate([c_all, c_far], axis=0)
     c_far = swap(c_all, "heads", 1)
-    grads = jnp.concatenate([grads, grads_far], axis=0)
-    for m in range(1, last):
-        grads_far = swap(grads, *over_docs[m])
-        if m < last - 1:
-            grads = jnp.concatenate([grads, grads_far], axis=0)
-    dap, vd = plain(
-        functools.partial(back_kernel, middle, rounds),
-        outs,
-        *inputs,
-        wv_full,
-        dap,
-        vd,
-        smem=2,
-        onto={8: 0, 9: 1},
-        flops=pass_flops * (rounds - middle) // rounds,
-        limit=16,
-    )
-    dap, value_far, grads_far, c_far = tie(dap, value_far, grads_far, c_far)
-    grads = jnp.concatenate([grads, grads_far], axis=0)
-    grads_far = swap(grads, *over_docs[last])
-    for m in range(1, last):
-        value_part = add(value_part, value_far)
-        value_far = swap(value_part, *near_first[m])
     sums = plain(
         key_sum_kernel,
         shape((ROWS, D)),
@@ -1108,7 +1119,6 @@
         n3,
         ff,
         smem=2,
-        flops=pass_flops,
     )
 
     def enc_grads(first, last, grads=None):
@@ -1123,55 +1133,58 @@
             hbm=() if grads is None else (len(args),),
             hbm_out=True,
             onto={} if grads is None else {len(args): 0},
-            flops=pass_flops * (last - first) // slots,
             scratch=[pltpu.VMEM((4, size, tokens, D), bf16), pltpu.SemaphoreType.DMA((4,))],
             limit=16,
         )
 
     sums = add(sums, swap(sums, "heads", 1))
-    steps = over_heads[1:] + near_first[:0:-1] + near_first[:1]
+    steps = near_first[:0:-1] + over_heads[1:] + near_first[:1]
+    sums, grads_far = tie(sums, grads_far)
+    grads = jnp.concatenate([grads, grads_far], axis=0)
+    grads_far = swap(grads, *over_docs[last])
     enc_grad = None
     third = slots // 3
     sum_a = sums
     for k, step in enumerate(steps):
+        ds_mine, sum_a = tie(ds_mine, sum_a)
         sum_b = swap(sum_a, *step)
-        if k < 2 or k == len(steps) - 1:
-            part = min(k, 2)
-            enc_grad = enc_grads(part * third, (part + 1) * third, enc_grad)
+        if k < 3:
+            enc_grad = enc_grads(k * third, (k + 1) * third, enc_grad)
             sum_b, enc_grad = tie(sum_b, enc_grad)
         if k == 1:
-            sum_b, value_far = tie(sum_b, value_far)
-            value_part = add(value_part, value_far)
-        if k == len(steps) - 2:
-            ready = plain(
-                functools.partial(weights_before_kernel, order, 384),
-                [
-                    shape((docs, D), bf16),
-                    shape((docs, hidden), bf16),
-                    shape((docs, hidden)),
-                    shape((docs, width), bf16),
-                ],
-                scal,
-                group_docs,
-                c_all,
-                c_far,
-                h1,
-                g_ff,
-                *wo_parts,
-                w_in,
-                smem=2,
-                flops=4 * docs * D * hidden,
-                limit=60 if docs > 384 else 16,
-                scratch=full,
-            )
-            sum_b, value_part, *ready = tie(sum_b, value_part, *ready)
-            value_b = swap(value_part, *near_first[last])
-        if k == len(steps) - 1:
-            sum_b, grads_far = tie(sum_b, grads_far)
-            grads = jnp.concatenate([grads, grads_far], axis=0)
-            grads_far = swap(grads, "heads", 1)
+            sum_b, value_far, c_far = tie(sum_b, value_far, c_far)
+            for step in near_first[1:-1]:
+                value_part = add(value_part, value_far)
+                value_far = swap(value_part, *step)
         if k < len(steps) - 1:
             sum_a = sum_a + sum_b
+    y3, u, slope, c_own = plain(
+        functools.partial(weights_before_kernel, order, 384),
+        [
+            shape((docs, D), bf16),
+            shape((docs, hidden), bf16),
+            shape((docs, hidden)),
+            shape((docs, width), bf16),
+        ],
+        scal,
+        group_docs,
+        c_all,
+        c_far,
+        h1,
+        g_ff,
+        wo_full,
+        w_in,
+        smem=2,
+        limit=60 if docs > 384 else 16,
+    )
+    sum_b, grads_far, value_far, y3, u, slope, c_own = tie(
+        sum_b, grads_far, value_far, y3, u, slope, c_own
+    )
+    value_part = add(value_part, value_far)
+    value_far = swap(value_part, *near_first[-1])
+    grads = jnp.concatenate([grads, grads_far], axis=0)
+    grads_far = swap(grads, "heads", 1)
+
     key_grad, query_grad, part = plain(
         key_kernel,
         [shape((width, D)), shape((width, D)), shape((8, D))],
@@ -1184,8 +1197,9 @@
         wq_t,
         smem=1,
     )
-    part_a, part_b = sum_last(part, over_heads)
-    y3, u, slope, c_own = ready
+    part = add(part, swap(part, "heads", 1))
+    part, grads_far = tie(part, grads_far)
+    part_a, part_b = part, swap(part, "heads", 2)
     w_in_grad, grads_docs = plain(
         functools.partial(weights_kernel, order, 384),
         [shape((D, hidden)), shape((docs, 2 * D), bf16)],
@@ -1198,7 +1212,6 @@
         ds_docs,
         w_down,
         smem=2,
-        flops=4 * docs * D * hidden,
         limit=60 if docs > 384 else 16,
     )
     part_b, w_in_grad, grads_docs = tie(part_b, w_in_grad, grads_docs)
@@ -1225,11 +1238,10 @@
         u,
         c_own,
         grads_docs,
-        flops=4 * docs * D * hidden,
         limit=60 if docs > 384 else 16,
     )
-    part_b, w_down_grad, value_b = tie(part_b, w_down_grad, value_b)
-    value_grad = (value_part.astype(f32) + value_b.astype(f32)).T
+    part_b, w_down_grad, value_far = tie(part_b, w_down_grad, value_far)
+    value_grad = (value_part.astype(f32) + value_far.astype(f32)).T
     self_gain, start_grad = plain(
         start_kernel, [shape((D,))] * 2, part_a, part_b, dh1, start_token, g_self
     )

time: 140 us -> 129 us (0.921)
  Pallas kernels: 70.6 us -> 63.6 us
  starting transfers between devices: 35.7 us -> 32 us
    pallas_call x25 -> x27, Pallas kernels: 64.7 us -> 57.7 us  [plain(): pl.pallas_call(kernel, out_shape=outs, in_specs=[whole_spec(space) for sp...]
    ppermute x41 -> x38, starting transfers between devices: 35.7 us -> 32 us  [swap(): return lax.ppermute(x, axis, [(i, i ^ bit) for i in range(size)])]
    ppermute x41 -> x38, waiting for transfers between devices: 30 us -> 30.2 us  [swap(): return lax.ppermute(x, axis, [(i, i ^ bit) for i in range(size)])]
  transfers between devices with their start and end apart: 41 -> 38, of which waited for: 17 -> 15; matrix products, arithmetic and copies ran while one was open for 0% -> 0% of each run, Pallas kernels for 41% -> 43%
where the time goes in v4:
time: 129 us
  Pallas kernels  63.6 us (49%)
  starting transfers between devices  32 us (25%)
  waiting for transfers between devices  30.2 us (23%)
  other arithmetic  1.34 us (1%)
    pallas_call x27, Pallas kernels, plain(): pl.pallas_call(kernel, out_shape=outs, in_specs=[whole_spec(space) for sp...  57.7 us
    ppermute x38, starting transfers between devices, swap(): return lax.ppermute(x, axis, [(i, i ^ bit) for i in range(size)])  32 us
    ppermute x38, waiting for transfers between devices, swap(): return lax.ppermute(x, axis, [(i, i ^ bit) for i in range(size)])  30.2 us
    pallas_call x2, Pallas kernels, load(): pl.pallas_call(functools.partial(load_kernel, first, last), out_shape=plt...  5.84 us
  transfers between devices with their start and end apart: 38, of which 15 were waited for; matrix products, arithmetic and copies ran while one was open for 0% of the time, Pallas kernels for 43%

profile of v4, /device:TPU:0, one launch (start us, length us, event | category | flops | bytes accessed | tf_op | source)
XLA Modules:
  0.0 128.6 jit_solution(935088689888425157)
XLA Ops:
  0.7 1.5 %self_kernel.1 = f32[8,768]{1,0:T(8,128)S(1)} custom-call(bf16[768]{0:T(1024)(128)(2,1)} %start.7, f32[768]{0:T(1024)} %g_self.5, bf16[192,768]{1,0:T(8,128)(2,1)} %bitcast.16, bf16[192,768]{1,0:T(8,128)(2,1)} %wos.3), custom_call_target="tpu_custom_call" | custom-call | tf_op jit(solution)/shard_map/self_kernel/pallas_call | solution.py:793
  2.2 0.5 collective-permute-start
  2.6 0.8 collective-permute-done
  3.5 2.9 %collective-permute-start.1 = (f32[8,768]{1,0:T(8,128)S(1)}, f32[8,768]{1,0:T(8,128)S(1)}, u32[]{:S(2)}, u32[]{:S(2)}) collective-permute-start(f32[8,768]{1,0:T(8,128)S(1)} %add.39.since.part_a), channel_id=1, source_target_pairs={{0,2},{1,3},{2,0},{3,1},{4,6},{5,7},{6,4},{7,5},{8,10},{9,11},{10,... | collective-permute-start | bytes 73736 | tf_op jit(solution)/shard_map/ppermute | solution.py:818
  6.4 2.4 %load_kernel.2.refs_0_ = bf16[96,128,768]{2,1,0:T(8,128)(2,1)S(1)} custom-call(bf16[96,128,768]{2,1,0:T(8,128)(2,1)} %enc.5, f32[8,768]{1,0:T(8,128)S(1)} %add.39.since.part_a, s32[2]{0:T(128)S(1)} %pad_add_fusion.scal), custom_call_target="tpu_custom_call" | custom-call | tf_op jit(solution)/shard_map/load_kernel/pallas_call | solution.py:884
  8.9 1.3 %collective-permute-start.4 = (bf16[192,768]{1,0:T(8,128)(2,1)S(1)}, bf16[192,768]{1,0:T(8,128)(2,1)S(1)}, u32[]{:S(2)}, u32[]{:S(2)}) collective-permute-start(bf16[192,768]{1,0:T(8,128)(2,1)S(1)} %bitcast.18), channel_id=1, source_target_pairs={{0,2},{1,3},{2,0},{3,1},{4,6},{5,7},{6,4},{7,5},{8,10},{9,11},{10,... | collective-permute-start | bytes 884744 | tf_op jit(solution)/shard_map/ppermute | solution.py:818
  10.2 1.5 %query_kernel.1 = (f32[16,768]{1,0:T(8,128)S(1)}, f32[1,768]{1,0:T(1,128)S(1)}) custom-call(s32[2]{0:T(128)S(1)} %pad_add_fusion.scal, f32[8,768]{1,0:T(8,128)S(1)} %add.39.since.part_a, f32[8,768]{1,0:T(8,128)S(1)} %collective-permute-done.1.part_b, bf16[768]{0:T(1024)(128)(2,1)} %start.7, f32[768]{0:T(1024)} %g_cross.5, bf16[192,768]{1,0:T(8,128)(2,1)} %bitcast.12, ...), custom_call_target="tpu_custom_call" | custom-call | tf_op jit(solution)/shard_map/query_kernel/pallas_call | solution.py:793
  11.7 1.2 collective-permute-done.2
  13.0 0.9 collective-permute-start.3
  13.9 3.4 %load_kernel.3._ = bf16[96,128,768]{2,1,0:T(8,128)(2,1)S(1)} custom-call(bf16[96,128,768]{2,1,0:T(8,128)(2,1)} %enc.5, f32[16,768]{1,0:T(8,128)S(1)} %add.40.since.qa, s32[2]{0:T(128)S(1)} %pad_add_fusion.scal, bf16[96,128,768]{2,1,0:T(8,128)(2,1)S(1)} %load_kernel.2.refs_0_), custom_call_target="tpu_custom_call", output_to_operand_aliasing={{}: (3, {})} | custom-call | tf_op jit(solution)/shard_map/load_kernel/pallas_call | solution.py:884
  17.3 1.5 %collective-permute-done.3.qb = f32[16,768]{1,0:T(8,128)S(1)} collective-permute-done((f32[16,768]{1,0:T(8,128)S(1)}, f32[16,768]{1,0:T(8,128)S(1)}, u32[]{:S(2)}, u32[]{:S(2)}) %collective-permute-start.3) | collective-permute-done | bytes 49184 | tf_op jit(solution)/shard_map/ppermute | solution.py:818
  19.4 6.2 %attend_kernel.1 = (bf16[96,128,768]{2,1,0:T(8,128)(2,1)S(1)}, f32[96,16,128]{2,1,0:T(8,128)S(1)}, f32[6,1536,128]{2,1,0:T(8,128)S(1)}, bf16[96,128]{1,0:T(8,128)(2,1)S(1)}) custom-call(s32[2]{0:T(128)S(1)} %pad_add_fusion.scal, s32[8]{0:T(128)S(1)} %copy-done.12, s32[384]{0:T(512)S(1)} %copy-done.15, ...), custom_call_target="tpu_custom_call", output_to_operand_aliasing={{0}: (6, {})} | custom-call | tf_op jit(solution)/shard_map/attend_kernel/pallas_call | solution.py:793
  25.6 2.7 %collective-permute-done.6.by2 = bf16[192,768]{1,0:T(8,128)(2,1)S(1)} collective-permute-done((bf16[192,768]{1,0:T(8,128)(2,1)S(1)}, bf16[192,768]{1,0:T(8,128)(2,1)S(1)}, u32[]{:S(2)}, u32[]{:S(2)}) %collective-permute-start.6) | collective-permute-done | bytes 294944 | tf_op jit(solution)/shard_map/ppermute | solution.py:818
  28.2 1.8 %project_kernel.1 = (bf16[96,896]{1,0:T(8,128)(2,1)S(1)}, bf16[12,96,768]{2,1,0:T(8,128)(2,1)S(1)}, bf16[768,768]{1,0:T(8,128)(2,1)S(1)}) custom-call(s32[2]{0:T(128)S(1)} %pad_add_fusion.scal, f32[6,1536,128]{2,1,0:T(8,128)S(1)} %get-tuple-element.149.summed, bf16[96,128]{1,0:T(8,128)(2,1)S(1)} %get-tuple-element.150.extra, bf16[192,768]{1,0:T(8,128)(2,1)S(1)} %bitcast.20, ...), custom_call_target="tpu_custom_call" | custom-call | tf_op jit(solution)/shard_map/project_kernel/pallas_call | solution.py:793
  30.1 0.5 collective-permute-start.10
  30.7 0.8 collective-permute-done.8.other
  31.5 1.0 merge_kernel.1.own
  32.9 0.6 target_kernel.1
  33.6 0.6 arrange_kernel.1.wo.wout
  34.3 4.7 %collective-permute-done.9.other = bf16[96,896]{1,0:T(8,128)(2,1)S(1)} collective-permute-done((bf16[96,896]{1,0:T(8,128)(2,1)S(1)}, bf16[96,896]{1,0:T(8,128)(2,1)S(1)}, u32[]{:S(2)}, u32[]{:S(2)}) %collective-permute-start.9) | collective-permute-done | bytes 172064 | tf_op jit(solution)/shard_map/ppermute | solution.py:818
  39.0 1.9 %forward_kernel.1 = (bf16[48,768]{1,0:T(8,128)(2,1)S(1)}, f32[96,768]{1,0:T(8,128)S(1)}, f32[96,128]{1,0:T(8,128)S(1)}, f32[96,768]{1,0:T(8,128)S(1)}, f32[96,76...) custom-call(s32[2]{0:T(128)S(1)} %pad_add_fusion.scal, bf16[96,896]{1,0:T(8,128)(2,1)S(1)} %merge_kernel.1.own, ...), custom_call_target="tpu_custom_call" | custom-call | tf_op jit(solution)/shard_map/forward_kernel/pallas_call | solution.py:793
  41.1 1.4 %collective-permute-done.12 = bf16[96,768]{1,0:T(8,128)(2,1)S(1)} collective-permute-done((bf16[96,768]{1,0:T(8,128)(2,1)S(1)}, bf16[96,768]{1,0:T(8,128)(2,1)S(1)}, u32[]{:S(2)}, u32[]{:S(2)}) %collective-permute-start.12) | collective-permute-done | bytes 147488 | tf_op jit(solution)/shard_map/ppermute | solution.py:818
  42.9 5.5 %collective-permute-done.13.part_b = bf16[96,768]{1,0:T(8,128)(2,1)S(1)} collective-permute-done((bf16[96,768]{1,0:T(8,128)(2,1)S(1)}, bf16[96,768]{1,0:T(8,128)(2,1)S(1)}, u32[]{:S(2)}, u32[]{:S(2)}) %collective-permute-start.13) | collective-permute-done | bytes 147488 | tf_op jit(solution)/shard_map/ppermute | solution.py:818
  48.4 0.5 score_kernel.1
  48.9 0.9 down_kernel.1
  49.9 1.4 %collective-permute-done.15 = bf16[96,768]{1,0:T(8,128)(2,1)S(1)} collective-permute-done((bf16[96,768]{1,0:T(8,128)(2,1)S(1)}, bf16[96,768]{1,0:T(8,128)(2,1)S(1)}, u32[]{:S(2)}, u32[]{:S(2)}) %collective-permute-start.15) | collective-permute-done | bytes 147488 | tf_op jit(solution)/shard_map/ppermute | solution.py:818
  51.3 0.9 share_kernel.1
  52.8 2.7 %collective-permute-start.14 = (bf16[48,896]{1,0:T(8,128)(2,1)S(1)}, bf16[48,896]{1,0:T(8,128)(2,1)S(1)}, u32[]{:S(2)}, u32[]{:S(2)}) collective-permute-start(bf16[48,896]{1,0:T(8,128)(2,1)S(1)} %get-tuple-element.175), channel_id=1, source_target_pairs={{0,16},{4,20},{8,24},{12,28},{16,0},{20,4},{24,8},{28,12},{1,17},{... | collective-permute-start | bytes 258056 | tf_op jit(solution)/shard_map/ppermute | solution.py:818
  55.6 0.6 away_kernel.1
  56.2 2.3 %collective-permute-done.16.part_b = bf16[96,768]{1,0:T(8,128)(2,1)S(1)} collective-permute-done((bf16[96,768]{1,0:T(8,128)(2,1)S(1)}, bf16[96,768]{1,0:T(8,128)(2,1)S(1)}, u32[]{:S(2)}, u32[]{:S(2)}) %collective-permute-start.16) | collective-permute-done | bytes 147488 | tf_op jit(solution)/shard_map/ppermute | solution.py:818
  58.6 1.5 %context_kernel.1 = (bf16[96,768]{1,0:T(8,128)(2,1)S(1)}, bf16[48,1536]{1,0:T(8,128)(2,1)S(1)}, bf16[96,768]{1,0:T(8,128)(2,1)S(1)}, bf16[96,192]{1,0:T(8,128)(2...) custom-call(s32[2]{0:T(128)S(1)} %pad_add_fusion.scal, bf16[96,768]{1,0:T(8,128)(2,1)S(1)} %add_convert_fusion.2.part_a, ...), custom_call_target="tpu_custom_call" | custom-call | tf_op jit(solution)/shard_map/context_kernel/pallas_call | solution.py:793
  60.1 1.6 %collective-permute-start.18 = (bf16[96,896]{1,0:T(8,128)(2,1)S(1)}, bf16[96,896]{1,0:T(8,128)(2,1)S(1)}, u32[]{:S(2)}, u32[]{:S(2)}) collective-permute-start(bf16[96,896]{1,0:T(8,128)(2,1)S(1)} %pad_maximum_fusion.3), channel_id=1, source_target_pairs={{0,8},{4,12},{8,0},{12,4},{16,24},{20,28},{24,16},{28,20},{1,9},{5... | collective-permute-start | bytes 516104 | tf_op jit(solution)/shard_map/ppermute | solution.py:818
  61.8 0.8 collective-permute-start.20
  62.5 3.7 %collective-permute-start.21 = (bf16[48,1536]{1,0:T(8,128)(2,1)S(1)}, bf16[48,1536]{1,0:T(8,128)(2,1)S(1)}, u32[]{:S(2)}, u32[]{:S(2)}) collective-permute-start(bf16[48,1536]{1,0:T(8,128)(2,1)S(1)} %get-tuple-element.187), channel_id=1, source_target_pairs={{0,16},{4,20},{8,24},{12,28},{16,0},{20,4},{24,8},{28,12},{1,17},{... | collective-permute-start | bytes 442376 | tf_op jit(solution)/shard_map/ppermute | solution.py:818
  66.2 3.3 %back_kernel.2 = (bf16[96,32,128]{2,1,0:T(8,128)(2,1)S(1)}, bf16[96,16,768]{2,1,0:T(8,128)(2,1)S(1)}) custom-call(s32[2]{0:T(128)S(1)} %pad_add_fusion.scal, s32[8]{0:T(128)S(1)} %copy-done.12, bf16[96,128,768]{2,1,0:T(8,128)(2,1)S(1)} %get-tuple-element.177.enc, f32[96,16,128]{2,1,0:T(8,128)S(1)} %get-tuple-element.178.p, ...), custom_call_target="tpu_custom_call" | custom-call | tf_op jit(solution)/shard_map/back_kernel/pallas_call | solution.py:793
  69.6 1.6 %collective-permute-start.19 = (bf16[192,896]{1,0:T(8,128)(2,1)S(1)}, bf16[192,896]{1,0:T(8,128)(2,1)S(1)}, u32[]{:S(2)}, u32[]{:S(2)}) collective-permute-start(bf16[192,896]{1,0:T(8,128)(2,1)S(1)} %pad_maximum_fusion.1), channel_id=1, source_target_pairs={{0,4},{4,0},{8,12},{12,8},{16,20},{20,16},{24,28},{28,24},{1,5},{5... | collective-permute-start | bytes 1032200 | tf_op jit(solution)/shard_map/ppermute | solution.py:818
  71.2 3.6 %back_kernel.3 = (bf16[96,32,128]{2,1,0:T(8,128)(2,1)S(1)}, bf16[96,16,768]{2,1,0:T(8,128)(2,1)S(1)}) custom-call(s32[2]{0:T(128)S(1)} %pad_add_fusion.scal, s32[8]{0:T(128)S(1)} %copy-done.12, bf16[96,128,768]{2,1,0:T(8,128)(2,1)S(1)} %get-tuple-element.177.enc, ...), custom_call_target="tpu_custom_call", output_to_operand_aliasing={{0}: (8, {}), {1}: (9, {})} | custom-call | tf_op jit(solution)/shard_map/back_kernel/pallas_call | solution.py:793
  74.8 3.7 %collective-permute-done.19 = bf16[192,896]{1,0:T(8,128)(2,1)S(1)} collective-permute-done((bf16[192,896]{1,0:T(8,128)(2,1)S(1)}, bf16[192,896]{1,0:T(8,128)(2,1)S(1)}, u32[]{:S(2)}, u32[]{:S(2)}) %collective-permute-start.19) | collective-permute-done | bytes 344096 | tf_op jit(solution)/shard_map/ppermute | solution.py:818
  79.1 1.4 %list_kernel.1 = (f32[384]{0:T(512)}, f32[1,1]{1,0:T(1,128)}, f32[1,384]{1,0:T(1,128)S(1)}, f32[8,128]{1,0:T(8,128)S(1)}) custom-call(s32[2]{0:T(128)S(1)} %pad_add_fusion.scal, s32[8]{0:T(128)S(1)} %copy-done.12, bf16[384,896]{1,0:T(8,128)(2,1)S(1)} %constant_dynamic-update-slice_fusion.rows.c_own, f32[24,384]{1,0:T(8,128)S(1)} %get-tuple-element.189.targets, ...), custom_call_target="tpu_custom_call" | custom-call | tf_op jit(solution)/shard_map/list_kernel/pallas_call | solution.py:793
  80.4 1.0 value_kernel.1
  81.5 2.7 %key_sum_kernel.1 = f32[16,768]{1,0:T(8,128)S(1)} custom-call(s32[2]{0:T(128)S(1)} %pad_add_fusion.scal, s32[8]{0:T(128)S(1)} %copy-done.12, f32[8,128]{1,0:T(8,128)S(1)} %get-tuple-element.214.ds, bf16[96,128,768]{2,1,0:T(8,128)(2,1)S(1)} %get-tuple-element.177.enc, bf16[96,32,128]{2,1,0:T(8,128)(2,1)S(1)} %get-tuple-element.197.dap, ...), custom_call_target="tpu_custom_call" | custom-call | tf_op jit(solution)/shard_map/key_sum_kernel/pallas_call | solution.py:793
  84.2 0.5 collective-permute-start.22
  84.7 1.5 %collective-permute-start.26 = (bf16[192,768]{1,0:T(8,128)(2,1)S(1)}, bf16[192,768]{1,0:T(8,128)(2,1)S(1)}, u32[]{:S(2)}, u32[]{:S(2)}) collective-permute-start(bf16[192,768]{1,0:T(8,128)(2,1)S(1)} %value_kernel.1), channel_id=1, source_target_pairs={{0,4},{4,0},{8,12},{12,8},{16,20},{20,16},{24,28},{28,24},{1,5},{5... | collective-permute-start | bytes 884744 | tf_op jit(solution)/shard_map/ppermute | solution.py:818
  86.6 3.4 %enc_grad_kernel.3.refs_0_ = bf16[96,128,768]{2,1,0:T(8,128)(2,1)} custom-call(f32[8,128]{1,0:T(8,128)S(1)} %get-tuple-element.214.ds, f32[16,768]{1,0:T(8,128)S(1)} %add.40.since.qa, f32[16,768]{1,0:T(8,128)S(1)} %collective-permute-done.3.qb, bf16[96,32,128]{2,1,0:T(8,128)(2,1)S(1)} %get-tuple-element.197.dap, bf16[96,16,768]{2,1,0:T(8,128)(2,1)S(1)} %get-tuple-element.205.vd), custom_call_target="tpu_custom_call" | custom-call | tf_op jit(solution)/shard_map/enc_grad_kernel/pallas_call | solution.py:793
  90.0 1.7 %collective-permute-done.24 = f32[16,768]{1,0:T(8,128)S(1)} collective-permute-done((f32[16,768]{1,0:T(8,128)S(1)}, f32[16,768]{1,0:T(8,128)S(1)}, u32[]{:S(2)}, u32[]{:S(2)}) %collective-permute-start.24) | collective-permute-done | bytes 49184 | tf_op jit(solution)/shard_map/ppermute | solution.py:818
  91.7 1.3 %collective-permute-start.25 = (f32[16,768]{1,0:T(8,128)S(1)}, f32[16,768]{1,0:T(8,128)S(1)}, u32[]{:S(2)}, u32[]{:S(2)}) collective-permute-start(f32[16,768]{1,0:T(8,128)S(1)} %add.44), channel_id=1, source_target_pairs={{0,8},{4,12},{8,0},{12,4},{16,24},{20,28},{24,16},{28,20},{1,9},{5... | collective-permute-start | bytes 147464 | tf_op jit(solution)/shard_map/ppermute | solution.py:818
  93.0 0.9 collective-permute-start.30
  94.0 3.4 %enc_grad_kernel.4.refs_0_ = bf16[96,128,768]{2,1,0:T(8,128)(2,1)} custom-call(f32[8,128]{1,0:T(8,128)S(1)} %get-tuple-element.214.ds, f32[16,768]{1,0:T(8,128)S(1)} %add.40.since.qa, f32[16,768]{1,0:T(8,128)S(1)} %collective-permute-done.3.qb, bf16[96,32,128]{2,1,0:T(8,128)(2,1)S(1)} %get-tuple-element.197.dap, ...), custom_call_target="tpu_custom_call", output_to_operand_aliasing={{}: (5, {})} | custom-call | tf_op jit(solution)/shard_map/enc_grad_kernel/pallas_call | solution.py:793
  97.4 1.8 %collective-permute-start.28 = (f32[16,768]{1,0:T(8,128)S(1)}, f32[16,768]{1,0:T(8,128)S(1)}, u32[]{:S(2)}, u32[]{:S(2)}) collective-permute-start(f32[16,768]{1,0:T(8,128)S(1)} %add.45), channel_id=1, source_target_pairs={{0,2},{1,3},{2,0},{3,1},{4,6},{5,7},{6,4},{7,5},{8,10},{9,11},{10,... | collective-permute-start | bytes 147464 | tf_op jit(solution)/shard_map/ppermute | solution.py:818
  99.3 1.1 collective-permute-start.31
  100.4 3.4 %enc_grad_kernel.5 = bf16[96,128,768]{2,1,0:T(8,128)(2,1)} custom-call(f32[8,128]{1,0:T(8,128)S(1)} %get-tuple-element.214.ds, f32[16,768]{1,0:T(8,128)S(1)} %add.40.since.qa, f32[16,768]{1,0:T(8,128)S(1)} %collective-permute-done.3.qb, bf16[96,32,128]{2,1,0:T(8,128)(2,1)S(1)} %get-tuple-element.197.dap, ...), custom_call_target="tpu_custom_call", output_to_operand_aliasing={{}: (5, {})} | custom-call | tf_op jit(solution)/shard_map/enc_grad_kernel/pallas_call | solution.py:793
  103.8 1.2 collective-permute-start.29
  105.0 3.4 %weights_before_kernel.1 = (bf16[384,768]{1,0:T(8,128)(2,1)S(1)}, bf16[384,768]{1,0:T(8,128)(2,1)S(1)}, f32[384,768]{1,0:T(8,128)S(1)}, bf16[384,192]{1,0:T(8,128)(2,1)S(1)}) custom-call(s32[2]{0:T(128)S(1)} %pad_add_fusion.scal, s32[8]{0:T(128)S(1)} %copy-done.12, bf16[384,896]{1,0:T(8,128)(2,1)S(1)} %constant_dynamic-update-slice_fusion.rows.c_own, ...), custom_call_target="tpu_custom_call" | custom-call | tf_op jit(solution)/shard_map/weights_before_kernel/pallas_call | solution.py:793
  108.7 1.7 %collective-permute-start.37 = (bf16[192,768]{1,0:T(8,128)(2,1)S(1)}, bf16[192,768]{1,0:T(8,128)(2,1)S(1)}, u32[]{:S(2)}, u32[]{:S(2)}) collective-permute-start(bf16[192,768]{1,0:T(8,128)(2,1)S(1)} %add_convert_fusion), channel_id=1, source_target_pairs={{0,16},{4,20},{8,24},{12,28},{16,0},{20,4},{24,8},{28,12},{1,17},{... | collective-permute-start | bytes 884744 | tf_op jit(solution)/shard_map/ppermute | solution.py:818
  110.5 2.1 %key_kernel.1 = (f32[192,768]{1,0:T(8,128)}, f32[192,768]{1,0:T(8,128)}, f32[8,768]{1,0:T(8,128)S(1)}) custom-call(s32[2]{0:T(128)S(1)} %pad_add_fusion.scal, f32[16,768]{1,0:T(8,128)S(1)} %add.46.sum_a, f32[16,768]{1,0:T(8,128)S(1)} %collective-permute-done.29.sum_b, f32[1,768]{1,0:T(1,128)S(1)} %get-tuple-element.157.h1, f32[768]{0:T(1024)S(1)} %copy-done.9, ...), custom_call_target="tpu_custom_call" | custom-call | tf_op jit(solution)/shard_map/key_kernel/pallas_call | solution.py:793
  112.8 1.0 collective-permute-done.32
  113.8 1.0 collective-permute-start.34
  114.8 5.2 %weights_kernel.1 = (f32[768,768]{1,0:T(8,128)}, bf16[384,1536]{1,0:T(8,128)(2,1)S(1)}) custom-call(s32[2]{0:T(128)S(1)} %pad_add_fusion.scal, s32[8]{0:T(128)S(1)} %copy-done.12, bf16[384,768]{1,0:T(8,128)(2,1)S(1)} %get-tuple-element.230.y3, f32[384,768]{1,0:T(8,128)S(1)} %get-tuple-element.231.slope, ...), custom_call_target="tpu_custom_call" | custom-call | tf_op jit(solution)/shard_map/weights_kernel/pallas_call | solution.py:793
  120.0 1.9 %hidden_kernel.1 = (f32[1,768]{1,0:T(1,128)S(1)}, f32[192,768]{1,0:T(8,128)}, f32[192,768]{1,0:T(8,128)}, f32[8,768]{1,0:T(8,128)S(1)}, f32[768]{0:T(1024)}, /*i...) custom-call(f32[8,768]{1,0:T(8,128)S(1)} %add.48.part_a, f32[8,768]{1,0:T(8,128)S(1)} %collective-permute-done.34.part_b, ...), custom_call_target="tpu_custom_call" | custom-call | tf_op jit(solution)/shard_map/hidden_kernel/pallas_call | solution.py:793
  121.9 1.2 collective-permute-done.35
  123.1 1.1 collective-permute-start.36
  124.2 2.6 %weights_after_kernel.1 = (f32[768,768]{1,0:T(8,128)}, f32[192,768]{1,0:T(8,128)}) custom-call(bf16[384,768]{1,0:T(8,128)(2,1)S(1)} %get-tuple-element.238.u, bf16[384,192]{1,0:T(8,128)(2,1)S(1)} %get-tuple-element.239.c, bf16[384,1536]{1,0:T(8,128)(2,1)S(1)} %get-tuple-element.240.grads), custom_call_target="tpu_custom_call" | custom-call | tf_op jit(solution)/shard_map/weights_after_kernel/pallas_call | solution.py:793
  126.9 0.9 add_bitcast_fusion
  127.8 0.8 start_kernel.1
  (103 shorter events, 4.4 us)
Async XLA Ops:
  2.2 1.3 %collective-permute-start = (f32[8,768]{1,0:T(8,128)S(1)}, f32[8,768]{1,0:T(8,128)S(1)}, u32[]{:S(2)}, u32[]{:S(2)}) collective-permute-start(f32[8,768]{1,0:T(8,128)S(1)} %self_kernel.1), channel_id=1, source_target_pairs={{0,1},{1,0},{2,3},{3,2},{4,5},{5,4},{6,7},{7,6},{8,9},{9,8},{10,11... | collective-permute-start | bytes 73736 | tf_op jit(solution)/shard_map/ppermute | solution.py:818
  3.5 5.4 %collective-permute-start.1 = (f32[8,768]{1,0:T(8,128)S(1)}, f32[8,768]{1,0:T(8,128)S(1)}, u32[]{:S(2)}, u32[]{:S(2)}) collective-permute-start(f32[8,768]{1,0:T(8,128)S(1)} %add.39.since.part_a), channel_id=1, source_target_pairs={{0,2},{1,3},{2,0},{3,1},{4,6},{5,7},{6,4},{7,5},{8,10},{9,11},{10,... | collective-permute-start | bytes 73736 | tf_op jit(solution)/shard_map/ppermute | solution.py:818
  6.4 2.5 %copy-start.7 = (bf16[768,192]{0,1:T(8,128)(2,1)S(1)}, bf16[768,192]{0,1:T(8,128)(2,1)}, u32[]{:S(2)}) copy-start(bf16[768,192]{0,1:T(8,128)(2,1)} %param.32) | copy-start | bytes 884740
  8.9 9.9 %collective-permute-start.4 = (bf16[192,768]{1,0:T(8,128)(2,1)S(1)}, bf16[192,768]{1,0:T(8,128)(2,1)S(1)}, u32[]{:S(2)}, u32[]{:S(2)}) collective-permute-start(bf16[192,768]{1,0:T(8,128)(2,1)S(1)} %bitcast.18), channel_id=1, source_target_pairs={{0,2},{1,3},{2,0},{3,1},{4,6},{5,7},{6,4},{7,5},{8,10},{9,11},{10,... | collective-permute-start | bytes 884744 | tf_op jit(solution)/shard_map/ppermute | solution.py:818
  11.7 1.3 collective-permute-start.2
  13.0 5.8 %copy-start.2 = (bf16[192,768]{1,0:T(8,128)(2,1)S(1)}, bf16[192,768]{1,0:T(8,128)(2,1)}, u32[]{:S(2)}) copy-start(bf16[192,768]{1,0:T(8,128)(2,1)} %wo_own.1) | copy-start | bytes 884740
  13.0 6.4 %copy-start.12 = (s32[8]{0:T(128)S(1)}, s32[8]{0:T(128)}, u32[]{:S(2)}) copy-start(s32[8]{0:T(128)} %sizes.13) | copy-start | bytes 100
  13.0 6.4 %copy-start.15 = (s32[384]{0:T(512)S(1)}, s32[384]{0:T(512)}, u32[]{:S(2)}) copy-start(s32[384]{0:T(512)} %lengths.1) | copy-start | bytes 4612
  13.0 5.8 %collective-permute-start.3 = (f32[16,768]{1,0:T(8,128)S(1)}, f32[16,768]{1,0:T(8,128)S(1)}, u32[]{:S(2)}, u32[]{:S(2)}) collective-permute-start(f32[16,768]{1,0:T(8,128)S(1)} %add.40.since.qa), channel_id=1, source_target_pairs={{0,2},{1,3},{2,0},{3,1},{4,6},{5,7},{6,4},{7,5},{8,10},{9,11},{10,... | collective-permute-start | bytes 147464 | tf_op jit(solution)/shard_map/ppermute | solution.py:818
  18.8 6.8 %collective-permute-start.5 = (bf16[192,768]{1,0:T(8,128)(2,1)S(1)}, bf16[192,768]{1,0:T(8,128)(2,1)S(1)}, u32[]{:S(2)}, u32[]{:S(2)}) collective-permute-start(bf16[192,768]{1,0:T(8,128)(2,1)S(1)} %collective-permute-done.4.by2), channel_id=1, source_target_pairs={{0,1},{1,0},{2,3},{3,2},{4,5},{5,4},{6,7},{7,6},{8,9},{9,8},{10,11... | collective-permute-start | bytes 884744 | tf_op jit(solution)/shard_map/ppermute | solution.py:818
  18.8 9.4 %collective-permute-start.6 = (bf16[192,768]{1,0:T(8,128)(2,1)S(1)}, bf16[192,768]{1,0:T(8,128)(2,1)S(1)}, u32[]{:S(2)}, u32[]{:S(2)}) collective-permute-start(bf16[192,768]{1,0:T(8,128)(2,1)S(1)} %copy-done.2), channel_id=1, source_target_pairs={{0,2},{1,3},{2,0},{3,1},{4,6},{5,7},{6,4},{7,5},{8,10},{9,11},{10,... | collective-permute-start | bytes 884744 | tf_op jit(solution)/shard_map/ppermute | solution.py:818
  19.2 9.0 %collective-permute-start.7 = (bf16[192,768]{1,0:T(8,128)(2,1)S(1)}, bf16[192,768]{1,0:T(8,128)(2,1)S(1)}, u32[]{:S(2)}, u32[]{:S(2)}) collective-permute-start(bf16[192,768]{1,0:T(8,128)(2,1)S(1)} %bitcast.19), channel_id=1, source_target_pairs={{0,1},{1,0},{2,3},{3,2},{4,5},{5,4},{6,7},{7,6},{8,9},{9,8},{10,11... | collective-permute-start | bytes 884744 | tf_op jit(solution)/shard_map/ppermute | solution.py:818
  28.2 4.7 %copy-start.16 = (f32[384]{0:T(512)S(1)}, f32[384]{0:T(512)}, u32[]{:S(2)}) copy-start(f32[384]{0:T(512)} %rel.1) | copy-start | bytes 4612
  28.2 4.7 %copy-start.17 = (s32[24]{0:T(128)S(1)}, s32[24]{0:T(128)}, u32[]{:S(2)}) copy-start(s32[24]{0:T(128)} %lens.1) | copy-start | bytes 292
  30.1 1.5 %collective-permute-start.8 = (bf16[96,896]{1,0:T(8,128)(2,1)S(1)}, bf16[96,896]{1,0:T(8,128)(2,1)S(1)}, u32[]{:S(2)}, u32[]{:S(2)}) collective-permute-start(bf16[96,896]{1,0:T(8,128)(2,1)S(1)} %get-tuple-element.152.own.first), channel_id=1, source_target_pairs={{0,1},{1,0},{2,3},{3,2},{4,5},{5,4},{6,7},{7,6},{8,9},{9,8},{10,11... | collective-permute-start | bytes 516104 | tf_op jit(solution)/shard_map/ppermute | solution.py:818
  30.1 3.5 %collective-permute-start.10 = (bf16[192,768]{1,0:T(8,128)(2,1)S(1)}, bf16[192,768]{1,0:T(8,128)(2,1)S(1)}, u32[]{:S(2)}, u32[]{:S(2)}) collective-permute-start(bf16[192,768]{1,0:T(8,128)(2,1)S(1)} %copy-done.2), channel_id=1, source_target_pairs={{0,1},{1,0},{2,3},{3,2},{4,5},{5,4},{6,7},{7,6},{8,9},{9,8},{10,11... | collective-permute-start | bytes 884744 | tf_op jit(solution)/shard_map/ppermute | solution.py:818
  30.6 3.0 %collective-permute-start.11 = (bf16[192,768]{1,0:T(8,128)(2,1)S(1)}, bf16[192,768]{1,0:T(8,128)(2,1)S(1)}, u32[]{:S(2)}, u32[]{:S(2)}) collective-permute-start(bf16[192,768]{1,0:T(8,128)(2,1)S(1)} %collective-permute-done.6.by2), channel_id=1, source_target_pairs={{0,1},{1,0},{2,3},{3,2},{4,5},{5,4},{6,7},{7,6},{8,9},{9,8},{10,11... | collective-permute-start | bytes 884744 | tf_op jit(solution)/shard_map/ppermute | solution.py:818
  32.5 6.5 %collective-permute-start.9 = (bf16[96,896]{1,0:T(8,128)(2,1)S(1)}, bf16[96,896]{1,0:T(8,128)(2,1)S(1)}, u32[]{:S(2)}, u32[]{:S(2)}) collective-permute-start(bf16[96,896]{1,0:T(8,128)(2,1)S(1)} %merge_kernel.1.own), channel_id=1, source_target_pairs={{0,2},{1,3},{2,0},{3,1},{4,6},{5,7},{6,4},{7,5},{8,10},{9,11},{10,... | collective-permute-start | bytes 516104 | tf_op jit(solution)/shard_map/ppermute | solution.py:818
  33.6 5.4 %copy-start = (bf16[768,768]{1,0:T(8,128)(2,1)S(1)}, bf16[768,768]{1,0:T(8,128)(2,1)}, u32[]{:S(2)}) copy-start(bf16[768,768]{1,0:T(8,128)(2,1)} %win.5) | copy-start | bytes 3538948
  33.6 5.4 %copy-start.1 = (bf16[768,768]{1,0:T(8,128)(2,1)S(1)}, bf16[768,768]{1,0:T(8,128)(2,1)}, u32[]{:S(2)}) copy-start(bf16[768,768]{1,0:T(8,128)(2,1)} %wdown.5) | copy-start | bytes 3538948
  33.6 5.4 %copy-start.8 = (f32[768]{0:T(1024)S(1)}, f32[768]{0:T(1024)}, u32[]{:S(2)}) copy-start(f32[768]{0:T(1024)} %g_ff.5) | copy-start | bytes 9220
  39.0 9.4 %copy-start.13 = (f32[768]{0:T(1024)S(1)}, f32[768]{0:T(1024)}, u32[]{:S(2)}) copy-start(f32[768]{0:T(1024)} %g_final.3) | copy-start | bytes 9220
  39.0 9.4 %copy-start.14 = (bf16[768]{0:T(1024)(128)(2,1)S(1)}, bf16[768]{0:T(1024)(128)(2,1)}, u32[]{:S(2)}) copy-start(bf16[768]{0:T(1024)(128)(2,1)} %row.3) | copy-start | bytes 4612
  41.0 1.4 %collective-permute-start.12 = (bf16[96,768]{1,0:T(8,128)(2,1)S(1)}, bf16[96,768]{1,0:T(8,128)(2,1)S(1)}, u32[]{:S(2)}, u32[]{:S(2)}) collective-permute-start(bf16[96,768]{1,0:T(8,128)(2,1)S(1)} %get-tuple-element.159), channel_id=1, source_target_pairs={{0,1},{1,0},{2,3},{3,2},{4,5},{5,4},{6,7},{7,6},{8,9},{9,8},{10,11... | collective-permute-start | bytes 442376 | tf_op jit(solution)/shard_map/ppermute | solution.py:818
  42.5 6.0 %collective-permute-start.13 = (bf16[96,768]{1,0:T(8,128)(2,1)S(1)}, bf16[96,768]{1,0:T(8,128)(2,1)S(1)}, u32[]{:S(2)}, u32[]{:S(2)}) collective-permute-start(bf16[96,768]{1,0:T(8,128)(2,1)S(1)} %add_convert_fusion.3.part_a), channel_id=1, source_target_pairs={{0,2},{1,3},{2,0},{3,1},{4,6},{5,7},{6,4},{7,5},{8,10},{9,11},{10,... | collective-permute-start | bytes 442376 | tf_op jit(solution)/shard_map/ppermute | solution.py:818
  49.9 1.4 %collective-permute-start.15 = (bf16[96,768]{1,0:T(8,128)(2,1)S(1)}, bf16[96,768]{1,0:T(8,128)(2,1)S(1)}, u32[]{:S(2)}, u32[]{:S(2)}) collective-permute-start(bf16[96,768]{1,0:T(8,128)(2,1)S(1)} %down_kernel.1), channel_id=1, source_target_pairs={{0,1},{1,0},{2,3},{3,2},{4,5},{5,4},{6,7},{7,6},{8,9},{9,8},{10,11... | collective-permute-start | bytes 442376 | tf_op jit(solution)/shard_map/ppermute | solution.py:818
  52.3 3.3 %collective-permute-start.17 = (bf16[2,3,96,768]{3,2,1,0:T(8,128)(2,1)S(1)}, bf16[2,3,96,768]{3,2,1,0:T(8,128)(2,1)S(1)}, u32[]{:S(2)}, u32[]{:S(2)}) collective-permute-start(bf16[2,3,96,768]{3,2,1,0:T(8,128)(2,1)S(1)} %get-tuple-element.170), channel_id=1, source_target_pairs={{0,1},{1,0},{2,3},{3,2},{4,5},{5,4},{6,7},{7,6},{8,9},{9,8},{10,11... | collective-permute-start | bytes 2654216 | tf_op jit(solution)/shard_map/ppermute | solution.py:818
  52.5 6.1 %collective-permute-start.16 = (bf16[96,768]{1,0:T(8,128)(2,1)S(1)}, bf16[96,768]{1,0:T(8,128)(2,1)S(1)}, u32[]{:S(2)}, u32[]{:S(2)}) collective-permute-start(bf16[96,768]{1,0:T(8,128)(2,1)S(1)} %add_convert_fusion.2.part_a), channel_id=1, source_target_pairs={{0,2},{1,3},{2,0},{3,1},{4,6},{5,7},{6,4},{7,5},{8,10},{9,11},{10,... | collective-permute-start | bytes 442376 | tf_op jit(solution)/shard_map/ppermute | solution.py:818
  52.8 7.2 %collective-permute-start.14 = (bf16[48,896]{1,0:T(8,128)(2,1)S(1)}, bf16[48,896]{1,0:T(8,128)(2,1)S(1)}, u32[]{:S(2)}, u32[]{:S(2)}) collective-permute-start(bf16[48,896]{1,0:T(8,128)(2,1)S(1)} %get-tuple-element.175), channel_id=1, source_target_pairs={{0,16},{4,20},{8,24},{12,28},{16,0},{20,4},{24,8},{28,12},{1,17},{... | collective-permute-start | bytes 258056 | tf_op jit(solution)/shard_map/ppermute | solution.py:818
  60.1 9.4 %collective-permute-start.18 = (bf16[96,896]{1,0:T(8,128)(2,1)S(1)}, bf16[96,896]{1,0:T(8,128)(2,1)S(1)}, u32[]{:S(2)}, u32[]{:S(2)}) collective-permute-start(bf16[96,896]{1,0:T(8,128)(2,1)S(1)} %pad_maximum_fusion.3), channel_id=1, source_target_pairs={{0,8},{4,12},{8,0},{12,4},{16,24},{20,28},{24,16},{28,20},{1,9},{5... | collective-permute-start | bytes 516104 | tf_op jit(solution)/shard_map/ppermute | solution.py:818
  61.8 13.1 %collective-permute-start.20 = (bf16[3,96,768]{2,1,0:T(8,128)(2,1)S(1)}, bf16[3,96,768]{2,1,0:T(8,128)(2,1)S(1)}, u32[]{:S(2)}, u32[]{:S(2)}) collective-permute-start(bf16[3,96,768]{2,1,0:T(8,128)(2,1)S(1)} %away_kernel.1), channel_id=1, source_target_pairs={{0,2},{1,3},{2,0},{3,1},{4,6},{5,7},{6,4},{7,5},{8,10},{9,11},{10,... | collective-permute-start | bytes 1327112 | tf_op jit(solution)/shard_map/ppermute | solution.py:818
  62.5 12.3 %collective-permute-start.21 = (bf16[48,1536]{1,0:T(8,128)(2,1)S(1)}, bf16[48,1536]{1,0:T(8,128)(2,1)S(1)}, u32[]{:S(2)}, u32[]{:S(2)}) collective-permute-start(bf16[48,1536]{1,0:T(8,128)(2,1)S(1)} %get-tuple-element.187), channel_id=1, source_target_pairs={{0,16},{4,20},{8,24},{12,28},{16,0},{20,4},{24,8},{28,12},{1,17},{... | collective-permute-start | bytes 442376 | tf_op jit(solution)/shard_map/ppermute | solution.py:818
  69.6 8.9 %collective-permute-start.19 = (bf16[192,896]{1,0:T(8,128)(2,1)S(1)}, bf16[192,896]{1,0:T(8,128)(2,1)S(1)}, u32[]{:S(2)}, u32[]{:S(2)}) collective-permute-start(bf16[192,896]{1,0:T(8,128)(2,1)S(1)} %pad_maximum_fusion.1), channel_id=1, source_target_pairs={{0,4},{4,0},{8,12},{12,8},{16,20},{20,16},{24,28},{28,24},{1,5},{5... | collective-permute-start | bytes 1032200 | tf_op jit(solution)/shard_map/ppermute | solution.py:818
  78.5 7.7 %collective-permute-start.23 = (bf16[96,1536]{1,0:T(8,128)(2,1)S(1)}, bf16[96,1536]{1,0:T(8,128)(2,1)S(1)}, u32[]{:S(2)}, u32[]{:S(2)}) collective-permute-start(bf16[96,1536]{1,0:T(8,128)(2,1)S(1)} %pad_maximum_fusion.2), channel_id=1, source_target_pairs={{0,8},{4,12},{8,0},{12,4},{16,24},{20,28},{24,16},{28,20},{1,9},{5... | collective-permute-start | bytes 884744 | tf_op jit(solution)/shard_map/ppermute | solution.py:818
  79.0 18.4 %collective-permute-start.27 = (bf16[384,896]{1,0:T(8,128)(2,1)S(1)}, bf16[384,896]{1,0:T(8,128)(2,1)S(1)}, u32[]{:S(2)}, u32[]{:S(2)}) collective-permute-start(bf16[384,896]{1,0:T(8,128)(2,1)S(1)} %constant_dynamic-update-slice_fusion.rows.c_own), channel_id=1, source_target_pairs={{0,1},{1,0},{2,3},{3,2},{4,5},{5,4},{6,7},{7,6},{8,9},{9,8},{10,11... | collective-permute-start | bytes 2064392 | tf_op jit(solution)/shard_map/ppermute | solution.py:818
  84.2 2.0 %collective-permute-start.22 = (f32[16,768]{1,0:T(8,128)S(1)}, f32[16,768]{1,0:T(8,128)S(1)}, u32[]{:S(2)}, u32[]{:S(2)}) collective-permute-start(f32[16,768]{1,0:T(8,128)S(1)} %key_sum_kernel.1), channel_id=1, source_target_pairs={{0,1},{1,0},{2,3},{3,2},{4,5},{5,4},{6,7},{7,6},{8,9},{9,8},{10,11... | collective-permute-start | bytes 147464 | tf_op jit(solution)/shard_map/ppermute | solution.py:818
  84.7 12.7 %collective-permute-start.26 = (bf16[192,768]{1,0:T(8,128)(2,1)S(1)}, bf16[192,768]{1,0:T(8,128)(2,1)S(1)}, u32[]{:S(2)}, u32[]{:S(2)}) collective-permute-start(bf16[192,768]{1,0:T(8,128)(2,1)S(1)} %value_kernel.1), channel_id=1, source_target_pairs={{0,4},{4,0},{8,12},{12,8},{16,20},{20,16},{24,28},{28,24},{1,5},{5... | collective-permute-start | bytes 884744 | tf_op jit(solution)/shard_map/ppermute | solution.py:818
  86.2 5.5 %collective-permute-start.24 = (f32[16,768]{1,0:T(8,128)S(1)}, f32[16,768]{1,0:T(8,128)S(1)}, u32[]{:S(2)}, u32[]{:S(2)}) collective-permute-start(f32[16,768]{1,0:T(8,128)S(1)} %add.43), channel_id=1, source_target_pairs={{0,16},{4,20},{8,24},{12,28},{16,0},{20,4},{24,8},{28,12},{1,17},{... | collective-permute-start | bytes 147464 | tf_op jit(solution)/shard_map/ppermute | solution.py:818
  91.7 5.6 %collective-permute-start.25 = (f32[16,768]{1,0:T(8,128)S(1)}, f32[16,768]{1,0:T(8,128)S(1)}, u32[]{:S(2)}, u32[]{:S(2)}) collective-permute-start(f32[16,768]{1,0:T(8,128)S(1)} %add.44), channel_id=1, source_target_pairs={{0,8},{4,12},{8,0},{12,4},{16,24},{20,28},{24,16},{28,20},{1,9},{5... | collective-permute-start | bytes 147464 | tf_op jit(solution)/shard_map/ppermute | solution.py:818
  93.0 15.5 %collective-permute-start.30 = (bf16[192,1536]{1,0:T(8,128)(2,1)S(1)}, bf16[192,1536]{1,0:T(8,128)(2,1)S(1)}, u32[]{:S(2)}, u32[]{:S(2)}) collective-permute-start(bf16[192,1536]{1,0:T(8,128)(2,1)S(1)} %pad_maximum_fusion), channel_id=1, source_target_pairs={{0,4},{4,0},{8,12},{12,8},{16,20},{20,16},{24,28},{28,24},{1,5},{5... | collective-permute-start | bytes 1769480 | tf_op jit(solution)/shard_map/ppermute | solution.py:818
  97.4 6.4 %collective-permute-start.28 = (f32[16,768]{1,0:T(8,128)S(1)}, f32[16,768]{1,0:T(8,128)S(1)}, u32[]{:S(2)}, u32[]{:S(2)}) collective-permute-start(f32[16,768]{1,0:T(8,128)S(1)} %add.45), channel_id=1, source_target_pairs={{0,2},{1,3},{2,0},{3,1},{4,6},{5,7},{6,4},{7,5},{8,10},{9,11},{10,... | collective-permute-start | bytes 147464 | tf_op jit(solution)/shard_map/ppermute | solution.py:818
  99.3 9.2 %collective-permute-start.31 = (bf16[192,768]{1,0:T(8,128)(2,1)S(1)}, bf16[192,768]{1,0:T(8,128)(2,1)S(1)}, u32[]{:S(2)}, u32[]{:S(2)}) collective-permute-start(bf16[192,768]{1,0:T(8,128)(2,1)S(1)} %add_convert_fusion.1), channel_id=1, source_target_pairs={{0,8},{4,12},{8,0},{12,4},{16,24},{20,28},{24,16},{28,20},{1,9},{5... | collective-permute-start | bytes 884744 | tf_op jit(solution)/shard_map/ppermute | solution.py:818
  103.8 4.7 %collective-permute-start.29 = (f32[16,768]{1,0:T(8,128)S(1)}, f32[16,768]{1,0:T(8,128)S(1)}, u32[]{:S(2)}, u32[]{:S(2)}) collective-permute-start(f32[16,768]{1,0:T(8,128)S(1)} %add.46.sum_a), channel_id=1, source_target_pairs={{0,4},{4,0},{8,12},{12,8},{16,20},{20,16},{24,28},{28,24},{1,5},{5... | collective-permute-start | bytes 147464 | tf_op jit(solution)/shard_map/ppermute | solution.py:818
  108.5 2.0 %copy-start.3 = (bf16[768,192]{0,1:T(8,128)(2,1)S(1)}, bf16[768,192]{0,1:T(8,128)(2,1)}, u32[]{:S(2)}) copy-start(bf16[768,192]{0,1:T(8,128)(2,1)} %param.30) | copy-start | bytes 884740
  108.5 2.0 %copy-start.4 = (bf16[768,192]{0,1:T(8,128)(2,1)S(1)}, bf16[768,192]{0,1:T(8,128)(2,1)}, u32[]{:S(2)}) copy-start(bf16[768,192]{0,1:T(8,128)(2,1)} %param.31) | copy-start | bytes 884740
  108.5 2.0 %copy-start.9 = (f32[768]{0:T(1024)S(1)}, f32[768]{0:T(1024)}, u32[]{:S(2)}) copy-start(f32[768]{0:T(1024)} %g_cross.5) | copy-start | bytes 9220
  108.6 5.3 %collective-permute-start.33 = (bf16[384,1536]{1,0:T(8,128)(2,1)S(1)}, bf16[384,1536]{1,0:T(8,128)(2,1)S(1)}, u32[]{:S(2)}, u32[]{:S(2)}) collective-permute-start(bf16[384,1536]{1,0:T(8,128)(2,1)S(1)} %constant_dynamic-update-slice_fusion.4.both_own), channel_id=1, source_target_pairs={{0,1},{1,0},{2,3},{3,2},{4,5},{5,4},{6,7},{7,6},{8,9},{9,8},{10,11... | collective-permute-start | bytes 3538952 | tf_op jit(solution)/shard_map/ppermute | solution.py:818
  108.7 18.0 %collective-permute-start.37 = (bf16[192,768]{1,0:T(8,128)(2,1)S(1)}, bf16[192,768]{1,0:T(8,128)(2,1)S(1)}, u32[]{:S(2)}, u32[]{:S(2)}) collective-permute-start(bf16[192,768]{1,0:T(8,128)(2,1)S(1)} %add_convert_fusion), channel_id=1, source_target_pairs={{0,16},{4,20},{8,24},{12,28},{16,0},{20,4},{24,8},{28,12},{1,17},{... | collective-permute-start | bytes 884744 | tf_op jit(solution)/shard_map/ppermute | solution.py:818
  112.6 1.2 collective-permute-start.32
  113.8 6.1 %collective-permute-start.34 = (f32[8,768]{1,0:T(8,128)S(1)}, f32[8,768]{1,0:T(8,128)S(1)}, u32[]{:S(2)}, u32[]{:S(2)}) collective-permute-start(f32[8,768]{1,0:T(8,128)S(1)} %add.48.part_a), channel_id=1, source_target_pairs={{0,2},{1,3},{2,0},{3,1},{4,6},{5,7},{6,4},{7,5},{8,10},{9,11},{10,... | collective-permute-start | bytes 73736 | tf_op jit(solution)/shard_map/ppermute | solution.py:818
  114.8 5.2 %copy-start.5 = (bf16[768,192]{0,1:T(8,128)(2,1)S(1)}, bf16[768,192]{0,1:T(8,128)(2,1)}, u32[]{:S(2)}) copy-start(bf16[768,192]{0,1:T(8,128)(2,1)} %param.27) | copy-start | bytes 884740
  114.8 5.2 %copy-start.6 = (bf16[192,768]{1,0:T(8,128)(2,1)S(1)}, bf16[192,768]{1,0:T(8,128)(2,1)}, u32[]{:S(2)}) copy-start(bf16[192,768]{1,0:T(8,128)(2,1)} %wos.3) | copy-start | bytes 884740
  114.8 5.2 %copy-start.10 = (f32[768]{0:T(1024)S(1)}, f32[768]{0:T(1024)}, u32[]{:S(2)}) copy-start(f32[768]{0:T(1024)} %g_self.5) | copy-start | bytes 9220
  114.8 5.2 %copy-start.11 = (bf16[768]{0:T(1024)(128)(2,1)S(1)}, bf16[768]{0:T(1024)(128)(2,1)}, u32[]{:S(2)}) copy-start(bf16[768]{0:T(1024)(128)(2,1)} %start.7) | copy-start | bytes 4612
  121.9 1.2 collective-permute-start.35
  123.1 3.8 %collective-permute-start.36 = (f32[8,768]{1,0:T(8,128)S(1)}, f32[8,768]{1,0:T(8,128)S(1)}, u32[]{:S(2)}, u32[]{:S(2)}) collective-permute-start(f32[8,768]{1,0:T(8,128)S(1)} %add.49.part_a), channel_id=1, source_target_pairs={{0,2},{1,3},{2,0},{3,1},{4,6},{5,7},{6,4},{7,5},{8,10},{9,11},{10,... | collective-permute-start | bytes 73736 | tf_op jit(solution)/shard_map/ppermute | solution.py:818

commit v5 on v4

--- a/solution.py
+++ b/solution.py
@@ -15,6 +15,7 @@
 SPAN = 2 * BLOCK
 LANES = 128
 PANELS = D // LANES
+COLUMNS = 256
 PARTS = 4
 
 EPSILON = 1e-06
@@ -392,7 +393,11 @@
     part_out[...] = nt(dz, win[...]).astype(bf16)
 
 
-def target_kernel(lens, rel, target_out, member_out):
+def target_kernel(order, scal, sizes, lens, rel, target_out, member_out, *picks_out):
+    if picks_out:
+        tile, held = picks_out[0].shape
+        for out, pick in zip(picks_out, document_picks(order, tile, scal, sizes, held, 0)):
+            out[...] = pick
     queries, docs = target_out.shape
     relevance = rel[...].reshape(1, docs)
     at = iota((queries, 1), 0)
@@ -639,13 +644,18 @@
         0, groups, one_group, (jnp.int32(0), zero, zero), unroll=groups <= 8
     )
     hit = iota((tile, held), 1) == at
-    mine = (hit & (upper == core)).astype(bf16)
-    theirs = (hit & (upper != core)).astype(bf16)
-
-    def rows(own, other, width):
-        return (nn(mine, own[:, :width]) + nn(theirs, other[:, :width])).astype(bf16)
-
-    return rows
+    return (hit & (upper == core)).astype(bf16), (hit & (upper != core)).astype(bf16)
+
+
+def in_order(picks, own, other, width):
+    mine, theirs = picks
+    return (nn(mine, own[:, :width]) + nn(theirs, other[:, :width])).astype(bf16)
+
+
+def picks_of(order, tile, scal, sizes, held, first, ready):
+    if ready:
+        return tuple(pick[...] for pick in ready)
+    return document_picks(order, tile, scal, sizes, held, first)
 
 
 def ds_column(ds, first, tile):
@@ -670,13 +680,14 @@
 
 
 def weights_before_kernel(
-    order, tile, scal, sizes, c_own, c_other, h1, g_ff, wout, win,
-    y3_out, u_out, slope_out, c_out,
+    order, tile, scal, sizes, c_own, c_other, h1, g_ff, wout, win, *refs
 ):
+    ready, (y3_out, u_out, slope_out, c_out) = refs[:-4], refs[-4:]
+
     def one_tile(first, new):
         here = pl.ds(first, tile)
-        rows = document_picks(order, tile, scal, sizes, c_own.shape[0], first)
-        c = rows(c_own, c_other, D)
+        picks = picks_of(order, tile, scal, sizes, c_own.shape[0], first, ready)
+        c = in_order(picks, c_own, c_other, D)
         h2 = h1[...] + nn(c, wout[...])
         n2, _ = rms_parts(h2)
         y3 = (n2 * row_of(g_ff)).astype(bf16)
@@ -691,32 +702,65 @@
     over_tiles(y3_out.shape[0], tile, one_tile)
 
 
-def weights_kernel(
-    order, tile, scal, sizes, y3, slope, both_own, both_other, ds, wdown,
-    win_out, grads_out,
-):
+def grads_kernel(order, tile, scal, sizes, slope, both_own, both_other, ds, wdown, *refs):
+    ready, (dz_out, both_out) = refs[:-2], refs[-2:]
+
     def one_tile(first, new):
         here = pl.ds(first, tile)
-        rows = document_picks(order, tile, scal, sizes, both_own.shape[0], first)
-        both = rows(both_own, both_other, 2 * D).astype(f32) * ds_column(ds, first, tile)
-        both = both.astype(bf16)
-        grads_out[here] = both
-        dz = (nt(both[:, :D], wdown[...]) * slope[here]).astype(bf16)
-        put(win_out, tn(y3[here], dz), new)
+        picks = picks_of(order, tile, scal, sizes, both_own.shape[0], first, ready)
+        both = in_order(picks, both_own, both_other, 2 * D).astype(f32)
+        both = (both * ds_column(ds, first, tile)).astype(bf16)
+        both_out[here] = both
+        dz_out[here] = (nt(both[:, :D], wdown[...]) * slope[here]).astype(bf16)
 
     over_tiles(ds.shape[1], tile, one_tile)
 
 
-def weights_after_kernel(tile, u, c, grads, wdown_out, wout_out):
-    def one_tile(first, new):
-        here = pl.ds(first, tile)
-        put(wdown_out, tn(u[here], grads[here, :D]), new)
-        put(wout_out, tn(c[here], grads[here, D:]), new)
-
-    over_tiles(u.shape[0], tile, one_tile)
-
-
-def key_kernel(scal, sum_a, sum_b, h1, g_cross, wk, wq, key_out, query_out, part_out):
+def outer_kernel(
+    tile, y3, dz, u, c, both, left1, right1, left2, right2,
+    win_out, wdown_out, wout_out, key_out, query_out, wos_out, wvs_out,
+    win_s, wdown_s, wout_s, key_s, query_s, wos_s, wvs_s, sems,
+):
+    copies = []
+
+    def leave(held, out):
+        copies.append(pltpu.make_async_copy(held, out, sems.at[len(copies)]))
+        copies[-1].start()
+
+    docs = y3.shape[0]
+
+    def total(held, left, right):
+        held[...] = tn(left[:tile], right[:tile])
+        if docs > tile:
+
+            @pl.loop(1, docs // tile)
+            def _(t):
+                here = pl.ds(pl.multiple_of(t * tile, tile), tile)
+                held[...] += tn(left[here], right[here])
+
+    def by_parts(held, out, left, right):
+        for k in range(held.shape[0] // COLUMNS):
+            part = pl.ds(k * COLUMNS, COLUMNS)
+            total(held.at[part], left.at[:, part], right)
+            leave(held.at[part], out.at[part])
+
+    key_s[...] = tn(left1[: 2 * ROWS], right1[: 2 * ROWS])
+    leave(key_s, key_out)
+    query_s[...] = tn(left1[2 * ROWS :], right1[2 * ROWS :])
+    leave(query_s, query_out)
+    wos_s[...] = tn(left2[:ROWS], right2[:ROWS])
+    leave(wos_s, wos_out)
+    wvs_s[...] = tn(left2[ROWS:], right2[ROWS:])
+    leave(wvs_s, wvs_out)
+    total(wout_s, c, both.at[:, D:])
+    leave(wout_s, wout_out)
+    by_parts(win_s, win_out, y3, dz)
+    by_parts(wdown_s, wdown_out, u, both.at[:, :D])
+    for copy in copies:
+        copy.wait()
+
+
+def key_kernel(scal, sum_a, sum_b, h1, g_cross, wk, wq, part_out, left_out, right_out):
     y2, qm = query_parts(scal, h1, g_cross, wq)
     g = sum_a[...] + sum_b[...]
     g = jnp.where(iota((ROWS, D), 0) < HEADS, g, 0.0)
@@ -728,16 +772,16 @@
     first = scal[0] * (width // HEAD_DIM)
     own = iota((ROWS, width), 0) == first + head_of((ROWS, width), 1)
     dq = jnp.sum(jnp.where(own, dq, 0.0), axis=0, keepdims=True)
-    key_out[...] = tn(jnp.concatenate([qm, qm], axis=0), both)
     dq_parts = stack3(dq)
-    query_out[...] = tn(dq_parts, repeat3(y2[0:1]))
+    left_out[...] = jnp.concatenate([qm, qm, dq_parts], axis=0)
+    right_out[...] = jnp.concatenate([both, repeat3(y2[0:1])], axis=0)
     part = jnp.sum(nn(dq_parts, wq[...]), axis=0, keepdims=True)
     part_out[...] = jnp.broadcast_to(part, (8, D))
 
 
 def hidden_kernel(
     part_a, part_b, sum_a, sum_b, h1, g_cross, start, g_self, wos, wvs, g_final, row,
-    dh1_out, wos_out, wvs_out, part_out, cross_out, final_out, row_out, ff_out,
+    dh1_out, part_out, left_out, right_out, cross_out, final_out, row_out, ff_out,
 ):
     y1, s1 = self_parts(start, g_self, wvs)
     dy2 = part_a[0:1] + part_b[0:1]
@@ -747,10 +791,10 @@
     dh1 = sums[HEADS : HEADS + 1] + rms_back(dy2 * row_of(g_cross), n1, r1)
     dh1_out[...] = dh1
     dh1_parts = stack3(dh1)
-    wos_out[...] = tn(repeat3(s1[0:1]), dh1_parts)
     ds1 = jnp.sum(nt(dh1_parts, wos[...]), axis=0, keepdims=True)
     ds1_parts = stack3(ds1)
-    wvs_out[...] = tn(ds1_parts, repeat3(y1[0:1]))
+    left_out[...] = jnp.concatenate([repeat3(s1[0:1]), ds1_parts], axis=0)
+    right_out[...] = jnp.concatenate([dh1_parts, repeat3(y1[0:1])], axis=0)
     part = jnp.sum(nn(ds1_parts, wvs[...]), axis=0, keepdims=True)
     part_out[...] = jnp.broadcast_to(part, (8, D))
     total = sums[HEADS + 1 : HEADS + 2] * FACTOR
@@ -759,7 +803,10 @@
     ff_out[...] = sums[HEADS + 2 : HEADS + 3].reshape(ff_out.shape)
 
 
-def start_kernel(part_a, part_b, dh1, start, g_self, gain_out, start_out):
+def start_kernel(
+    part_a, part_b, dh1, start, g_self, value_a, value_b, gain_out, start_out, value_out
+):
+    value_out[...] = value_a[...].astype(f32) + value_b[...].astype(f32)
     dy1 = part_a[0:1] + part_b[0:1]
     n0, r0 = rms_parts(row_of(start))
     gain_out[...] = (dy1 * n0).reshape(gain_out.shape)
@@ -958,10 +1005,21 @@
     )
     other = swap(merged, "heads", 2)
     wo_full = plain(arrange_kernel, shape((D, D), bf16), scal, *wo_parts, smem=1)
-    target, member = plain(
-        target_kernel, [shape((list_len.shape[0], docs))] * 2, list_len, relevance, smem=1
-    )
-    other, wo_full, target, member = lax.optimization_barrier((other, wo_full, target, member))
+    tile = 384
+    held_rows = groups * slots // 2
+    picks_shape = [shape((tile, held_rows), bf16)] * 2 if docs == tile else []
+    target, member, *picks = plain(
+        functools.partial(target_kernel, order),
+        [shape((list_len.shape[0], docs))] * 2 + picks_shape,
+        scal,
+        group_docs,
+        list_len,
+        relevance,
+        smem=3,
+    )
+    other, wo_full, target, member, *picks = lax.optimization_barrier(
+        (other, wo_full, target, member, *picks)
+    )
 
     c, c32, scale, h2, z, part = plain(
         forward_kernel,
@@ -1159,7 +1217,7 @@
         if k < len(steps) - 1:
             sum_a = sum_a + sum_b
     y3, u, slope, c_own = plain(
-        functools.partial(weights_before_kernel, order, 384),
+        functools.partial(weights_before_kernel, order, tile),
         [
             shape((docs, D), bf16),
             shape((docs, hidden), bf16),
@@ -1174,6 +1232,7 @@
         g_ff,
         wo_full,
         w_in,
+        *picks,
         smem=2,
         limit=60 if docs > 384 else 16,
     )
@@ -1185,9 +1244,9 @@
     grads = jnp.concatenate([grads, grads_far], axis=0)
     grads_far = swap(grads, "heads", 1)
 
-    key_grad, query_grad, part = plain(
+    part, left1, right1 = plain(
         key_kernel,
-        [shape((width, D)), shape((width, D)), shape((8, D))],
+        [shape((8, D)), shape((3 * ROWS, width), bf16), shape((3 * ROWS, D), bf16)],
         scal,
         sum_a,
         sum_b,
@@ -1200,24 +1259,30 @@
     part = add(part, swap(part, "heads", 1))
     part, grads_far = tie(part, grads_far)
     part_a, part_b = part, swap(part, "heads", 2)
-    w_in_grad, grads_docs = plain(
-        functools.partial(weights_kernel, order, 384),
-        [shape((D, hidden)), shape((docs, 2 * D), bf16)],
+    dz, both = plain(
+        functools.partial(grads_kernel, order, tile),
+        [shape((docs, hidden), bf16), shape((docs, 2 * D), bf16)],
         scal,
         group_docs,
-        y3,
         slope,
         grads,
         grads_far,
         ds_docs,
         w_down,
+        *picks,
         smem=2,
         limit=60 if docs > 384 else 16,
     )
-    part_b, w_in_grad, grads_docs = tie(part_b, w_in_grad, grads_docs)
-    dh1, wos_grad, wvs_grad, part, cross, final_gain, row_grad, ff_gain = plain(
+    part_b, dz, both = tie(part_b, dz, both)
+    dh1, part, left2, right2, cross, final_gain, row_grad, ff_gain = plain(
         hidden_kernel,
-        [shape((1, D)), shape((width, D)), shape((width, D)), shape((8, D))] + [shape((D,))] * 4,
+        [
+            shape((1, D)),
+            shape((8, D)),
+            shape((2 * ROWS, width), bf16),
+            shape((2 * ROWS, D), bf16),
+        ]
+        + [shape((D,))] * 4,
         part_a,
         part_b,
         sum_a,
@@ -1232,18 +1297,34 @@
         score_row,
     )
     part_a, part_b = sum_last(part, over_heads)
-    w_down_grad, w_out_grad = plain(
-        functools.partial(weights_after_kernel, 384),
-        [shape((hidden, D)), shape((width, D))],
+    dims = [(D, hidden), (hidden, D), (width, D)] + [(width, D)] * 4
+    w_in_grad, w_down_grad, w_out_grad, key_grad, query_grad, wos_grad, wvs_grad = plain(
+        functools.partial(outer_kernel, tile),
+        [pltpu.HBM(dim, f32) for dim in dims],
+        y3,
+        dz,
         u,
         c_own,
-        grads_docs,
-        limit=60 if docs > 384 else 16,
+        both,
+        left1,
+        right1,
+        left2,
+        right2,
+        hbm_out=True,
+        scratch=[pltpu.VMEM(dim, f32) for dim in dims] + [pltpu.SemaphoreType.DMA((16,))],
+        limit=60 if docs > 384 else 24,
     )
     part_b, w_down_grad, value_far = tie(part_b, w_down_grad, value_far)
-    value_grad = (value_part.astype(f32) + value_far.astype(f32)).T
-    self_gain, start_grad = plain(
-        start_kernel, [shape((D,))] * 2, part_a, part_b, dh1, start_token, g_self
+    self_gain, start_grad, value_grad = plain(
+        start_kernel,
+        [shape((D,)), shape((D,)), shape((width, D))],
+        part_a,
+        part_b,
+        dh1,
+        start_token,
+        g_self,
+        value_part,
+        value_far,
     )
 
     return (
@@ -1258,7 +1339,7 @@
         cross,
         query_grad.T,
         key_grad.T,
-        value_grad,
+        value_grad.T,
         w_out_grad,
         ff_gain,
         w_in_grad,

time: 129 us -> 127 us (0.984)
  Pallas kernels: 63.6 us -> 60.5 us
  starting transfers between devices: 32 us -> 33.9 us
    pallas_call x27, Pallas kernels: 57.7 us -> 54.6 us  [plain(): pl.pallas_call(kernel, out_shape=outs, in_specs=[whole_spec(space) for sp...]
    ppermute x38, starting transfers between devices: 32 us -> 33.9 us  [swap(): return lax.ppermute(x, axis, [(i, i ^ bit) for i in range(size)])]
  transfers between devices with their start and end apart: 38 -> 38, of which waited for: 15 -> 17; matrix products, arithmetic and copies ran while one was open for 0% -> 0% of each run, Pallas kernels for 43% -> 41%
where the time goes in v5:
time: 127 us
  Pallas kernels  60.5 us (48%)
  starting transfers between devices  33.9 us (27%)
  waiting for transfers between devices  30.5 us (24%)
    pallas_call x27, Pallas kernels, plain(): pl.pallas_call(kernel, out_shape=outs, in_specs=[whole_spec(space) for sp...  54.6 us
    ppermute x38, starting transfers between devices, swap(): return lax.ppermute(x, axis, [(i, i ^ bit) for i in range(size)])  33.9 us
    ppermute x38, waiting for transfers between devices, swap(): return lax.ppermute(x, axis, [(i, i ^ bit) for i in range(size)])  30.5 us
    pallas_call x2, Pallas kernels, load(): pl.pallas_call(functools.partial(load_kernel, first, last), out_shape=plt...  5.84 us
  transfers between devices with their start and end apart: 38, of which 17 were waited for; matrix products, arithmetic and copies ran while one was open for 0% of the time, Pallas kernels for 41%

profile of v5, /device:TPU:0, one launch (start us, length us, event | category | flops | bytes accessed | tf_op | source)
XLA Modules:
  0.0 126.8 jit_solution(2672374216414409156)
XLA Ops:
  0.7 1.5 %self_kernel.1 = f32[8,768]{1,0:T(8,128)S(1)} custom-call(bf16[768]{0:T(1024)(128)(2,1)} %start.7, f32[768]{0:T(1024)} %g_self.5, bf16[192,768]{1,0:T(8,128)(2,1)} %bitcast.15, bf16[192,768]{1,0:T(8,128)(2,1)} %wos.3), custom_call_target="tpu_custom_call" | custom-call | tf_op jit(solution)/shard_map/self_kernel/pallas_call | solution.py:840
  2.6 0.8 collective-permute-done
  3.5 2.9 %collective-permute-start.1 = (f32[8,768]{1,0:T(8,128)S(1)}, f32[8,768]{1,0:T(8,128)S(1)}, u32[]{:S(2)}, u32[]{:S(2)}) collective-permute-start(f32[8,768]{1,0:T(8,128)S(1)} %add.36.since.part_a), channel_id=1, source_target_pairs={{0,2},{1,3},{2,0},{3,1},{4,6},{5,7},{6,4},{7,5},{8,10},{9,11},{10,... | collective-permute-start | bytes 73736 | tf_op jit(solution)/shard_map/ppermute | solution.py:865
  6.4 2.4 %load_kernel.2.refs_0_ = bf16[96,128,768]{2,1,0:T(8,128)(2,1)S(1)} custom-call(bf16[96,128,768]{2,1,0:T(8,128)(2,1)} %enc.5, f32[8,768]{1,0:T(8,128)S(1)} %add.36.since.part_a, s32[2]{0:T(128)S(1)} %pad_add_fusion.scal), custom_call_target="tpu_custom_call" | custom-call | tf_op jit(solution)/shard_map/load_kernel/pallas_call | solution.py:931
  8.9 1.3 %collective-permute-start.4 = (bf16[192,768]{1,0:T(8,128)(2,1)S(1)}, bf16[192,768]{1,0:T(8,128)(2,1)S(1)}, u32[]{:S(2)}, u32[]{:S(2)}) collective-permute-start(bf16[192,768]{1,0:T(8,128)(2,1)S(1)} %bitcast.17), channel_id=1, source_target_pairs={{0,2},{1,3},{2,0},{3,1},{4,6},{5,7},{6,4},{7,5},{8,10},{9,11},{10,... | collective-permute-start | bytes 884744 | tf_op jit(solution)/shard_map/ppermute | solution.py:865
  10.2 1.5 %query_kernel.1 = (f32[16,768]{1,0:T(8,128)S(1)}, f32[1,768]{1,0:T(1,128)S(1)}) custom-call(s32[2]{0:T(128)S(1)} %pad_add_fusion.scal, f32[8,768]{1,0:T(8,128)S(1)} %add.36.since.part_a, f32[8,768]{1,0:T(8,128)S(1)} %collective-permute-done.1.part_b, bf16[768]{0:T(1024)(128)(2,1)} %start.7, f32[768]{0:T(1024)} %g_cross.5, bf16[192,768]{1,0:T(8,128)(2,1)} %bitcast.11, ...), custom_call_target="tpu_custom_call" | custom-call | tf_op jit(solution)/shard_map/query_kernel/pallas_call | solution.py:840
  11.7 1.2 collective-permute-done.2
  13.0 0.9 collective-permute-start.3
  13.9 3.4 %load_kernel.3._ = bf16[96,128,768]{2,1,0:T(8,128)(2,1)S(1)} custom-call(bf16[96,128,768]{2,1,0:T(8,128)(2,1)} %enc.5, f32[16,768]{1,0:T(8,128)S(1)} %add.37.since.qa, s32[2]{0:T(128)S(1)} %pad_add_fusion.scal, bf16[96,128,768]{2,1,0:T(8,128)(2,1)S(1)} %load_kernel.2.refs_0_), custom_call_target="tpu_custom_call", output_to_operand_aliasing={{}: (3, {})} | custom-call | tf_op jit(solution)/shard_map/load_kernel/pallas_call | solution.py:931
  17.3 1.5 %collective-permute-done.3.qb = f32[16,768]{1,0:T(8,128)S(1)} collective-permute-done((f32[16,768]{1,0:T(8,128)S(1)}, f32[16,768]{1,0:T(8,128)S(1)}, u32[]{:S(2)}, u32[]{:S(2)}) %collective-permute-start.3) | collective-permute-done | bytes 49184 | tf_op jit(solution)/shard_map/ppermute | solution.py:865
  19.4 6.1 %attend_kernel.1 = (bf16[96,128,768]{2,1,0:T(8,128)(2,1)S(1)}, f32[96,16,128]{2,1,0:T(8,128)S(1)}, f32[6,1536,128]{2,1,0:T(8,128)S(1)}, bf16[96,128]{1,0:T(8,128)(2,1)S(1)}) custom-call(s32[2]{0:T(128)S(1)} %pad_add_fusion.scal, s32[8]{0:T(128)S(1)} %copy-done.11, s32[384]{0:T(512)S(1)} %copy-done.15, ...), custom_call_target="tpu_custom_call", output_to_operand_aliasing={{0}: (6, {})} | custom-call | tf_op jit(solution)/shard_map/attend_kernel/pallas_call | solution.py:840
  25.6 2.7 %collective-permute-done.6.by2 = bf16[192,768]{1,0:T(8,128)(2,1)S(1)} collective-permute-done((bf16[192,768]{1,0:T(8,128)(2,1)S(1)}, bf16[192,768]{1,0:T(8,128)(2,1)S(1)}, u32[]{:S(2)}, u32[]{:S(2)}) %collective-permute-start.6) | collective-permute-done | bytes 294944 | tf_op jit(solution)/shard_map/ppermute | solution.py:865
  28.2 1.8 %project_kernel.1 = (bf16[96,896]{1,0:T(8,128)(2,1)S(1)}, bf16[12,96,768]{2,1,0:T(8,128)(2,1)S(1)}, bf16[768,768]{1,0:T(8,128)(2,1)S(1)}) custom-call(s32[2]{0:T(128)S(1)} %pad_add_fusion.scal, f32[6,1536,128]{2,1,0:T(8,128)S(1)} %get-tuple-element.159.summed, bf16[96,128]{1,0:T(8,128)(2,1)S(1)} %get-tuple-element.160.extra, bf16[192,768]{1,0:T(8,128)(2,1)S(1)} %bitcast.19, ...), custom_call_target="tpu_custom_call" | custom-call | tf_op jit(solution)/shard_map/project_kernel/pallas_call | solution.py:840
  30.1 0.5 collective-permute-start.10
  30.7 0.8 collective-permute-done.8.other
  31.5 1.0 merge_kernel.1.own
  32.9 1.6 %target_kernel.1 = (f32[24,384]{1,0:T(8,128)S(1)}, f32[24,384]{1,0:T(8,128)S(1)}, bf16[384,384]{1,0:T(8,128)(2,1)S(1)}, bf16[384,384]{1,0:T(8,128)(2,1)S(1)}) custom-call(s32[2]{0:T(128)S(1)} %pad_add_fusion.scal, s32[8]{0:T(128)S(1)} %copy-done.11, s32[24]{0:T(128)S(1)} %copy-done.17, f32[384]{0:T(512)S(1)} %copy-done.16), custom_call_target="tpu_custom_call" | custom-call | tf_op jit(solution)/shard_map/target_kernel/pallas_call | solution.py:840
  34.6 0.6 arrange_kernel.1.wo.wout
  35.2 3.8 %collective-permute-done.9.other = bf16[96,896]{1,0:T(8,128)(2,1)S(1)} collective-permute-done((bf16[96,896]{1,0:T(8,128)(2,1)S(1)}, bf16[96,896]{1,0:T(8,128)(2,1)S(1)}, u32[]{:S(2)}, u32[]{:S(2)}) %collective-permute-start.9) | collective-permute-done | bytes 172064 | tf_op jit(solution)/shard_map/ppermute | solution.py:865
  39.0 1.9 %forward_kernel.1 = (bf16[48,768]{1,0:T(8,128)(2,1)S(1)}, f32[96,768]{1,0:T(8,128)S(1)}, f32[96,128]{1,0:T(8,128)S(1)}, f32[96,768]{1,0:T(8,128)S(1)}, f32[96,76...) custom-call(s32[2]{0:T(128)S(1)} %pad_add_fusion.scal, bf16[96,896]{1,0:T(8,128)(2,1)S(1)} %merge_kernel.1.own, ...), custom_call_target="tpu_custom_call" | custom-call | tf_op jit(solution)/shard_map/forward_kernel/pallas_call | solution.py:840
  41.1 1.4 %collective-permute-done.12 = bf16[96,768]{1,0:T(8,128)(2,1)S(1)} collective-permute-done((bf16[96,768]{1,0:T(8,128)(2,1)S(1)}, bf16[96,768]{1,0:T(8,128)(2,1)S(1)}, u32[]{:S(2)}, u32[]{:S(2)}) %collective-permute-start.12) | collective-permute-done | bytes 147488 | tf_op jit(solution)/shard_map/ppermute | solution.py:865
  42.9 5.5 %collective-permute-done.13.part_b = bf16[96,768]{1,0:T(8,128)(2,1)S(1)} collective-permute-done((bf16[96,768]{1,0:T(8,128)(2,1)S(1)}, bf16[96,768]{1,0:T(8,128)(2,1)S(1)}, u32[]{:S(2)}, u32[]{:S(2)}) %collective-permute-start.13) | collective-permute-done | bytes 147488 | tf_op jit(solution)/shard_map/ppermute | solution.py:865
  48.4 0.5 score_kernel.1
  48.9 0.9 down_kernel.1
  49.9 1.4 %collective-permute-done.15 = bf16[96,768]{1,0:T(8,128)(2,1)S(1)} collective-permute-done((bf16[96,768]{1,0:T(8,128)(2,1)S(1)}, bf16[96,768]{1,0:T(8,128)(2,1)S(1)}, u32[]{:S(2)}, u32[]{:S(2)}) %collective-permute-start.15) | collective-permute-done | bytes 147488 | tf_op jit(solution)/shard_map/ppermute | solution.py:865
  51.3 0.9 share_kernel.1
  52.8 2.7 %collective-permute-start.14 = (bf16[48,896]{1,0:T(8,128)(2,1)S(1)}, bf16[48,896]{1,0:T(8,128)(2,1)S(1)}, u32[]{:S(2)}, u32[]{:S(2)}) collective-permute-start(bf16[48,896]{1,0:T(8,128)(2,1)S(1)} %get-tuple-element.187), channel_id=1, source_target_pairs={{0,16},{4,20},{8,24},{12,28},{16,0},{20,4},{24,8},{28,12},{1,17},{... | collective-permute-start | bytes 258056 | tf_op jit(solution)/shard_map/ppermute | solution.py:865
  55.6 0.6 away_kernel.1
  56.2 2.3 %collective-permute-done.16.part_b = bf16[96,768]{1,0:T(8,128)(2,1)S(1)} collective-permute-done((bf16[96,768]{1,0:T(8,128)(2,1)S(1)}, bf16[96,768]{1,0:T(8,128)(2,1)S(1)}, u32[]{:S(2)}, u32[]{:S(2)}) %collective-permute-start.16) | collective-permute-done | bytes 147488 | tf_op jit(solution)/shard_map/ppermute | solution.py:865
  58.6 1.5 %context_kernel.1 = (bf16[96,768]{1,0:T(8,128)(2,1)S(1)}, bf16[48,1536]{1,0:T(8,128)(2,1)S(1)}, bf16[96,768]{1,0:T(8,128)(2,1)S(1)}, bf16[96,192]{1,0:T(8,128)(2...) custom-call(s32[2]{0:T(128)S(1)} %pad_add_fusion.scal, bf16[96,768]{1,0:T(8,128)(2,1)S(1)} %add_convert_fusion.2.part_a, ...), custom_call_target="tpu_custom_call" | custom-call | tf_op jit(solution)/shard_map/context_kernel/pallas_call | solution.py:840
  60.1 1.9 %collective-permute-start.18 = (bf16[96,896]{1,0:T(8,128)(2,1)S(1)}, bf16[96,896]{1,0:T(8,128)(2,1)S(1)}, u32[]{:S(2)}, u32[]{:S(2)}) collective-permute-start(bf16[96,896]{1,0:T(8,128)(2,1)S(1)} %pad_maximum_fusion.3), channel_id=1, source_target_pairs={{0,8},{4,12},{8,0},{12,4},{16,24},{20,28},{24,16},{28,20},{1,9},{5... | collective-permute-start | bytes 516104 | tf_op jit(solution)/shard_map/ppermute | solution.py:865
  62.0 1.5 %collective-permute-start.20 = (bf16[3,96,768]{2,1,0:T(8,128)(2,1)S(1)}, bf16[3,96,768]{2,1,0:T(8,128)(2,1)S(1)}, u32[]{:S(2)}, u32[]{:S(2)}) collective-permute-start(bf16[3,96,768]{2,1,0:T(8,128)(2,1)S(1)} %away_kernel.1), channel_id=1, source_target_pairs={{0,2},{1,3},{2,0},{3,1},{4,6},{5,7},{6,4},{7,5},{8,10},{9,11},{10,... | collective-permute-start | bytes 1327112 | tf_op jit(solution)/shard_map/ppermute | solution.py:865
  63.6 2.3 %collective-permute-start.21 = (bf16[48,1536]{1,0:T(8,128)(2,1)S(1)}, bf16[48,1536]{1,0:T(8,128)(2,1)S(1)}, u32[]{:S(2)}, u32[]{:S(2)}) collective-permute-start(bf16[48,1536]{1,0:T(8,128)(2,1)S(1)} %get-tuple-element.199), channel_id=1, source_target_pairs={{0,16},{4,20},{8,24},{12,28},{16,0},{20,4},{24,8},{28,12},{1,17},{... | collective-permute-start | bytes 442376 | tf_op jit(solution)/shard_map/ppermute | solution.py:865
  65.9 3.5 %back_kernel.2 = (bf16[96,32,128]{2,1,0:T(8,128)(2,1)S(1)}, bf16[96,16,768]{2,1,0:T(8,128)(2,1)S(1)}) custom-call(s32[2]{0:T(128)S(1)} %pad_add_fusion.scal, s32[8]{0:T(128)S(1)} %copy-done.11, bf16[96,128,768]{2,1,0:T(8,128)(2,1)S(1)} %get-tuple-element.189.enc, f32[96,16,128]{2,1,0:T(8,128)S(1)} %get-tuple-element.190.p, ...), custom_call_target="tpu_custom_call" | custom-call | tf_op jit(solution)/shard_map/back_kernel/pallas_call | solution.py:840
  69.5 1.8 %collective-permute-start.19 = (bf16[192,896]{1,0:T(8,128)(2,1)S(1)}, bf16[192,896]{1,0:T(8,128)(2,1)S(1)}, u32[]{:S(2)}, u32[]{:S(2)}) collective-permute-start(bf16[192,896]{1,0:T(8,128)(2,1)S(1)} %pad_maximum_fusion.1), channel_id=1, source_target_pairs={{0,4},{4,0},{8,12},{12,8},{16,20},{20,16},{24,28},{28,24},{1,5},{5... | collective-permute-start | bytes 1032200 | tf_op jit(solution)/shard_map/ppermute | solution.py:865
  71.3 3.4 %back_kernel.3 = (bf16[96,32,128]{2,1,0:T(8,128)(2,1)S(1)}, bf16[96,16,768]{2,1,0:T(8,128)(2,1)S(1)}) custom-call(s32[2]{0:T(128)S(1)} %pad_add_fusion.scal, s32[8]{0:T(128)S(1)} %copy-done.11, bf16[96,128,768]{2,1,0:T(8,128)(2,1)S(1)} %get-tuple-element.189.enc, ...), custom_call_target="tpu_custom_call", output_to_operand_aliasing={{0}: (8, {}), {1}: (9, {})} | custom-call | tf_op jit(solution)/shard_map/back_kernel/pallas_call | solution.py:840
  74.8 3.9 %collective-permute-done.19 = bf16[192,896]{1,0:T(8,128)(2,1)S(1)} collective-permute-done((bf16[192,896]{1,0:T(8,128)(2,1)S(1)}, bf16[192,896]{1,0:T(8,128)(2,1)S(1)}, u32[]{:S(2)}, u32[]{:S(2)}) %collective-permute-start.19) | collective-permute-done | bytes 344096 | tf_op jit(solution)/shard_map/ppermute | solution.py:865
  79.3 1.4 %list_kernel.1 = (f32[384]{0:T(512)}, f32[1,1]{1,0:T(1,128)}, f32[1,384]{1,0:T(1,128)S(1)}, f32[8,128]{1,0:T(8,128)S(1)}) custom-call(s32[2]{0:T(128)S(1)} %pad_add_fusion.scal, s32[8]{0:T(128)S(1)} %copy-done.11, bf16[384,896]{1,0:T(8,128)(2,1)S(1)} %constant_dynamic-update-slice_fusion.rows.c_own, f32[24,384]{1,0:T(8,128)S(1)} %get-tuple-element.201.targets, ...), custom_call_target="tpu_custom_call" | custom-call | tf_op jit(solution)/shard_map/list_kernel/pallas_call | solution.py:840
  80.6 1.0 value_kernel.1
  81.6 2.7 %key_sum_kernel.1 = f32[16,768]{1,0:T(8,128)S(1)} custom-call(s32[2]{0:T(128)S(1)} %pad_add_fusion.scal, s32[8]{0:T(128)S(1)} %copy-done.11, f32[8,128]{1,0:T(8,128)S(1)} %get-tuple-element.226.ds, bf16[96,128,768]{2,1,0:T(8,128)(2,1)S(1)} %get-tuple-element.189.enc, bf16[96,32,128]{2,1,0:T(8,128)(2,1)S(1)} %get-tuple-element.209.dap, ...), custom_call_target="tpu_custom_call" | custom-call | tf_op jit(solution)/shard_map/key_sum_kernel/pallas_call | solution.py:840
  84.4 0.5 collective-permute-start.22
  84.9 1.5 %collective-permute-start.26 = (bf16[192,768]{1,0:T(8,128)(2,1)S(1)}, bf16[192,768]{1,0:T(8,128)(2,1)S(1)}, u32[]{:S(2)}, u32[]{:S(2)}) collective-permute-start(bf16[192,768]{1,0:T(8,128)(2,1)S(1)} %value_kernel.1), channel_id=1, source_target_pairs={{0,4},{4,0},{8,12},{12,8},{16,20},{20,16},{24,28},{28,24},{1,5},{5... | collective-permute-start | bytes 884744 | tf_op jit(solution)/shard_map/ppermute | solution.py:865
  86.4 1.5 %collective-permute-start.24 = (f32[16,768]{1,0:T(8,128)S(1)}, f32[16,768]{1,0:T(8,128)S(1)}, u32[]{:S(2)}, u32[]{:S(2)}) collective-permute-start(f32[16,768]{1,0:T(8,128)S(1)} %add.40), channel_id=1, source_target_pairs={{0,16},{4,20},{8,24},{12,28},{16,0},{20,4},{24,8},{28,12},{1,17},{... | collective-permute-start | bytes 147464 | tf_op jit(solution)/shard_map/ppermute | solution.py:865
  87.9 3.4 %enc_grad_kernel.3.refs_0_ = bf16[96,128,768]{2,1,0:T(8,128)(2,1)} custom-call(f32[8,128]{1,0:T(8,128)S(1)} %get-tuple-element.226.ds, f32[16,768]{1,0:T(8,128)S(1)} %add.37.since.qa, f32[16,768]{1,0:T(8,128)S(1)} %collective-permute-done.3.qb, bf16[96,32,128]{2,1,0:T(8,128)(2,1)S(1)} %get-tuple-element.209.dap, bf16[96,16,768]{2,1,0:T(8,128)(2,1)S(1)} %get-tuple-element.217.vd), custom_call_target="tpu_custom_call" | custom-call | tf_op jit(solution)/shard_map/enc_grad_kernel/pallas_call | solution.py:840
  91.4 2.1 %collective-permute-start.25 = (f32[16,768]{1,0:T(8,128)S(1)}, f32[16,768]{1,0:T(8,128)S(1)}, u32[]{:S(2)}, u32[]{:S(2)}) collective-permute-start(f32[16,768]{1,0:T(8,128)S(1)} %add.41), channel_id=1, source_target_pairs={{0,8},{4,12},{8,0},{12,4},{16,24},{20,28},{24,16},{28,20},{1,9},{5... | collective-permute-start | bytes 147464 | tf_op jit(solution)/shard_map/ppermute | solution.py:865
  93.6 1.2 collective-permute-start.30
  94.8 3.4 %enc_grad_kernel.4.refs_0_ = bf16[96,128,768]{2,1,0:T(8,128)(2,1)} custom-call(f32[8,128]{1,0:T(8,128)S(1)} %get-tuple-element.226.ds, f32[16,768]{1,0:T(8,128)S(1)} %add.37.since.qa, f32[16,768]{1,0:T(8,128)S(1)} %collective-permute-done.3.qb, bf16[96,32,128]{2,1,0:T(8,128)(2,1)S(1)} %get-tuple-element.209.dap, ...), custom_call_target="tpu_custom_call", output_to_operand_aliasing={{}: (5, {})} | custom-call | tf_op jit(solution)/shard_map/enc_grad_kernel/pallas_call | solution.py:840
  98.2 1.0 collective-permute-start.28
  99.3 1.4 %collective-permute-start.31 = (bf16[192,768]{1,0:T(8,128)(2,1)S(1)}, bf16[192,768]{1,0:T(8,128)(2,1)S(1)}, u32[]{:S(2)}, u32[]{:S(2)}) collective-permute-start(bf16[192,768]{1,0:T(8,128)(2,1)S(1)} %add_convert_fusion.1), channel_id=1, source_target_pairs={{0,8},{4,12},{8,0},{12,4},{16,24},{20,28},{24,16},{28,20},{1,9},{5... | collective-permute-start | bytes 884744 | tf_op jit(solution)/shard_map/ppermute | solution.py:865
  100.7 3.4 %enc_grad_kernel.5 = bf16[96,128,768]{2,1,0:T(8,128)(2,1)} custom-call(f32[8,128]{1,0:T(8,128)S(1)} %get-tuple-element.226.ds, f32[16,768]{1,0:T(8,128)S(1)} %add.37.since.qa, f32[16,768]{1,0:T(8,128)S(1)} %collective-permute-done.3.qb, bf16[96,32,128]{2,1,0:T(8,128)(2,1)S(1)} %get-tuple-element.209.dap, ...), custom_call_target="tpu_custom_call", output_to_operand_aliasing={{}: (5, {})} | custom-call | tf_op jit(solution)/shard_map/enc_grad_kernel/pallas_call | solution.py:840
  104.1 0.9 collective-permute-start.29
  105.1 2.9 %weights_before_kernel.1 = (bf16[384,768]{1,0:T(8,128)(2,1)S(1)}, bf16[384,768]{1,0:T(8,128)(2,1)S(1)}, f32[384,768]{1,0:T(8,128)S(1)}, bf16[384,192]{1,0:T(8,128)(2,1)S(1)}) custom-call(s32[2]{0:T(128)S(1)} %pad_add_fusion.scal, s32[8]{0:T(128)S(1)} %copy-done.11, bf16[384,896]{1,0:T(8,128)(2,1)S(1)} %constant_dynamic-update-slice_fusion.rows.c_own, ...), custom_call_target="tpu_custom_call" | custom-call | tf_op jit(solution)/shard_map/weights_before_kernel/pallas_call | solution.py:840
  108.0 0.9 collective-permute-done.29.sum_b
  109.1 2.3 %collective-permute-start.37 = (bf16[192,768]{1,0:T(8,128)(2,1)S(1)}, bf16[192,768]{1,0:T(8,128)(2,1)S(1)}, u32[]{:S(2)}, u32[]{:S(2)}) collective-permute-start(bf16[192,768]{1,0:T(8,128)(2,1)S(1)} %add_convert_fusion.value_a), channel_id=1, source_target_pairs={{0,16},{4,20},{8,24},{12,28},{16,0},{20,4},{24,8},{28,12},{1,17},{... | collective-permute-start | bytes 884744 | tf_op jit(solution)/shard_map/ppermute | solution.py:865
  111.3 1.0 key_kernel.1
  112.6 1.0 collective-permute-done.32
  113.6 1.0 collective-permute-start.34
  114.6 2.4 %grads_kernel.1 = (bf16[384,768]{1,0:T(8,128)(2,1)S(1)}, bf16[384,1536]{1,0:T(8,128)(2,1)S(1)}) custom-call(s32[2]{0:T(128)S(1)} %pad_add_fusion.scal, s32[8]{0:T(128)S(1)} %copy-done.11, f32[384,768]{1,0:T(8,128)S(1)} %get-tuple-element.244.slope, bf16[384,1536]{1,0:T(8,128)(2,1)S(1)} %constant_dynamic-update-slice_fusion.4.both_own, ...), custom_call_target="tpu_custom_call" | custom-call | tf_op jit(solution)/shard_map/grads_kernel/pallas_call | solution.py:840
  117.5 1.1 hidden_kernel.1
  118.6 1.2 collective-permute-done.35
  119.8 0.9 collective-permute-start.36
  120.7 3.5 %outer_kernel.1 = (f32[768,768]{1,0:T(8,128)}, f32[768,768]{1,0:T(8,128)}, f32[192,768]{1,0:T(8,128)}, f32[192,768]{1,0:T(8,128)}, f32[192,768]{1,0:T(8,128)}, /*index=5*/f32[192,768]{1,0:T(8,128)}, f32[192,768]{1,0:T(8,128)}) custom-call(bf16[384,768]{1,0:T(8,128)(2,1)S(1)} %get-tuple-element.251.y3, bf16[384,768]{1,0:T(8,128)(2,1)S(1)} %get-tuple-element.252.dz, ...), custom_call_target="tpu_custom_call" | custom-call | tf_op jit(solution)/shard_map/outer_kernel/pallas_call | solution.py:840
  124.3 1.5 %collective-permute-done.37.value_b = bf16[192,768]{1,0:T(8,128)(2,1)S(1)} collective-permute-done((bf16[192,768]{1,0:T(8,128)(2,1)S(1)}, bf16[192,768]{1,0:T(8,128)(2,1)S(1)}, u32[]{:S(2)}, u32[]{:S(2)}) %collective-permute-start.37) | collective-permute-done | bytes 294944 | tf_op jit(solution)/shard_map/ppermute | solution.py:865
  125.7 1.0 start_kernel.1
  (102 shorter events, 5.0 us)
Async XLA Ops:
  2.2 1.3 %collective-permute-start = (f32[8,768]{1,0:T(8,128)S(1)}, f32[8,768]{1,0:T(8,128)S(1)}, u32[]{:S(2)}, u32[]{:S(2)}) collective-permute-start(f32[8,768]{1,0:T(8,128)S(1)} %self_kernel.1), channel_id=1, source_target_pairs={{0,1},{1,0},{2,3},{3,2},{4,5},{5,4},{6,7},{7,6},{8,9},{9,8},{10,11... | collective-permute-start | bytes 73736 | tf_op jit(solution)/shard_map/ppermute | solution.py:865
  3.5 5.4 %collective-permute-start.1 = (f32[8,768]{1,0:T(8,128)S(1)}, f32[8,768]{1,0:T(8,128)S(1)}, u32[]{:S(2)}, u32[]{:S(2)}) collective-permute-start(f32[8,768]{1,0:T(8,128)S(1)} %add.36.since.part_a), channel_id=1, source_target_pairs={{0,2},{1,3},{2,0},{3,1},{4,6},{5,7},{6,4},{7,5},{8,10},{9,11},{10,... | collective-permute-start | bytes 73736 | tf_op jit(solution)/shard_map/ppermute | solution.py:865
  6.4 2.5 %copy-start.7 = (bf16[768,192]{0,1:T(8,128)(2,1)S(1)}, bf16[768,192]{0,1:T(8,128)(2,1)}, u32[]{:S(2)}) copy-start(bf16[768,192]{0,1:T(8,128)(2,1)} %param.32) | copy-start | bytes 884740
  8.9 9.9 %collective-permute-start.4 = (bf16[192,768]{1,0:T(8,128)(2,1)S(1)}, bf16[192,768]{1,0:T(8,128)(2,1)S(1)}, u32[]{:S(2)}, u32[]{:S(2)}) collective-permute-start(bf16[192,768]{1,0:T(8,128)(2,1)S(1)} %bitcast.17), channel_id=1, source_target_pairs={{0,2},{1,3},{2,0},{3,1},{4,6},{5,7},{6,4},{7,5},{8,10},{9,11},{10,... | collective-permute-start | bytes 884744 | tf_op jit(solution)/shard_map/ppermute | solution.py:865
  11.7 1.3 collective-permute-start.2
  13.0 5.8 %copy-start.2 = (bf16[192,768]{1,0:T(8,128)(2,1)S(1)}, bf16[192,768]{1,0:T(8,128)(2,1)}, u32[]{:S(2)}) copy-start(bf16[192,768]{1,0:T(8,128)(2,1)} %wo_own.1) | copy-start | bytes 884740
  13.0 6.4 %copy-start.11 = (s32[8]{0:T(128)S(1)}, s32[8]{0:T(128)}, u32[]{:S(2)}) copy-start(s32[8]{0:T(128)} %sizes.15) | copy-start | bytes 100
  13.0 6.4 %copy-start.15 = (s32[384]{0:T(512)S(1)}, s32[384]{0:T(512)}, u32[]{:S(2)}) copy-start(s32[384]{0:T(512)} %lengths.1) | copy-start | bytes 4612
  13.0 5.8 %collective-permute-start.3 = (f32[16,768]{1,0:T(8,128)S(1)}, f32[16,768]{1,0:T(8,128)S(1)}, u32[]{:S(2)}, u32[]{:S(2)}) collective-permute-start(f32[16,768]{1,0:T(8,128)S(1)} %add.37.since.qa), channel_id=1, source_target_pairs={{0,2},{1,3},{2,0},{3,1},{4,6},{5,7},{6,4},{7,5},{8,10},{9,11},{10,... | collective-permute-start | bytes 147464 | tf_op jit(solution)/shard_map/ppermute | solution.py:865
  18.8 6.7 %collective-permute-start.5 = (bf16[192,768]{1,0:T(8,128)(2,1)S(1)}, bf16[192,768]{1,0:T(8,128)(2,1)S(1)}, u32[]{:S(2)}, u32[]{:S(2)}) collective-permute-start(bf16[192,768]{1,0:T(8,128)(2,1)S(1)} %collective-permute-done.4.by2), channel_id=1, source_target_pairs={{0,1},{1,0},{2,3},{3,2},{4,5},{5,4},{6,7},{7,6},{8,9},{9,8},{10,11... | collective-permute-start | bytes 884744 | tf_op jit(solution)/shard_map/ppermute | solution.py:865
  18.8 9.4 %collective-permute-start.6 = (bf16[192,768]{1,0:T(8,128)(2,1)S(1)}, bf16[192,768]{1,0:T(8,128)(2,1)S(1)}, u32[]{:S(2)}, u32[]{:S(2)}) collective-permute-start(bf16[192,768]{1,0:T(8,128)(2,1)S(1)} %copy-done.2), channel_id=1, source_target_pairs={{0,2},{1,3},{2,0},{3,1},{4,6},{5,7},{6,4},{7,5},{8,10},{9,11},{10,... | collective-permute-start | bytes 884744 | tf_op jit(solution)/shard_map/ppermute | solution.py:865
  19.2 9.0 %collective-permute-start.7 = (bf16[192,768]{1,0:T(8,128)(2,1)S(1)}, bf16[192,768]{1,0:T(8,128)(2,1)S(1)}, u32[]{:S(2)}, u32[]{:S(2)}) collective-permute-start(bf16[192,768]{1,0:T(8,128)(2,1)S(1)} %bitcast.18), channel_id=1, source_target_pairs={{0,1},{1,0},{2,3},{3,2},{4,5},{5,4},{6,7},{7,6},{8,9},{9,8},{10,11... | collective-permute-start | bytes 884744 | tf_op jit(solution)/shard_map/ppermute | solution.py:865
  28.2 4.7 %copy-start.16 = (f32[384]{0:T(512)S(1)}, f32[384]{0:T(512)}, u32[]{:S(2)}) copy-start(f32[384]{0:T(512)} %rel.1) | copy-start | bytes 4612
  28.2 4.7 %copy-start.17 = (s32[24]{0:T(128)S(1)}, s32[24]{0:T(128)}, u32[]{:S(2)}) copy-start(s32[24]{0:T(128)} %lens.1) | copy-start | bytes 292
  30.1 1.5 %collective-permute-start.8 = (bf16[96,896]{1,0:T(8,128)(2,1)S(1)}, bf16[96,896]{1,0:T(8,128)(2,1)S(1)}, u32[]{:S(2)}, u32[]{:S(2)}) collective-permute-start(bf16[96,896]{1,0:T(8,128)(2,1)S(1)} %get-tuple-element.162.own.first), channel_id=1, source_target_pairs={{0,1},{1,0},{2,3},{3,2},{4,5},{5,4},{6,7},{7,6},{8,9},{9,8},{10,11... | collective-permute-start | bytes 516104 | tf_op jit(solution)/shard_map/ppermute | solution.py:865
  30.1 4.4 %collective-permute-start.10 = (bf16[192,768]{1,0:T(8,128)(2,1)S(1)}, bf16[192,768]{1,0:T(8,128)(2,1)S(1)}, u32[]{:S(2)}, u32[]{:S(2)}) collective-permute-start(bf16[192,768]{1,0:T(8,128)(2,1)S(1)} %copy-done.2), channel_id=1, source_target_pairs={{0,1},{1,0},{2,3},{3,2},{4,5},{5,4},{6,7},{7,6},{8,9},{9,8},{10,11... | collective-permute-start | bytes 884744 | tf_op jit(solution)/shard_map/ppermute | solution.py:865
  30.6 4.0 %collective-permute-start.11 = (bf16[192,768]{1,0:T(8,128)(2,1)S(1)}, bf16[192,768]{1,0:T(8,128)(2,1)S(1)}, u32[]{:S(2)}, u32[]{:S(2)}) collective-permute-start(bf16[192,768]{1,0:T(8,128)(2,1)S(1)} %collective-permute-done.6.by2), channel_id=1, source_target_pairs={{0,1},{1,0},{2,3},{3,2},{4,5},{5,4},{6,7},{7,6},{8,9},{9,8},{10,11... | collective-permute-start | bytes 884744 | tf_op jit(solution)/shard_map/ppermute | solution.py:865
  32.5 6.5 %collective-permute-start.9 = (bf16[96,896]{1,0:T(8,128)(2,1)S(1)}, bf16[96,896]{1,0:T(8,128)(2,1)S(1)}, u32[]{:S(2)}, u32[]{:S(2)}) collective-permute-start(bf16[96,896]{1,0:T(8,128)(2,1)S(1)} %merge_kernel.1.own), channel_id=1, source_target_pairs={{0,2},{1,3},{2,0},{3,1},{4,6},{5,7},{6,4},{7,5},{8,10},{9,11},{10,... | collective-permute-start | bytes 516104 | tf_op jit(solution)/shard_map/ppermute | solution.py:865
  34.5 4.5 %copy-start = (bf16[768,768]{1,0:T(8,128)(2,1)S(1)}, bf16[768,768]{1,0:T(8,128)(2,1)}, u32[]{:S(2)}) copy-start(bf16[768,768]{1,0:T(8,128)(2,1)} %wdown.5) | copy-start | bytes 3538948
  34.6 4.5 %copy-start.1 = (bf16[768,768]{1,0:T(8,128)(2,1)S(1)}, bf16[768,768]{1,0:T(8,128)(2,1)}, u32[]{:S(2)}) copy-start(bf16[768,768]{1,0:T(8,128)(2,1)} %win.5) | copy-start | bytes 3538948
  34.6 4.4 %copy-start.10 = (f32[768]{0:T(1024)S(1)}, f32[768]{0:T(1024)}, u32[]{:S(2)}) copy-start(f32[768]{0:T(1024)} %g_ff.5) | copy-start | bytes 9220
  39.0 9.4 %copy-start.13 = (f32[768]{0:T(1024)S(1)}, f32[768]{0:T(1024)}, u32[]{:S(2)}) copy-start(f32[768]{0:T(1024)} %g_final.3) | copy-start | bytes 9220
  39.0 9.4 %copy-start.14 = (bf16[768]{0:T(1024)(128)(2,1)S(1)}, bf16[768]{0:T(1024)(128)(2,1)}, u32[]{:S(2)}) copy-start(bf16[768]{0:T(1024)(128)(2,1)} %row.3) | copy-start | bytes 4612
  41.0 1.4 %collective-permute-start.12 = (bf16[96,768]{1,0:T(8,128)(2,1)S(1)}, bf16[96,768]{1,0:T(8,128)(2,1)S(1)}, u32[]{:S(2)}, u32[]{:S(2)}) collective-permute-start(bf16[96,768]{1,0:T(8,128)(2,1)S(1)} %get-tuple-element.171), channel_id=1, source_target_pairs={{0,1},{1,0},{2,3},{3,2},{4,5},{5,4},{6,7},{7,6},{8,9},{9,8},{10,11... | collective-permute-start | bytes 442376 | tf_op jit(solution)/shard_map/ppermute | solution.py:865
  42.5 6.0 %collective-permute-start.13 = (bf16[96,768]{1,0:T(8,128)(2,1)S(1)}, bf16[96,768]{1,0:T(8,128)(2,1)S(1)}, u32[]{:S(2)}, u32[]{:S(2)}) collective-permute-start(bf16[96,768]{1,0:T(8,128)(2,1)S(1)} %add_convert_fusion.3.part_a), channel_id=1, source_target_pairs={{0,2},{1,3},{2,0},{3,1},{4,6},{5,7},{6,4},{7,5},{8,10},{9,11},{10,... | collective-permute-start | bytes 442376 | tf_op jit(solution)/shard_map/ppermute | solution.py:865
  49.8 1.4 %collective-permute-start.15 = (bf16[96,768]{1,0:T(8,128)(2,1)S(1)}, bf16[96,768]{1,0:T(8,128)(2,1)S(1)}, u32[]{:S(2)}, u32[]{:S(2)}) collective-permute-start(bf16[96,768]{1,0:T(8,128)(2,1)S(1)} %down_kernel.1), channel_id=1, source_target_pairs={{0,1},{1,0},{2,3},{3,2},{4,5},{5,4},{6,7},{7,6},{8,9},{9,8},{10,11... | collective-permute-start | bytes 442376 | tf_op jit(solution)/shard_map/ppermute | solution.py:865
  52.2 3.3 %collective-permute-start.17 = (bf16[2,3,96,768]{3,2,1,0:T(8,128)(2,1)S(1)}, bf16[2,3,96,768]{3,2,1,0:T(8,128)(2,1)S(1)}, u32[]{:S(2)}, u32[]{:S(2)}) collective-permute-start(bf16[2,3,96,768]{3,2,1,0:T(8,128)(2,1)S(1)} %get-tuple-element.182), channel_id=1, source_target_pairs={{0,1},{1,0},{2,3},{3,2},{4,5},{5,4},{6,7},{7,6},{8,9},{9,8},{10,11... | collective-permute-start | bytes 2654216 | tf_op jit(solution)/shard_map/ppermute | solution.py:865
  52.5 6.1 %collective-permute-start.16 = (bf16[96,768]{1,0:T(8,128)(2,1)S(1)}, bf16[96,768]{1,0:T(8,128)(2,1)S(1)}, u32[]{:S(2)}, u32[]{:S(2)}) collective-permute-start(bf16[96,768]{1,0:T(8,128)(2,1)S(1)} %add_convert_fusion.2.part_a), channel_id=1, source_target_pairs={{0,2},{1,3},{2,0},{3,1},{4,6},{5,7},{6,4},{7,5},{8,10},{9,11},{10,... | collective-permute-start | bytes 442376 | tf_op jit(solution)/shard_map/ppermute | solution.py:865
  52.8 7.2 %collective-permute-start.14 = (bf16[48,896]{1,0:T(8,128)(2,1)S(1)}, bf16[48,896]{1,0:T(8,128)(2,1)S(1)}, u32[]{:S(2)}, u32[]{:S(2)}) collective-permute-start(bf16[48,896]{1,0:T(8,128)(2,1)S(1)} %get-tuple-element.187), channel_id=1, source_target_pairs={{0,16},{4,20},{8,24},{12,28},{16,0},{20,4},{24,8},{28,12},{1,17},{... | collective-permute-start | bytes 258056 | tf_op jit(solution)/shard_map/ppermute | solution.py:865
  60.1 9.3 %collective-permute-start.18 = (bf16[96,896]{1,0:T(8,128)(2,1)S(1)}, bf16[96,896]{1,0:T(8,128)(2,1)S(1)}, u32[]{:S(2)}, u32[]{:S(2)}) collective-permute-start(bf16[96,896]{1,0:T(8,128)(2,1)S(1)} %pad_maximum_fusion.3), channel_id=1, source_target_pairs={{0,8},{4,12},{8,0},{12,4},{16,24},{20,28},{24,16},{28,20},{1,9},{5... | collective-permute-start | bytes 516104 | tf_op jit(solution)/shard_map/ppermute | solution.py:865
  62.0 12.7 %collective-permute-start.20 = (bf16[3,96,768]{2,1,0:T(8,128)(2,1)S(1)}, bf16[3,96,768]{2,1,0:T(8,128)(2,1)S(1)}, u32[]{:S(2)}, u32[]{:S(2)}) collective-permute-start(bf16[3,96,768]{2,1,0:T(8,128)(2,1)S(1)} %away_kernel.1), channel_id=1, source_target_pairs={{0,2},{1,3},{2,0},{3,1},{4,6},{5,7},{6,4},{7,5},{8,10},{9,11},{10,... | collective-permute-start | bytes 1327112 | tf_op jit(solution)/shard_map/ppermute | solution.py:865
  63.6 11.2 %collective-permute-start.21 = (bf16[48,1536]{1,0:T(8,128)(2,1)S(1)}, bf16[48,1536]{1,0:T(8,128)(2,1)S(1)}, u32[]{:S(2)}, u32[]{:S(2)}) collective-permute-start(bf16[48,1536]{1,0:T(8,128)(2,1)S(1)} %get-tuple-element.199), channel_id=1, source_target_pairs={{0,16},{4,20},{8,24},{12,28},{16,0},{20,4},{24,8},{28,12},{1,17},{... | collective-permute-start | bytes 442376 | tf_op jit(solution)/shard_map/ppermute | solution.py:865
  69.5 9.2 %collective-permute-start.19 = (bf16[192,896]{1,0:T(8,128)(2,1)S(1)}, bf16[192,896]{1,0:T(8,128)(2,1)S(1)}, u32[]{:S(2)}, u32[]{:S(2)}) collective-permute-start(bf16[192,896]{1,0:T(8,128)(2,1)S(1)} %pad_maximum_fusion.1), channel_id=1, source_target_pairs={{0,4},{4,0},{8,12},{12,8},{16,20},{20,16},{24,28},{28,24},{1,5},{5... | collective-permute-start | bytes 1032200 | tf_op jit(solution)/shard_map/ppermute | solution.py:865
  78.7 7.7 %collective-permute-start.23 = (bf16[96,1536]{1,0:T(8,128)(2,1)S(1)}, bf16[96,1536]{1,0:T(8,128)(2,1)S(1)}, u32[]{:S(2)}, u32[]{:S(2)}) collective-permute-start(bf16[96,1536]{1,0:T(8,128)(2,1)S(1)} %pad_maximum_fusion.2), channel_id=1, source_target_pairs={{0,8},{4,12},{8,0},{12,4},{16,24},{20,28},{24,16},{28,20},{1,9},{5... | collective-permute-start | bytes 884744 | tf_op jit(solution)/shard_map/ppermute | solution.py:865
  79.2 19.0 %collective-permute-start.27 = (bf16[384,896]{1,0:T(8,128)(2,1)S(1)}, bf16[384,896]{1,0:T(8,128)(2,1)S(1)}, u32[]{:S(2)}, u32[]{:S(2)}) collective-permute-start(bf16[384,896]{1,0:T(8,128)(2,1)S(1)} %constant_dynamic-update-slice_fusion.rows.c_own), channel_id=1, source_target_pairs={{0,1},{1,0},{2,3},{3,2},{4,5},{5,4},{6,7},{7,6},{8,9},{9,8},{10,11... | collective-permute-start | bytes 2064392 | tf_op jit(solution)/shard_map/ppermute | solution.py:865
  84.4 2.0 %collective-permute-start.22 = (f32[16,768]{1,0:T(8,128)S(1)}, f32[16,768]{1,0:T(8,128)S(1)}, u32[]{:S(2)}, u32[]{:S(2)}) collective-permute-start(f32[16,768]{1,0:T(8,128)S(1)} %key_sum_kernel.1), channel_id=1, source_target_pairs={{0,1},{1,0},{2,3},{3,2},{4,5},{5,4},{6,7},{7,6},{8,9},{9,8},{10,11... | collective-permute-start | bytes 147464 | tf_op jit(solution)/shard_map/ppermute | solution.py:865
  84.9 13.3 %collective-permute-start.26 = (bf16[192,768]{1,0:T(8,128)(2,1)S(1)}, bf16[192,768]{1,0:T(8,128)(2,1)S(1)}, u32[]{:S(2)}, u32[]{:S(2)}) collective-permute-start(bf16[192,768]{1,0:T(8,128)(2,1)S(1)} %value_kernel.1), channel_id=1, source_target_pairs={{0,4},{4,0},{8,12},{12,8},{16,20},{20,16},{24,28},{28,24},{1,5},{5... | collective-permute-start | bytes 884744 | tf_op jit(solution)/shard_map/ppermute | solution.py:865
  86.4 5.1 %collective-permute-start.24 = (f32[16,768]{1,0:T(8,128)S(1)}, f32[16,768]{1,0:T(8,128)S(1)}, u32[]{:S(2)}, u32[]{:S(2)}) collective-permute-start(f32[16,768]{1,0:T(8,128)S(1)} %add.40), channel_id=1, source_target_pairs={{0,16},{4,20},{8,24},{12,28},{16,0},{20,4},{24,8},{28,12},{1,17},{... | collective-permute-start | bytes 147464 | tf_op jit(solution)/shard_map/ppermute | solution.py:865
  91.4 6.7 %collective-permute-start.25 = (f32[16,768]{1,0:T(8,128)S(1)}, f32[16,768]{1,0:T(8,128)S(1)}, u32[]{:S(2)}, u32[]{:S(2)}) collective-permute-start(f32[16,768]{1,0:T(8,128)S(1)} %add.41), channel_id=1, source_target_pairs={{0,8},{4,12},{8,0},{12,4},{16,24},{20,28},{24,16},{28,20},{1,9},{5... | collective-permute-start | bytes 147464 | tf_op jit(solution)/shard_map/ppermute | solution.py:865
  93.6 15.3 %collective-permute-start.30 = (bf16[192,1536]{1,0:T(8,128)(2,1)S(1)}, bf16[192,1536]{1,0:T(8,128)(2,1)S(1)}, u32[]{:S(2)}, u32[]{:S(2)}) collective-permute-start(bf16[192,1536]{1,0:T(8,128)(2,1)S(1)} %pad_maximum_fusion), channel_id=1, source_target_pairs={{0,4},{4,0},{8,12},{12,8},{16,20},{20,16},{24,28},{28,24},{1,5},{5... | collective-permute-start | bytes 1769480 | tf_op jit(solution)/shard_map/ppermute | solution.py:865
  98.2 5.9 %collective-permute-start.28 = (f32[16,768]{1,0:T(8,128)S(1)}, f32[16,768]{1,0:T(8,128)S(1)}, u32[]{:S(2)}, u32[]{:S(2)}) collective-permute-start(f32[16,768]{1,0:T(8,128)S(1)} %add.42), channel_id=1, source_target_pairs={{0,2},{1,3},{2,0},{3,1},{4,6},{5,7},{6,4},{7,5},{8,10},{9,11},{10,... | collective-permute-start | bytes 147464 | tf_op jit(solution)/shard_map/ppermute | solution.py:865
  99.3 9.6 %collective-permute-start.31 = (bf16[192,768]{1,0:T(8,128)(2,1)S(1)}, bf16[192,768]{1,0:T(8,128)(2,1)S(1)}, u32[]{:S(2)}, u32[]{:S(2)}) collective-permute-start(bf16[192,768]{1,0:T(8,128)(2,1)S(1)} %add_convert_fusion.1), channel_id=1, source_target_pairs={{0,8},{4,12},{8,0},{12,4},{16,24},{20,28},{24,16},{28,20},{1,9},{5... | collective-permute-start | bytes 884744 | tf_op jit(solution)/shard_map/ppermute | solution.py:865
  104.1 4.7 %collective-permute-start.29 = (f32[16,768]{1,0:T(8,128)S(1)}, f32[16,768]{1,0:T(8,128)S(1)}, u32[]{:S(2)}, u32[]{:S(2)}) collective-permute-start(f32[16,768]{1,0:T(8,128)S(1)} %add.43.sum_a), channel_id=1, source_target_pairs={{0,4},{4,0},{8,12},{12,8},{16,20},{20,16},{24,28},{28,24},{1,5},{5... | collective-permute-start | bytes 147464 | tf_op jit(solution)/shard_map/ppermute | solution.py:865
  108.0 3.4 %copy-start.3 = (bf16[768,192]{0,1:T(8,128)(2,1)S(1)}, bf16[768,192]{0,1:T(8,128)(2,1)}, u32[]{:S(2)}) copy-start(bf16[768,192]{0,1:T(8,128)(2,1)} %param.30) | copy-start | bytes 884740
  108.0 3.4 %copy-start.4 = (bf16[768,192]{0,1:T(8,128)(2,1)S(1)}, bf16[768,192]{0,1:T(8,128)(2,1)}, u32[]{:S(2)}) copy-start(bf16[768,192]{0,1:T(8,128)(2,1)} %param.31) | copy-start | bytes 884740
  108.0 3.4 %copy-start.8 = (f32[768]{0:T(1024)S(1)}, f32[768]{0:T(1024)}, u32[]{:S(2)}) copy-start(f32[768]{0:T(1024)} %g_cross.5) | copy-start | bytes 9220
  108.9 4.7 %collective-permute-start.33 = (bf16[384,1536]{1,0:T(8,128)(2,1)S(1)}, bf16[384,1536]{1,0:T(8,128)(2,1)S(1)}, u32[]{:S(2)}, u32[]{:S(2)}) collective-permute-start(bf16[384,1536]{1,0:T(8,128)(2,1)S(1)} %constant_dynamic-update-slice_fusion.4.both_own), channel_id=1, source_target_pairs={{0,1},{1,0},{2,3},{3,2},{4,5},{5,4},{6,7},{7,6},{8,9},{9,8},{10,11... | collective-permute-start | bytes 3538952 | tf_op jit(solution)/shard_map/ppermute | solution.py:865
  109.1 16.7 %collective-permute-start.37 = (bf16[192,768]{1,0:T(8,128)(2,1)S(1)}, bf16[192,768]{1,0:T(8,128)(2,1)S(1)}, u32[]{:S(2)}, u32[]{:S(2)}) collective-permute-start(bf16[192,768]{1,0:T(8,128)(2,1)S(1)} %add_convert_fusion.value_a), channel_id=1, source_target_pairs={{0,16},{4,20},{8,24},{12,28},{16,0},{20,4},{24,8},{28,12},{1,17},{... | collective-permute-start | bytes 884744 | tf_op jit(solution)/shard_map/ppermute | solution.py:865
  112.3 1.3 collective-permute-start.32
  113.6 3.9 %collective-permute-start.34 = (f32[8,768]{1,0:T(8,128)S(1)}, f32[8,768]{1,0:T(8,128)S(1)}, u32[]{:S(2)}, u32[]{:S(2)}) collective-permute-start(f32[8,768]{1,0:T(8,128)S(1)} %add.45.part_a), channel_id=1, source_target_pairs={{0,2},{1,3},{2,0},{3,1},{4,6},{5,7},{6,4},{7,5},{8,10},{9,11},{10,... | collective-permute-start | bytes 73736 | tf_op jit(solution)/shard_map/ppermute | solution.py:865
  114.6 2.9 %copy-start.5 = (bf16[768,192]{0,1:T(8,128)(2,1)S(1)}, bf16[768,192]{0,1:T(8,128)(2,1)}, u32[]{:S(2)}) copy-start(bf16[768,192]{0,1:T(8,128)(2,1)} %param.27) | copy-start | bytes 884740
  114.6 2.9 %copy-start.6 = (bf16[192,768]{1,0:T(8,128)(2,1)S(1)}, bf16[192,768]{1,0:T(8,128)(2,1)}, u32[]{:S(2)}) copy-start(bf16[192,768]{1,0:T(8,128)(2,1)} %wos.3) | copy-start | bytes 884740
  114.6 2.9 %copy-start.9 = (f32[768]{0:T(1024)S(1)}, f32[768]{0:T(1024)}, u32[]{:S(2)}) copy-start(f32[768]{0:T(1024)} %g_self.5) | copy-start | bytes 9220
  114.6 2.9 %copy-start.12 = (bf16[768]{0:T(1024)(128)(2,1)S(1)}, bf16[768]{0:T(1024)(128)(2,1)}, u32[]{:S(2)}) copy-start(bf16[768]{0:T(1024)(128)(2,1)} %start.7) | copy-start | bytes 4612
  118.6 1.2 collective-permute-start.35
  119.8 6.0 %collective-permute-start.36 = (f32[8,768]{1,0:T(8,128)S(1)}, f32[8,768]{1,0:T(8,128)S(1)}, u32[]{:S(2)}, u32[]{:S(2)}) collective-permute-start(f32[8,768]{1,0:T(8,128)S(1)} %add.46.part_a), channel_id=1, source_target_pairs={{0,2},{1,3},{2,0},{3,1},{4,6},{5,7},{6,4},{7,5},{8,10},{9,11},{10,... | collective-permute-start | bytes 73736 | tf_op jit(solution)/shard_map/ppermute | solution.py:865

commit v6 on v5

--- a/solution.py
+++ b/solution.py
@@ -1056,6 +1056,10 @@
     near_first = over_docs[::-1]
     part = add(part, swap(part, "heads", 1))
     part_a, part_b = part, swap(part, "heads", 2)
+    keep, sent = plain(
+        share_kernel, [shape((2, own_heads, slots, D), bf16)] * 2, scal, summed, scale, smem=1
+    )
+    part_b, keep, sent = tie(part_b, keep, sent)
     c_all, n3, dh3 = plain(
         score_kernel,
         [shape((half, D + LANES), bf16), shape((slots, D)), shape((slots, D), bf16)],
@@ -1068,12 +1072,8 @@
     )
     part = plain(down_kernel, shape((slots, D), bf16), dh3, z, w_down, w_in)
     part = add(part, swap(part, "heads", 1))
-    part, summed = tie(part, summed)
     part_a, part_b = part, swap(part, "heads", 2)
     c_far = swap(c_all, *over_docs[0])
-    keep, sent = plain(
-        share_kernel, [shape((2, own_heads, slots, D), bf16)] * 2, scal, summed, scale, smem=1
-    )
     got = swap(sent, "heads", 1)
     away = plain(
         away_kernel, shape((own_heads, slots, D), bf16), scal, keep, got, smem=1
@@ -1151,20 +1151,6 @@
         member,
         smem=2,
     )
-    value_part = plain(
-        value_kernel,
-        shape((width, D), bf16),
-        scal,
-        keep,
-        got,
-        other,
-        dc_own,
-        ds_mine,
-        smem=1,
-    )
-    dap, value_part = tie(dap, value_part)
-    value_far = swap(value_part, *near_first[0])
-    c_far = swap(c_all, "heads", 1)
     sums = plain(
         key_sum_kernel,
         shape((ROWS, D)),
@@ -1195,6 +1181,20 @@
             limit=16,
         )
 
+    sums, dc_own = tie(sums, dc_own)
+    value_part = plain(
+        value_kernel,
+        shape((width, D), bf16),
+        scal,
+        keep,
+        got,
+        other,
+        dc_own,
+        ds_mine,
+        smem=1,
+    )
+    value_far = swap(value_part, *near_first[0])
+    c_far = swap(c_all, "heads", 1)
     sums = add(sums, swap(sums, "heads", 1))
     steps = near_first[:0:-1] + over_heads[1:] + near_first[:1]
     sums, grads_far = tie(sums, grads_far)

time: 127 us -> 125 us (0.984)
  Pallas kernels: 60.5 us -> 54.2 us
  starting transfers between devices: 33.9 us -> 37.8 us
    pallas_call x27, Pallas kernels: 54.6 us -> 48.4 us  [plain(): pl.pallas_call(kernel, out_shape=outs, in_specs=[whole_spec(space) for sp...]
    ppermute x38, starting transfers between devices: 33.9 us -> 37.8 us  [swap(): return lax.ppermute(x, axis, [(i, i ^ bit) for i in range(size)])]
  transfers between devices with their start and end apart: 38 -> 38, of which waited for: 17 -> 17; matrix products, arithmetic and copies ran while one was open for 0% -> 0% of each run, Pallas kernels for 41% -> 39%
where the time goes in v6:
time: 125 us; the launch traced here: 124 us
  Pallas kernels  54.2 us (43%)
  starting transfers between devices  37.8 us (30%)
  waiting for transfers between devices  30.4 us (24%)
    pallas_call x27, Pallas kernels, plain(): pl.pallas_call(kernel, out_shape=outs, in_specs=[whole_spec(space) for sp...  48.4 us
    ppermute x38, starting transfers between devices, swap(): return lax.ppermute(x, axis, [(i, i ^ bit) for i in range(size)])  37.8 us
    ppermute x38, waiting for transfers between devices, swap(): return lax.ppermute(x, axis, [(i, i ^ bit) for i in range(size)])  30.4 us
    pallas_call x2, Pallas kernels, load(): pl.pallas_call(functools.partial(load_kernel, first, last), out_shape=plt...  5.84 us
  transfers between devices with their start and end apart: 38, of which 17 were waited for; matrix products, arithmetic and copies ran while one was open for 0% of the time, Pallas kernels for 39%

profile of v6, /device:TPU:0, one launch (start us, length us, event | category | flops | bytes accessed | tf_op | source)
XLA Modules:
  0.0 124.3 jit_solution(10773674943242384289)
XLA Ops:
  0.7 1.5 %self_kernel.1 = f32[8,768]{1,0:T(8,128)S(1)} custom-call(bf16[768]{0:T(1024)(128)(2,1)} %start.7, f32[768]{0:T(1024)} %g_self.5, bf16[192,768]{1,0:T(8,128)(2,1)} %bitcast.15, bf16[192,768]{1,0:T(8,128)(2,1)} %wos.3), custom_call_target="tpu_custom_call" | custom-call | tf_op jit(solution)/shard_map/self_kernel/pallas_call | solution.py:840
  2.6 0.8 collective-permute-done
  3.5 2.9 %collective-permute-start.1 = (f32[8,768]{1,0:T(8,128)S(1)}, f32[8,768]{1,0:T(8,128)S(1)}, u32[]{:S(2)}, u32[]{:S(2)}) collective-permute-start(f32[8,768]{1,0:T(8,128)S(1)} %add.36.since.part_a), channel_id=1, source_target_pairs={{0,2},{1,3},{2,0},{3,1},{4,6},{5,7},{6,4},{7,5},{8,10},{9,11},{10,... | collective-permute-start | bytes 73736 | tf_op jit(solution)/shard_map/ppermute | solution.py:865
  6.4 2.4 %load_kernel.2.refs_0_ = bf16[96,128,768]{2,1,0:T(8,128)(2,1)S(1)} custom-call(bf16[96,128,768]{2,1,0:T(8,128)(2,1)} %enc.5, f32[8,768]{1,0:T(8,128)S(1)} %add.36.since.part_a, s32[2]{0:T(128)S(1)} %pad_add_fusion.scal), custom_call_target="tpu_custom_call" | custom-call | tf_op jit(solution)/shard_map/load_kernel/pallas_call | solution.py:931
  8.9 1.3 %collective-permute-start.4 = (bf16[192,768]{1,0:T(8,128)(2,1)S(1)}, bf16[192,768]{1,0:T(8,128)(2,1)S(1)}, u32[]{:S(2)}, u32[]{:S(2)}) collective-permute-start(bf16[192,768]{1,0:T(8,128)(2,1)S(1)} %bitcast.17), channel_id=1, source_target_pairs={{0,2},{1,3},{2,0},{3,1},{4,6},{5,7},{6,4},{7,5},{8,10},{9,11},{10,... | collective-permute-start | bytes 884744 | tf_op jit(solution)/shard_map/ppermute | solution.py:865
  10.2 1.5 %query_kernel.1 = (f32[16,768]{1,0:T(8,128)S(1)}, f32[1,768]{1,0:T(1,128)S(1)}) custom-call(s32[2]{0:T(128)S(1)} %pad_add_fusion.scal, f32[8,768]{1,0:T(8,128)S(1)} %add.36.since.part_a, f32[8,768]{1,0:T(8,128)S(1)} %collective-permute-done.1.part_b, bf16[768]{0:T(1024)(128)(2,1)} %start.7, f32[768]{0:T(1024)} %g_cross.5, bf16[192,768]{1,0:T(8,128)(2,1)} %bitcast.11, ...), custom_call_target="tpu_custom_call" | custom-call | tf_op jit(solution)/shard_map/query_kernel/pallas_call | solution.py:840
  11.7 1.2 collective-permute-done.2
  13.0 0.9 collective-permute-start.3
  13.9 3.4 %load_kernel.3._ = bf16[96,128,768]{2,1,0:T(8,128)(2,1)S(1)} custom-call(bf16[96,128,768]{2,1,0:T(8,128)(2,1)} %enc.5, f32[16,768]{1,0:T(8,128)S(1)} %add.37.since.qa, s32[2]{0:T(128)S(1)} %pad_add_fusion.scal, bf16[96,128,768]{2,1,0:T(8,128)(2,1)S(1)} %load_kernel.2.refs_0_), custom_call_target="tpu_custom_call", output_to_operand_aliasing={{}: (3, {})} | custom-call | tf_op jit(solution)/shard_map/load_kernel/pallas_call | solution.py:931
  17.3 1.5 %collective-permute-done.3.qb = f32[16,768]{1,0:T(8,128)S(1)} collective-permute-done((f32[16,768]{1,0:T(8,128)S(1)}, f32[16,768]{1,0:T(8,128)S(1)}, u32[]{:S(2)}, u32[]{:S(2)}) %collective-permute-start.3) | collective-permute-done | bytes 49184 | tf_op jit(solution)/shard_map/ppermute | solution.py:865
  19.7 3.6 %attend_kernel.1 = (bf16[96,128,768]{2,1,0:T(8,128)(2,1)S(1)}, f32[96,16,128]{2,1,0:T(8,128)S(1)}, f32[6,1536,128]{2,1,0:T(8,128)S(1)}, bf16[96,128]{1,0:T(8,128)(2,1)S(1)}) custom-call(s32[2]{0:T(128)S(1)} %pad_add_fusion.scal, s32[8]{0:T(128)S(1)} %copy-done.11, s32[384]{0:T(512)S(1)} %copy-done.15, ...), custom_call_target="tpu_custom_call", output_to_operand_aliasing={{0}: (6, {})} | custom-call | tf_op jit(solution)/shard_map/attend_kernel/pallas_call | solution.py:840
  23.3 3.5 %collective-permute-done.6.by2 = bf16[192,768]{1,0:T(8,128)(2,1)S(1)} collective-permute-done((bf16[192,768]{1,0:T(8,128)(2,1)S(1)}, bf16[192,768]{1,0:T(8,128)(2,1)S(1)}, u32[]{:S(2)}, u32[]{:S(2)}) %collective-permute-start.6) | collective-permute-done | bytes 294944 | tf_op jit(solution)/shard_map/ppermute | solution.py:865
  26.8 1.8 %project_kernel.1 = (bf16[96,896]{1,0:T(8,128)(2,1)S(1)}, bf16[12,96,768]{2,1,0:T(8,128)(2,1)S(1)}, bf16[768,768]{1,0:T(8,128)(2,1)S(1)}) custom-call(s32[2]{0:T(128)S(1)} %pad_add_fusion.scal, f32[6,1536,128]{2,1,0:T(8,128)S(1)} %get-tuple-element.160.summed, bf16[96,128]{1,0:T(8,128)(2,1)S(1)} %get-tuple-element.161.extra, bf16[192,768]{1,0:T(8,128)(2,1)S(1)} %bitcast.19, ...), custom_call_target="tpu_custom_call" | custom-call | tf_op jit(solution)/shard_map/project_kernel/pallas_call | solution.py:840
  29.3 0.8 collective-permute-done.8.other
  30.1 1.0 merge_kernel.1.own
  31.0 0.7 collective-permute-start.9
  31.8 1.6 %target_kernel.1 = (f32[24,384]{1,0:T(8,128)S(1)}, f32[24,384]{1,0:T(8,128)S(1)}, bf16[384,384]{1,0:T(8,128)(2,1)S(1)}, bf16[384,384]{1,0:T(8,128)(2,1)S(1)}) custom-call(s32[2]{0:T(128)S(1)} %pad_add_fusion.scal, s32[8]{0:T(128)S(1)} %copy-done.11, s32[24]{0:T(128)S(1)} %copy-done.17, f32[384]{0:T(512)S(1)} %copy-done.16), custom_call_target="tpu_custom_call" | custom-call | tf_op jit(solution)/shard_map/target_kernel/pallas_call | solution.py:840
  33.4 0.6 arrange_kernel.1.wo.wout
  34.1 3.5 %collective-permute-done.9.other = bf16[96,896]{1,0:T(8,128)(2,1)S(1)} collective-permute-done((bf16[96,896]{1,0:T(8,128)(2,1)S(1)}, bf16[96,896]{1,0:T(8,128)(2,1)S(1)}, u32[]{:S(2)}, u32[]{:S(2)}) %collective-permute-start.9) | collective-permute-done | bytes 172064 | tf_op jit(solution)/shard_map/ppermute | solution.py:865
  37.5 1.9 %forward_kernel.1 = (bf16[48,768]{1,0:T(8,128)(2,1)S(1)}, f32[96,768]{1,0:T(8,128)S(1)}, f32[96,128]{1,0:T(8,128)S(1)}, f32[96,768]{1,0:T(8,128)S(1)}, f32[96,76...) custom-call(s32[2]{0:T(128)S(1)} %pad_add_fusion.scal, bf16[96,896]{1,0:T(8,128)(2,1)S(1)} %merge_kernel.1.own, ...), custom_call_target="tpu_custom_call" | custom-call | tf_op jit(solution)/shard_map/forward_kernel/pallas_call | solution.py:840
  39.6 1.4 %collective-permute-done.12 = bf16[96,768]{1,0:T(8,128)(2,1)S(1)} collective-permute-done((bf16[96,768]{1,0:T(8,128)(2,1)S(1)}, bf16[96,768]{1,0:T(8,128)(2,1)S(1)}, u32[]{:S(2)}, u32[]{:S(2)}) %collective-permute-start.12) | collective-permute-done | bytes 147488 | tf_op jit(solution)/shard_map/ppermute | solution.py:865
  41.0 0.7 collective-permute-start.13
  41.7 0.9 share_kernel.1
  42.6 4.3 %collective-permute-done.13.part_b = bf16[96,768]{1,0:T(8,128)(2,1)S(1)} collective-permute-done((bf16[96,768]{1,0:T(8,128)(2,1)S(1)}, bf16[96,768]{1,0:T(8,128)(2,1)S(1)}, u32[]{:S(2)}, u32[]{:S(2)}) %collective-permute-start.13) | collective-permute-done | bytes 147488 | tf_op jit(solution)/shard_map/ppermute | solution.py:865
  47.5 0.9 down_kernel.1
  49.0 1.0 collective-permute-done.15
  50.0 0.7 collective-permute-start.16
  50.7 2.6 %collective-permute-start.14 = (bf16[48,896]{1,0:T(8,128)(2,1)S(1)}, bf16[48,896]{1,0:T(8,128)(2,1)S(1)}, u32[]{:S(2)}, u32[]{:S(2)}) collective-permute-start(bf16[48,896]{1,0:T(8,128)(2,1)S(1)} %get-tuple-element.189), channel_id=1, source_target_pairs={{0,16},{4,20},{8,24},{12,28},{16,0},{20,4},{24,8},{28,12},{1,17},{... | collective-permute-start | bytes 258056 | tf_op jit(solution)/shard_map/ppermute | solution.py:865
  53.3 0.6 away_kernel.1
  54.0 2.2 %collective-permute-done.16.part_b = bf16[96,768]{1,0:T(8,128)(2,1)S(1)} collective-permute-done((bf16[96,768]{1,0:T(8,128)(2,1)S(1)}, bf16[96,768]{1,0:T(8,128)(2,1)S(1)}, u32[]{:S(2)}, u32[]{:S(2)}) %collective-permute-start.16) | collective-permute-done | bytes 147488 | tf_op jit(solution)/shard_map/ppermute | solution.py:865
  56.2 1.5 %context_kernel.1 = (bf16[96,768]{1,0:T(8,128)(2,1)S(1)}, bf16[48,1536]{1,0:T(8,128)(2,1)S(1)}, bf16[96,768]{1,0:T(8,128)(2,1)S(1)}, bf16[96,192]{1,0:T(8,128)(2...) custom-call(s32[2]{0:T(128)S(1)} %pad_add_fusion.scal, bf16[96,768]{1,0:T(8,128)(2,1)S(1)} %add_convert_fusion.2.part_a, ...), custom_call_target="tpu_custom_call" | custom-call | tf_op jit(solution)/shard_map/context_kernel/pallas_call | solution.py:840
  57.7 3.5 %collective-permute-start.18 = (bf16[96,896]{1,0:T(8,128)(2,1)S(1)}, bf16[96,896]{1,0:T(8,128)(2,1)S(1)}, u32[]{:S(2)}, u32[]{:S(2)}) collective-permute-start(bf16[96,896]{1,0:T(8,128)(2,1)S(1)} %pad_maximum_fusion.3), channel_id=1, source_target_pairs={{0,8},{4,12},{8,0},{12,4},{16,24},{20,28},{24,16},{28,20},{1,9},{5... | collective-permute-start | bytes 516104 | tf_op jit(solution)/shard_map/ppermute | solution.py:865
  61.2 1.5 %collective-permute-start.20 = (bf16[3,96,768]{2,1,0:T(8,128)(2,1)S(1)}, bf16[3,96,768]{2,1,0:T(8,128)(2,1)S(1)}, u32[]{:S(2)}, u32[]{:S(2)}) collective-permute-start(bf16[3,96,768]{2,1,0:T(8,128)(2,1)S(1)} %away_kernel.1), channel_id=1, source_target_pairs={{0,2},{1,3},{2,0},{3,1},{4,6},{5,7},{6,4},{7,5},{8,10},{9,11},{10,... | collective-permute-start | bytes 1327112 | tf_op jit(solution)/shard_map/ppermute | solution.py:865
  62.7 0.8 collective-permute-start.21
  63.5 3.5 %back_kernel.2 = (bf16[96,32,128]{2,1,0:T(8,128)(2,1)S(1)}, bf16[96,16,768]{2,1,0:T(8,128)(2,1)S(1)}) custom-call(s32[2]{0:T(128)S(1)} %pad_add_fusion.scal, s32[8]{0:T(128)S(1)} %copy-done.11, bf16[96,128,768]{2,1,0:T(8,128)(2,1)S(1)} %get-tuple-element.191.enc, f32[96,16,128]{2,1,0:T(8,128)S(1)} %get-tuple-element.192.p, ...), custom_call_target="tpu_custom_call" | custom-call | tf_op jit(solution)/shard_map/back_kernel/pallas_call | solution.py:840
  67.1 2.2 %collective-permute-start.19 = (bf16[192,896]{1,0:T(8,128)(2,1)S(1)}, bf16[192,896]{1,0:T(8,128)(2,1)S(1)}, u32[]{:S(2)}, u32[]{:S(2)}) collective-permute-start(bf16[192,896]{1,0:T(8,128)(2,1)S(1)} %pad_maximum_fusion.1), channel_id=1, source_target_pairs={{0,4},{4,0},{8,12},{12,8},{16,20},{20,16},{24,28},{28,24},{1,5},{5... | collective-permute-start | bytes 1032200 | tf_op jit(solution)/shard_map/ppermute | solution.py:865
  69.3 0.7 back_kernel.3
  70.1 1.4 %collective-permute-done.21 = bf16[48,1536]{1,0:T(8,128)(2,1)S(1)} collective-permute-done((bf16[48,1536]{1,0:T(8,128)(2,1)S(1)}, bf16[48,1536]{1,0:T(8,128)(2,1)S(1)}, u32[]{:S(2)}, u32[]{:S(2)}) %collective-permute-start.21) | collective-permute-done | bytes 147488 | tf_op jit(solution)/shard_map/ppermute | solution.py:865
  71.5 1.0 collective-permute-done.20.other
  72.5 3.8 %collective-permute-done.19 = bf16[192,896]{1,0:T(8,128)(2,1)S(1)} collective-permute-done((bf16[192,896]{1,0:T(8,128)(2,1)S(1)}, bf16[192,896]{1,0:T(8,128)(2,1)S(1)}, u32[]{:S(2)}, u32[]{:S(2)}) %collective-permute-start.19) | collective-permute-done | bytes 344096 | tf_op jit(solution)/shard_map/ppermute | solution.py:865
  76.9 1.4 %list_kernel.1 = (f32[384]{0:T(512)}, f32[1,1]{1,0:T(1,128)}, f32[1,384]{1,0:T(1,128)S(1)}, f32[8,128]{1,0:T(8,128)S(1)}) custom-call(s32[2]{0:T(128)S(1)} %pad_add_fusion.scal, s32[8]{0:T(128)S(1)} %copy-done.11, bf16[384,896]{1,0:T(8,128)(2,1)S(1)} %constant_dynamic-update-slice_fusion.rows.c_own, f32[24,384]{1,0:T(8,128)S(1)} %get-tuple-element.203.targets, ...), custom_call_target="tpu_custom_call" | custom-call | tf_op jit(solution)/shard_map/list_kernel/pallas_call | solution.py:840
  78.2 1.8 %key_sum_kernel.1 = f32[16,768]{1,0:T(8,128)S(1)} custom-call(s32[2]{0:T(128)S(1)} %pad_add_fusion.scal, s32[8]{0:T(128)S(1)} %copy-done.11, f32[8,128]{1,0:T(8,128)S(1)} %get-tuple-element.228.ds, bf16[96,128,768]{2,1,0:T(8,128)(2,1)S(1)} %get-tuple-element.191.enc, bf16[96,32,128]{2,1,0:T(8,128)(2,1)S(1)} %get-tuple-element.208.dap, ...), custom_call_target="tpu_custom_call" | custom-call | tf_op jit(solution)/shard_map/key_sum_kernel/pallas_call | solution.py:840
  80.5 1.0 value_kernel.1
  81.5 3.5 %collective-permute-start.26 = (bf16[192,768]{1,0:T(8,128)(2,1)S(1)}, bf16[192,768]{1,0:T(8,128)(2,1)S(1)}, u32[]{:S(2)}, u32[]{:S(2)}) collective-permute-start(bf16[192,768]{1,0:T(8,128)(2,1)S(1)} %value_kernel.1), channel_id=1, source_target_pairs={{0,4},{4,0},{8,12},{12,8},{16,20},{20,16},{24,28},{28,24},{1,5},{5... | collective-permute-start | bytes 884744 | tf_op jit(solution)/shard_map/ppermute | solution.py:865
  85.0 1.3 %collective-permute-start.24 = (f32[16,768]{1,0:T(8,128)S(1)}, f32[16,768]{1,0:T(8,128)S(1)}, u32[]{:S(2)}, u32[]{:S(2)}) collective-permute-start(f32[16,768]{1,0:T(8,128)S(1)} %add.40), channel_id=1, source_target_pairs={{0,16},{4,20},{8,24},{12,28},{16,0},{20,4},{24,8},{28,12},{1,17},{... | collective-permute-start | bytes 147464 | tf_op jit(solution)/shard_map/ppermute | solution.py:865
  86.4 3.4 %enc_grad_kernel.3.refs_0_ = bf16[96,128,768]{2,1,0:T(8,128)(2,1)} custom-call(f32[8,128]{1,0:T(8,128)S(1)} %get-tuple-element.228.ds, f32[16,768]{1,0:T(8,128)S(1)} %add.37.since.qa, f32[16,768]{1,0:T(8,128)S(1)} %collective-permute-done.3.qb, bf16[96,32,128]{2,1,0:T(8,128)(2,1)S(1)} %get-tuple-element.208.dap, bf16[96,16,768]{2,1,0:T(8,128)(2,1)S(1)} %get-tuple-element.218.vd), custom_call_target="tpu_custom_call" | custom-call | tf_op jit(solution)/shard_map/enc_grad_kernel/pallas_call | solution.py:840
  89.7 0.9 collective-permute-done.24
  91.0 1.5 %collective-permute-start.30 = (bf16[192,1536]{1,0:T(8,128)(2,1)S(1)}, bf16[192,1536]{1,0:T(8,128)(2,1)S(1)}, u32[]{:S(2)}, u32[]{:S(2)}) collective-permute-start(bf16[192,1536]{1,0:T(8,128)(2,1)S(1)} %pad_maximum_fusion), channel_id=1, source_target_pairs={{0,4},{4,0},{8,12},{12,8},{16,20},{20,16},{24,28},{28,24},{1,5},{5... | collective-permute-start | bytes 1769480 | tf_op jit(solution)/shard_map/ppermute | solution.py:865
  92.5 3.4 %enc_grad_kernel.4.refs_0_ = bf16[96,128,768]{2,1,0:T(8,128)(2,1)} custom-call(f32[8,128]{1,0:T(8,128)S(1)} %get-tuple-element.228.ds, f32[16,768]{1,0:T(8,128)S(1)} %add.37.since.qa, f32[16,768]{1,0:T(8,128)S(1)} %collective-permute-done.3.qb, bf16[96,32,128]{2,1,0:T(8,128)(2,1)S(1)} %get-tuple-element.208.dap, ...), custom_call_target="tpu_custom_call", output_to_operand_aliasing={{}: (5, {})} | custom-call | tf_op jit(solution)/shard_map/enc_grad_kernel/pallas_call | solution.py:840
  96.4 2.0 %collective-permute-start.28 = (f32[16,768]{1,0:T(8,128)S(1)}, f32[16,768]{1,0:T(8,128)S(1)}, u32[]{:S(2)}, u32[]{:S(2)}) collective-permute-start(f32[16,768]{1,0:T(8,128)S(1)} %add.42), channel_id=1, source_target_pairs={{0,2},{1,3},{2,0},{3,1},{4,6},{5,7},{6,4},{7,5},{8,10},{9,11},{10,... | collective-permute-start | bytes 147464 | tf_op jit(solution)/shard_map/ppermute | solution.py:865
  98.4 3.4 %enc_grad_kernel.5 = bf16[96,128,768]{2,1,0:T(8,128)(2,1)} custom-call(f32[8,128]{1,0:T(8,128)S(1)} %get-tuple-element.228.ds, f32[16,768]{1,0:T(8,128)S(1)} %add.37.since.qa, f32[16,768]{1,0:T(8,128)S(1)} %collective-permute-done.3.qb, bf16[96,32,128]{2,1,0:T(8,128)(2,1)S(1)} %get-tuple-element.208.dap, ...), custom_call_target="tpu_custom_call", output_to_operand_aliasing={{}: (5, {})} | custom-call | tf_op jit(solution)/shard_map/enc_grad_kernel/pallas_call | solution.py:840
  101.8 1.6 %collective-permute-start.29 = (f32[16,768]{1,0:T(8,128)S(1)}, f32[16,768]{1,0:T(8,128)S(1)}, u32[]{:S(2)}, u32[]{:S(2)}) collective-permute-start(f32[16,768]{1,0:T(8,128)S(1)} %add.43.sum_a), channel_id=1, source_target_pairs={{0,4},{4,0},{8,12},{12,8},{16,20},{20,16},{24,28},{28,24},{1,5},{5... | collective-permute-start | bytes 147464 | tf_op jit(solution)/shard_map/ppermute | solution.py:865
  103.4 2.9 %weights_before_kernel.1 = (bf16[384,768]{1,0:T(8,128)(2,1)S(1)}, bf16[384,768]{1,0:T(8,128)(2,1)S(1)}, f32[384,768]{1,0:T(8,128)S(1)}, bf16[384,192]{1,0:T(8,128)(2,1)S(1)}) custom-call(s32[2]{0:T(128)S(1)} %pad_add_fusion.scal, s32[8]{0:T(128)S(1)} %copy-done.11, bf16[384,896]{1,0:T(8,128)(2,1)S(1)} %constant_dynamic-update-slice_fusion.rows.c_own, ...), custom_call_target="tpu_custom_call" | custom-call | tf_op jit(solution)/shard_map/weights_before_kernel/pallas_call | solution.py:840
  106.6 1.5 %collective-permute-start.37 = (bf16[192,768]{1,0:T(8,128)(2,1)S(1)}, bf16[192,768]{1,0:T(8,128)(2,1)S(1)}, u32[]{:S(2)}, u32[]{:S(2)}) collective-permute-start(bf16[192,768]{1,0:T(8,128)(2,1)S(1)} %add_convert_fusion.value_a), channel_id=1, source_target_pairs={{0,16},{4,20},{8,24},{12,28},{16,0},{20,4},{24,8},{28,12},{1,17},{... | collective-permute-start | bytes 884744 | tf_op jit(solution)/shard_map/ppermute | solution.py:865
  108.1 1.0 key_kernel.1
  109.4 1.0 collective-permute-done.32
  110.4 2.4 %collective-permute-start.34 = (f32[8,768]{1,0:T(8,128)S(1)}, f32[8,768]{1,0:T(8,128)S(1)}, u32[]{:S(2)}, u32[]{:S(2)}) collective-permute-start(f32[8,768]{1,0:T(8,128)S(1)} %add.45.part_a), channel_id=1, source_target_pairs={{0,2},{1,3},{2,0},{3,1},{4,6},{5,7},{6,4},{7,5},{8,10},{9,11},{10,... | collective-permute-start | bytes 73736 | tf_op jit(solution)/shard_map/ppermute | solution.py:865
  112.8 2.5 %grads_kernel.1 = (bf16[384,768]{1,0:T(8,128)(2,1)S(1)}, bf16[384,1536]{1,0:T(8,128)(2,1)S(1)}) custom-call(s32[2]{0:T(128)S(1)} %pad_add_fusion.scal, s32[8]{0:T(128)S(1)} %copy-done.11, f32[384,768]{1,0:T(8,128)S(1)} %get-tuple-element.246.slope, bf16[384,1536]{1,0:T(8,128)(2,1)S(1)} %constant_dynamic-update-slice_fusion.4.both_own, ...), custom_call_target="tpu_custom_call" | custom-call | tf_op jit(solution)/shard_map/grads_kernel/pallas_call | solution.py:840
  115.3 1.1 hidden_kernel.1
  116.3 1.2 collective-permute-done.35
  117.5 1.3 %collective-permute-start.36 = (f32[8,768]{1,0:T(8,128)S(1)}, f32[8,768]{1,0:T(8,128)S(1)}, u32[]{:S(2)}, u32[]{:S(2)}) collective-permute-start(f32[8,768]{1,0:T(8,128)S(1)} %add.46.part_a), channel_id=1, source_target_pairs={{0,2},{1,3},{2,0},{3,1},{4,6},{5,7},{6,4},{7,5},{8,10},{9,11},{10,... | collective-permute-start | bytes 73736 | tf_op jit(solution)/shard_map/ppermute | solution.py:865
  118.9 3.5 %outer_kernel.1 = (f32[768,768]{1,0:T(8,128)}, f32[768,768]{1,0:T(8,128)}, f32[192,768]{1,0:T(8,128)}, f32[192,768]{1,0:T(8,128)}, f32[192,768]{1,0:T(8,128)}, /*index=5*/f32[192,768]{1,0:T(8,128)}, f32[192,768]{1,0:T(8,128)}) custom-call(bf16[384,768]{1,0:T(8,128)(2,1)S(1)} %get-tuple-element.253.y3, bf16[384,768]{1,0:T(8,128)(2,1)S(1)} %get-tuple-element.254.dz, ...), custom_call_target="tpu_custom_call" | custom-call | tf_op jit(solution)/shard_map/outer_kernel/pallas_call | solution.py:840
  122.4 0.9 collective-permute-done.37.value_b
  123.3 1.0 start_kernel.1
  (102 shorter events, 6.0 us)
Async XLA Ops:
  2.2 1.3 %collective-permute-start = (f32[8,768]{1,0:T(8,128)S(1)}, f32[8,768]{1,0:T(8,128)S(1)}, u32[]{:S(2)}, u32[]{:S(2)}) collective-permute-start(f32[8,768]{1,0:T(8,128)S(1)} %self_kernel.1), channel_id=1, source_target_pairs={{0,1},{1,0},{2,3},{3,2},{4,5},{5,4},{6,7},{7,6},{8,9},{9,8},{10,11... | collective-permute-start | bytes 73736 | tf_op jit(solution)/shard_map/ppermute | solution.py:865
  3.5 5.4 %collective-permute-start.1 = (f32[8,768]{1,0:T(8,128)S(1)}, f32[8,768]{1,0:T(8,128)S(1)}, u32[]{:S(2)}, u32[]{:S(2)}) collective-permute-start(f32[8,768]{1,0:T(8,128)S(1)} %add.36.since.part_a), channel_id=1, source_target_pairs={{0,2},{1,3},{2,0},{3,1},{4,6},{5,7},{6,4},{7,5},{8,10},{9,11},{10,... | collective-permute-start | bytes 73736 | tf_op jit(solution)/shard_map/ppermute | solution.py:865
  6.4 2.5 %copy-start.7 = (bf16[768,192]{0,1:T(8,128)(2,1)S(1)}, bf16[768,192]{0,1:T(8,128)(2,1)}, u32[]{:S(2)}) copy-start(bf16[768,192]{0,1:T(8,128)(2,1)} %param.32) | copy-start | bytes 884740
  8.9 9.9 %collective-permute-start.4 = (bf16[192,768]{1,0:T(8,128)(2,1)S(1)}, bf16[192,768]{1,0:T(8,128)(2,1)S(1)}, u32[]{:S(2)}, u32[]{:S(2)}) collective-permute-start(bf16[192,768]{1,0:T(8,128)(2,1)S(1)} %bitcast.17), channel_id=1, source_target_pairs={{0,2},{1,3},{2,0},{3,1},{4,6},{5,7},{6,4},{7,5},{8,10},{9,11},{10,... | collective-permute-start | bytes 884744 | tf_op jit(solution)/shard_map/ppermute | solution.py:865
  11.7 1.3 %collective-permute-start.2 = (f32[16,768]{1,0:T(8,128)S(1)}, f32[16,768]{1,0:T(8,128)S(1)}, u32[]{:S(2)}, u32[]{:S(2)}) collective-permute-start(f32[16,768]{1,0:T(8,128)S(1)} %get-tuple-element.150), channel_id=1, source_target_pairs={{0,1},{1,0},{2,3},{3,2},{4,5},{5,4},{6,7},{7,6},{8,9},{9,8},{10,11... | collective-permute-start | bytes 147464 | tf_op jit(solution)/shard_map/ppermute | solution.py:865
  13.0 5.8 %copy-start.2 = (bf16[192,768]{1,0:T(8,128)(2,1)S(1)}, bf16[192,768]{1,0:T(8,128)(2,1)}, u32[]{:S(2)}) copy-start(bf16[192,768]{1,0:T(8,128)(2,1)} %wo_own.1) | copy-start | bytes 884740
  13.0 6.7 %copy-start.11 = (s32[8]{0:T(128)S(1)}, s32[8]{0:T(128)}, u32[]{:S(2)}) copy-start(s32[8]{0:T(128)} %sizes.15) | copy-start | bytes 100
  13.0 6.7 %copy-start.15 = (s32[384]{0:T(512)S(1)}, s32[384]{0:T(512)}, u32[]{:S(2)}) copy-start(s32[384]{0:T(512)} %lengths.1) | copy-start | bytes 4612
  13.0 5.8 %collective-permute-start.3 = (f32[16,768]{1,0:T(8,128)S(1)}, f32[16,768]{1,0:T(8,128)S(1)}, u32[]{:S(2)}, u32[]{:S(2)}) collective-permute-start(f32[16,768]{1,0:T(8,128)S(1)} %add.37.since.qa), channel_id=1, source_target_pairs={{0,2},{1,3},{2,0},{3,1},{4,6},{5,7},{6,4},{7,5},{8,10},{9,11},{10,... | collective-permute-start | bytes 147464 | tf_op jit(solution)/shard_map/ppermute | solution.py:865
  18.8 7.9 %collective-permute-start.6 = (bf16[192,768]{1,0:T(8,128)(2,1)S(1)}, bf16[192,768]{1,0:T(8,128)(2,1)S(1)}, u32[]{:S(2)}, u32[]{:S(2)}) collective-permute-start(bf16[192,768]{1,0:T(8,128)(2,1)S(1)} %copy-done.2), channel_id=1, source_target_pairs={{0,2},{1,3},{2,0},{3,1},{4,6},{5,7},{6,4},{7,5},{8,10},{9,11},{10,... | collective-permute-start | bytes 884744 | tf_op jit(solution)/shard_map/ppermute | solution.py:865
  19.2 7.6 %collective-permute-start.5 = (bf16[192,768]{1,0:T(8,128)(2,1)S(1)}, bf16[192,768]{1,0:T(8,128)(2,1)S(1)}, u32[]{:S(2)}, u32[]{:S(2)}) collective-permute-start(bf16[192,768]{1,0:T(8,128)(2,1)S(1)} %collective-permute-done.4.by2), channel_id=1, source_target_pairs={{0,1},{1,0},{2,3},{3,2},{4,5},{5,4},{6,7},{7,6},{8,9},{9,8},{10,11... | collective-permute-start | bytes 884744 | tf_op jit(solution)/shard_map/ppermute | solution.py:865
  19.2 7.6 %collective-permute-start.7 = (bf16[192,768]{1,0:T(8,128)(2,1)S(1)}, bf16[192,768]{1,0:T(8,128)(2,1)S(1)}, u32[]{:S(2)}, u32[]{:S(2)}) collective-permute-start(bf16[192,768]{1,0:T(8,128)(2,1)S(1)} %bitcast.18), channel_id=1, source_target_pairs={{0,1},{1,0},{2,3},{3,2},{4,5},{5,4},{6,7},{7,6},{8,9},{9,8},{10,11... | collective-permute-start | bytes 884744 | tf_op jit(solution)/shard_map/ppermute | solution.py:865
  26.7 5.0 %copy-start.16 = (f32[384]{0:T(512)S(1)}, f32[384]{0:T(512)}, u32[]{:S(2)}) copy-start(f32[384]{0:T(512)} %rel.1) | copy-start | bytes 4612
  26.8 5.0 %copy-start.17 = (s32[24]{0:T(128)S(1)}, s32[24]{0:T(128)}, u32[]{:S(2)}) copy-start(s32[24]{0:T(128)} %lens.1) | copy-start | bytes 292
  28.6 1.5 %collective-permute-start.8 = (bf16[96,896]{1,0:T(8,128)(2,1)S(1)}, bf16[96,896]{1,0:T(8,128)(2,1)S(1)}, u32[]{:S(2)}, u32[]{:S(2)}) collective-permute-start(bf16[96,896]{1,0:T(8,128)(2,1)S(1)} %get-tuple-element.163.own.first), channel_id=1, source_target_pairs={{0,1},{1,0},{2,3},{3,2},{4,5},{5,4},{6,7},{7,6},{8,9},{9,8},{10,11... | collective-permute-start | bytes 516104 | tf_op jit(solution)/shard_map/ppermute | solution.py:865
  28.7 4.7 %collective-permute-start.10 = (bf16[192,768]{1,0:T(8,128)(2,1)S(1)}, bf16[192,768]{1,0:T(8,128)(2,1)S(1)}, u32[]{:S(2)}, u32[]{:S(2)}) collective-permute-start(bf16[192,768]{1,0:T(8,128)(2,1)S(1)} %copy-done.2), channel_id=1, source_target_pairs={{0,1},{1,0},{2,3},{3,2},{4,5},{5,4},{6,7},{7,6},{8,9},{9,8},{10,11... | collective-permute-start | bytes 884744 | tf_op jit(solution)/shard_map/ppermute | solution.py:865
  29.2 4.3 %collective-permute-start.11 = (bf16[192,768]{1,0:T(8,128)(2,1)S(1)}, bf16[192,768]{1,0:T(8,128)(2,1)S(1)}, u32[]{:S(2)}, u32[]{:S(2)}) collective-permute-start(bf16[192,768]{1,0:T(8,128)(2,1)S(1)} %collective-permute-done.6.by2), channel_id=1, source_target_pairs={{0,1},{1,0},{2,3},{3,2},{4,5},{5,4},{6,7},{7,6},{8,9},{9,8},{10,11... | collective-permute-start | bytes 884744 | tf_op jit(solution)/shard_map/ppermute | solution.py:865
  31.0 6.5 %collective-permute-start.9 = (bf16[96,896]{1,0:T(8,128)(2,1)S(1)}, bf16[96,896]{1,0:T(8,128)(2,1)S(1)}, u32[]{:S(2)}, u32[]{:S(2)}) collective-permute-start(bf16[96,896]{1,0:T(8,128)(2,1)S(1)} %merge_kernel.1.own), channel_id=1, source_target_pairs={{0,2},{1,3},{2,0},{3,1},{4,6},{5,7},{6,4},{7,5},{8,10},{9,11},{10,... | collective-permute-start | bytes 516104 | tf_op jit(solution)/shard_map/ppermute | solution.py:865
  33.4 4.2 %copy-start = (bf16[768,768]{1,0:T(8,128)(2,1)S(1)}, bf16[768,768]{1,0:T(8,128)(2,1)}, u32[]{:S(2)}) copy-start(bf16[768,768]{1,0:T(8,128)(2,1)} %wdown.5) | copy-start | bytes 3538948
  33.4 4.1 %copy-start.1 = (bf16[768,768]{1,0:T(8,128)(2,1)S(1)}, bf16[768,768]{1,0:T(8,128)(2,1)}, u32[]{:S(2)}) copy-start(bf16[768,768]{1,0:T(8,128)(2,1)} %win.5) | copy-start | bytes 3538948
  33.4 4.1 %copy-start.10 = (f32[768]{0:T(1024)S(1)}, f32[768]{0:T(1024)}, u32[]{:S(2)}) copy-start(f32[768]{0:T(1024)} %g_ff.5) | copy-start | bytes 9220
  39.5 7.5 %copy-start.13 = (f32[768]{0:T(1024)S(1)}, f32[768]{0:T(1024)}, u32[]{:S(2)}) copy-start(f32[768]{0:T(1024)} %g_final.3) | copy-start | bytes 9220
  39.5 7.5 %copy-start.14 = (bf16[768]{0:T(1024)(128)(2,1)S(1)}, bf16[768]{0:T(1024)(128)(2,1)}, u32[]{:S(2)}) copy-start(bf16[768]{0:T(1024)(128)(2,1)} %row.3) | copy-start | bytes 4612
  39.5 1.4 %collective-permute-start.12 = (bf16[96,768]{1,0:T(8,128)(2,1)S(1)}, bf16[96,768]{1,0:T(8,128)(2,1)S(1)}, u32[]{:S(2)}, u32[]{:S(2)}) collective-permute-start(bf16[96,768]{1,0:T(8,128)(2,1)S(1)} %get-tuple-element.172), channel_id=1, source_target_pairs={{0,1},{1,0},{2,3},{3,2},{4,5},{5,4},{6,7},{7,6},{8,9},{9,8},{10,11... | collective-permute-start | bytes 442376 | tf_op jit(solution)/shard_map/ppermute | solution.py:865
  41.0 6.0 %collective-permute-start.13 = (bf16[96,768]{1,0:T(8,128)(2,1)S(1)}, bf16[96,768]{1,0:T(8,128)(2,1)S(1)}, u32[]{:S(2)}, u32[]{:S(2)}) collective-permute-start(bf16[96,768]{1,0:T(8,128)(2,1)S(1)} %add_convert_fusion.3.part_a), channel_id=1, source_target_pairs={{0,2},{1,3},{2,0},{3,1},{4,6},{5,7},{6,4},{7,5},{8,10},{9,11},{10,... | collective-permute-start | bytes 442376 | tf_op jit(solution)/shard_map/ppermute | solution.py:865
  46.9 6.4 %collective-permute-start.17 = (bf16[2,3,96,768]{3,2,1,0:T(8,128)(2,1)S(1)}, bf16[2,3,96,768]{3,2,1,0:T(8,128)(2,1)S(1)}, u32[]{:S(2)}, u32[]{:S(2)}) collective-permute-start(bf16[2,3,96,768]{3,2,1,0:T(8,128)(2,1)S(1)} %get-tuple-element.184), channel_id=1, source_target_pairs={{0,1},{1,0},{2,3},{3,2},{4,5},{5,4},{6,7},{7,6},{8,9},{9,8},{10,11... | collective-permute-start | bytes 2654216 | tf_op jit(solution)/shard_map/ppermute | solution.py:865
  48.4 1.6 %collective-permute-start.15 = (bf16[96,768]{1,0:T(8,128)(2,1)S(1)}, bf16[96,768]{1,0:T(8,128)(2,1)S(1)}, u32[]{:S(2)}, u32[]{:S(2)}) collective-permute-start(bf16[96,768]{1,0:T(8,128)(2,1)S(1)} %down_kernel.1), channel_id=1, source_target_pairs={{0,1},{1,0},{2,3},{3,2},{4,5},{5,4},{6,7},{7,6},{8,9},{9,8},{10,11... | collective-permute-start | bytes 442376 | tf_op jit(solution)/shard_map/ppermute | solution.py:865
  50.0 6.2 %collective-permute-start.16 = (bf16[96,768]{1,0:T(8,128)(2,1)S(1)}, bf16[96,768]{1,0:T(8,128)(2,1)S(1)}, u32[]{:S(2)}, u32[]{:S(2)}) collective-permute-start(bf16[96,768]{1,0:T(8,128)(2,1)S(1)} %add_convert_fusion.2.part_a), channel_id=1, source_target_pairs={{0,2},{1,3},{2,0},{3,1},{4,6},{5,7},{6,4},{7,5},{8,10},{9,11},{10,... | collective-permute-start | bytes 442376 | tf_op jit(solution)/shard_map/ppermute | solution.py:865
  50.7 6.9 %collective-permute-start.14 = (bf16[48,896]{1,0:T(8,128)(2,1)S(1)}, bf16[48,896]{1,0:T(8,128)(2,1)S(1)}, u32[]{:S(2)}, u32[]{:S(2)}) collective-permute-start(bf16[48,896]{1,0:T(8,128)(2,1)S(1)} %get-tuple-element.189), channel_id=1, source_target_pairs={{0,16},{4,20},{8,24},{12,28},{16,0},{20,4},{24,8},{28,12},{1,17},{... | collective-permute-start | bytes 258056 | tf_op jit(solution)/shard_map/ppermute | solution.py:865
  57.7 9.3 %collective-permute-start.18 = (bf16[96,896]{1,0:T(8,128)(2,1)S(1)}, bf16[96,896]{1,0:T(8,128)(2,1)S(1)}, u32[]{:S(2)}, u32[]{:S(2)}) collective-permute-start(bf16[96,896]{1,0:T(8,128)(2,1)S(1)} %pad_maximum_fusion.3), channel_id=1, source_target_pairs={{0,8},{4,12},{8,0},{12,4},{16,24},{20,28},{24,16},{28,20},{1,9},{5... | collective-permute-start | bytes 516104 | tf_op jit(solution)/shard_map/ppermute | solution.py:865
  61.2 11.3 %collective-permute-start.20 = (bf16[3,96,768]{2,1,0:T(8,128)(2,1)S(1)}, bf16[3,96,768]{2,1,0:T(8,128)(2,1)S(1)}, u32[]{:S(2)}, u32[]{:S(2)}) collective-permute-start(bf16[3,96,768]{2,1,0:T(8,128)(2,1)S(1)} %away_kernel.1), channel_id=1, source_target_pairs={{0,2},{1,3},{2,0},{3,1},{4,6},{5,7},{6,4},{7,5},{8,10},{9,11},{10,... | collective-permute-start | bytes 1327112 | tf_op jit(solution)/shard_map/ppermute | solution.py:865
  62.7 8.8 %collective-permute-start.21 = (bf16[48,1536]{1,0:T(8,128)(2,1)S(1)}, bf16[48,1536]{1,0:T(8,128)(2,1)S(1)}, u32[]{:S(2)}, u32[]{:S(2)}) collective-permute-start(bf16[48,1536]{1,0:T(8,128)(2,1)S(1)} %get-tuple-element.201), channel_id=1, source_target_pairs={{0,16},{4,20},{8,24},{12,28},{16,0},{20,4},{24,8},{28,12},{1,17},{... | collective-permute-start | bytes 442376 | tf_op jit(solution)/shard_map/ppermute | solution.py:865
  67.1 9.2 %collective-permute-start.19 = (bf16[192,896]{1,0:T(8,128)(2,1)S(1)}, bf16[192,896]{1,0:T(8,128)(2,1)S(1)}, u32[]{:S(2)}, u32[]{:S(2)}) collective-permute-start(bf16[192,896]{1,0:T(8,128)(2,1)S(1)} %pad_maximum_fusion.1), channel_id=1, source_target_pairs={{0,4},{4,0},{8,12},{12,8},{16,20},{20,16},{24,28},{28,24},{1,5},{5... | collective-permute-start | bytes 1032200 | tf_op jit(solution)/shard_map/ppermute | solution.py:865
  76.3 8.7 %collective-permute-start.23 = (bf16[96,1536]{1,0:T(8,128)(2,1)S(1)}, bf16[96,1536]{1,0:T(8,128)(2,1)S(1)}, u32[]{:S(2)}, u32[]{:S(2)}) collective-permute-start(bf16[96,1536]{1,0:T(8,128)(2,1)S(1)} %pad_maximum_fusion.2), channel_id=1, source_target_pairs={{0,8},{4,12},{8,0},{12,4},{16,24},{20,28},{24,16},{28,20},{1,9},{5... | collective-permute-start | bytes 884744 | tf_op jit(solution)/shard_map/ppermute | solution.py:865
  76.8 19.1 %collective-permute-start.27 = (bf16[384,896]{1,0:T(8,128)(2,1)S(1)}, bf16[384,896]{1,0:T(8,128)(2,1)S(1)}, u32[]{:S(2)}, u32[]{:S(2)}) collective-permute-start(bf16[384,896]{1,0:T(8,128)(2,1)S(1)} %constant_dynamic-update-slice_fusion.rows.c_own), channel_id=1, source_target_pairs={{0,1},{1,0},{2,3},{3,2},{4,5},{5,4},{6,7},{7,6},{8,9},{9,8},{10,11... | collective-permute-start | bytes 2064392 | tf_op jit(solution)/shard_map/ppermute | solution.py:865
  80.0 5.0 %collective-permute-start.22 = (f32[16,768]{1,0:T(8,128)S(1)}, f32[16,768]{1,0:T(8,128)S(1)}, u32[]{:S(2)}, u32[]{:S(2)}) collective-permute-start(f32[16,768]{1,0:T(8,128)S(1)} %key_sum_kernel.1), channel_id=1, source_target_pairs={{0,1},{1,0},{2,3},{3,2},{4,5},{5,4},{6,7},{7,6},{8,9},{9,8},{10,11... | collective-permute-start | bytes 147464 | tf_op jit(solution)/shard_map/ppermute | solution.py:865
  81.5 14.4 %collective-permute-start.26 = (bf16[192,768]{1,0:T(8,128)(2,1)S(1)}, bf16[192,768]{1,0:T(8,128)(2,1)S(1)}, u32[]{:S(2)}, u32[]{:S(2)}) collective-permute-start(bf16[192,768]{1,0:T(8,128)(2,1)S(1)} %value_kernel.1), channel_id=1, source_target_pairs={{0,4},{4,0},{8,12},{12,8},{16,20},{20,16},{24,28},{28,24},{1,5},{5... | collective-permute-start | bytes 884744 | tf_op jit(solution)/shard_map/ppermute | solution.py:865
  85.0 5.6 %collective-permute-start.24 = (f32[16,768]{1,0:T(8,128)S(1)}, f32[16,768]{1,0:T(8,128)S(1)}, u32[]{:S(2)}, u32[]{:S(2)}) collective-permute-start(f32[16,768]{1,0:T(8,128)S(1)} %add.40), channel_id=1, source_target_pairs={{0,16},{4,20},{8,24},{12,28},{16,0},{20,4},{24,8},{28,12},{1,17},{... | collective-permute-start | bytes 147464 | tf_op jit(solution)/shard_map/ppermute | solution.py:865
  90.6 5.2 %collective-permute-start.25 = (f32[16,768]{1,0:T(8,128)S(1)}, f32[16,768]{1,0:T(8,128)S(1)}, u32[]{:S(2)}, u32[]{:S(2)}) collective-permute-start(f32[16,768]{1,0:T(8,128)S(1)} %add.41), channel_id=1, source_target_pairs={{0,8},{4,12},{8,0},{12,4},{16,24},{20,28},{24,16},{28,20},{1,9},{5... | collective-permute-start | bytes 147464 | tf_op jit(solution)/shard_map/ppermute | solution.py:865
  91.0 15.4 %collective-permute-start.30 = (bf16[192,1536]{1,0:T(8,128)(2,1)S(1)}, bf16[192,1536]{1,0:T(8,128)(2,1)S(1)}, u32[]{:S(2)}, u32[]{:S(2)}) collective-permute-start(bf16[192,1536]{1,0:T(8,128)(2,1)S(1)} %pad_maximum_fusion), channel_id=1, source_target_pairs={{0,4},{4,0},{8,12},{12,8},{16,20},{20,16},{24,28},{28,24},{1,5},{5... | collective-permute-start | bytes 1769480 | tf_op jit(solution)/shard_map/ppermute | solution.py:865
  95.9 10.5 %collective-permute-start.31 = (bf16[192,768]{1,0:T(8,128)(2,1)S(1)}, bf16[192,768]{1,0:T(8,128)(2,1)S(1)}, u32[]{:S(2)}, u32[]{:S(2)}) collective-permute-start(bf16[192,768]{1,0:T(8,128)(2,1)S(1)} %add_convert_fusion.1), channel_id=1, source_target_pairs={{0,8},{4,12},{8,0},{12,4},{16,24},{20,28},{24,16},{28,20},{1,9},{5... | collective-permute-start | bytes 884744 | tf_op jit(solution)/shard_map/ppermute | solution.py:865
  96.4 5.4 %collective-permute-start.28 = (f32[16,768]{1,0:T(8,128)S(1)}, f32[16,768]{1,0:T(8,128)S(1)}, u32[]{:S(2)}, u32[]{:S(2)}) collective-permute-start(f32[16,768]{1,0:T(8,128)S(1)} %add.42), channel_id=1, source_target_pairs={{0,2},{1,3},{2,0},{3,1},{4,6},{5,7},{6,4},{7,5},{8,10},{9,11},{10,... | collective-permute-start | bytes 147464 | tf_op jit(solution)/shard_map/ppermute | solution.py:865
  101.8 4.5 %collective-permute-start.29 = (f32[16,768]{1,0:T(8,128)S(1)}, f32[16,768]{1,0:T(8,128)S(1)}, u32[]{:S(2)}, u32[]{:S(2)}) collective-permute-start(f32[16,768]{1,0:T(8,128)S(1)} %add.43.sum_a), channel_id=1, source_target_pairs={{0,4},{4,0},{8,12},{12,8},{16,20},{20,16},{24,28},{28,24},{1,5},{5... | collective-permute-start | bytes 147464 | tf_op jit(solution)/shard_map/ppermute | solution.py:865
  106.3 1.8 %copy-start.3 = (bf16[768,192]{0,1:T(8,128)(2,1)S(1)}, bf16[768,192]{0,1:T(8,128)(2,1)}, u32[]{:S(2)}) copy-start(bf16[768,192]{0,1:T(8,128)(2,1)} %param.30) | copy-start | bytes 884740
  106.3 1.8 %copy-start.4 = (bf16[768,192]{0,1:T(8,128)(2,1)S(1)}, bf16[768,192]{0,1:T(8,128)(2,1)}, u32[]{:S(2)}) copy-start(bf16[768,192]{0,1:T(8,128)(2,1)} %param.31) | copy-start | bytes 884740
  106.3 1.8 %copy-start.8 = (f32[768]{0:T(1024)S(1)}, f32[768]{0:T(1024)}, u32[]{:S(2)}) copy-start(f32[768]{0:T(1024)} %g_cross.5) | copy-start | bytes 9220
  106.4 3.9 %collective-permute-start.33 = (bf16[384,1536]{1,0:T(8,128)(2,1)S(1)}, bf16[384,1536]{1,0:T(8,128)(2,1)S(1)}, u32[]{:S(2)}, u32[]{:S(2)}) collective-permute-start(bf16[384,1536]{1,0:T(8,128)(2,1)S(1)} %constant_dynamic-update-slice_fusion.4.both_own), channel_id=1, source_target_pairs={{0,1},{1,0},{2,3},{3,2},{4,5},{5,4},{6,7},{7,6},{8,9},{9,8},{10,11... | collective-permute-start | bytes 3538952 | tf_op jit(solution)/shard_map/ppermute | solution.py:865
  106.6 16.7 %collective-permute-start.37 = (bf16[192,768]{1,0:T(8,128)(2,1)S(1)}, bf16[192,768]{1,0:T(8,128)(2,1)S(1)}, u32[]{:S(2)}, u32[]{:S(2)}) collective-permute-start(bf16[192,768]{1,0:T(8,128)(2,1)S(1)} %add_convert_fusion.value_a), channel_id=1, source_target_pairs={{0,16},{4,20},{8,24},{12,28},{16,0},{20,4},{24,8},{28,12},{1,17},{... | collective-permute-start | bytes 884744 | tf_op jit(solution)/shard_map/ppermute | solution.py:865
  109.1 1.3 %collective-permute-start.32 = (f32[8,768]{1,0:T(8,128)S(1)}, f32[8,768]{1,0:T(8,128)S(1)}, u32[]{:S(2)}, u32[]{:S(2)}) collective-permute-start(f32[8,768]{1,0:T(8,128)S(1)} %get-tuple-element.243), channel_id=1, source_target_pairs={{0,1},{1,0},{2,3},{3,2},{4,5},{5,4},{6,7},{7,6},{8,9},{9,8},{10,11... | collective-permute-start | bytes 73736 | tf_op jit(solution)/shard_map/ppermute | solution.py:865
  110.4 4.9 %collective-permute-start.34 = (f32[8,768]{1,0:T(8,128)S(1)}, f32[8,768]{1,0:T(8,128)S(1)}, u32[]{:S(2)}, u32[]{:S(2)}) collective-permute-start(f32[8,768]{1,0:T(8,128)S(1)} %add.45.part_a), channel_id=1, source_target_pairs={{0,2},{1,3},{2,0},{3,1},{4,6},{5,7},{6,4},{7,5},{8,10},{9,11},{10,... | collective-permute-start | bytes 73736 | tf_op jit(solution)/shard_map/ppermute | solution.py:865
  112.8 2.5 %copy-start.5 = (bf16[768,192]{0,1:T(8,128)(2,1)S(1)}, bf16[768,192]{0,1:T(8,128)(2,1)}, u32[]{:S(2)}) copy-start(bf16[768,192]{0,1:T(8,128)(2,1)} %param.27) | copy-start | bytes 884740
  112.8 2.5 %copy-start.6 = (bf16[192,768]{1,0:T(8,128)(2,1)S(1)}, bf16[192,768]{1,0:T(8,128)(2,1)}, u32[]{:S(2)}) copy-start(bf16[192,768]{1,0:T(8,128)(2,1)} %wos.3) | copy-start | bytes 884740
  112.8 2.5 %copy-start.9 = (f32[768]{0:T(1024)S(1)}, f32[768]{0:T(1024)}, u32[]{:S(2)}) copy-start(f32[768]{0:T(1024)} %g_self.5) | copy-start | bytes 9220
  112.8 2.5 %copy-start.12 = (bf16[768]{0:T(1024)(128)(2,1)S(1)}, bf16[768]{0:T(1024)(128)(2,1)}, u32[]{:S(2)}) copy-start(bf16[768]{0:T(1024)(128)(2,1)} %start.7) | copy-start | bytes 4612
  116.3 1.2 collective-permute-start.35
  117.5 5.7 %collective-permute-start.36 = (f32[8,768]{1,0:T(8,128)S(1)}, f32[8,768]{1,0:T(8,128)S(1)}, u32[]{:S(2)}, u32[]{:S(2)}) collective-permute-start(f32[8,768]{1,0:T(8,128)S(1)} %add.46.part_a), channel_id=1, source_target_pairs={{0,2},{1,3},{2,0},{3,1},{4,6},{5,7},{6,4},{7,5},{8,10},{9,11},{10,... | collective-permute-start | bytes 73736 | tf_op jit(solution)/shard_map/ppermute | solution.py:865

commit v7 on v6

--- a/solution.py
+++ b/solution.py
@@ -571,26 +571,27 @@
 
 
 def enc_grad_kernel(first, last, ds, qa, qb, dap, vd, *refs):
-    grad_out, slots, sems = refs[-3:]
-    pieces, size = slots.shape[:2]
+    grad_out, held, sems = refs[-3:]
     qk = qa[...] + qb[...]
     lane = iota((1, LANES), 1)
     copies = []
-    for k in range((last - first) // size):
-        if k >= pieces:
-            copies[k - pieces].wait()
-        start = first + k * size
-        for b in range(size):
-            scale = jnp.sum(jnp.where(lane == start + b, ds[0:1], 0.0), axis=1, keepdims=True)
-            right = jnp.concatenate([qk, vd[start + b].astype(f32)], axis=0) * scale
-            slots[k % pieces, b] = tn(dap[start + b], right.astype(bf16)).astype(bf16)
+    begin = first
+    while begin < last:
+        size = 4
+        for b in range(begin, begin + size):
+            scale = jnp.sum(jnp.where(lane == b, ds[0:1], 0.0), axis=1, keepdims=True)
+            right = jnp.concatenate([qk, vd[b].astype(f32)], axis=0) * scale
+            held[b - first] = tn(dap[b], right.astype(bf16)).astype(bf16)
         copies.append(
             pltpu.make_async_copy(
-                slots.at[k % pieces], grad_out.at[pl.ds(start, size)], sems.at[k % pieces]
+                held.at[pl.ds(begin - first, size)],
+                grad_out.at[pl.ds(begin, size)],
+                sems.at[len(copies)],
             )
         )
         copies[-1].start()
-    for copy in copies[-pieces:]:
+        begin += size
+    for copy in copies:
         copy.wait()
 
 
@@ -1078,7 +1079,6 @@
     away = plain(
         away_kernel, shape((own_heads, slots, D), bf16), scal, keep, got, smem=1
     )
-    other = swap(away, "heads", 2)
     part_b, away = tie(part_b, away)
     dh2, grads, dc, dc_own, inner, ff = plain(
         context_kernel,
@@ -1130,6 +1130,8 @@
         )
 
     dap, vd = back(0, 1)
+    dap, away = tie(dap, away)
+    other = swap(away, "heads", 2)
     dap, c_far = tie(dap, c_far)
     c_all = jnp.concatenate([c_all, c_far], axis=0)
     c_far = swap(c_all, *over_docs[last])
@@ -1167,7 +1169,6 @@
 
     def enc_grads(first, last, grads=None):
         outs = pltpu.HBM(enc_out.shape, bf16)
-        size = 8
         args = (ds_mine, qk_a, qk_b, dap, vd)
         return plain(
             functools.partial(enc_grad_kernel, first, last),
@@ -1177,7 +1178,7 @@
             hbm=() if grads is None else (len(args),),
             hbm_out=True,
             onto={} if grads is None else {len(args): 0},
-            scratch=[pltpu.VMEM((4, size, tokens, D), bf16), pltpu.SemaphoreType.DMA((4,))],
+            scratch=[pltpu.VMEM((last - first, tokens, D), bf16), pltpu.SemaphoreType.DMA((8,))],
             limit=16,
         )
 

time: 125 us -> 126 us (level); the launches traced: 124 us -> 127 us
  Pallas kernels: 54.2 us -> 66.1 us
  starting transfers between devices: 37.8 us -> 33 us
  waiting for transfers between devices: 30.4 us -> 26.1 us
    pallas_call x27, Pallas kernels: 48.4 us -> 60.3 us  [plain(): pl.pallas_call(kernel, out_shape=outs, in_specs=[whole_spec(space) for sp...]
    ppermute x38, starting transfers between devices: 37.8 us -> 33 us  [swap(): return lax.ppermute(x, axis, [(i, i ^ bit) for i in range(size)])]
    ppermute x38, waiting for transfers between devices: 30.4 us -> 26.1 us  [swap(): return lax.ppermute(x, axis, [(i, i ^ bit) for i in range(size)])]
  transfers between devices with their start and end apart: 38 -> 38, of which waited for: 17 -> 16; matrix products, arithmetic and copies ran while one was open for 0% -> 0% of each run, Pallas kernels for 39% -> 47%
where the time goes in v7:
time: 126 us; the launch traced here: 127 us
  Pallas kernels  66.1 us (52%)
  starting transfers between devices  33 us (26%)
  waiting for transfers between devices  26.1 us (21%)
    pallas_call x27, Pallas kernels, plain(): pl.pallas_call(kernel, out_shape=outs, in_specs=[whole_spec(space) for sp...  60.3 us
    ppermute x38, starting transfers between devices, swap(): return lax.ppermute(x, axis, [(i, i ^ bit) for i in range(size)])  33 us
    ppermute x38, waiting for transfers between devices, swap(): return lax.ppermute(x, axis, [(i, i ^ bit) for i in range(size)])  26.1 us
    pallas_call x2, Pallas kernels, load(): pl.pallas_call(functools.partial(load_kernel, first, last), out_shape=plt...  5.84 us
  transfers between devices with their start and end apart: 38, of which 16 were waited for; matrix products, arithmetic and copies ran while one was open for 0% of the time, Pallas kernels for 47%

profile of v7, /device:TPU:0, one launch (start us, length us, event | category | flops | bytes accessed | tf_op | source)
XLA Modules:
  0.0 127.2 jit_solution(3884389416866955552)
XLA Ops:
  0.7 1.5 %self_kernel.1 = f32[8,768]{1,0:T(8,128)S(1)} custom-call(bf16[768]{0:T(1024)(128)(2,1)} %start.7, f32[768]{0:T(1024)} %g_self.5, bf16[192,768]{1,0:T(8,128)(2,1)} %bitcast.15, bf16[192,768]{1,0:T(8,128)(2,1)} %wos.3), custom_call_target="tpu_custom_call" | custom-call | tf_op jit(solution)/shard_map/self_kernel/pallas_call | solution.py:841
  2.6 0.8 collective-permute-done
  3.5 2.9 %collective-permute-start.1 = (f32[8,768]{1,0:T(8,128)S(1)}, f32[8,768]{1,0:T(8,128)S(1)}, u32[]{:S(2)}, u32[]{:S(2)}) collective-permute-start(f32[8,768]{1,0:T(8,128)S(1)} %add.36.since.part_a), channel_id=1, source_target_pairs={{0,2},{1,3},{2,0},{3,1},{4,6},{5,7},{6,4},{7,5},{8,10},{9,11},{10,... | collective-permute-start | bytes 73736 | tf_op jit(solution)/shard_map/ppermute | solution.py:866
  6.4 2.4 %load_kernel.2.refs_0_ = bf16[96,128,768]{2,1,0:T(8,128)(2,1)S(1)} custom-call(bf16[96,128,768]{2,1,0:T(8,128)(2,1)} %enc.5, f32[8,768]{1,0:T(8,128)S(1)} %add.36.since.part_a, s32[2]{0:T(128)S(1)} %pad_add_fusion.scal), custom_call_target="tpu_custom_call" | custom-call | tf_op jit(solution)/shard_map/load_kernel/pallas_call | solution.py:932
  8.9 1.3 %collective-permute-start.4 = (bf16[192,768]{1,0:T(8,128)(2,1)S(1)}, bf16[192,768]{1,0:T(8,128)(2,1)S(1)}, u32[]{:S(2)}, u32[]{:S(2)}) collective-permute-start(bf16[192,768]{1,0:T(8,128)(2,1)S(1)} %bitcast.17), channel_id=1, source_target_pairs={{0,2},{1,3},{2,0},{3,1},{4,6},{5,7},{6,4},{7,5},{8,10},{9,11},{10,... | collective-permute-start | bytes 884744 | tf_op jit(solution)/shard_map/ppermute | solution.py:866
  10.2 1.5 %query_kernel.1 = (f32[16,768]{1,0:T(8,128)S(1)}, f32[1,768]{1,0:T(1,128)S(1)}) custom-call(s32[2]{0:T(128)S(1)} %pad_add_fusion.scal, f32[8,768]{1,0:T(8,128)S(1)} %add.36.since.part_a, f32[8,768]{1,0:T(8,128)S(1)} %collective-permute-done.1.part_b, bf16[768]{0:T(1024)(128)(2,1)} %start.7, f32[768]{0:T(1024)} %g_cross.5, bf16[192,768]{1,0:T(8,128)(2,1)} %bitcast.11, ...), custom_call_target="tpu_custom_call" | custom-call | tf_op jit(solution)/shard_map/query_kernel/pallas_call | solution.py:841
  11.7 1.2 collective-permute-done.2
  13.0 0.9 collective-permute-start.3
  13.9 3.4 %load_kernel.3._ = bf16[96,128,768]{2,1,0:T(8,128)(2,1)S(1)} custom-call(bf16[96,128,768]{2,1,0:T(8,128)(2,1)} %enc.5, f32[16,768]{1,0:T(8,128)S(1)} %add.37.since.qa, s32[2]{0:T(128)S(1)} %pad_add_fusion.scal, bf16[96,128,768]{2,1,0:T(8,128)(2,1)S(1)} %load_kernel.2.refs_0_), custom_call_target="tpu_custom_call", output_to_operand_aliasing={{}: (3, {})} | custom-call | tf_op jit(solution)/shard_map/load_kernel/pallas_call | solution.py:932
  17.3 1.5 %collective-permute-done.3.qb = f32[16,768]{1,0:T(8,128)S(1)} collective-permute-done((f32[16,768]{1,0:T(8,128)S(1)}, f32[16,768]{1,0:T(8,128)S(1)}, u32[]{:S(2)}, u32[]{:S(2)}) %collective-permute-start.3) | collective-permute-done | bytes 49184 | tf_op jit(solution)/shard_map/ppermute | solution.py:866
  19.2 0.5 collective-permute-start.7
  19.7 8.7 %attend_kernel.1 = (bf16[96,128,768]{2,1,0:T(8,128)(2,1)S(1)}, f32[96,16,128]{2,1,0:T(8,128)S(1)}, f32[6,1536,128]{2,1,0:T(8,128)S(1)}, bf16[96,128]{1,0:T(8,128)(2,1)S(1)}) custom-call(s32[2]{0:T(128)S(1)} %pad_add_fusion.scal, s32[8]{0:T(128)S(1)} %copy-done.11, s32[384]{0:T(512)S(1)} %copy-done.15, ...), custom_call_target="tpu_custom_call", output_to_operand_aliasing={{0}: (6, {})} | custom-call | tf_op jit(solution)/shard_map/attend_kernel/pallas_call | solution.py:841
  28.4 1.8 %project_kernel.1 = (bf16[96,896]{1,0:T(8,128)(2,1)S(1)}, bf16[12,96,768]{2,1,0:T(8,128)(2,1)S(1)}, bf16[768,768]{1,0:T(8,128)(2,1)S(1)}) custom-call(s32[2]{0:T(128)S(1)} %pad_add_fusion.scal, f32[6,1536,128]{2,1,0:T(8,128)S(1)} %get-tuple-element.163.summed, bf16[96,128]{1,0:T(8,128)(2,1)S(1)} %get-tuple-element.164.extra, bf16[192,768]{1,0:T(8,128)(2,1)S(1)} %bitcast.19, ...), custom_call_target="tpu_custom_call" | custom-call | tf_op jit(solution)/shard_map/project_kernel/pallas_call | solution.py:841
  30.4 0.5 collective-permute-start.10
  30.9 0.8 collective-permute-done.8.other
  31.8 1.0 merge_kernel.1.own
  32.7 1.7 %collective-permute-start.9 = (bf16[96,896]{1,0:T(8,128)(2,1)S(1)}, bf16[96,896]{1,0:T(8,128)(2,1)S(1)}, u32[]{:S(2)}, u32[]{:S(2)}) collective-permute-start(bf16[96,896]{1,0:T(8,128)(2,1)S(1)} %merge_kernel.1.own), channel_id=1, source_target_pairs={{0,2},{1,3},{2,0},{3,1},{4,6},{5,7},{6,4},{7,5},{8,10},{9,11},{10,... | collective-permute-start | bytes 516104 | tf_op jit(solution)/shard_map/ppermute | solution.py:866
  34.5 1.6 %target_kernel.1 = (f32[24,384]{1,0:T(8,128)S(1)}, f32[24,384]{1,0:T(8,128)S(1)}, bf16[384,384]{1,0:T(8,128)(2,1)S(1)}, bf16[384,384]{1,0:T(8,128)(2,1)S(1)}) custom-call(s32[2]{0:T(128)S(1)} %pad_add_fusion.scal, s32[8]{0:T(128)S(1)} %copy-done.11, s32[24]{0:T(128)S(1)} %copy-done.17, f32[384]{0:T(512)S(1)} %copy-done.16), custom_call_target="tpu_custom_call" | custom-call | tf_op jit(solution)/shard_map/target_kernel/pallas_call | solution.py:841
  36.1 0.6 arrange_kernel.1.wo.wout
  36.8 2.4 %collective-permute-done.9.other = bf16[96,896]{1,0:T(8,128)(2,1)S(1)} collective-permute-done((bf16[96,896]{1,0:T(8,128)(2,1)S(1)}, bf16[96,896]{1,0:T(8,128)(2,1)S(1)}, u32[]{:S(2)}, u32[]{:S(2)}) %collective-permute-start.9) | collective-permute-done | bytes 172064 | tf_op jit(solution)/shard_map/ppermute | solution.py:866
  39.2 1.9 %forward_kernel.1 = (bf16[48,768]{1,0:T(8,128)(2,1)S(1)}, f32[96,768]{1,0:T(8,128)S(1)}, f32[96,128]{1,0:T(8,128)S(1)}, f32[96,768]{1,0:T(8,128)S(1)}, f32[96,76...) custom-call(s32[2]{0:T(128)S(1)} %pad_add_fusion.scal, bf16[96,896]{1,0:T(8,128)(2,1)S(1)} %merge_kernel.1.own, ...), custom_call_target="tpu_custom_call" | custom-call | tf_op jit(solution)/shard_map/forward_kernel/pallas_call | solution.py:841
  41.3 1.4 %collective-permute-done.12 = bf16[96,768]{1,0:T(8,128)(2,1)S(1)} collective-permute-done((bf16[96,768]{1,0:T(8,128)(2,1)S(1)}, bf16[96,768]{1,0:T(8,128)(2,1)S(1)}, u32[]{:S(2)}, u32[]{:S(2)}) %collective-permute-start.12) | collective-permute-done | bytes 147488 | tf_op jit(solution)/shard_map/ppermute | solution.py:866
  42.7 1.7 %collective-permute-start.13 = (bf16[96,768]{1,0:T(8,128)(2,1)S(1)}, bf16[96,768]{1,0:T(8,128)(2,1)S(1)}, u32[]{:S(2)}, u32[]{:S(2)}) collective-permute-start(bf16[96,768]{1,0:T(8,128)(2,1)S(1)} %add_convert_fusion.3.part_a), channel_id=1, source_target_pairs={{0,2},{1,3},{2,0},{3,1},{4,6},{5,7},{6,4},{7,5},{8,10},{9,11},{10,... | collective-permute-start | bytes 442376 | tf_op jit(solution)/shard_map/ppermute | solution.py:866
  44.4 0.9 share_kernel.1
  45.3 3.3 %collective-permute-done.13.part_b = bf16[96,768]{1,0:T(8,128)(2,1)S(1)} collective-permute-done((bf16[96,768]{1,0:T(8,128)(2,1)S(1)}, bf16[96,768]{1,0:T(8,128)(2,1)S(1)}, u32[]{:S(2)}, u32[]{:S(2)}) %collective-permute-start.13) | collective-permute-done | bytes 147488 | tf_op jit(solution)/shard_map/ppermute | solution.py:866
  49.1 0.9 down_kernel.1
  50.1 0.6 collective-permute-start.15
  50.6 1.0 collective-permute-done.15
  51.7 1.8 %collective-permute-start.16 = (bf16[96,768]{1,0:T(8,128)(2,1)S(1)}, bf16[96,768]{1,0:T(8,128)(2,1)S(1)}, u32[]{:S(2)}, u32[]{:S(2)}) collective-permute-start(bf16[96,768]{1,0:T(8,128)(2,1)S(1)} %add_convert_fusion.2.part_a), channel_id=1, source_target_pairs={{0,2},{1,3},{2,0},{3,1},{4,6},{5,7},{6,4},{7,5},{8,10},{9,11},{10,... | collective-permute-start | bytes 442376 | tf_op jit(solution)/shard_map/ppermute | solution.py:866
  53.5 0.6 away_kernel.1
  54.1 3.8 %collective-permute-done.16.part_b = bf16[96,768]{1,0:T(8,128)(2,1)S(1)} collective-permute-done((bf16[96,768]{1,0:T(8,128)(2,1)S(1)}, bf16[96,768]{1,0:T(8,128)(2,1)S(1)}, u32[]{:S(2)}, u32[]{:S(2)}) %collective-permute-start.16) | collective-permute-done | bytes 147488 | tf_op jit(solution)/shard_map/ppermute | solution.py:866
  57.9 1.5 %context_kernel.1 = (bf16[96,768]{1,0:T(8,128)(2,1)S(1)}, bf16[48,1536]{1,0:T(8,128)(2,1)S(1)}, bf16[96,768]{1,0:T(8,128)(2,1)S(1)}, bf16[96,192]{1,0:T(8,128)(2...) custom-call(s32[2]{0:T(128)S(1)} %pad_add_fusion.scal, bf16[96,768]{1,0:T(8,128)(2,1)S(1)} %add_convert_fusion.2.part_a, ...), custom_call_target="tpu_custom_call" | custom-call | tf_op jit(solution)/shard_map/context_kernel/pallas_call | solution.py:841
  59.5 3.5 %back_kernel.2 = (bf16[96,32,128]{2,1,0:T(8,128)(2,1)S(1)}, bf16[96,16,768]{2,1,0:T(8,128)(2,1)S(1)}) custom-call(s32[2]{0:T(128)S(1)} %pad_add_fusion.scal, s32[8]{0:T(128)S(1)} %copy-done.11, bf16[96,128,768]{2,1,0:T(8,128)(2,1)S(1)} %get-tuple-element.194.enc, f32[96,16,128]{2,1,0:T(8,128)S(1)} %get-tuple-element.195.p, ...), custom_call_target="tpu_custom_call" | custom-call | tf_op jit(solution)/shard_map/back_kernel/pallas_call | solution.py:841
  63.0 1.7 %collective-permute-start.20 = (bf16[3,96,768]{2,1,0:T(8,128)(2,1)S(1)}, bf16[3,96,768]{2,1,0:T(8,128)(2,1)S(1)}, u32[]{:S(2)}, u32[]{:S(2)}) collective-permute-start(bf16[3,96,768]{2,1,0:T(8,128)(2,1)S(1)} %away_kernel.1), channel_id=1, source_target_pairs={{0,2},{1,3},{2,0},{3,1},{4,6},{5,7},{6,4},{7,5},{8,10},{9,11},{10,... | collective-permute-start | bytes 1327112 | tf_op jit(solution)/shard_map/ppermute | solution.py:866
  64.7 2.3 %collective-permute-start.21 = (bf16[48,1536]{1,0:T(8,128)(2,1)S(1)}, bf16[48,1536]{1,0:T(8,128)(2,1)S(1)}, u32[]{:S(2)}, u32[]{:S(2)}) collective-permute-start(bf16[48,1536]{1,0:T(8,128)(2,1)S(1)} %get-tuple-element.207), channel_id=1, source_target_pairs={{0,16},{4,20},{8,24},{12,28},{16,0},{20,4},{24,8},{28,12},{1,17},{... | collective-permute-start | bytes 442376 | tf_op jit(solution)/shard_map/ppermute | solution.py:866
  67.1 3.4 %collective-permute-start.19 = (bf16[192,896]{1,0:T(8,128)(2,1)S(1)}, bf16[192,896]{1,0:T(8,128)(2,1)S(1)}, u32[]{:S(2)}, u32[]{:S(2)}) collective-permute-start(bf16[192,896]{1,0:T(8,128)(2,1)S(1)} %pad_maximum_fusion.1), channel_id=1, source_target_pairs={{0,4},{4,0},{8,12},{12,8},{16,20},{20,16},{24,28},{28,24},{1,5},{5... | collective-permute-start | bytes 1032200 | tf_op jit(solution)/shard_map/ppermute | solution.py:866
  70.5 6.1 %back_kernel.3 = (bf16[96,32,128]{2,1,0:T(8,128)(2,1)S(1)}, bf16[96,16,768]{2,1,0:T(8,128)(2,1)S(1)}) custom-call(s32[2]{0:T(128)S(1)} %pad_add_fusion.scal, s32[8]{0:T(128)S(1)} %copy-done.11, bf16[96,128,768]{2,1,0:T(8,128)(2,1)S(1)} %get-tuple-element.194.enc, ...), custom_call_target="tpu_custom_call", output_to_operand_aliasing={{0}: (8, {}), {1}: (9, {})} | custom-call | tf_op jit(solution)/shard_map/back_kernel/pallas_call | solution.py:841
  76.7 1.2 collective-permute-done.19
  78.4 1.4 %list_kernel.1 = (f32[384]{0:T(512)}, f32[1,1]{1,0:T(1,128)}, f32[1,384]{1,0:T(1,128)S(1)}, f32[8,128]{1,0:T(8,128)S(1)}) custom-call(s32[2]{0:T(128)S(1)} %pad_add_fusion.scal, s32[8]{0:T(128)S(1)} %copy-done.11, bf16[384,896]{1,0:T(8,128)(2,1)S(1)} %constant_dynamic-update-slice_fusion.rows.c_own, f32[24,384]{1,0:T(8,128)S(1)} %get-tuple-element.209.targets, ...), custom_call_target="tpu_custom_call" | custom-call | tf_op jit(solution)/shard_map/list_kernel/pallas_call | solution.py:841
  79.8 3.7 %key_sum_kernel.1 = f32[16,768]{1,0:T(8,128)S(1)} custom-call(s32[2]{0:T(128)S(1)} %pad_add_fusion.scal, s32[8]{0:T(128)S(1)} %copy-done.11, f32[8,128]{1,0:T(8,128)S(1)} %get-tuple-element.234.ds, bf16[96,128,768]{2,1,0:T(8,128)(2,1)S(1)} %get-tuple-element.194.enc, bf16[96,32,128]{2,1,0:T(8,128)(2,1)S(1)} %get-tuple-element.214.dap, ...), custom_call_target="tpu_custom_call" | custom-call | tf_op jit(solution)/shard_map/key_sum_kernel/pallas_call | solution.py:841
  83.5 0.5 collective-permute-start.22
  84.0 1.0 value_kernel.1
  85.5 3.5 %collective-permute-start.24 = (f32[16,768]{1,0:T(8,128)S(1)}, f32[16,768]{1,0:T(8,128)S(1)}, u32[]{:S(2)}, u32[]{:S(2)}) collective-permute-start(f32[16,768]{1,0:T(8,128)S(1)} %add.40), channel_id=1, source_target_pairs={{0,16},{4,20},{8,24},{12,28},{16,0},{20,4},{24,8},{28,12},{1,17},{... | collective-permute-start | bytes 147464 | tf_op jit(solution)/shard_map/ppermute | solution.py:866
  89.0 3.2 %enc_grad_kernel.3.refs_0_ = bf16[96,128,768]{2,1,0:T(8,128)(2,1)} custom-call(f32[8,128]{1,0:T(8,128)S(1)} %get-tuple-element.234.ds, f32[16,768]{1,0:T(8,128)S(1)} %add.37.since.qa, f32[16,768]{1,0:T(8,128)S(1)} %collective-permute-done.3.qb, bf16[96,32,128]{2,1,0:T(8,128)(2,1)S(1)} %get-tuple-element.214.dap, bf16[96,16,768]{2,1,0:T(8,128)(2,1)S(1)} %get-tuple-element.224.vd), custom_call_target="tpu_custom_call" | custom-call | tf_op jit(solution)/shard_map/enc_grad_kernel/pallas_call | solution.py:841
  92.2 1.8 %collective-permute-start.25 = (f32[16,768]{1,0:T(8,128)S(1)}, f32[16,768]{1,0:T(8,128)S(1)}, u32[]{:S(2)}, u32[]{:S(2)}) collective-permute-start(f32[16,768]{1,0:T(8,128)S(1)} %add.41), channel_id=1, source_target_pairs={{0,8},{4,12},{8,0},{12,4},{16,24},{20,28},{24,16},{28,20},{1,9},{5... | collective-permute-start | bytes 147464 | tf_op jit(solution)/shard_map/ppermute | solution.py:866
  94.1 3.2 %enc_grad_kernel.4.refs_0_ = bf16[96,128,768]{2,1,0:T(8,128)(2,1)} custom-call(f32[8,128]{1,0:T(8,128)S(1)} %get-tuple-element.234.ds, f32[16,768]{1,0:T(8,128)S(1)} %add.37.since.qa, f32[16,768]{1,0:T(8,128)S(1)} %collective-permute-done.3.qb, bf16[96,32,128]{2,1,0:T(8,128)(2,1)S(1)} %get-tuple-element.214.dap, ...), custom_call_target="tpu_custom_call", output_to_operand_aliasing={{}: (5, {})} | custom-call | tf_op jit(solution)/shard_map/enc_grad_kernel/pallas_call | solution.py:841
  97.4 1.0 collective-permute-start.31
  98.4 1.4 %collective-permute-start.28 = (f32[16,768]{1,0:T(8,128)S(1)}, f32[16,768]{1,0:T(8,128)S(1)}, u32[]{:S(2)}, u32[]{:S(2)}) collective-permute-start(f32[16,768]{1,0:T(8,128)S(1)} %add.42), channel_id=1, source_target_pairs={{0,2},{1,3},{2,0},{3,1},{4,6},{5,7},{6,4},{7,5},{8,10},{9,11},{10,... | collective-permute-start | bytes 147464 | tf_op jit(solution)/shard_map/ppermute | solution.py:866
  99.8 3.2 %enc_grad_kernel.5 = bf16[96,128,768]{2,1,0:T(8,128)(2,1)} custom-call(f32[8,128]{1,0:T(8,128)S(1)} %get-tuple-element.234.ds, f32[16,768]{1,0:T(8,128)S(1)} %add.37.since.qa, f32[16,768]{1,0:T(8,128)S(1)} %collective-permute-done.3.qb, bf16[96,32,128]{2,1,0:T(8,128)(2,1)S(1)} %get-tuple-element.214.dap, ...), custom_call_target="tpu_custom_call", output_to_operand_aliasing={{}: (5, {})} | custom-call | tf_op jit(solution)/shard_map/enc_grad_kernel/pallas_call | solution.py:841
  103.0 0.9 collective-permute-start.29
  104.0 2.9 %weights_before_kernel.1 = (bf16[384,768]{1,0:T(8,128)(2,1)S(1)}, bf16[384,768]{1,0:T(8,128)(2,1)S(1)}, f32[384,768]{1,0:T(8,128)S(1)}, bf16[384,192]{1,0:T(8,128)(2,1)S(1)}) custom-call(s32[2]{0:T(128)S(1)} %pad_add_fusion.scal, s32[8]{0:T(128)S(1)} %copy-done.11, bf16[384,896]{1,0:T(8,128)(2,1)S(1)} %constant_dynamic-update-slice_fusion.rows.c_own, ...), custom_call_target="tpu_custom_call" | custom-call | tf_op jit(solution)/shard_map/weights_before_kernel/pallas_call | solution.py:841
  106.9 2.7 %collective-permute-done.29.sum_b = f32[16,768]{1,0:T(8,128)S(1)} collective-permute-done((f32[16,768]{1,0:T(8,128)S(1)}, f32[16,768]{1,0:T(8,128)S(1)}, u32[]{:S(2)}, u32[]{:S(2)}) %collective-permute-start.29) | collective-permute-done | bytes 49184 | tf_op jit(solution)/shard_map/ppermute | solution.py:866
  109.8 1.2 collective-permute-start.37
  111.0 1.0 key_kernel.1
  112.3 1.0 collective-permute-done.32
  113.3 0.6 collective-permute-start.34
  113.8 2.4 %grads_kernel.1 = (bf16[384,768]{1,0:T(8,128)(2,1)S(1)}, bf16[384,1536]{1,0:T(8,128)(2,1)S(1)}) custom-call(s32[2]{0:T(128)S(1)} %pad_add_fusion.scal, s32[8]{0:T(128)S(1)} %copy-done.11, f32[384,768]{1,0:T(8,128)S(1)} %get-tuple-element.252.slope, bf16[384,1536]{1,0:T(8,128)(2,1)S(1)} %constant_dynamic-update-slice_fusion.4.both_own, ...), custom_call_target="tpu_custom_call" | custom-call | tf_op jit(solution)/shard_map/grads_kernel/pallas_call | solution.py:841
  116.3 0.9 collective-permute-done.34.part_b
  117.2 1.1 hidden_kernel.1
  118.2 1.2 collective-permute-done.35
  119.4 0.7 collective-permute-start.36
  120.1 3.5 %outer_kernel.1 = (f32[768,768]{1,0:T(8,128)}, f32[768,768]{1,0:T(8,128)}, f32[192,768]{1,0:T(8,128)}, f32[192,768]{1,0:T(8,128)}, f32[192,768]{1,0:T(8,128)}, /*index=5*/f32[192,768]{1,0:T(8,128)}, f32[192,768]{1,0:T(8,128)}) custom-call(bf16[384,768]{1,0:T(8,128)(2,1)S(1)} %get-tuple-element.259.y3, bf16[384,768]{1,0:T(8,128)(2,1)S(1)} %get-tuple-element.260.dz, ...), custom_call_target="tpu_custom_call" | custom-call | tf_op jit(solution)/shard_map/outer_kernel/pallas_call | solution.py:841
  123.7 2.5 %collective-permute-done.37.value_b = bf16[192,768]{1,0:T(8,128)(2,1)S(1)} collective-permute-done((bf16[192,768]{1,0:T(8,128)(2,1)S(1)}, bf16[192,768]{1,0:T(8,128)(2,1)S(1)}, u32[]{:S(2)}, u32[]{:S(2)}) %collective-permute-start.37) | collective-permute-done | bytes 294944 | tf_op jit(solution)/shard_map/ppermute | solution.py:866
  126.2 1.0 start_kernel.1
  (102 shorter events, 3.7 us)
Async XLA Ops:
  2.2 1.3 %collective-permute-start = (f32[8,768]{1,0:T(8,128)S(1)}, f32[8,768]{1,0:T(8,128)S(1)}, u32[]{:S(2)}, u32[]{:S(2)}) collective-permute-start(f32[8,768]{1,0:T(8,128)S(1)} %self_kernel.1), channel_id=1, source_target_pairs={{0,1},{1,0},{2,3},{3,2},{4,5},{5,4},{6,7},{7,6},{8,9},{9,8},{10,11... | collective-permute-start | bytes 73736 | tf_op jit(solution)/shard_map/ppermute | solution.py:866
  3.5 5.4 %collective-permute-start.1 = (f32[8,768]{1,0:T(8,128)S(1)}, f32[8,768]{1,0:T(8,128)S(1)}, u32[]{:S(2)}, u32[]{:S(2)}) collective-permute-start(f32[8,768]{1,0:T(8,128)S(1)} %add.36.since.part_a), channel_id=1, source_target_pairs={{0,2},{1,3},{2,0},{3,1},{4,6},{5,7},{6,4},{7,5},{8,10},{9,11},{10,... | collective-permute-start | bytes 73736 | tf_op jit(solution)/shard_map/ppermute | solution.py:866
  6.4 2.5 %copy-start.7 = (bf16[768,192]{0,1:T(8,128)(2,1)S(1)}, bf16[768,192]{0,1:T(8,128)(2,1)}, u32[]{:S(2)}) copy-start(bf16[768,192]{0,1:T(8,128)(2,1)} %param.32) | copy-start | bytes 884740
  8.9 9.9 %collective-permute-start.4 = (bf16[192,768]{1,0:T(8,128)(2,1)S(1)}, bf16[192,768]{1,0:T(8,128)(2,1)S(1)}, u32[]{:S(2)}, u32[]{:S(2)}) collective-permute-start(bf16[192,768]{1,0:T(8,128)(2,1)S(1)} %bitcast.17), channel_id=1, source_target_pairs={{0,2},{1,3},{2,0},{3,1},{4,6},{5,7},{6,4},{7,5},{8,10},{9,11},{10,... | collective-permute-start | bytes 884744 | tf_op jit(solution)/shard_map/ppermute | solution.py:866
  11.7 1.3 collective-permute-start.2
  13.0 5.8 %copy-start.2 = (bf16[192,768]{1,0:T(8,128)(2,1)S(1)}, bf16[192,768]{1,0:T(8,128)(2,1)}, u32[]{:S(2)}) copy-start(bf16[192,768]{1,0:T(8,128)(2,1)} %wo_own.1) | copy-start | bytes 884740
  13.0 6.7 %copy-start.11 = (s32[8]{0:T(128)S(1)}, s32[8]{0:T(128)}, u32[]{:S(2)}) copy-start(s32[8]{0:T(128)} %sizes.15) | copy-start | bytes 100
  13.0 6.7 %copy-start.15 = (s32[384]{0:T(512)S(1)}, s32[384]{0:T(512)}, u32[]{:S(2)}) copy-start(s32[384]{0:T(512)} %lengths.1) | copy-start | bytes 4612
  13.0 5.8 %collective-permute-start.3 = (f32[16,768]{1,0:T(8,128)S(1)}, f32[16,768]{1,0:T(8,128)S(1)}, u32[]{:S(2)}, u32[]{:S(2)}) collective-permute-start(f32[16,768]{1,0:T(8,128)S(1)} %add.37.since.qa), channel_id=1, source_target_pairs={{0,2},{1,3},{2,0},{3,1},{4,6},{5,7},{6,4},{7,5},{8,10},{9,11},{10,... | collective-permute-start | bytes 147464 | tf_op jit(solution)/shard_map/ppermute | solution.py:866
  18.8 9.6 %collective-permute-start.6 = (bf16[192,768]{1,0:T(8,128)(2,1)S(1)}, bf16[192,768]{1,0:T(8,128)(2,1)S(1)}, u32[]{:S(2)}, u32[]{:S(2)}) collective-permute-start(bf16[192,768]{1,0:T(8,128)(2,1)S(1)} %copy-done.2), channel_id=1, source_target_pairs={{0,2},{1,3},{2,0},{3,1},{4,6},{5,7},{6,4},{7,5},{8,10},{9,11},{10,... | collective-permute-start | bytes 884744 | tf_op jit(solution)/shard_map/ppermute | solution.py:866
  19.2 9.2 %collective-permute-start.5 = (bf16[192,768]{1,0:T(8,128)(2,1)S(1)}, bf16[192,768]{1,0:T(8,128)(2,1)S(1)}, u32[]{:S(2)}, u32[]{:S(2)}) collective-permute-start(bf16[192,768]{1,0:T(8,128)(2,1)S(1)} %collective-permute-done.4.by2), channel_id=1, source_target_pairs={{0,1},{1,0},{2,3},{3,2},{4,5},{5,4},{6,7},{7,6},{8,9},{9,8},{10,11... | collective-permute-start | bytes 884744 | tf_op jit(solution)/shard_map/ppermute | solution.py:866
  19.2 9.3 %collective-permute-start.7 = (bf16[192,768]{1,0:T(8,128)(2,1)S(1)}, bf16[192,768]{1,0:T(8,128)(2,1)S(1)}, u32[]{:S(2)}, u32[]{:S(2)}) collective-permute-start(bf16[192,768]{1,0:T(8,128)(2,1)S(1)} %bitcast.18), channel_id=1, source_target_pairs={{0,1},{1,0},{2,3},{3,2},{4,5},{5,4},{6,7},{7,6},{8,9},{9,8},{10,11... | collective-permute-start | bytes 884744 | tf_op jit(solution)/shard_map/ppermute | solution.py:866
  28.4 6.0 %copy-start.16 = (f32[384]{0:T(512)S(1)}, f32[384]{0:T(512)}, u32[]{:S(2)}) copy-start(f32[384]{0:T(512)} %rel.1) | copy-start | bytes 4612
  28.4 6.0 %copy-start.17 = (s32[24]{0:T(128)S(1)}, s32[24]{0:T(128)}, u32[]{:S(2)}) copy-start(s32[24]{0:T(128)} %lens.1) | copy-start | bytes 292
  30.3 1.5 %collective-permute-start.8 = (bf16[96,896]{1,0:T(8,128)(2,1)S(1)}, bf16[96,896]{1,0:T(8,128)(2,1)S(1)}, u32[]{:S(2)}, u32[]{:S(2)}) collective-permute-start(bf16[96,896]{1,0:T(8,128)(2,1)S(1)} %get-tuple-element.166.own.first), channel_id=1, source_target_pairs={{0,1},{1,0},{2,3},{3,2},{4,5},{5,4},{6,7},{7,6},{8,9},{9,8},{10,11... | collective-permute-start | bytes 516104 | tf_op jit(solution)/shard_map/ppermute | solution.py:866
  30.4 5.8 %collective-permute-start.10 = (bf16[192,768]{1,0:T(8,128)(2,1)S(1)}, bf16[192,768]{1,0:T(8,128)(2,1)S(1)}, u32[]{:S(2)}, u32[]{:S(2)}) collective-permute-start(bf16[192,768]{1,0:T(8,128)(2,1)S(1)} %copy-done.2), channel_id=1, source_target_pairs={{0,1},{1,0},{2,3},{3,2},{4,5},{5,4},{6,7},{7,6},{8,9},{9,8},{10,11... | collective-permute-start | bytes 884744 | tf_op jit(solution)/shard_map/ppermute | solution.py:866
  30.9 5.3 %collective-permute-start.11 = (bf16[192,768]{1,0:T(8,128)(2,1)S(1)}, bf16[192,768]{1,0:T(8,128)(2,1)S(1)}, u32[]{:S(2)}, u32[]{:S(2)}) collective-permute-start(bf16[192,768]{1,0:T(8,128)(2,1)S(1)} %collective-permute-done.6.by2), channel_id=1, source_target_pairs={{0,1},{1,0},{2,3},{3,2},{4,5},{5,4},{6,7},{7,6},{8,9},{9,8},{10,11... | collective-permute-start | bytes 884744 | tf_op jit(solution)/shard_map/ppermute | solution.py:866
  32.7 6.5 %collective-permute-start.9 = (bf16[96,896]{1,0:T(8,128)(2,1)S(1)}, bf16[96,896]{1,0:T(8,128)(2,1)S(1)}, u32[]{:S(2)}, u32[]{:S(2)}) collective-permute-start(bf16[96,896]{1,0:T(8,128)(2,1)S(1)} %merge_kernel.1.own), channel_id=1, source_target_pairs={{0,2},{1,3},{2,0},{3,1},{4,6},{5,7},{6,4},{7,5},{8,10},{9,11},{10,... | collective-permute-start | bytes 516104 | tf_op jit(solution)/shard_map/ppermute | solution.py:866
  36.1 3.1 %copy-start = (bf16[768,768]{1,0:T(8,128)(2,1)S(1)}, bf16[768,768]{1,0:T(8,128)(2,1)}, u32[]{:S(2)}) copy-start(bf16[768,768]{1,0:T(8,128)(2,1)} %wdown.5) | copy-start | bytes 3538948
  36.1 3.1 %copy-start.1 = (bf16[768,768]{1,0:T(8,128)(2,1)S(1)}, bf16[768,768]{1,0:T(8,128)(2,1)}, u32[]{:S(2)}) copy-start(bf16[768,768]{1,0:T(8,128)(2,1)} %win.5) | copy-start | bytes 3538948
  36.1 3.1 %copy-start.10 = (f32[768]{0:T(1024)S(1)}, f32[768]{0:T(1024)}, u32[]{:S(2)}) copy-start(f32[768]{0:T(1024)} %g_ff.5) | copy-start | bytes 9220
  41.2 7.5 %copy-start.13 = (f32[768]{0:T(1024)S(1)}, f32[768]{0:T(1024)}, u32[]{:S(2)}) copy-start(f32[768]{0:T(1024)} %g_final.3) | copy-start | bytes 9220
  41.2 7.5 %copy-start.14 = (bf16[768]{0:T(1024)(128)(2,1)S(1)}, bf16[768]{0:T(1024)(128)(2,1)}, u32[]{:S(2)}) copy-start(bf16[768]{0:T(1024)(128)(2,1)} %row.3) | copy-start | bytes 4612
  41.2 1.4 %collective-permute-start.12 = (bf16[96,768]{1,0:T(8,128)(2,1)S(1)}, bf16[96,768]{1,0:T(8,128)(2,1)S(1)}, u32[]{:S(2)}, u32[]{:S(2)}) collective-permute-start(bf16[96,768]{1,0:T(8,128)(2,1)S(1)} %get-tuple-element.175), channel_id=1, source_target_pairs={{0,1},{1,0},{2,3},{3,2},{4,5},{5,4},{6,7},{7,6},{8,9},{9,8},{10,11... | collective-permute-start | bytes 442376 | tf_op jit(solution)/shard_map/ppermute | solution.py:866
  42.7 6.0 %collective-permute-start.13 = (bf16[96,768]{1,0:T(8,128)(2,1)S(1)}, bf16[96,768]{1,0:T(8,128)(2,1)S(1)}, u32[]{:S(2)}, u32[]{:S(2)}) collective-permute-start(bf16[96,768]{1,0:T(8,128)(2,1)S(1)} %add_convert_fusion.3.part_a), channel_id=1, source_target_pairs={{0,2},{1,3},{2,0},{3,1},{4,6},{5,7},{6,4},{7,5},{8,10},{9,11},{10,... | collective-permute-start | bytes 442376 | tf_op jit(solution)/shard_map/ppermute | solution.py:866
  48.6 4.8 %collective-permute-start.17 = (bf16[2,3,96,768]{3,2,1,0:T(8,128)(2,1)S(1)}, bf16[2,3,96,768]{3,2,1,0:T(8,128)(2,1)S(1)}, u32[]{:S(2)}, u32[]{:S(2)}) collective-permute-start(bf16[2,3,96,768]{3,2,1,0:T(8,128)(2,1)S(1)} %get-tuple-element.187), channel_id=1, source_target_pairs={{0,1},{1,0},{2,3},{3,2},{4,5},{5,4},{6,7},{7,6},{8,9},{9,8},{10,11... | collective-permute-start | bytes 2654216 | tf_op jit(solution)/shard_map/ppermute | solution.py:866
  50.1 1.6 %collective-permute-start.15 = (bf16[96,768]{1,0:T(8,128)(2,1)S(1)}, bf16[96,768]{1,0:T(8,128)(2,1)S(1)}, u32[]{:S(2)}, u32[]{:S(2)}) collective-permute-start(bf16[96,768]{1,0:T(8,128)(2,1)S(1)} %down_kernel.1), channel_id=1, source_target_pairs={{0,1},{1,0},{2,3},{3,2},{4,5},{5,4},{6,7},{7,6},{8,9},{9,8},{10,11... | collective-permute-start | bytes 442376 | tf_op jit(solution)/shard_map/ppermute | solution.py:866
  51.7 6.2 %collective-permute-start.16 = (bf16[96,768]{1,0:T(8,128)(2,1)S(1)}, bf16[96,768]{1,0:T(8,128)(2,1)S(1)}, u32[]{:S(2)}, u32[]{:S(2)}) collective-permute-start(bf16[96,768]{1,0:T(8,128)(2,1)S(1)} %add_convert_fusion.2.part_a), channel_id=1, source_target_pairs={{0,2},{1,3},{2,0},{3,1},{4,6},{5,7},{6,4},{7,5},{8,10},{9,11},{10,... | collective-permute-start | bytes 442376 | tf_op jit(solution)/shard_map/ppermute | solution.py:866
  53.4 5.9 %collective-permute-start.14 = (bf16[48,896]{1,0:T(8,128)(2,1)S(1)}, bf16[48,896]{1,0:T(8,128)(2,1)S(1)}, u32[]{:S(2)}, u32[]{:S(2)}) collective-permute-start(bf16[48,896]{1,0:T(8,128)(2,1)S(1)} %get-tuple-element.192), channel_id=1, source_target_pairs={{0,16},{4,20},{8,24},{12,28},{16,0},{20,4},{24,8},{28,12},{1,17},{... | collective-permute-start | bytes 258056 | tf_op jit(solution)/shard_map/ppermute | solution.py:866
  59.4 7.7 %collective-permute-start.18 = (bf16[96,896]{1,0:T(8,128)(2,1)S(1)}, bf16[96,896]{1,0:T(8,128)(2,1)S(1)}, u32[]{:S(2)}, u32[]{:S(2)}) collective-permute-start(bf16[96,896]{1,0:T(8,128)(2,1)S(1)} %pad_maximum_fusion.3), channel_id=1, source_target_pairs={{0,8},{4,12},{8,0},{12,4},{16,24},{20,28},{24,16},{28,20},{1,9},{5... | collective-permute-start | bytes 516104 | tf_op jit(solution)/shard_map/ppermute | solution.py:866
  63.0 13.7 %collective-permute-start.20 = (bf16[3,96,768]{2,1,0:T(8,128)(2,1)S(1)}, bf16[3,96,768]{2,1,0:T(8,128)(2,1)S(1)}, u32[]{:S(2)}, u32[]{:S(2)}) collective-permute-start(bf16[3,96,768]{2,1,0:T(8,128)(2,1)S(1)} %away_kernel.1), channel_id=1, source_target_pairs={{0,2},{1,3},{2,0},{3,1},{4,6},{5,7},{6,4},{7,5},{8,10},{9,11},{10,... | collective-permute-start | bytes 1327112 | tf_op jit(solution)/shard_map/ppermute | solution.py:866
  64.7 12.0 %collective-permute-start.21 = (bf16[48,1536]{1,0:T(8,128)(2,1)S(1)}, bf16[48,1536]{1,0:T(8,128)(2,1)S(1)}, u32[]{:S(2)}, u32[]{:S(2)}) collective-permute-start(bf16[48,1536]{1,0:T(8,128)(2,1)S(1)} %get-tuple-element.207), channel_id=1, source_target_pairs={{0,16},{4,20},{8,24},{12,28},{16,0},{20,4},{24,8},{28,12},{1,17},{... | collective-permute-start | bytes 442376 | tf_op jit(solution)/shard_map/ppermute | solution.py:866
  67.1 10.8 %collective-permute-start.19 = (bf16[192,896]{1,0:T(8,128)(2,1)S(1)}, bf16[192,896]{1,0:T(8,128)(2,1)S(1)}, u32[]{:S(2)}, u32[]{:S(2)}) collective-permute-start(bf16[192,896]{1,0:T(8,128)(2,1)S(1)} %pad_maximum_fusion.1), channel_id=1, source_target_pairs={{0,4},{4,0},{8,12},{12,8},{16,20},{20,16},{24,28},{28,24},{1,5},{5... | collective-permute-start | bytes 1032200 | tf_op jit(solution)/shard_map/ppermute | solution.py:866
  78.0 7.5 %collective-permute-start.23 = (bf16[96,1536]{1,0:T(8,128)(2,1)S(1)}, bf16[96,1536]{1,0:T(8,128)(2,1)S(1)}, u32[]{:S(2)}, u32[]{:S(2)}) collective-permute-start(bf16[96,1536]{1,0:T(8,128)(2,1)S(1)} %pad_maximum_fusion.2), channel_id=1, source_target_pairs={{0,8},{4,12},{8,0},{12,4},{16,24},{20,28},{24,16},{28,20},{1,9},{5... | collective-permute-start | bytes 884744 | tf_op jit(solution)/shard_map/ppermute | solution.py:866
  78.4 19.0 %collective-permute-start.27 = (bf16[384,896]{1,0:T(8,128)(2,1)S(1)}, bf16[384,896]{1,0:T(8,128)(2,1)S(1)}, u32[]{:S(2)}, u32[]{:S(2)}) collective-permute-start(bf16[384,896]{1,0:T(8,128)(2,1)S(1)} %constant_dynamic-update-slice_fusion.rows.c_own), channel_id=1, source_target_pairs={{0,1},{1,0},{2,3},{3,2},{4,5},{5,4},{6,7},{7,6},{8,9},{9,8},{10,11... | collective-permute-start | bytes 2064392 | tf_op jit(solution)/shard_map/ppermute | solution.py:866
  83.5 1.6 %collective-permute-start.22 = (f32[16,768]{1,0:T(8,128)S(1)}, f32[16,768]{1,0:T(8,128)S(1)}, u32[]{:S(2)}, u32[]{:S(2)}) collective-permute-start(f32[16,768]{1,0:T(8,128)S(1)} %key_sum_kernel.1), channel_id=1, source_target_pairs={{0,1},{1,0},{2,3},{3,2},{4,5},{5,4},{6,7},{7,6},{8,9},{9,8},{10,11... | collective-permute-start | bytes 147464 | tf_op jit(solution)/shard_map/ppermute | solution.py:866
  85.0 12.3 %collective-permute-start.26 = (bf16[192,768]{1,0:T(8,128)(2,1)S(1)}, bf16[192,768]{1,0:T(8,128)(2,1)S(1)}, u32[]{:S(2)}, u32[]{:S(2)}) collective-permute-start(bf16[192,768]{1,0:T(8,128)(2,1)S(1)} %value_kernel.1), channel_id=1, source_target_pairs={{0,4},{4,0},{8,12},{12,8},{16,20},{20,16},{24,28},{28,24},{1,5},{5... | collective-permute-start | bytes 884744 | tf_op jit(solution)/shard_map/ppermute | solution.py:866
  85.5 6.7 %collective-permute-start.24 = (f32[16,768]{1,0:T(8,128)S(1)}, f32[16,768]{1,0:T(8,128)S(1)}, u32[]{:S(2)}, u32[]{:S(2)}) collective-permute-start(f32[16,768]{1,0:T(8,128)S(1)} %add.40), channel_id=1, source_target_pairs={{0,16},{4,20},{8,24},{12,28},{16,0},{20,4},{24,8},{28,12},{1,17},{... | collective-permute-start | bytes 147464 | tf_op jit(solution)/shard_map/ppermute | solution.py:866
  92.2 5.1 %collective-permute-start.25 = (f32[16,768]{1,0:T(8,128)S(1)}, f32[16,768]{1,0:T(8,128)S(1)}, u32[]{:S(2)}, u32[]{:S(2)}) collective-permute-start(f32[16,768]{1,0:T(8,128)S(1)} %add.41), channel_id=1, source_target_pairs={{0,8},{4,12},{8,0},{12,4},{16,24},{20,28},{24,16},{28,20},{1,9},{5... | collective-permute-start | bytes 147464 | tf_op jit(solution)/shard_map/ppermute | solution.py:866
  94.0 15.5 %collective-permute-start.30 = (bf16[192,1536]{1,0:T(8,128)(2,1)S(1)}, bf16[192,1536]{1,0:T(8,128)(2,1)S(1)}, u32[]{:S(2)}, u32[]{:S(2)}) collective-permute-start(bf16[192,1536]{1,0:T(8,128)(2,1)S(1)} %pad_maximum_fusion), channel_id=1, source_target_pairs={{0,4},{4,0},{8,12},{12,8},{16,20},{20,16},{24,28},{28,24},{1,5},{5... | collective-permute-start | bytes 1769480 | tf_op jit(solution)/shard_map/ppermute | solution.py:866
  97.4 12.2 %collective-permute-start.31 = (bf16[192,768]{1,0:T(8,128)(2,1)S(1)}, bf16[192,768]{1,0:T(8,128)(2,1)S(1)}, u32[]{:S(2)}, u32[]{:S(2)}) collective-permute-start(bf16[192,768]{1,0:T(8,128)(2,1)S(1)} %add_convert_fusion.1), channel_id=1, source_target_pairs={{0,8},{4,12},{8,0},{12,4},{16,24},{20,28},{24,16},{28,20},{1,9},{5... | collective-permute-start | bytes 884744 | tf_op jit(solution)/shard_map/ppermute | solution.py:866
  98.4 4.6 %collective-permute-start.28 = (f32[16,768]{1,0:T(8,128)S(1)}, f32[16,768]{1,0:T(8,128)S(1)}, u32[]{:S(2)}, u32[]{:S(2)}) collective-permute-start(f32[16,768]{1,0:T(8,128)S(1)} %add.42), channel_id=1, source_target_pairs={{0,2},{1,3},{2,0},{3,1},{4,6},{5,7},{6,4},{7,5},{8,10},{9,11},{10,... | collective-permute-start | bytes 147464 | tf_op jit(solution)/shard_map/ppermute | solution.py:866
  103.0 6.5 %collective-permute-start.29 = (f32[16,768]{1,0:T(8,128)S(1)}, f32[16,768]{1,0:T(8,128)S(1)}, u32[]{:S(2)}, u32[]{:S(2)}) collective-permute-start(f32[16,768]{1,0:T(8,128)S(1)} %add.43.sum_a), channel_id=1, source_target_pairs={{0,4},{4,0},{8,12},{12,8},{16,20},{20,16},{24,28},{28,24},{1,5},{5... | collective-permute-start | bytes 147464 | tf_op jit(solution)/shard_map/ppermute | solution.py:866
  106.8 4.2 %copy-start.3 = (bf16[768,192]{0,1:T(8,128)(2,1)S(1)}, bf16[768,192]{0,1:T(8,128)(2,1)}, u32[]{:S(2)}) copy-start(bf16[768,192]{0,1:T(8,128)(2,1)} %param.30) | copy-start | bytes 884740
  106.9 4.1 %copy-start.4 = (bf16[768,192]{0,1:T(8,128)(2,1)S(1)}, bf16[768,192]{0,1:T(8,128)(2,1)}, u32[]{:S(2)}) copy-start(bf16[768,192]{0,1:T(8,128)(2,1)} %param.31) | copy-start | bytes 884740
  106.9 4.1 %copy-start.8 = (f32[768]{0:T(1024)S(1)}, f32[768]{0:T(1024)}, u32[]{:S(2)}) copy-start(f32[768]{0:T(1024)} %g_cross.5) | copy-start | bytes 9220
  109.6 3.7 %collective-permute-start.33 = (bf16[384,1536]{1,0:T(8,128)(2,1)S(1)}, bf16[384,1536]{1,0:T(8,128)(2,1)S(1)}, u32[]{:S(2)}, u32[]{:S(2)}) collective-permute-start(bf16[384,1536]{1,0:T(8,128)(2,1)S(1)} %constant_dynamic-update-slice_fusion.4.both_own), channel_id=1, source_target_pairs={{0,1},{1,0},{2,3},{3,2},{4,5},{5,4},{6,7},{7,6},{8,9},{9,8},{10,11... | collective-permute-start | bytes 3538952 | tf_op jit(solution)/shard_map/ppermute | solution.py:866
  109.8 16.4 %collective-permute-start.37 = (bf16[192,768]{1,0:T(8,128)(2,1)S(1)}, bf16[192,768]{1,0:T(8,128)(2,1)S(1)}, u32[]{:S(2)}, u32[]{:S(2)}) collective-permute-start(bf16[192,768]{1,0:T(8,128)(2,1)S(1)} %add_convert_fusion.value_a), channel_id=1, source_target_pairs={{0,16},{4,20},{8,24},{12,28},{16,0},{20,4},{24,8},{28,12},{1,17},{... | collective-permute-start | bytes 884744 | tf_op jit(solution)/shard_map/ppermute | solution.py:866
  112.0 1.3 collective-permute-start.32
  113.3 3.9 %collective-permute-start.34 = (f32[8,768]{1,0:T(8,128)S(1)}, f32[8,768]{1,0:T(8,128)S(1)}, u32[]{:S(2)}, u32[]{:S(2)}) collective-permute-start(f32[8,768]{1,0:T(8,128)S(1)} %add.45.part_a), channel_id=1, source_target_pairs={{0,2},{1,3},{2,0},{3,1},{4,6},{5,7},{6,4},{7,5},{8,10},{9,11},{10,... | collective-permute-start | bytes 73736 | tf_op jit(solution)/shard_map/ppermute | solution.py:866
  113.8 3.3 %copy-start.5 = (bf16[768,192]{0,1:T(8,128)(2,1)S(1)}, bf16[768,192]{0,1:T(8,128)(2,1)}, u32[]{:S(2)}) copy-start(bf16[768,192]{0,1:T(8,128)(2,1)} %param.27) | copy-start | bytes 884740
  113.8 3.3 %copy-start.6 = (bf16[192,768]{1,0:T(8,128)(2,1)S(1)}, bf16[192,768]{1,0:T(8,128)(2,1)}, u32[]{:S(2)}) copy-start(bf16[192,768]{1,0:T(8,128)(2,1)} %wos.3) | copy-start | bytes 884740
  113.8 3.3 %copy-start.9 = (f32[768]{0:T(1024)S(1)}, f32[768]{0:T(1024)}, u32[]{:S(2)}) copy-start(f32[768]{0:T(1024)} %g_self.5) | copy-start | bytes 9220
  113.8 3.3 %copy-start.12 = (bf16[768]{0:T(1024)(128)(2,1)S(1)}, bf16[768]{0:T(1024)(128)(2,1)}, u32[]{:S(2)}) copy-start(bf16[768]{0:T(1024)(128)(2,1)} %start.7) | copy-start | bytes 4612
  118.2 1.2 collective-permute-start.35
  119.4 6.8 %collective-permute-start.36 = (f32[8,768]{1,0:T(8,128)S(1)}, f32[8,768]{1,0:T(8,128)S(1)}, u32[]{:S(2)}, u32[]{:S(2)}) collective-permute-start(f32[8,768]{1,0:T(8,128)S(1)} %add.46.part_a), channel_id=1, source_target_pairs={{0,2},{1,3},{2,0},{3,1},{4,6},{5,7},{6,4},{7,5},{8,10},{9,11},{10,... | collective-permute-start | bytes 73736 | tf_op jit(solution)/shard_map/ppermute | solution.py:866

commit v8 on v7

--- a/solution.py
+++ b/solution.py
@@ -15,7 +15,7 @@
 SPAN = 2 * BLOCK
 LANES = 128
 PANELS = D // LANES
-COLUMNS = 256
+COLUMNS = 384
 PARTS = 4
 
 EPSILON = 1e-06

time: 126 us -> 126 us (level)
  starting transfers between devices: 33 us -> 35.6 us
  waiting for transfers between devices: 26.1 us -> 23.5 us
    ppermute x38, starting transfers between devices: 33 us -> 35.6 us  [swap(): return lax.ppermute(x, axis, [(i, i ^ bit) for i in range(size)])]
    ppermute x38, waiting for transfers between devices: 26.1 us -> 23.5 us  [swap(): return lax.ppermute(x, axis, [(i, i ^ bit) for i in range(size)])]
where the time goes in v8:
time: 126 us; the launch traced here: 127 us
  Pallas kernels  66.1 us (52%)
  starting transfers between devices  35.6 us (28%)
  waiting for transfers between devices  23.5 us (19%)
    pallas_call x27, Pallas kernels, plain(): pl.pallas_call(kernel, out_shape=outs, in_specs=[whole_spec(space) for sp...  60.3 us
    ppermute x38, starting transfers between devices, swap(): return lax.ppermute(x, axis, [(i, i ^ bit) for i in range(size)])  35.6 us
    ppermute x38, waiting for transfers between devices, swap(): return lax.ppermute(x, axis, [(i, i ^ bit) for i in range(size)])  23.5 us
    pallas_call x2, Pallas kernels, load(): pl.pallas_call(functools.partial(load_kernel, first, last), out_shape=plt...  5.84 us
  transfers between devices with their start and end apart: 38, of which 16 were waited for; matrix products, arithmetic and copies ran while one was open for 0% of the time, Pallas kernels for 47%

profile of v8, /device:TPU:0, one launch (start us, length us, event | category | flops | bytes accessed | tf_op | source)
XLA Modules:
  0.0 127.2 jit_solution(10493056944779485843)
XLA Ops:
  0.7 1.5 %self_kernel.1 = f32[8,768]{1,0:T(8,128)S(1)} custom-call(bf16[768]{0:T(1024)(128)(2,1)} %start.7, f32[768]{0:T(1024)} %g_self.5, bf16[192,768]{1,0:T(8,128)(2,1)} %bitcast.15, bf16[192,768]{1,0:T(8,128)(2,1)} %wos.3), custom_call_target="tpu_custom_call" | custom-call | tf_op jit(solution)/shard_map/self_kernel/pallas_call | solution.py:841
  2.6 0.8 collective-permute-done
  3.5 2.9 %collective-permute-start.1 = (f32[8,768]{1,0:T(8,128)S(1)}, f32[8,768]{1,0:T(8,128)S(1)}, u32[]{:S(2)}, u32[]{:S(2)}) collective-permute-start(f32[8,768]{1,0:T(8,128)S(1)} %add.36.since.part_a), channel_id=1, source_target_pairs={{0,2},{1,3},{2,0},{3,1},{4,6},{5,7},{6,4},{7,5},{8,10},{9,11},{10,... | collective-permute-start | bytes 73736 | tf_op jit(solution)/shard_map/ppermute | solution.py:866
  6.4 2.4 %load_kernel.2.refs_0_ = bf16[96,128,768]{2,1,0:T(8,128)(2,1)S(1)} custom-call(bf16[96,128,768]{2,1,0:T(8,128)(2,1)} %enc.5, f32[8,768]{1,0:T(8,128)S(1)} %add.36.since.part_a, s32[2]{0:T(128)S(1)} %pad_add_fusion.scal), custom_call_target="tpu_custom_call" | custom-call | tf_op jit(solution)/shard_map/load_kernel/pallas_call | solution.py:932
  8.9 1.3 %collective-permute-start.4 = (bf16[192,768]{1,0:T(8,128)(2,1)S(1)}, bf16[192,768]{1,0:T(8,128)(2,1)S(1)}, u32[]{:S(2)}, u32[]{:S(2)}) collective-permute-start(bf16[192,768]{1,0:T(8,128)(2,1)S(1)} %bitcast.17), channel_id=1, source_target_pairs={{0,2},{1,3},{2,0},{3,1},{4,6},{5,7},{6,4},{7,5},{8,10},{9,11},{10,... | collective-permute-start | bytes 884744 | tf_op jit(solution)/shard_map/ppermute | solution.py:866
  10.2 1.5 %query_kernel.1 = (f32[16,768]{1,0:T(8,128)S(1)}, f32[1,768]{1,0:T(1,128)S(1)}) custom-call(s32[2]{0:T(128)S(1)} %pad_add_fusion.scal, f32[8,768]{1,0:T(8,128)S(1)} %add.36.since.part_a, f32[8,768]{1,0:T(8,128)S(1)} %collective-permute-done.1.part_b, bf16[768]{0:T(1024)(128)(2,1)} %start.7, f32[768]{0:T(1024)} %g_cross.5, bf16[192,768]{1,0:T(8,128)(2,1)} %bitcast.11, ...), custom_call_target="tpu_custom_call" | custom-call | tf_op jit(solution)/shard_map/query_kernel/pallas_call | solution.py:841
  11.7 1.2 collective-permute-done.2
  13.0 0.9 collective-permute-start.3
  13.9 3.4 %load_kernel.3._ = bf16[96,128,768]{2,1,0:T(8,128)(2,1)S(1)} custom-call(bf16[96,128,768]{2,1,0:T(8,128)(2,1)} %enc.5, f32[16,768]{1,0:T(8,128)S(1)} %add.37.since.qa, s32[2]{0:T(128)S(1)} %pad_add_fusion.scal, bf16[96,128,768]{2,1,0:T(8,128)(2,1)S(1)} %load_kernel.2.refs_0_), custom_call_target="tpu_custom_call", output_to_operand_aliasing={{}: (3, {})} | custom-call | tf_op jit(solution)/shard_map/load_kernel/pallas_call | solution.py:932
  17.3 1.5 %collective-permute-done.3.qb = f32[16,768]{1,0:T(8,128)S(1)} collective-permute-done((f32[16,768]{1,0:T(8,128)S(1)}, f32[16,768]{1,0:T(8,128)S(1)}, u32[]{:S(2)}, u32[]{:S(2)}) %collective-permute-start.3) | collective-permute-done | bytes 49184 | tf_op jit(solution)/shard_map/ppermute | solution.py:866
  19.2 0.5 collective-permute-start.7
  19.7 8.7 %attend_kernel.1 = (bf16[96,128,768]{2,1,0:T(8,128)(2,1)S(1)}, f32[96,16,128]{2,1,0:T(8,128)S(1)}, f32[6,1536,128]{2,1,0:T(8,128)S(1)}, bf16[96,128]{1,0:T(8,128)(2,1)S(1)}) custom-call(s32[2]{0:T(128)S(1)} %pad_add_fusion.scal, s32[8]{0:T(128)S(1)} %copy-done.11, s32[384]{0:T(512)S(1)} %copy-done.15, ...), custom_call_target="tpu_custom_call", output_to_operand_aliasing={{0}: (6, {})} | custom-call | tf_op jit(solution)/shard_map/attend_kernel/pallas_call | solution.py:841
  28.4 1.8 %project_kernel.1 = (bf16[96,896]{1,0:T(8,128)(2,1)S(1)}, bf16[12,96,768]{2,1,0:T(8,128)(2,1)S(1)}, bf16[768,768]{1,0:T(8,128)(2,1)S(1)}) custom-call(s32[2]{0:T(128)S(1)} %pad_add_fusion.scal, f32[6,1536,128]{2,1,0:T(8,128)S(1)} %get-tuple-element.163.summed, bf16[96,128]{1,0:T(8,128)(2,1)S(1)} %get-tuple-element.164.extra, bf16[192,768]{1,0:T(8,128)(2,1)S(1)} %bitcast.19, ...), custom_call_target="tpu_custom_call" | custom-call | tf_op jit(solution)/shard_map/project_kernel/pallas_call | solution.py:841
  30.4 0.5 collective-permute-start.10
  30.9 0.8 collective-permute-done.8.other
  31.8 1.0 merge_kernel.1.own
  32.7 1.7 %collective-permute-start.9 = (bf16[96,896]{1,0:T(8,128)(2,1)S(1)}, bf16[96,896]{1,0:T(8,128)(2,1)S(1)}, u32[]{:S(2)}, u32[]{:S(2)}) collective-permute-start(bf16[96,896]{1,0:T(8,128)(2,1)S(1)} %merge_kernel.1.own), channel_id=1, source_target_pairs={{0,2},{1,3},{2,0},{3,1},{4,6},{5,7},{6,4},{7,5},{8,10},{9,11},{10,... | collective-permute-start | bytes 516104 | tf_op jit(solution)/shard_map/ppermute | solution.py:866
  34.5 1.6 %target_kernel.1 = (f32[24,384]{1,0:T(8,128)S(1)}, f32[24,384]{1,0:T(8,128)S(1)}, bf16[384,384]{1,0:T(8,128)(2,1)S(1)}, bf16[384,384]{1,0:T(8,128)(2,1)S(1)}) custom-call(s32[2]{0:T(128)S(1)} %pad_add_fusion.scal, s32[8]{0:T(128)S(1)} %copy-done.11, s32[24]{0:T(128)S(1)} %copy-done.17, f32[384]{0:T(512)S(1)} %copy-done.16), custom_call_target="tpu_custom_call" | custom-call | tf_op jit(solution)/shard_map/target_kernel/pallas_call | solution.py:841
  36.1 0.6 arrange_kernel.1.wo.wout
  36.8 2.4 %collective-permute-done.9.other = bf16[96,896]{1,0:T(8,128)(2,1)S(1)} collective-permute-done((bf16[96,896]{1,0:T(8,128)(2,1)S(1)}, bf16[96,896]{1,0:T(8,128)(2,1)S(1)}, u32[]{:S(2)}, u32[]{:S(2)}) %collective-permute-start.9) | collective-permute-done | bytes 172064 | tf_op jit(solution)/shard_map/ppermute | solution.py:866
  39.2 1.9 %forward_kernel.1 = (bf16[48,768]{1,0:T(8,128)(2,1)S(1)}, f32[96,768]{1,0:T(8,128)S(1)}, f32[96,128]{1,0:T(8,128)S(1)}, f32[96,768]{1,0:T(8,128)S(1)}, f32[96,76...) custom-call(s32[2]{0:T(128)S(1)} %pad_add_fusion.scal, bf16[96,896]{1,0:T(8,128)(2,1)S(1)} %merge_kernel.1.own, ...), custom_call_target="tpu_custom_call" | custom-call | tf_op jit(solution)/shard_map/forward_kernel/pallas_call | solution.py:841
  41.3 1.4 %collective-permute-done.12 = bf16[96,768]{1,0:T(8,128)(2,1)S(1)} collective-permute-done((bf16[96,768]{1,0:T(8,128)(2,1)S(1)}, bf16[96,768]{1,0:T(8,128)(2,1)S(1)}, u32[]{:S(2)}, u32[]{:S(2)}) %collective-permute-start.12) | collective-permute-done | bytes 147488 | tf_op jit(solution)/shard_map/ppermute | solution.py:866
  42.7 1.7 %collective-permute-start.13 = (bf16[96,768]{1,0:T(8,128)(2,1)S(1)}, bf16[96,768]{1,0:T(8,128)(2,1)S(1)}, u32[]{:S(2)}, u32[]{:S(2)}) collective-permute-start(bf16[96,768]{1,0:T(8,128)(2,1)S(1)} %add_convert_fusion.3.part_a), channel_id=1, source_target_pairs={{0,2},{1,3},{2,0},{3,1},{4,6},{5,7},{6,4},{7,5},{8,10},{9,11},{10,... | collective-permute-start | bytes 442376 | tf_op jit(solution)/shard_map/ppermute | solution.py:866
  44.4 0.9 share_kernel.1
  45.3 3.3 %collective-permute-done.13.part_b = bf16[96,768]{1,0:T(8,128)(2,1)S(1)} collective-permute-done((bf16[96,768]{1,0:T(8,128)(2,1)S(1)}, bf16[96,768]{1,0:T(8,128)(2,1)S(1)}, u32[]{:S(2)}, u32[]{:S(2)}) %collective-permute-start.13) | collective-permute-done | bytes 147488 | tf_op jit(solution)/shard_map/ppermute | solution.py:866
  49.1 0.9 down_kernel.1
  50.1 0.6 collective-permute-start.15
  50.6 1.0 collective-permute-done.15
  51.7 1.8 %collective-permute-start.16 = (bf16[96,768]{1,0:T(8,128)(2,1)S(1)}, bf16[96,768]{1,0:T(8,128)(2,1)S(1)}, u32[]{:S(2)}, u32[]{:S(2)}) collective-permute-start(bf16[96,768]{1,0:T(8,128)(2,1)S(1)} %add_convert_fusion.2.part_a), channel_id=1, source_target_pairs={{0,2},{1,3},{2,0},{3,1},{4,6},{5,7},{6,4},{7,5},{8,10},{9,11},{10,... | collective-permute-start | bytes 442376 | tf_op jit(solution)/shard_map/ppermute | solution.py:866
  53.4 2.6 %collective-permute-start.14 = (bf16[48,896]{1,0:T(8,128)(2,1)S(1)}, bf16[48,896]{1,0:T(8,128)(2,1)S(1)}, u32[]{:S(2)}, u32[]{:S(2)}) collective-permute-start(bf16[48,896]{1,0:T(8,128)(2,1)S(1)} %get-tuple-element.192), channel_id=1, source_target_pairs={{0,16},{4,20},{8,24},{12,28},{16,0},{20,4},{24,8},{28,12},{1,17},{... | collective-permute-start | bytes 258056 | tf_op jit(solution)/shard_map/ppermute | solution.py:866
  56.0 0.6 away_kernel.1
  56.7 1.2 collective-permute-done.16.part_b
  57.9 1.5 %context_kernel.1 = (bf16[96,768]{1,0:T(8,128)(2,1)S(1)}, bf16[48,1536]{1,0:T(8,128)(2,1)S(1)}, bf16[96,768]{1,0:T(8,128)(2,1)S(1)}, bf16[96,192]{1,0:T(8,128)(2...) custom-call(s32[2]{0:T(128)S(1)} %pad_add_fusion.scal, bf16[96,768]{1,0:T(8,128)(2,1)S(1)} %add_convert_fusion.2.part_a, ...), custom_call_target="tpu_custom_call" | custom-call | tf_op jit(solution)/shard_map/context_kernel/pallas_call | solution.py:841
  59.5 3.5 %back_kernel.2 = (bf16[96,32,128]{2,1,0:T(8,128)(2,1)S(1)}, bf16[96,16,768]{2,1,0:T(8,128)(2,1)S(1)}) custom-call(s32[2]{0:T(128)S(1)} %pad_add_fusion.scal, s32[8]{0:T(128)S(1)} %copy-done.11, bf16[96,128,768]{2,1,0:T(8,128)(2,1)S(1)} %get-tuple-element.194.enc, f32[96,16,128]{2,1,0:T(8,128)S(1)} %get-tuple-element.195.p, ...), custom_call_target="tpu_custom_call" | custom-call | tf_op jit(solution)/shard_map/back_kernel/pallas_call | solution.py:841
  63.0 1.7 %collective-permute-start.20 = (bf16[3,96,768]{2,1,0:T(8,128)(2,1)S(1)}, bf16[3,96,768]{2,1,0:T(8,128)(2,1)S(1)}, u32[]{:S(2)}, u32[]{:S(2)}) collective-permute-start(bf16[3,96,768]{2,1,0:T(8,128)(2,1)S(1)} %away_kernel.1), channel_id=1, source_target_pairs={{0,2},{1,3},{2,0},{3,1},{4,6},{5,7},{6,4},{7,5},{8,10},{9,11},{10,... | collective-permute-start | bytes 1327112 | tf_op jit(solution)/shard_map/ppermute | solution.py:866
  64.7 2.6 %collective-permute-start.21 = (bf16[48,1536]{1,0:T(8,128)(2,1)S(1)}, bf16[48,1536]{1,0:T(8,128)(2,1)S(1)}, u32[]{:S(2)}, u32[]{:S(2)}) collective-permute-start(bf16[48,1536]{1,0:T(8,128)(2,1)S(1)} %get-tuple-element.207), channel_id=1, source_target_pairs={{0,16},{4,20},{8,24},{12,28},{16,0},{20,4},{24,8},{28,12},{1,17},{... | collective-permute-start | bytes 442376 | tf_op jit(solution)/shard_map/ppermute | solution.py:866
  67.4 3.1 %collective-permute-start.19 = (bf16[192,896]{1,0:T(8,128)(2,1)S(1)}, bf16[192,896]{1,0:T(8,128)(2,1)S(1)}, u32[]{:S(2)}, u32[]{:S(2)}) collective-permute-start(bf16[192,896]{1,0:T(8,128)(2,1)S(1)} %pad_maximum_fusion.1), channel_id=1, source_target_pairs={{0,4},{4,0},{8,12},{12,8},{16,20},{20,16},{24,28},{28,24},{1,5},{5... | collective-permute-start | bytes 1032200 | tf_op jit(solution)/shard_map/ppermute | solution.py:866
  70.5 6.1 %back_kernel.3 = (bf16[96,32,128]{2,1,0:T(8,128)(2,1)S(1)}, bf16[96,16,768]{2,1,0:T(8,128)(2,1)S(1)}) custom-call(s32[2]{0:T(128)S(1)} %pad_add_fusion.scal, s32[8]{0:T(128)S(1)} %copy-done.11, bf16[96,128,768]{2,1,0:T(8,128)(2,1)S(1)} %get-tuple-element.194.enc, ...), custom_call_target="tpu_custom_call", output_to_operand_aliasing={{0}: (8, {}), {1}: (9, {})} | custom-call | tf_op jit(solution)/shard_map/back_kernel/pallas_call | solution.py:841
  76.7 1.2 collective-permute-done.19
  78.4 1.4 %list_kernel.1 = (f32[384]{0:T(512)}, f32[1,1]{1,0:T(1,128)}, f32[1,384]{1,0:T(1,128)S(1)}, f32[8,128]{1,0:T(8,128)S(1)}) custom-call(s32[2]{0:T(128)S(1)} %pad_add_fusion.scal, s32[8]{0:T(128)S(1)} %copy-done.11, bf16[384,896]{1,0:T(8,128)(2,1)S(1)} %constant_dynamic-update-slice_fusion.rows.c_own, f32[24,384]{1,0:T(8,128)S(1)} %get-tuple-element.209.targets, ...), custom_call_target="tpu_custom_call" | custom-call | tf_op jit(solution)/shard_map/list_kernel/pallas_call | solution.py:841
  79.8 3.7 %key_sum_kernel.1 = f32[16,768]{1,0:T(8,128)S(1)} custom-call(s32[2]{0:T(128)S(1)} %pad_add_fusion.scal, s32[8]{0:T(128)S(1)} %copy-done.11, f32[8,128]{1,0:T(8,128)S(1)} %get-tuple-element.234.ds, bf16[96,128,768]{2,1,0:T(8,128)(2,1)S(1)} %get-tuple-element.194.enc, bf16[96,32,128]{2,1,0:T(8,128)(2,1)S(1)} %get-tuple-element.214.dap, ...), custom_call_target="tpu_custom_call" | custom-call | tf_op jit(solution)/shard_map/key_sum_kernel/pallas_call | solution.py:841
  84.0 1.0 value_kernel.1
  85.5 3.5 %collective-permute-start.24 = (f32[16,768]{1,0:T(8,128)S(1)}, f32[16,768]{1,0:T(8,128)S(1)}, u32[]{:S(2)}, u32[]{:S(2)}) collective-permute-start(f32[16,768]{1,0:T(8,128)S(1)} %add.40), channel_id=1, source_target_pairs={{0,16},{4,20},{8,24},{12,28},{16,0},{20,4},{24,8},{28,12},{1,17},{... | collective-permute-start | bytes 147464 | tf_op jit(solution)/shard_map/ppermute | solution.py:866
  89.0 3.2 %enc_grad_kernel.3.refs_0_ = bf16[96,128,768]{2,1,0:T(8,128)(2,1)} custom-call(f32[8,128]{1,0:T(8,128)S(1)} %get-tuple-element.234.ds, f32[16,768]{1,0:T(8,128)S(1)} %add.37.since.qa, f32[16,768]{1,0:T(8,128)S(1)} %collective-permute-done.3.qb, bf16[96,32,128]{2,1,0:T(8,128)(2,1)S(1)} %get-tuple-element.214.dap, bf16[96,16,768]{2,1,0:T(8,128)(2,1)S(1)} %get-tuple-element.224.vd), custom_call_target="tpu_custom_call" | custom-call | tf_op jit(solution)/shard_map/enc_grad_kernel/pallas_call | solution.py:841
  92.2 1.8 %collective-permute-start.25 = (f32[16,768]{1,0:T(8,128)S(1)}, f32[16,768]{1,0:T(8,128)S(1)}, u32[]{:S(2)}, u32[]{:S(2)}) collective-permute-start(f32[16,768]{1,0:T(8,128)S(1)} %add.41), channel_id=1, source_target_pairs={{0,8},{4,12},{8,0},{12,4},{16,24},{20,28},{24,16},{28,20},{1,9},{5... | collective-permute-start | bytes 147464 | tf_op jit(solution)/shard_map/ppermute | solution.py:866
  94.1 3.2 %enc_grad_kernel.4.refs_0_ = bf16[96,128,768]{2,1,0:T(8,128)(2,1)} custom-call(f32[8,128]{1,0:T(8,128)S(1)} %get-tuple-element.234.ds, f32[16,768]{1,0:T(8,128)S(1)} %add.37.since.qa, f32[16,768]{1,0:T(8,128)S(1)} %collective-permute-done.3.qb, bf16[96,32,128]{2,1,0:T(8,128)(2,1)S(1)} %get-tuple-element.214.dap, ...), custom_call_target="tpu_custom_call", output_to_operand_aliasing={{}: (5, {})} | custom-call | tf_op jit(solution)/shard_map/enc_grad_kernel/pallas_call | solution.py:841
  97.4 1.0 collective-permute-start.31
  98.4 1.2 collective-permute-start.28
  99.6 3.2 %enc_grad_kernel.5 = bf16[96,128,768]{2,1,0:T(8,128)(2,1)} custom-call(f32[8,128]{1,0:T(8,128)S(1)} %get-tuple-element.234.ds, f32[16,768]{1,0:T(8,128)S(1)} %add.37.since.qa, f32[16,768]{1,0:T(8,128)S(1)} %collective-permute-done.3.qb, bf16[96,32,128]{2,1,0:T(8,128)(2,1)S(1)} %get-tuple-element.214.dap, ...), custom_call_target="tpu_custom_call", output_to_operand_aliasing={{}: (5, {})} | custom-call | tf_op jit(solution)/shard_map/enc_grad_kernel/pallas_call | solution.py:841
  102.8 1.2 collective-permute-start.29
  104.0 2.9 %weights_before_kernel.1 = (bf16[384,768]{1,0:T(8,128)(2,1)S(1)}, bf16[384,768]{1,0:T(8,128)(2,1)S(1)}, f32[384,768]{1,0:T(8,128)S(1)}, bf16[384,192]{1,0:T(8,128)(2,1)S(1)}) custom-call(s32[2]{0:T(128)S(1)} %pad_add_fusion.scal, s32[8]{0:T(128)S(1)} %copy-done.11, bf16[384,896]{1,0:T(8,128)(2,1)S(1)} %constant_dynamic-update-slice_fusion.rows.c_own, ...), custom_call_target="tpu_custom_call" | custom-call | tf_op jit(solution)/shard_map/weights_before_kernel/pallas_call | solution.py:841
  106.9 2.7 %collective-permute-done.29.sum_b = f32[16,768]{1,0:T(8,128)S(1)} collective-permute-done((f32[16,768]{1,0:T(8,128)S(1)}, f32[16,768]{1,0:T(8,128)S(1)}, u32[]{:S(2)}, u32[]{:S(2)}) %collective-permute-start.29) | collective-permute-done | bytes 49184 | tf_op jit(solution)/shard_map/ppermute | solution.py:866
  109.8 1.2 collective-permute-start.37
  111.0 1.0 key_kernel.1
  112.3 1.0 collective-permute-done.32
  113.3 0.6 collective-permute-start.34
  113.8 2.4 %grads_kernel.1 = (bf16[384,768]{1,0:T(8,128)(2,1)S(1)}, bf16[384,1536]{1,0:T(8,128)(2,1)S(1)}) custom-call(s32[2]{0:T(128)S(1)} %pad_add_fusion.scal, s32[8]{0:T(128)S(1)} %copy-done.11, f32[384,768]{1,0:T(8,128)S(1)} %get-tuple-element.252.slope, bf16[384,1536]{1,0:T(8,128)(2,1)S(1)} %constant_dynamic-update-slice_fusion.4.both_own, ...), custom_call_target="tpu_custom_call" | custom-call | tf_op jit(solution)/shard_map/grads_kernel/pallas_call | solution.py:841
  116.3 0.9 collective-permute-done.34.part_b
  117.2 1.1 hidden_kernel.1
  118.2 1.2 collective-permute-done.35
  119.4 0.7 collective-permute-start.36
  120.1 3.5 %outer_kernel.1 = (f32[768,768]{1,0:T(8,128)}, f32[768,768]{1,0:T(8,128)}, f32[192,768]{1,0:T(8,128)}, f32[192,768]{1,0:T(8,128)}, f32[192,768]{1,0:T(8,128)}, /*index=5*/f32[192,768]{1,0:T(8,128)}, f32[192,768]{1,0:T(8,128)}) custom-call(bf16[384,768]{1,0:T(8,128)(2,1)S(1)} %get-tuple-element.259.y3, bf16[384,768]{1,0:T(8,128)(2,1)S(1)} %get-tuple-element.260.dz, ...), custom_call_target="tpu_custom_call" | custom-call | tf_op jit(solution)/shard_map/outer_kernel/pallas_call | solution.py:841
  123.7 2.5 %collective-permute-done.37.value_b = bf16[192,768]{1,0:T(8,128)(2,1)S(1)} collective-permute-done((bf16[192,768]{1,0:T(8,128)(2,1)S(1)}, bf16[192,768]{1,0:T(8,128)(2,1)S(1)}, u32[]{:S(2)}, u32[]{:S(2)}) %collective-permute-start.37) | collective-permute-done | bytes 294944 | tf_op jit(solution)/shard_map/ppermute | solution.py:866
  126.2 1.0 start_kernel.1
  (102 shorter events, 4.2 us)
Async XLA Ops:
  2.2 1.3 %collective-permute-start = (f32[8,768]{1,0:T(8,128)S(1)}, f32[8,768]{1,0:T(8,128)S(1)}, u32[]{:S(2)}, u32[]{:S(2)}) collective-permute-start(f32[8,768]{1,0:T(8,128)S(1)} %self_kernel.1), channel_id=1, source_target_pairs={{0,1},{1,0},{2,3},{3,2},{4,5},{5,4},{6,7},{7,6},{8,9},{9,8},{10,11... | collective-permute-start | bytes 73736 | tf_op jit(solution)/shard_map/ppermute | solution.py:866
  3.5 5.4 %collective-permute-start.1 = (f32[8,768]{1,0:T(8,128)S(1)}, f32[8,768]{1,0:T(8,128)S(1)}, u32[]{:S(2)}, u32[]{:S(2)}) collective-permute-start(f32[8,768]{1,0:T(8,128)S(1)} %add.36.since.part_a), channel_id=1, source_target_pairs={{0,2},{1,3},{2,0},{3,1},{4,6},{5,7},{6,4},{7,5},{8,10},{9,11},{10,... | collective-permute-start | bytes 73736 | tf_op jit(solution)/shard_map/ppermute | solution.py:866
  6.4 2.5 %copy-start.7 = (bf16[768,192]{0,1:T(8,128)(2,1)S(1)}, bf16[768,192]{0,1:T(8,128)(2,1)}, u32[]{:S(2)}) copy-start(bf16[768,192]{0,1:T(8,128)(2,1)} %param.32) | copy-start | bytes 884740
  8.9 9.9 %collective-permute-start.4 = (bf16[192,768]{1,0:T(8,128)(2,1)S(1)}, bf16[192,768]{1,0:T(8,128)(2,1)S(1)}, u32[]{:S(2)}, u32[]{:S(2)}) collective-permute-start(bf16[192,768]{1,0:T(8,128)(2,1)S(1)} %bitcast.17), channel_id=1, source_target_pairs={{0,2},{1,3},{2,0},{3,1},{4,6},{5,7},{6,4},{7,5},{8,10},{9,11},{10,... | collective-permute-start | bytes 884744 | tf_op jit(solution)/shard_map/ppermute | solution.py:866
  11.7 1.3 collective-permute-start.2
  13.0 5.8 %copy-start.2 = (bf16[192,768]{1,0:T(8,128)(2,1)S(1)}, bf16[192,768]{1,0:T(8,128)(2,1)}, u32[]{:S(2)}) copy-start(bf16[192,768]{1,0:T(8,128)(2,1)} %wo_own.1) | copy-start | bytes 884740
  13.0 6.7 %copy-start.11 = (s32[8]{0:T(128)S(1)}, s32[8]{0:T(128)}, u32[]{:S(2)}) copy-start(s32[8]{0:T(128)} %sizes.15) | copy-start | bytes 100
  13.0 6.7 %copy-start.15 = (s32[384]{0:T(512)S(1)}, s32[384]{0:T(512)}, u32[]{:S(2)}) copy-start(s32[384]{0:T(512)} %lengths.1) | copy-start | bytes 4612
  13.0 5.8 %collective-permute-start.3 = (f32[16,768]{1,0:T(8,128)S(1)}, f32[16,768]{1,0:T(8,128)S(1)}, u32[]{:S(2)}, u32[]{:S(2)}) collective-permute-start(f32[16,768]{1,0:T(8,128)S(1)} %add.37.since.qa), channel_id=1, source_target_pairs={{0,2},{1,3},{2,0},{3,1},{4,6},{5,7},{6,4},{7,5},{8,10},{9,11},{10,... | collective-permute-start | bytes 147464 | tf_op jit(solution)/shard_map/ppermute | solution.py:866
  18.8 9.6 %collective-permute-start.6 = (bf16[192,768]{1,0:T(8,128)(2,1)S(1)}, bf16[192,768]{1,0:T(8,128)(2,1)S(1)}, u32[]{:S(2)}, u32[]{:S(2)}) collective-permute-start(bf16[192,768]{1,0:T(8,128)(2,1)S(1)} %copy-done.2), channel_id=1, source_target_pairs={{0,2},{1,3},{2,0},{3,1},{4,6},{5,7},{6,4},{7,5},{8,10},{9,11},{10,... | collective-permute-start | bytes 884744 | tf_op jit(solution)/shard_map/ppermute | solution.py:866
  19.2 9.2 %collective-permute-start.5 = (bf16[192,768]{1,0:T(8,128)(2,1)S(1)}, bf16[192,768]{1,0:T(8,128)(2,1)S(1)}, u32[]{:S(2)}, u32[]{:S(2)}) collective-permute-start(bf16[192,768]{1,0:T(8,128)(2,1)S(1)} %collective-permute-done.4.by2), channel_id=1, source_target_pairs={{0,1},{1,0},{2,3},{3,2},{4,5},{5,4},{6,7},{7,6},{8,9},{9,8},{10,11... | collective-permute-start | bytes 884744 | tf_op jit(solution)/shard_map/ppermute | solution.py:866
  19.2 9.3 %collective-permute-start.7 = (bf16[192,768]{1,0:T(8,128)(2,1)S(1)}, bf16[192,768]{1,0:T(8,128)(2,1)S(1)}, u32[]{:S(2)}, u32[]{:S(2)}) collective-permute-start(bf16[192,768]{1,0:T(8,128)(2,1)S(1)} %bitcast.18), channel_id=1, source_target_pairs={{0,1},{1,0},{2,3},{3,2},{4,5},{5,4},{6,7},{7,6},{8,9},{9,8},{10,11... | collective-permute-start | bytes 884744 | tf_op jit(solution)/shard_map/ppermute | solution.py:866
  28.4 6.0 %copy-start.16 = (f32[384]{0:T(512)S(1)}, f32[384]{0:T(512)}, u32[]{:S(2)}) copy-start(f32[384]{0:T(512)} %rel.1) | copy-start | bytes 4612
  28.4 6.0 %copy-start.17 = (s32[24]{0:T(128)S(1)}, s32[24]{0:T(128)}, u32[]{:S(2)}) copy-start(s32[24]{0:T(128)} %lens.1) | copy-start | bytes 292
  30.3 1.5 %collective-permute-start.8 = (bf16[96,896]{1,0:T(8,128)(2,1)S(1)}, bf16[96,896]{1,0:T(8,128)(2,1)S(1)}, u32[]{:S(2)}, u32[]{:S(2)}) collective-permute-start(bf16[96,896]{1,0:T(8,128)(2,1)S(1)} %get-tuple-element.166.own.first), channel_id=1, source_target_pairs={{0,1},{1,0},{2,3},{3,2},{4,5},{5,4},{6,7},{7,6},{8,9},{9,8},{10,11... | collective-permute-start | bytes 516104 | tf_op jit(solution)/shard_map/ppermute | solution.py:866
  30.4 5.8 %collective-permute-start.10 = (bf16[192,768]{1,0:T(8,128)(2,1)S(1)}, bf16[192,768]{1,0:T(8,128)(2,1)S(1)}, u32[]{:S(2)}, u32[]{:S(2)}) collective-permute-start(bf16[192,768]{1,0:T(8,128)(2,1)S(1)} %copy-done.2), channel_id=1, source_target_pairs={{0,1},{1,0},{2,3},{3,2},{4,5},{5,4},{6,7},{7,6},{8,9},{9,8},{10,11... | collective-permute-start | bytes 884744 | tf_op jit(solution)/shard_map/ppermute | solution.py:866
  30.9 5.3 %collective-permute-start.11 = (bf16[192,768]{1,0:T(8,128)(2,1)S(1)}, bf16[192,768]{1,0:T(8,128)(2,1)S(1)}, u32[]{:S(2)}, u32[]{:S(2)}) collective-permute-start(bf16[192,768]{1,0:T(8,128)(2,1)S(1)} %collective-permute-done.6.by2), channel_id=1, source_target_pairs={{0,1},{1,0},{2,3},{3,2},{4,5},{5,4},{6,7},{7,6},{8,9},{9,8},{10,11... | collective-permute-start | bytes 884744 | tf_op jit(solution)/shard_map/ppermute | solution.py:866
  32.7 6.5 %collective-permute-start.9 = (bf16[96,896]{1,0:T(8,128)(2,1)S(1)}, bf16[96,896]{1,0:T(8,128)(2,1)S(1)}, u32[]{:S(2)}, u32[]{:S(2)}) collective-permute-start(bf16[96,896]{1,0:T(8,128)(2,1)S(1)} %merge_kernel.1.own), channel_id=1, source_target_pairs={{0,2},{1,3},{2,0},{3,1},{4,6},{5,7},{6,4},{7,5},{8,10},{9,11},{10,... | collective-permute-start | bytes 516104 | tf_op jit(solution)/shard_map/ppermute | solution.py:866
  36.1 3.1 %copy-start = (bf16[768,768]{1,0:T(8,128)(2,1)S(1)}, bf16[768,768]{1,0:T(8,128)(2,1)}, u32[]{:S(2)}) copy-start(bf16[768,768]{1,0:T(8,128)(2,1)} %wdown.5) | copy-start | bytes 3538948
  36.1 3.1 %copy-start.1 = (bf16[768,768]{1,0:T(8,128)(2,1)S(1)}, bf16[768,768]{1,0:T(8,128)(2,1)}, u32[]{:S(2)}) copy-start(bf16[768,768]{1,0:T(8,128)(2,1)} %win.5) | copy-start | bytes 3538948
  36.1 3.1 %copy-start.10 = (f32[768]{0:T(1024)S(1)}, f32[768]{0:T(1024)}, u32[]{:S(2)}) copy-start(f32[768]{0:T(1024)} %g_ff.5) | copy-start | bytes 9220
  41.2 7.5 %copy-start.13 = (f32[768]{0:T(1024)S(1)}, f32[768]{0:T(1024)}, u32[]{:S(2)}) copy-start(f32[768]{0:T(1024)} %g_final.3) | copy-start | bytes 9220
  41.2 7.5 %copy-start.14 = (bf16[768]{0:T(1024)(128)(2,1)S(1)}, bf16[768]{0:T(1024)(128)(2,1)}, u32[]{:S(2)}) copy-start(bf16[768]{0:T(1024)(128)(2,1)} %row.3) | copy-start | bytes 4612
  41.2 1.4 %collective-permute-start.12 = (bf16[96,768]{1,0:T(8,128)(2,1)S(1)}, bf16[96,768]{1,0:T(8,128)(2,1)S(1)}, u32[]{:S(2)}, u32[]{:S(2)}) collective-permute-start(bf16[96,768]{1,0:T(8,128)(2,1)S(1)} %get-tuple-element.175), channel_id=1, source_target_pairs={{0,1},{1,0},{2,3},{3,2},{4,5},{5,4},{6,7},{7,6},{8,9},{9,8},{10,11... | collective-permute-start | bytes 442376 | tf_op jit(solution)/shard_map/ppermute | solution.py:866
  42.7 6.0 %collective-permute-start.13 = (bf16[96,768]{1,0:T(8,128)(2,1)S(1)}, bf16[96,768]{1,0:T(8,128)(2,1)S(1)}, u32[]{:S(2)}, u32[]{:S(2)}) collective-permute-start(bf16[96,768]{1,0:T(8,128)(2,1)S(1)} %add_convert_fusion.3.part_a), channel_id=1, source_target_pairs={{0,2},{1,3},{2,0},{3,1},{4,6},{5,7},{6,4},{7,5},{8,10},{9,11},{10,... | collective-permute-start | bytes 442376 | tf_op jit(solution)/shard_map/ppermute | solution.py:866
  48.6 7.4 %collective-permute-start.17 = (bf16[2,3,96,768]{3,2,1,0:T(8,128)(2,1)S(1)}, bf16[2,3,96,768]{3,2,1,0:T(8,128)(2,1)S(1)}, u32[]{:S(2)}, u32[]{:S(2)}) collective-permute-start(bf16[2,3,96,768]{3,2,1,0:T(8,128)(2,1)S(1)} %get-tuple-element.187), channel_id=1, source_target_pairs={{0,1},{1,0},{2,3},{3,2},{4,5},{5,4},{6,7},{7,6},{8,9},{9,8},{10,11... | collective-permute-start | bytes 2654216 | tf_op jit(solution)/shard_map/ppermute | solution.py:866
  50.1 1.6 %collective-permute-start.15 = (bf16[96,768]{1,0:T(8,128)(2,1)S(1)}, bf16[96,768]{1,0:T(8,128)(2,1)S(1)}, u32[]{:S(2)}, u32[]{:S(2)}) collective-permute-start(bf16[96,768]{1,0:T(8,128)(2,1)S(1)} %down_kernel.1), channel_id=1, source_target_pairs={{0,1},{1,0},{2,3},{3,2},{4,5},{5,4},{6,7},{7,6},{8,9},{9,8},{10,11... | collective-permute-start | bytes 442376 | tf_op jit(solution)/shard_map/ppermute | solution.py:866
  51.7 6.2 %collective-permute-start.16 = (bf16[96,768]{1,0:T(8,128)(2,1)S(1)}, bf16[96,768]{1,0:T(8,128)(2,1)S(1)}, u32[]{:S(2)}, u32[]{:S(2)}) collective-permute-start(bf16[96,768]{1,0:T(8,128)(2,1)S(1)} %add_convert_fusion.2.part_a), channel_id=1, source_target_pairs={{0,2},{1,3},{2,0},{3,1},{4,6},{5,7},{6,4},{7,5},{8,10},{9,11},{10,... | collective-permute-start | bytes 442376 | tf_op jit(solution)/shard_map/ppermute | solution.py:866
  53.4 5.9 %collective-permute-start.14 = (bf16[48,896]{1,0:T(8,128)(2,1)S(1)}, bf16[48,896]{1,0:T(8,128)(2,1)S(1)}, u32[]{:S(2)}, u32[]{:S(2)}) collective-permute-start(bf16[48,896]{1,0:T(8,128)(2,1)S(1)} %get-tuple-element.192), channel_id=1, source_target_pairs={{0,16},{4,20},{8,24},{12,28},{16,0},{20,4},{24,8},{28,12},{1,17},{... | collective-permute-start | bytes 258056 | tf_op jit(solution)/shard_map/ppermute | solution.py:866
  59.4 7.9 %collective-permute-start.18 = (bf16[96,896]{1,0:T(8,128)(2,1)S(1)}, bf16[96,896]{1,0:T(8,128)(2,1)S(1)}, u32[]{:S(2)}, u32[]{:S(2)}) collective-permute-start(bf16[96,896]{1,0:T(8,128)(2,1)S(1)} %pad_maximum_fusion.3), channel_id=1, source_target_pairs={{0,8},{4,12},{8,0},{12,4},{16,24},{20,28},{24,16},{28,20},{1,9},{5... | collective-permute-start | bytes 516104 | tf_op jit(solution)/shard_map/ppermute | solution.py:866
  63.0 13.7 %collective-permute-start.20 = (bf16[3,96,768]{2,1,0:T(8,128)(2,1)S(1)}, bf16[3,96,768]{2,1,0:T(8,128)(2,1)S(1)}, u32[]{:S(2)}, u32[]{:S(2)}) collective-permute-start(bf16[3,96,768]{2,1,0:T(8,128)(2,1)S(1)} %away_kernel.1), channel_id=1, source_target_pairs={{0,2},{1,3},{2,0},{3,1},{4,6},{5,7},{6,4},{7,5},{8,10},{9,11},{10,... | collective-permute-start | bytes 1327112 | tf_op jit(solution)/shard_map/ppermute | solution.py:866
  64.7 12.0 %collective-permute-start.21 = (bf16[48,1536]{1,0:T(8,128)(2,1)S(1)}, bf16[48,1536]{1,0:T(8,128)(2,1)S(1)}, u32[]{:S(2)}, u32[]{:S(2)}) collective-permute-start(bf16[48,1536]{1,0:T(8,128)(2,1)S(1)} %get-tuple-element.207), channel_id=1, source_target_pairs={{0,16},{4,20},{8,24},{12,28},{16,0},{20,4},{24,8},{28,12},{1,17},{... | collective-permute-start | bytes 442376 | tf_op jit(solution)/shard_map/ppermute | solution.py:866
  67.4 10.6 %collective-permute-start.19 = (bf16[192,896]{1,0:T(8,128)(2,1)S(1)}, bf16[192,896]{1,0:T(8,128)(2,1)S(1)}, u32[]{:S(2)}, u32[]{:S(2)}) collective-permute-start(bf16[192,896]{1,0:T(8,128)(2,1)S(1)} %pad_maximum_fusion.1), channel_id=1, source_target_pairs={{0,4},{4,0},{8,12},{12,8},{16,20},{20,16},{24,28},{28,24},{1,5},{5... | collective-permute-start | bytes 1032200 | tf_op jit(solution)/shard_map/ppermute | solution.py:866
  78.0 7.5 %collective-permute-start.23 = (bf16[96,1536]{1,0:T(8,128)(2,1)S(1)}, bf16[96,1536]{1,0:T(8,128)(2,1)S(1)}, u32[]{:S(2)}, u32[]{:S(2)}) collective-permute-start(bf16[96,1536]{1,0:T(8,128)(2,1)S(1)} %pad_maximum_fusion.2), channel_id=1, source_target_pairs={{0,8},{4,12},{8,0},{12,4},{16,24},{20,28},{24,16},{28,20},{1,9},{5... | collective-permute-start | bytes 884744 | tf_op jit(solution)/shard_map/ppermute | solution.py:866
  78.4 19.0 %collective-permute-start.27 = (bf16[384,896]{1,0:T(8,128)(2,1)S(1)}, bf16[384,896]{1,0:T(8,128)(2,1)S(1)}, u32[]{:S(2)}, u32[]{:S(2)}) collective-permute-start(bf16[384,896]{1,0:T(8,128)(2,1)S(1)} %constant_dynamic-update-slice_fusion.rows.c_own), channel_id=1, source_target_pairs={{0,1},{1,0},{2,3},{3,2},{4,5},{5,4},{6,7},{7,6},{8,9},{9,8},{10,11... | collective-permute-start | bytes 2064392 | tf_op jit(solution)/shard_map/ppermute | solution.py:866
  83.5 1.6 %collective-permute-start.22 = (f32[16,768]{1,0:T(8,128)S(1)}, f32[16,768]{1,0:T(8,128)S(1)}, u32[]{:S(2)}, u32[]{:S(2)}) collective-permute-start(f32[16,768]{1,0:T(8,128)S(1)} %key_sum_kernel.1), channel_id=1, source_target_pairs={{0,1},{1,0},{2,3},{3,2},{4,5},{5,4},{6,7},{7,6},{8,9},{9,8},{10,11... | collective-permute-start | bytes 147464 | tf_op jit(solution)/shard_map/ppermute | solution.py:866
  85.0 12.3 %collective-permute-start.26 = (bf16[192,768]{1,0:T(8,128)(2,1)S(1)}, bf16[192,768]{1,0:T(8,128)(2,1)S(1)}, u32[]{:S(2)}, u32[]{:S(2)}) collective-permute-start(bf16[192,768]{1,0:T(8,128)(2,1)S(1)} %value_kernel.1), channel_id=1, source_target_pairs={{0,4},{4,0},{8,12},{12,8},{16,20},{20,16},{24,28},{28,24},{1,5},{5... | collective-permute-start | bytes 884744 | tf_op jit(solution)/shard_map/ppermute | solution.py:866
  85.5 6.7 %collective-permute-start.24 = (f32[16,768]{1,0:T(8,128)S(1)}, f32[16,768]{1,0:T(8,128)S(1)}, u32[]{:S(2)}, u32[]{:S(2)}) collective-permute-start(f32[16,768]{1,0:T(8,128)S(1)} %add.40), channel_id=1, source_target_pairs={{0,16},{4,20},{8,24},{12,28},{16,0},{20,4},{24,8},{28,12},{1,17},{... | collective-permute-start | bytes 147464 | tf_op jit(solution)/shard_map/ppermute | solution.py:866
  92.2 5.1 %collective-permute-start.25 = (f32[16,768]{1,0:T(8,128)S(1)}, f32[16,768]{1,0:T(8,128)S(1)}, u32[]{:S(2)}, u32[]{:S(2)}) collective-permute-start(f32[16,768]{1,0:T(8,128)S(1)} %add.41), channel_id=1, source_target_pairs={{0,8},{4,12},{8,0},{12,4},{16,24},{20,28},{24,16},{28,20},{1,9},{5... | collective-permute-start | bytes 147464 | tf_op jit(solution)/shard_map/ppermute | solution.py:866
  94.0 15.5 %collective-permute-start.30 = (bf16[192,1536]{1,0:T(8,128)(2,1)S(1)}, bf16[192,1536]{1,0:T(8,128)(2,1)S(1)}, u32[]{:S(2)}, u32[]{:S(2)}) collective-permute-start(bf16[192,1536]{1,0:T(8,128)(2,1)S(1)} %pad_maximum_fusion), channel_id=1, source_target_pairs={{0,4},{4,0},{8,12},{12,8},{16,20},{20,16},{24,28},{28,24},{1,5},{5... | collective-permute-start | bytes 1769480 | tf_op jit(solution)/shard_map/ppermute | solution.py:866
  97.4 12.2 %collective-permute-start.31 = (bf16[192,768]{1,0:T(8,128)(2,1)S(1)}, bf16[192,768]{1,0:T(8,128)(2,1)S(1)}, u32[]{:S(2)}, u32[]{:S(2)}) collective-permute-start(bf16[192,768]{1,0:T(8,128)(2,1)S(1)} %add_convert_fusion.1), channel_id=1, source_target_pairs={{0,8},{4,12},{8,0},{12,4},{16,24},{20,28},{24,16},{28,20},{1,9},{5... | collective-permute-start | bytes 884744 | tf_op jit(solution)/shard_map/ppermute | solution.py:866
  98.4 4.4 %collective-permute-start.28 = (f32[16,768]{1,0:T(8,128)S(1)}, f32[16,768]{1,0:T(8,128)S(1)}, u32[]{:S(2)}, u32[]{:S(2)}) collective-permute-start(f32[16,768]{1,0:T(8,128)S(1)} %add.42), channel_id=1, source_target_pairs={{0,2},{1,3},{2,0},{3,1},{4,6},{5,7},{6,4},{7,5},{8,10},{9,11},{10,... | collective-permute-start | bytes 147464 | tf_op jit(solution)/shard_map/ppermute | solution.py:866
  102.8 6.8 %collective-permute-start.29 = (f32[16,768]{1,0:T(8,128)S(1)}, f32[16,768]{1,0:T(8,128)S(1)}, u32[]{:S(2)}, u32[]{:S(2)}) collective-permute-start(f32[16,768]{1,0:T(8,128)S(1)} %add.43.sum_a), channel_id=1, source_target_pairs={{0,4},{4,0},{8,12},{12,8},{16,20},{20,16},{24,28},{28,24},{1,5},{5... | collective-permute-start | bytes 147464 | tf_op jit(solution)/shard_map/ppermute | solution.py:866
  106.8 4.2 %copy-start.3 = (bf16[768,192]{0,1:T(8,128)(2,1)S(1)}, bf16[768,192]{0,1:T(8,128)(2,1)}, u32[]{:S(2)}) copy-start(bf16[768,192]{0,1:T(8,128)(2,1)} %param.30) | copy-start | bytes 884740
  106.9 4.1 %copy-start.4 = (bf16[768,192]{0,1:T(8,128)(2,1)S(1)}, bf16[768,192]{0,1:T(8,128)(2,1)}, u32[]{:S(2)}) copy-start(bf16[768,192]{0,1:T(8,128)(2,1)} %param.31) | copy-start | bytes 884740
  106.9 4.1 %copy-start.8 = (f32[768]{0:T(1024)S(1)}, f32[768]{0:T(1024)}, u32[]{:S(2)}) copy-start(f32[768]{0:T(1024)} %g_cross.5) | copy-start | bytes 9220
  109.6 3.7 %collective-permute-start.33 = (bf16[384,1536]{1,0:T(8,128)(2,1)S(1)}, bf16[384,1536]{1,0:T(8,128)(2,1)S(1)}, u32[]{:S(2)}, u32[]{:S(2)}) collective-permute-start(bf16[384,1536]{1,0:T(8,128)(2,1)S(1)} %constant_dynamic-update-slice_fusion.4.both_own), channel_id=1, source_target_pairs={{0,1},{1,0},{2,3},{3,2},{4,5},{5,4},{6,7},{7,6},{8,9},{9,8},{10,11... | collective-permute-start | bytes 3538952 | tf_op jit(solution)/shard_map/ppermute | solution.py:866
  109.8 16.4 %collective-permute-start.37 = (bf16[192,768]{1,0:T(8,128)(2,1)S(1)}, bf16[192,768]{1,0:T(8,128)(2,1)S(1)}, u32[]{:S(2)}, u32[]{:S(2)}) collective-permute-start(bf16[192,768]{1,0:T(8,128)(2,1)S(1)} %add_convert_fusion.value_a), channel_id=1, source_target_pairs={{0,16},{4,20},{8,24},{12,28},{16,0},{20,4},{24,8},{28,12},{1,17},{... | collective-permute-start | bytes 884744 | tf_op jit(solution)/shard_map/ppermute | solution.py:866
  112.0 1.3 collective-permute-start.32
  113.3 3.9 %collective-permute-start.34 = (f32[8,768]{1,0:T(8,128)S(1)}, f32[8,768]{1,0:T(8,128)S(1)}, u32[]{:S(2)}, u32[]{:S(2)}) collective-permute-start(f32[8,768]{1,0:T(8,128)S(1)} %add.45.part_a), channel_id=1, source_target_pairs={{0,2},{1,3},{2,0},{3,1},{4,6},{5,7},{6,4},{7,5},{8,10},{9,11},{10,... | collective-permute-start | bytes 73736 | tf_op jit(solution)/shard_map/ppermute | solution.py:866
  113.8 3.3 %copy-start.5 = (bf16[768,192]{0,1:T(8,128)(2,1)S(1)}, bf16[768,192]{0,1:T(8,128)(2,1)}, u32[]{:S(2)}) copy-start(bf16[768,192]{0,1:T(8,128)(2,1)} %param.27) | copy-start | bytes 884740
  113.8 3.3 %copy-start.6 = (bf16[192,768]{1,0:T(8,128)(2,1)S(1)}, bf16[192,768]{1,0:T(8,128)(2,1)}, u32[]{:S(2)}) copy-start(bf16[192,768]{1,0:T(8,128)(2,1)} %wos.3) | copy-start | bytes 884740
  113.8 3.3 %copy-start.9 = (f32[768]{0:T(1024)S(1)}, f32[768]{0:T(1024)}, u32[]{:S(2)}) copy-start(f32[768]{0:T(1024)} %g_self.5) | copy-start | bytes 9220
  113.8 3.3 %copy-start.12 = (bf16[768]{0:T(1024)(128)(2,1)S(1)}, bf16[768]{0:T(1024)(128)(2,1)}, u32[]{:S(2)}) copy-start(bf16[768]{0:T(1024)(128)(2,1)} %start.7) | copy-start | bytes 4612
  118.2 1.2 collective-permute-start.35
  119.4 6.8 %collective-permute-start.36 = (f32[8,768]{1,0:T(8,128)S(1)}, f32[8,768]{1,0:T(8,128)S(1)}, u32[]{:S(2)}, u32[]{:S(2)}) collective-permute-start(f32[8,768]{1,0:T(8,128)S(1)} %add.46.part_a), channel_id=1, source_target_pairs={{0,2},{1,3},{2,0},{3,1},{4,6},{5,7},{6,4},{7,5},{8,10},{9,11},{10,... | collective-permute-start | bytes 73736 | tf_op jit(solution)/shard_map/ppermute | solution.py:866
